TPU v7x, 512 devices: a whole 4x4x16 slice. The times are simulated.
512 devices in a mesh: dp: 32 (over y, x, core), prompt: 16 (over z).
Axes of the slice: x: 4, y: 4, z: 16, core: 2. Of those that a mesh axis runs over, the one named last changes fastest.
Arguments:
- queries: bfloat16 [16, 32, 256, 4096], P('prompt', 'dp'), may hold values from -27 to 27
- send_list: int32 [16, 32, 256], P('prompt', 'dp'), may hold values from 0 to 255, each once within a row
- recv_list: int32 [16, 32, 256], P('prompt', 'dp'), may hold values from 0 to 255, each once within a row
- slot_pos: int32 [16, 32, 256], P('prompt', 'dp'), may hold values from 0 to 383
- pack_seq: int32 [16, 32, 16], P('prompt', 'dp'), may hold values from 0 to 15, each once within a row
- seq_kv: bfloat16 [32, 16, 384, 1024], P('dp', 'prompt'), may hold values from -6 to 6
Outputs:
- attended: bfloat16 [16, 32, 256, 4096], P('prompt', 'dp')
Inputs may be any that keep to these rules, and one draw needn't show every extreme that they name: Each pack device's row of pack_seq names every sequence once.
All inputs are finite; a program needn't handle non-finite values.
Results may differ from a plain program's by a relative error of at most 0.0036.
Values may be sent and summed in bfloat16 or wider, within the bound.
No kernel may reach another device: no remote copies, remote signals or barrier semaphores. Data moves between devices by JAX's collectives and lax.ppermute only.
A program may use at most 128 MiB of HBM per device.

v0:
```python
import math

import jax
import jax.numpy as jnp
from jax import lax
from jax.sharding import PartitionSpec as P

HD = 128
QH = 32
KVH = 4


def attend(query_rows, seq_block, positions):
    groups = QH // KVH
    row_count = query_rows.shape[0]
    cache_len = seq_block.shape[0]
    row_pos = jnp.repeat(positions, groups)
    visible = jnp.arange(cache_len, dtype=jnp.int32)[None, :] <= row_pos[:, None]
    pieces = []
    for kv_index in range(KVH):
        query_part = query_rows[:, kv_index * groups * HD : (kv_index + 1) * groups * HD].reshape(
            row_count * groups, HD
        )
        key_part = seq_block[:, kv_index * HD : (kv_index + 1) * HD]
        value_part = seq_block[:, (KVH + kv_index) * HD : (KVH + kv_index + 1) * HD]
        scores = lax.dot_general(
            query_part, key_part, (((1,), (1,)), ((), ())), preferred_element_type=jnp.float32
        ) / math.sqrt(HD)
        scores = jnp.where(visible, scores, -jnp.inf)
        row_max = jnp.max(scores, axis=-1, keepdims=True)
        exponent = jnp.exp(scores - row_max)
        row_total = jnp.sum(exponent, axis=-1, keepdims=True)
        weights = exponent.astype(jnp.bfloat16)
        mixed = jnp.dot(weights, value_part, preferred_element_type=jnp.float32) / row_total
        pieces.append(mixed.reshape(row_count, groups * HD))
    return jnp.concatenate(pieces, axis=1)


def body(queries, send_list, recv_list, slot_pos, pack_seq, seq_kv):
    query_rows = queries[0, 0]
    row_count = query_rows.shape[0]
    dp_count = lax.axis_size("dp")
    seq_count = lax.axis_size("prompt")
    per_peer = row_count // dp_count
    group_rows = row_count // seq_count
    ordered = jnp.zeros_like(query_rows).at[send_list[0, 0]].set(query_rows)
    arrived = lax.all_to_all(
        ordered.reshape(dp_count, per_peer, -1), "dp", split_axis=0, concat_axis=0, tiled=True
    )
    arrived = arrived.reshape(row_count, -1)
    packed = jnp.zeros_like(arrived).at[recv_list[0, 0]].set(arrived)
    sequences = pack_seq[0, 0]
    grouped = packed.reshape(seq_count, group_rows, -1)
    grouped_pos = slot_pos[0, 0].reshape(seq_count, group_rows)
    local_kv = seq_kv[0]
    gathered = lax.all_gather(local_kv, "prompt", axis=0, tiled=True)

    def one_group(inputs):
        rows, pos, seq_id = inputs
        seq_block = lax.dynamic_index_in_dim(gathered, seq_id, 0, keepdims=False)
        return attend(rows, seq_block, pos)

    out_groups = lax.map(one_group, (grouped, grouped_pos, sequences))
    result = out_groups.reshape(row_count, -1)
    return result.astype(jnp.bfloat16)[None, None]


def solution(mesh):
    return jax.shard_map(
        body,
        mesh=mesh,
        in_specs=(
            P("prompt", "dp", None, None),
            P("prompt", "dp", None),
            P("prompt", "dp", None),
            P("prompt", "dp", None),
            P("prompt", "dp", None),
            P("dp", "prompt", None, None),
        ),
        out_specs=P("prompt", "dp", None, None),
        check_vma=False,
    )
```

profile of v0, /device:TPU:1, one launch (start us, length us, event | category | flops | bytes accessed | tf_op | source)
XLA Modules:
  0.0 307.7 jit_solution(9518557497496272109)
XLA Ops:
  6.5 0.7 all-gather.3.cloned.1.call-update
  7.3 0.7 compare_select_fusion
  8.1 5.0 %scatter_custom_fusion = bf16[256,4096]{1,0:T(8,128)(2,1)} fusion(s32[256]{0:T(256)S(1)} %bitcast.54, bf16[1,1,256,4096]{3,2,1,0:T(8,128)(2,1)S(1)} %copy-done, bf16[]{:T(256)} %constant.33.clone.1), kind=kCustom, calls=%fused_computation.47 | custom fusion | bytes 4194306 | tf_op jit(solution)/shard_map/scatter | solution.py:46
  13.1 11.3 %all-to-all-start = ((bf16[32,8,4096]{2,1,0:T(8,128)(2,1)}), bf16[32,8,4096]{2,1,0:T(8,128)(2,1)}, u32[]{:S(2)}, u32[]{:S(2)}) async-start(bf16[32,8,4096]{2,1,0:T(8,128)(2,1)} %bitcast.50), calls=%async_computation | async-start | bytes 4194304 | tf_op jit(solution)/shard_map/all_to_all | solution.py:47
  25.0 0.7 reduce.3
  25.8 26.6 %all-to-all-done = bf16[32,8,4096]{2,1,0:T(8,128)(2,1)} async-done(((bf16[32,8,4096]{2,1,0:T(8,128)(2,1)}), bf16[32,8,4096]{2,1,0:T(8,128)(2,1)}, u32[]{:S(2)}, u32[]{:S(2)}) %all-to-all-start) | async-done | bytes 2097184 | tf_op jit(solution)/shard_map/all_to_all | solution.py:47
  52.4 6.0 %scatter_custom_fusion.1 = bf16[256,4096]{1,0:T(8,128)(2,1)} fusion(s32[256]{0:T(256)S(1)} %bitcast.53, bf16[32,8,4096]{2,1,0:T(8,128)(2,1)} %all-to-all-done, bf16[]{:T(256)} %constant.33.clone.1), kind=kCustom, calls=%fused_computation.45 | custom fusion | bytes 4194306 | tf_op jit(solution)/shard_map/scatter | solution.py:51
  58.5 104.4 %all-gather.3.cloned.1.call-done = bf16[16,1,384,1024]{3,2,1,0:T(8,128)(2,1)} async-done(((bf16[1,1,384,1024]{3,2,1,0:T(8,128)(2,1)}), bf16[16,1,384,1024]{3,2,1,0:T(8,128)(2,1)}) %all-gather.3.cloned.1.call-update) | async-done | bytes 12582928 | tf_op jit(solution)/shard_map/all_gather | solution.py:56
  162.9 138.0 %while.10 = (s32[]{:T(128)}, bf16[16,16,4096]{2,1,0:T(8,128)(2,1)}, s32[16,16]{1,0:T(8,128)S(1)}, bf16[16,16,4096]{2,1,0:T(8,128)(2,1)}, s32[16]{0:T(128)S(1)}, ...) while((s32[]{:T(128)}, bf16[16,16,4096]{2,1,0:T(8,128)(2,1)}, ...), condition=%wide.region_11.12_spmd, body=%wide.region_2.11_spmd.sunk | while | flops 102890496 | bytes 6306135 | solution.py:63
  165.4 1.2 dynamic-slice_bitcast_fusion.5
  166.6 0.9 dynamic-slice_bitcast_fusion.4
  170.8 0.7 fusion.90
  174.0 1.2 dynamic-slice_bitcast_fusion.5
  175.2 0.9 dynamic-slice_bitcast_fusion.4
  179.4 0.7 fusion.90
  182.7 1.2 dynamic-slice_bitcast_fusion.5
  183.9 0.9 dynamic-slice_bitcast_fusion.4
  188.1 0.7 fusion.90
  191.3 1.2 dynamic-slice_bitcast_fusion.5
  192.5 0.9 dynamic-slice_bitcast_fusion.4
  199.9 1.2 dynamic-slice_bitcast_fusion.5
  201.1 0.9 dynamic-slice_bitcast_fusion.4
  205.3 0.7 fusion.90
  208.5 1.2 dynamic-slice_bitcast_fusion.5
  209.7 0.9 dynamic-slice_bitcast_fusion.4
  213.9 0.7 fusion.90
  217.2 1.2 dynamic-slice_bitcast_fusion.5
  218.4 0.9 dynamic-slice_bitcast_fusion.4
  225.8 1.2 dynamic-slice_bitcast_fusion.5
  227.0 0.9 dynamic-slice_bitcast_fusion.4
  234.4 1.2 dynamic-slice_bitcast_fusion.5
  235.6 0.9 dynamic-slice_bitcast_fusion.4
  239.8 0.7 fusion.90
  243.0 1.2 dynamic-slice_bitcast_fusion.5
  244.2 0.9 dynamic-slice_bitcast_fusion.4
  248.4 0.7 fusion.90
  251.7 1.2 dynamic-slice_bitcast_fusion.5
  252.9 0.9 dynamic-slice_bitcast_fusion.4
  260.3 1.2 dynamic-slice_bitcast_fusion.5
  261.5 0.9 dynamic-slice_bitcast_fusion.4
  268.9 1.2 dynamic-slice_bitcast_fusion.5
  270.1 0.9 dynamic-slice_bitcast_fusion.4
  277.5 1.2 dynamic-slice_bitcast_fusion.5
  278.7 0.9 dynamic-slice_bitcast_fusion.4
  286.2 1.2 dynamic-slice_bitcast_fusion.5
  287.4 0.9 dynamic-slice_bitcast_fusion.4
  294.8 1.2 dynamic-slice_bitcast_fusion.5
  296.0 0.9 dynamic-slice_bitcast_fusion.4
  (422 shorter events, 68.1 us)
Async XLA Ops:
  6.5 1.6 copy-start
  6.5 156.3 %all-gather.3.cloned.1.call-start = ((), (), s32[]{:S(2)}) async-start(), calls=%async_computation.1 | async-start | bytes 13369344 | tf_op jit(solution)/shard_map/all_gather | solution.py:56
  13.1 12.0 %copy-start.1 = (s32[1,1,256]{2,1,0:T(1,128)S(1)}, s32[1,1,256]{2,1,0:T(1,128)}, u32[]{:S(2)}) copy-start(s32[1,1,256]{2,1,0:T(1,128)} %param.11) | copy-start | bytes 3076
  13.1 12.8 %copy-start.2 = (s32[1,1,256]{2,1,0:T(1,128)S(1)}, s32[1,1,256]{2,1,0:T(1,128)}, u32[]{:S(2)}) copy-start(s32[1,1,256]{2,1,0:T(1,128)} %param.10) | copy-start | bytes 3076
  13.1 39.3 %all-to-all-start = ((bf16[32,8,4096]{2,1,0:T(8,128)(2,1)}), bf16[32,8,4096]{2,1,0:T(8,128)(2,1)}, u32[]{:S(2)}, u32[]{:S(2)}) async-start(bf16[32,8,4096]{2,1,0:T(8,128)(2,1)} %bitcast.50), calls=%async_computation | async-start | bytes 4194304 | tf_op jit(solution)/shard_map/all_to_all | solution.py:47
  52.4 110.4 %copy-start.3 = (s32[1,1,16]{2,1,0:T(1,128)S(1)}, s32[1,1,16]{2,1,0:T(1,128)}, u32[]{:S(2)}) copy-start(s32[1,1,16]{2,1,0:T(1,128)} %param.12) | copy-start | bytes 196
Sparse Core Ops, SparseCore 0:
  9.4 153.3 all-gather.2
where the time goes:
time: 309 us; the launch traced here: 308 us
  waiting for transfers between devices  132 us (43%)
  local copies, waits for them, and re-layouts  61.3 us (20%)
  matrix products  33.2 us (11%)
  loops' own time  32.4 us (10%)
  other arithmetic  24.3 us (8%)
  between operations  13.4 us (4%)
  starting transfers between devices  11.4 us (4%)
    all_gather x1, waiting for transfers between devices, body(): gathered = lax.all_gather(local_kv, 'prompt', axis=0, tiled=True)  104 us
    another operation x1, loops' own time, body(): out_groups = lax.map(one_group, (grouped, grouped_pos, sequences))  32.4 us
    all_to_all x1, waiting for transfers between devices, body(): lax.all_to_all(ordered.reshape(dp_count, per_peer, -1), 'dp', split_axis=...  26.6 us
    squeeze x16, local copies, waits for them, and re-layouts, one_group(): seq_block = lax.dynamic_index_in_dim(gathered, seq_id, 0, keepdims=False)  19 us
    dot_general x64, matrix products, attend(): lax.dot_general(query_part, key_part, (((1,), (1,)), ((), ())), preferred...  17.6 us
    dot_general x64, matrix products, attend(): jnp.dot(weights, value_part, preferred_element_type=jnp.float32) / row_total  15.7 us
    squeeze x32, local copies, waits for them, and re-layouts, body(): out_groups = lax.map(one_group, (grouped, grouped_pos, sequences))  14.9 us
    reduce_sum x64, other arithmetic, attend(): row_total = jnp.sum(exponent, axis=-1, keepdims=True)  12.2 us
  transfers between devices with their start and end apart: 2, of which 2 were waited for; matrix products, arithmetic and copies ran while one was open for 4% of the time, Pallas kernels for 0%

commit v1 on v0

v1 whole, which is shorter than its diff:
```python
import functools
import math

import jax
import jax.numpy as jnp
from jax import lax
from jax.experimental import pallas as pl
from jax.experimental.pallas import tpu as pltpu
from jax.sharding import PartitionSpec as P

HD = 128
QH = 32
KVH = 4
GROUPS = QH // KVH
SCALE = math.log2(math.e) / math.sqrt(HD)


def attend_kernel(spots, halves, prev_ref, where_ref, pos_ref, q_ref, *refs):
    del prev_ref
    n = len(spots) * halves
    blocks, out_ref, held, sems = refs[:n], refs[n], refs[n + 1], refs[n + 2]
    copies = []
    for i, spot in enumerate(spots):
        rows = q_ref.shape[0] // len(spots)
        cache_len = blocks[0].shape[0]
        limit = pos_ref[:, spot : spot + 1]
        visible = lax.broadcasted_iota(jnp.int32, (rows, cache_len), 1) <= limit
        for half in range(halves):
            block = blocks[i * halves + half]
            kv_heads = KVH // halves
            for k in range(kv_heads):
                head = half * kv_heads + k
                query = jnp.concatenate(
                    [
                        q_ref[i * rows : (i + 1) * rows, (head * GROUPS + g) * HD : (head * GROUPS + g + 1) * HD]
                        for g in range(GROUPS)
                    ],
                    axis=0,
                )
                scores = lax.dot_general(
                    query,
                    block[:, k * HD : (k + 1) * HD],
                    (((1,), (1,)), ((), ())),
                    preferred_element_type=jnp.float32,
                ).reshape(GROUPS, rows, cache_len)
                scores = jnp.where(visible[None], scores, -jnp.inf)
                row_max = jnp.max(scores, axis=-1, keepdims=True)
                exponent = jnp.exp2((scores - row_max) * SCALE)
                row_total = jnp.sum(exponent, axis=-1, keepdims=True)
                weights = exponent.astype(jnp.bfloat16).reshape(GROUPS * rows, cache_len)
                mixed = jnp.dot(
                    weights,
                    block[:, (kv_heads + k) * HD : (kv_heads + k + 1) * HD],
                    preferred_element_type=jnp.float32,
                ).reshape(GROUPS, rows, HD)
                mixed = (mixed / row_total).astype(jnp.bfloat16)
                for g in range(GROUPS):
                    held[i, :, (head * GROUPS + g) * HD : (head * GROUPS + g + 1) * HD] = mixed[g]
        start = pl.multiple_of(where_ref[spot] * rows, rows)
        copy = pltpu.make_async_copy(held.at[i], out_ref.at[pl.ds(start, rows), :], sems.at[i])
        copy.start()
        copies.append(copy)
    for copy in copies:
        copy.wait()


def attend(prev, where, pos, queries, spots, blocks, first):
    rows = 16
    halves = len(blocks) // len(spots)
    width = queries.shape[1]
    vmem = pl.BlockSpec(memory_space=pltpu.VMEM)
    q_block = spots[0] // len(spots)
    body = functools.partial(attend_kernel, spots, halves)
    in_specs = [pl.BlockSpec(memory_space=pl.ANY), pl.BlockSpec(memory_space=pltpu.SMEM), vmem]
    in_specs += [pl.BlockSpec((rows * len(spots), width), lambda _: (q_block, 0))]
    in_specs += [pl.BlockSpec(b.shape, lambda _: (0, 0)) for b in blocks]
    args = [prev, where, pos, queries, *blocks]
    if first:
        del in_specs[0], args[0]
        inner = body

        def body(*refs):
            inner(None, *refs)

    cache_len = blocks[0].shape[0]
    work = rows * len(spots) * QH * cache_len
    return pl.pallas_call(
        body,
        grid=(1,),
        out_shape=jax.ShapeDtypeStruct(queries.shape, queries.dtype),
        in_specs=in_specs,
        out_specs=pl.BlockSpec(memory_space=pl.ANY),
        scratch_shapes=[
            pltpu.VMEM((len(spots), rows, width), jnp.bfloat16),
            pltpu.SemaphoreType.DMA((len(spots),)),
        ],
        input_output_aliases={} if first else {0: 0},
        compiler_params=pltpu.CompilerParams(vmem_limit_bytes=24 * 2**20),
        cost_estimate=pl.CostEstimate(
            flops=4 * work * HD, bytes_accessed=8 * 2**20, transcendentals=work
        ),
        name="attend_%d" % spots[0],
    )(*args)


def move_rows(targets, rows):
    count = rows.shape[0]
    pick = (jnp.arange(count, dtype=jnp.int32)[:, None] == targets[None, :]).astype(rows.dtype)
    return jnp.dot(pick, rows, preferred_element_type=jnp.float32).astype(rows.dtype)


def body(queries, send_list, recv_list, slot_pos, pack_seq, seq_kv):
    query_rows = queries[0, 0]
    row_count, width = query_rows.shape
    dp_count = lax.axis_size("dp")
    ring = lax.axis_size("prompt")
    group_rows = row_count // ring
    me = lax.axis_index("prompt")
    kv = seq_kv[0, 0]

    span = KVH * HD
    own = [
        jnp.concatenate([kv[:, lo : lo + span // 2], kv[:, span + lo : span + lo + span // 2]], axis=1)
        for lo in (0, span // 2)
    ]
    forward = [(i, (i + 1) % ring) for i in range(ring)]
    backward = [(i, (i - 1) % ring) for i in range(ring)]
    up, down = list(own), list(own)
    arrived_kv = []
    for step in range(ring // 2):
        for half in range(2):
            up[half] = lax.ppermute(up[half], "prompt", forward)
            if step < ring // 2 - 1:
                down[half] = lax.ppermute(down[half], "prompt", backward)
        arrived_kv.append((tuple(up), tuple(down)))

    ordered = move_rows(send_list[0, 0], query_rows)
    arrived = lax.all_to_all(
        ordered.reshape(dp_count, row_count // dp_count, width), "dp", split_axis=0, concat_axis=0, tiled=True
    ).reshape(row_count, width)

    sequences = pack_seq[0, 0]
    behind = (me - sequences) % ring
    half_way = ring // 2
    place = jnp.where(
        behind == 0,
        ring - 1,
        jnp.where(behind <= half_way, 2 * (behind - 1), 2 * (ring - behind - 1) + 1),
    )
    spots = jnp.arange(ring, dtype=jnp.int32)
    at_place = place[None, :] == spots[:, None]
    where = jnp.sum(jnp.where(at_place, spots[None, :], 0), axis=1)
    grouped_pos = slot_pos[0, 0].reshape(ring, group_rows)
    pos = jnp.sum(jnp.where(at_place[:, :, None], grouped_pos[None], 0), axis=1).T
    slot = recv_list[0, 0]
    of_group = (slot // group_rows)[:, None] == spots[None, :]
    target = jnp.sum(jnp.where(of_group, place[None, :], 0), axis=1) * group_rows + slot % group_rows
    packed = move_rows(target, arrived)

    out = attend(None, where, pos, packed, (ring - 1,), own, True)
    for step in range(ring // 2):
        up, down = arrived_kv[step]
        if step < ring // 2 - 1:
            out = attend(out, where, pos, packed, (2 * step, 2 * step + 1), (*up, *down), False)
        else:
            out = attend(out, where, pos, packed, (2 * step,), up, False)
    return out[None, None]


def solution(mesh):
    return jax.shard_map(
        body,
        mesh=mesh,
        in_specs=(
            P("prompt", "dp", None, None),
            P("prompt", "dp", None),
            P("prompt", "dp", None),
            P("prompt", "dp", None),
            P("prompt", "dp", None),
            P("dp", "prompt", None, None),
        ),
        out_specs=P("prompt", "dp", None, None),
        check_vma=False,
    )
```

time: 309 us -> 187 us (0.61)
  the two profiles are of different devices: /device:TPU:1 before, /device:TPU:2 now
where the time goes in v1:
time: 187 us; the launch traced here: 185 us
  starting transfers between devices  114 us (61%)
  Pallas kernels  34.7 us (19%)
  waiting for transfers between devices  27.9 us (15%)
  matrix products  4.34 us (2%)
  local copies, waits for them, and re-layouts  2.87 us (2%)
    ppermute x14, starting transfers between devices, body(): down[half] = lax.ppermute(down[half], 'prompt', backward)  68.5 us
    ppermute x16, starting transfers between devices, body(): up[half] = lax.ppermute(up[half], 'prompt', forward)  37.5 us
    pallas_call x9, Pallas kernels, attend(): pl.pallas_call(body, grid=(1,), out_shape=jax.ShapeDtypeStruct(queries.sh...  34.7 us
    ppermute x16, waiting for transfers between devices, body(): up[half] = lax.ppermute(up[half], 'prompt', forward)  20.7 us
    all_to_all x1, starting transfers between devices, body(): lax.all_to_all(ordered.reshape(dp_count, row_count // dp_count, width), '...  7.81 us
    ppermute x14, waiting for transfers between devices, body(): down[half] = lax.ppermute(down[half], 'prompt', backward)  7.15 us
    dot_general x2, matrix products, move_rows(): jnp.dot(pick, rows, preferred_element_type=jnp.float32).astype(rows.dtype)  4.34 us
  transfers between devices with their start and end apart: 31, of which 10 were waited for; matrix products, arithmetic and copies ran while one was open for 3% of the time, Pallas kernels for 17%

profile of v1, /device:TPU:2, one launch (start us, length us, event | category | flops | bytes accessed | tf_op | source)
XLA Modules:
  0.0 185.3 jit_solution(9000246030128959979)
XLA Ops:
  1.5 3.8 %collective-permute-start = (bf16[384,512]{1,0:T(8,128)(2,1)S(1)}, bf16[384,512]{1,0:T(8,128)(2,1)S(1)}, u32[]{:S(2)}, u32[]{:S(2)}) collective-permute-start(bf16[384,512]{1,0:T(8,128)(2,1)S(1)} %pad_maximum_fusion.refs_3_), channel_id=1, source_target_pairs={{0,1},{1,2},{2,3},{3,4},{4,5},{5,6},{6,7},{7,8},{8,9},{9,10},{10,1... | collective-permute-start | bytes 1179656 | tf_op jit(solution)/shard_map/ppermute | solution.py:132
  5.3 3.8 %collective-permute-start.1 = (bf16[384,512]{1,0:T(8,128)(2,1)S(1)}, bf16[384,512]{1,0:T(8,128)(2,1)S(1)}, u32[]{:S(2)}, u32[]{:S(2)}) collective-permute-start(bf16[384,512]{1,0:T(8,128)(2,1)S(1)} %pad_maximum_fusion.1.refs_4_), channel_id=1, source_target_pairs={{0,1},{1,2},{2,3},{3,4},{4,5},{5,6},{6,7},{7,8},{8,9},{9,10},{10,1... | collective-permute-start | bytes 1179656 | tf_op jit(solution)/shard_map/ppermute | solution.py:132
  9.2 7.6 %collective-permute-start.2 = (bf16[384,512]{1,0:T(8,128)(2,1)S(1)}, bf16[384,512]{1,0:T(8,128)(2,1)}, u32[]{:S(2)}, u32[]{:S(2)}) collective-permute-start(bf16[384,512]{1,0:T(8,128)(2,1)S(1)} %pad_maximum_fusion.refs_3_), channel_id=1, source_target_pairs={{0,15},{1,0},{2,1},{3,2},{4,3},{5,4},{6,5},{7,6},{8,7},{9,8},{10,9... | collective-permute-start | bytes 1179656 | tf_op jit(solution)/shard_map/ppermute | solution.py:134
  16.8 3.9 %collective-permute-start.3 = (bf16[384,512]{1,0:T(8,128)(2,1)S(1)}, bf16[384,512]{1,0:T(8,128)(2,1)}, u32[]{:S(2)}, u32[]{:S(2)}) collective-permute-start(bf16[384,512]{1,0:T(8,128)(2,1)S(1)} %pad_maximum_fusion.1.refs_4_), channel_id=1, source_target_pairs={{0,15},{1,0},{2,1},{3,2},{4,3},{5,4},{6,5},{7,6},{8,7},{9,8},{10,9... | collective-permute-start | bytes 1179656 | tf_op jit(solution)/shard_map/ppermute | solution.py:134
  20.7 2.1 %collective-permute-done.refs_0_ = bf16[384,512]{1,0:T(8,128)(2,1)S(1)} collective-permute-done((bf16[384,512]{1,0:T(8,128)(2,1)S(1)}, bf16[384,512]{1,0:T(8,128)(2,1)S(1)}, u32[]{:S(2)}, u32[]{:S(2)}) %collective-permute-start) | collective-permute-done | bytes 393248 | tf_op jit(solution)/shard_map/ppermute | solution.py:132
  22.8 1.9 %collective-permute-start.4 = (bf16[384,512]{1,0:T(8,128)(2,1)S(1)}, bf16[384,512]{1,0:T(8,128)(2,1)}, u32[]{:S(2)}, u32[]{:S(2)}) collective-permute-start(bf16[384,512]{1,0:T(8,128)(2,1)S(1)} %collective-permute-done.refs_0_), channel_id=1, source_target_pairs={{0,1},{1,2},{2,3},{3,4},{4,5},{5,6},{6,7},{7,8},{8,9},{9,10},{10,1... | collective-permute-start | bytes 1179656 | tf_op jit(solution)/shard_map/ppermute | solution.py:132
  24.7 6.5 %collective-permute-done.1.refs_1_ = bf16[384,512]{1,0:T(8,128)(2,1)S(1)} collective-permute-done((bf16[384,512]{1,0:T(8,128)(2,1)S(1)}, bf16[384,512]{1,0:T(8,128)(2,1)S(1)}, u32[]{:S(2)}, u32[]{:S(2)}) %collective-permute-start.1) | collective-permute-done | bytes 393248 | tf_op jit(solution)/shard_map/ppermute | solution.py:132
  31.2 1.9 %collective-permute-start.5 = (bf16[384,512]{1,0:T(8,128)(2,1)S(1)}, bf16[384,512]{1,0:T(8,128)(2,1)}, u32[]{:S(2)}, u32[]{:S(2)}) collective-permute-start(bf16[384,512]{1,0:T(8,128)(2,1)S(1)} %collective-permute-done.1.refs_1_), channel_id=1, source_target_pairs={{0,1},{1,2},{2,3},{3,4},{4,5},{5,6},{6,7},{7,8},{8,9},{9,10},{10,1... | collective-permute-start | bytes 1179656 | tf_op jit(solution)/shard_map/ppermute | solution.py:132
  33.9 5.1 %collective-permute-start.6 = (bf16[384,512]{1,0:T(8,128)(2,1)}, bf16[384,512]{1,0:T(8,128)(2,1)}, u32[]{:S(2)}, u32[]{:S(2)}) collective-permute-start(bf16[384,512]{1,0:T(8,128)(2,1)} %collective-permute-done.2.refs_2_), channel_id=1, source_target_pairs={{0,15},{1,0},{2,1},{3,2},{4,3},{5,4},{6,5},{7,6},{8,7},{9,8},{10,9... | collective-permute-start | bytes 1179656 | tf_op jit(solution)/shard_map/ppermute | solution.py:134
  39.1 2.8 %collective-permute-start.7 = (bf16[384,512]{1,0:T(8,128)(2,1)}, bf16[384,512]{1,0:T(8,128)(2,1)}, u32[]{:S(2)}, u32[]{:S(2)}) collective-permute-start(bf16[384,512]{1,0:T(8,128)(2,1)} %collective-permute-done.3.refs_3_), channel_id=1, source_target_pairs={{0,15},{1,0},{2,1},{3,2},{4,3},{5,4},{6,5},{7,6},{8,7},{9,8},{10,9... | collective-permute-start | bytes 1179656 | tf_op jit(solution)/shard_map/ppermute | solution.py:134
  41.8 3.1 %collective-permute-start.8 = (bf16[384,512]{1,0:T(8,128)(2,1)}, bf16[384,512]{1,0:T(8,128)(2,1)}, u32[]{:S(2)}, u32[]{:S(2)}) collective-permute-start(bf16[384,512]{1,0:T(8,128)(2,1)} %collective-permute-done.4.refs_0_), channel_id=1, source_target_pairs={{0,1},{1,2},{2,3},{3,4},{4,5},{5,6},{6,7},{7,8},{8,9},{9,10},{10,1... | collective-permute-start | bytes 1179656 | tf_op jit(solution)/shard_map/ppermute | solution.py:132
  44.9 3.3 %collective-permute-done.5.refs_1_ = bf16[384,512]{1,0:T(8,128)(2,1)} collective-permute-done((bf16[384,512]{1,0:T(8,128)(2,1)S(1)}, bf16[384,512]{1,0:T(8,128)(2,1)}, u32[]{:S(2)}, u32[]{:S(2)}) %collective-permute-start.5) | collective-permute-done | bytes 393248 | tf_op jit(solution)/shard_map/ppermute | solution.py:132
  50.1 2.0 %fusion = bf16[32,8,4096]{2,1,0:T(8,128)(2,1)} fusion(bf16[1,1,256,4096]{3,2,1,0:T(8,128)(2,1)S(1)} %copy-done, s32[256]{0:T(256)S(1)} %bitcast.27), kind=kOutput, calls=%fused_computation.2 | convolution fusion | flops 537985024 | bytes 4195328 | tf_op jit(solution)/shard_map/dot_general | solution.py:109
  52.2 7.8 %all-to-all-start = ((bf16[32,8,4096]{2,1,0:T(8,128)(2,1)}), bf16[32,8,4096]{2,1,0:T(8,128)(2,1)}, u32[]{:S(2)}, u32[]{:S(2)}) async-start(bf16[32,8,4096]{2,1,0:T(8,128)(2,1)} %fusion), calls=%async_computation | async-start | bytes 4194304 | tf_op jit(solution)/shard_map/all_to_all | solution.py:138
  60.0 5.1 %collective-permute-start.10 = (bf16[384,512]{1,0:T(8,128)(2,1)}, bf16[384,512]{1,0:T(8,128)(2,1)}, u32[]{:S(2)}, u32[]{:S(2)}) collective-permute-start(bf16[384,512]{1,0:T(8,128)(2,1)} %collective-permute-done.6.refs_2_), channel_id=1, source_target_pairs={{0,15},{1,0},{2,1},{3,2},{4,3},{5,4},{6,5},{7,6},{8,7},{9,8},{10,9... | collective-permute-start | bytes 1179656 | tf_op jit(solution)/shard_map/ppermute | solution.py:134
  65.1 2.7 %collective-permute-start.11 = (bf16[384,512]{1,0:T(8,128)(2,1)}, bf16[384,512]{1,0:T(8,128)(2,1)}, u32[]{:S(2)}, u32[]{:S(2)}) collective-permute-start(bf16[384,512]{1,0:T(8,128)(2,1)} %collective-permute-done.7.refs_3_), channel_id=1, source_target_pairs={{0,15},{1,0},{2,1},{3,2},{4,3},{5,4},{6,5},{7,6},{8,7},{9,8},{10,9... | collective-permute-start | bytes 1179656 | tf_op jit(solution)/shard_map/ppermute | solution.py:134
  67.9 3.1 %collective-permute-start.12 = (bf16[384,512]{1,0:T(8,128)(2,1)}, bf16[384,512]{1,0:T(8,128)(2,1)}, u32[]{:S(2)}, u32[]{:S(2)}) collective-permute-start(bf16[384,512]{1,0:T(8,128)(2,1)} %collective-permute-done.8.refs_0_), channel_id=1, source_target_pairs={{0,1},{1,2},{2,3},{3,4},{4,5},{5,6},{6,7},{7,8},{8,9},{9,10},{10,1... | collective-permute-start | bytes 1179656 | tf_op jit(solution)/shard_map/ppermute | solution.py:132
  71.0 1.9 %collective-permute-start.13 = (bf16[384,512]{1,0:T(8,128)(2,1)}, bf16[384,512]{1,0:T(8,128)(2,1)}, u32[]{:S(2)}, u32[]{:S(2)}) collective-permute-start(bf16[384,512]{1,0:T(8,128)(2,1)} %collective-permute-done.9.refs_1_), channel_id=1, source_target_pairs={{0,1},{1,2},{2,3},{3,4},{4,5},{5,6},{6,7},{7,8},{8,9},{9,10},{10,1... | collective-permute-start | bytes 1179656 | tf_op jit(solution)/shard_map/ppermute | solution.py:132
  73.0 1.9 %collective-permute-done.10.refs_2_ = bf16[384,512]{1,0:T(8,128)(2,1)} collective-permute-done((bf16[384,512]{1,0:T(8,128)(2,1)}, bf16[384,512]{1,0:T(8,128)(2,1)}, u32[]{:S(2)}, u32[]{:S(2)}) %collective-permute-start.10) | collective-permute-done | bytes 393248 | tf_op jit(solution)/shard_map/ppermute | solution.py:134
  74.9 5.6 %collective-permute-start.14 = (bf16[384,512]{1,0:T(8,128)(2,1)}, bf16[384,512]{1,0:T(8,128)(2,1)}, u32[]{:S(2)}, u32[]{:S(2)}) collective-permute-start(bf16[384,512]{1,0:T(8,128)(2,1)} %collective-permute-done.10.refs_2_), channel_id=1, source_target_pairs={{0,15},{1,0},{2,1},{3,2},{4,3},{5,4},{6,5},{7,6},{8,7},{9,8},{10,9... | collective-permute-start | bytes 1179656 | tf_op jit(solution)/shard_map/ppermute | solution.py:134
  80.5 2.8 %collective-permute-done.11.refs_3_ = bf16[384,512]{1,0:T(8,128)(2,1)} collective-permute-done((bf16[384,512]{1,0:T(8,128)(2,1)}, bf16[384,512]{1,0:T(8,128)(2,1)}, u32[]{:S(2)}, u32[]{:S(2)}) %collective-permute-start.11) | collective-permute-done | bytes 393248 | tf_op jit(solution)/shard_map/ppermute | solution.py:134
  83.3 5.6 %collective-permute-start.15 = (bf16[384,512]{1,0:T(8,128)(2,1)}, bf16[384,512]{1,0:T(8,128)(2,1)}, u32[]{:S(2)}, u32[]{:S(2)}) collective-permute-start(bf16[384,512]{1,0:T(8,128)(2,1)} %collective-permute-done.11.refs_3_), channel_id=1, source_target_pairs={{0,15},{1,0},{2,1},{3,2},{4,3},{5,4},{6,5},{7,6},{8,7},{9,8},{10,9... | collective-permute-start | bytes 1179656 | tf_op jit(solution)/shard_map/ppermute | solution.py:134
  88.9 1.9 %collective-permute-start.16 = (bf16[384,512]{1,0:T(8,128)(2,1)}, bf16[384,512]{1,0:T(8,128)(2,1)}, u32[]{:S(2)}, u32[]{:S(2)}) collective-permute-start(bf16[384,512]{1,0:T(8,128)(2,1)} %collective-permute-done.12.refs_0_), channel_id=1, source_target_pairs={{0,1},{1,2},{2,3},{3,4},{4,5},{5,6},{6,7},{7,8},{8,9},{9,10},{10,1... | collective-permute-start | bytes 1179656 | tf_op jit(solution)/shard_map/ppermute | solution.py:132
  90.9 1.9 %collective-permute-start.17 = (bf16[384,512]{1,0:T(8,128)(2,1)}, bf16[384,512]{1,0:T(8,128)(2,1)}, u32[]{:S(2)}, u32[]{:S(2)}) collective-permute-start(bf16[384,512]{1,0:T(8,128)(2,1)} %collective-permute-done.13.refs_1_), channel_id=1, source_target_pairs={{0,1},{1,2},{2,3},{3,4},{4,5},{5,6},{6,7},{7,8},{8,9},{9,10},{10,1... | collective-permute-start | bytes 1179656 | tf_op jit(solution)/shard_map/ppermute | solution.py:132
  92.9 5.1 %collective-permute-start.18 = (bf16[384,512]{1,0:T(8,128)(2,1)}, bf16[384,512]{1,0:T(8,128)(2,1)}, u32[]{:S(2)}, u32[]{:S(2)}) collective-permute-start(bf16[384,512]{1,0:T(8,128)(2,1)} %collective-permute-done.14.refs_2_), channel_id=1, source_target_pairs={{0,15},{1,0},{2,1},{3,2},{4,3},{5,4},{6,5},{7,6},{8,7},{9,8},{10,9... | collective-permute-start | bytes 1179656 | tf_op jit(solution)/shard_map/ppermute | solution.py:134
  98.0 2.2 %collective-permute-done.15.refs_3_ = bf16[384,512]{1,0:T(8,128)(2,1)} collective-permute-done((bf16[384,512]{1,0:T(8,128)(2,1)}, bf16[384,512]{1,0:T(8,128)(2,1)}, u32[]{:S(2)}, u32[]{:S(2)}) %collective-permute-start.15) | collective-permute-done | bytes 393248 | tf_op jit(solution)/shard_map/ppermute | solution.py:134
  100.2 5.6 %collective-permute-start.19 = (bf16[384,512]{1,0:T(8,128)(2,1)}, bf16[384,512]{1,0:T(8,128)(2,1)}, u32[]{:S(2)}, u32[]{:S(2)}) collective-permute-start(bf16[384,512]{1,0:T(8,128)(2,1)} %collective-permute-done.15.refs_3_), channel_id=1, source_target_pairs={{0,15},{1,0},{2,1},{3,2},{4,3},{5,4},{6,5},{7,6},{8,7},{9,8},{10,9... | collective-permute-start | bytes 1179656 | tf_op jit(solution)/shard_map/ppermute | solution.py:134
  105.8 1.9 %collective-permute-start.20 = (bf16[384,512]{1,0:T(8,128)(2,1)}, bf16[384,512]{1,0:T(8,128)(2,1)}, u32[]{:S(2)}, u32[]{:S(2)}) collective-permute-start(bf16[384,512]{1,0:T(8,128)(2,1)} %collective-permute-done.16.refs_0_), channel_id=1, source_target_pairs={{0,1},{1,2},{2,3},{3,4},{4,5},{5,6},{6,7},{7,8},{8,9},{9,10},{10,1... | collective-permute-start | bytes 1179656 | tf_op jit(solution)/shard_map/ppermute | solution.py:132
  107.7 2.3 %collective-permute-done.17.refs_1_ = bf16[384,512]{1,0:T(8,128)(2,1)} collective-permute-done((bf16[384,512]{1,0:T(8,128)(2,1)}, bf16[384,512]{1,0:T(8,128)(2,1)}, u32[]{:S(2)}, u32[]{:S(2)}) %collective-permute-start.17) | collective-permute-done | bytes 393248 | tf_op jit(solution)/shard_map/ppermute | solution.py:132
  113.4 5.1 %collective-permute-start.22 = (bf16[384,512]{1,0:T(8,128)(2,1)}, bf16[384,512]{1,0:T(8,128)(2,1)}, u32[]{:S(2)}, u32[]{:S(2)}) collective-permute-start(bf16[384,512]{1,0:T(8,128)(2,1)} %collective-permute-done.18.refs_2_), channel_id=1, source_target_pairs={{0,15},{1,0},{2,1},{3,2},{4,3},{5,4},{6,5},{7,6},{8,7},{9,8},{10,9... | collective-permute-start | bytes 1179656 | tf_op jit(solution)/shard_map/ppermute | solution.py:134
  118.5 3.5 %collective-permute-start.23 = (bf16[384,512]{1,0:T(8,128)(2,1)}, bf16[384,512]{1,0:T(8,128)(2,1)}, u32[]{:S(2)}, u32[]{:S(2)}) collective-permute-start(bf16[384,512]{1,0:T(8,128)(2,1)} %collective-permute-done.19.refs_3_), channel_id=1, source_target_pairs={{0,15},{1,0},{2,1},{3,2},{4,3},{5,4},{6,5},{7,6},{8,7},{9,8},{10,9... | collective-permute-start | bytes 1179656 | tf_op jit(solution)/shard_map/ppermute | solution.py:134
  122.0 2.4 %collective-permute-start.24 = (bf16[384,512]{1,0:T(8,128)(2,1)}, bf16[384,512]{1,0:T(8,128)(2,1)}, u32[]{:S(2)}, u32[]{:S(2)}) collective-permute-start(bf16[384,512]{1,0:T(8,128)(2,1)} %collective-permute-done.20.refs_0_), channel_id=1, source_target_pairs={{0,1},{1,2},{2,3},{3,4},{4,5},{5,6},{6,7},{7,8},{8,9},{9,10},{10,1... | collective-permute-start | bytes 1179656 | tf_op jit(solution)/shard_map/ppermute | solution.py:132
  124.4 2.5 %collective-permute-done.21.refs_1_ = bf16[384,512]{1,0:T(8,128)(2,1)} collective-permute-done((bf16[384,512]{1,0:T(8,128)(2,1)}, bf16[384,512]{1,0:T(8,128)(2,1)}, u32[]{:S(2)}, u32[]{:S(2)}) %collective-permute-start.21) | collective-permute-done | bytes 393248 | tf_op jit(solution)/shard_map/ppermute | solution.py:132
  129.1 5.1 %collective-permute-start.26 = (bf16[384,512]{1,0:T(8,128)(2,1)}, bf16[384,512]{1,0:T(8,128)(2,1)}, u32[]{:S(2)}, u32[]{:S(2)}) collective-permute-start(bf16[384,512]{1,0:T(8,128)(2,1)} %collective-permute-done.22.refs_2_), channel_id=1, source_target_pairs={{0,15},{1,0},{2,1},{3,2},{4,3},{5,4},{6,5},{7,6},{8,7},{9,8},{10,9... | collective-permute-start | bytes 1179656 | tf_op jit(solution)/shard_map/ppermute | solution.py:134
  134.4 5.6 %collective-permute-start.27 = (bf16[384,512]{1,0:T(8,128)(2,1)}, bf16[384,512]{1,0:T(8,128)(2,1)}, u32[]{:S(2)}, u32[]{:S(2)}) collective-permute-start(bf16[384,512]{1,0:T(8,128)(2,1)} %collective-permute-done.23.refs_3_), channel_id=1, source_target_pairs={{0,15},{1,0},{2,1},{3,2},{4,3},{5,4},{6,5},{7,6},{8,7},{9,8},{10,9... | collective-permute-start | bytes 1179656 | tf_op jit(solution)/shard_map/ppermute | solution.py:134
  140.0 1.9 %collective-permute-start.28 = (bf16[384,512]{1,0:T(8,128)(2,1)}, bf16[384,512]{1,0:T(8,128)(2,1)}, u32[]{:S(2)}, u32[]{:S(2)}) collective-permute-start(bf16[384,512]{1,0:T(8,128)(2,1)} %collective-permute-done.24.refs_0_), channel_id=1, source_target_pairs={{0,1},{1,2},{2,3},{3,4},{4,5},{5,6},{6,7},{7,8},{8,9},{9,10},{10,1... | collective-permute-start | bytes 1179656 | tf_op jit(solution)/shard_map/ppermute | solution.py:132
  142.0 4.0 %collective-permute-done.25.refs_1_ = bf16[384,512]{1,0:T(8,128)(2,1)} collective-permute-done((bf16[384,512]{1,0:T(8,128)(2,1)}, bf16[384,512]{1,0:T(8,128)(2,1)}, u32[]{:S(2)}, u32[]{:S(2)}) %collective-permute-start.25) | collective-permute-done | bytes 393248 | tf_op jit(solution)/shard_map/ppermute | solution.py:132
  145.9 2.1 %collective-permute-start.29 = (bf16[384,512]{1,0:T(8,128)(2,1)}, bf16[384,512]{1,0:T(8,128)(2,1)}, u32[]{:S(2)}, u32[]{:S(2)}) collective-permute-start(bf16[384,512]{1,0:T(8,128)(2,1)} %collective-permute-done.25.refs_1_), channel_id=1, source_target_pairs={{0,1},{1,2},{2,3},{3,4},{4,5},{5,6},{6,7},{7,8},{8,9},{9,10},{10,1... | collective-permute-start | bytes 1179656 | tf_op jit(solution)/shard_map/ppermute | solution.py:132
  148.1 2.3 %convolution_convert_fusion.refs_2_.q_ref = bf16[256,4096]{1,0:T(8,128)(2,1)S(1)} fusion(bf16[32,8,4096]{2,1,0:T(8,128)(2,1)} %all-to-all-done, s32[256]{0:T(256)S(1)} %fusion.5), kind=kOutput, calls=%fused_computation | convolution fusion | flops 537985024 | bytes 4195328 | tf_op jit(solution)/shard_map/dot_general | solution.py:109
  150.4 2.4 %attend_15.1.prev_ref = bf16[256,4096]{1,0:T(8,128)(2,1)} custom-call(s32[16]{0:T(128)S(1)} %select_reduce_fusion.2.refs_0_.where_ref, s32[16,16]{1,0:T(8,128)S(1)} %bitcast.17, bf16[256,4096]{1,0:T(8,128)(2,1)S(1)} %convolution_convert_fusion.refs_2_.q_ref, bf16[384,512]{1,0:T(8,128)(2,1)S(1)} %pad_maximum_fusion.refs_3_, ...), custom_call_target="tpu_custom_call" | custom-call | flops 100663296 | bytes 8388608 | tf_op jit(solution)/shard_map/attend_15/pallas_call | solution.py:87
  152.8 4.0 %attend_0.1.prev_ref = bf16[256,4096]{1,0:T(8,128)(2,1)} custom-call(bf16[256,4096]{1,0:T(8,128)(2,1)} %attend_15.1.prev_ref, s32[16]{0:T(128)S(1)} %select_reduce_fusion.2.refs_0_.where_ref, s32[16,16]{1,0:T(8,128)S(1)} %bitcast.18, bf16[256,4096]{1,0:T(8,128)(2,1)S(1)} %convolution_convert_fusion.refs_2_.q_ref, ...), custom_call_target="tpu_custom_call", output_to_operand_aliasing={{}: (0, {})} | custom-call | flops 201326592 | bytes 8388608 | tf_op jit(solution)/shard_map/attend_0/pallas_call | solution.py:87
  156.8 4.2 %attend_2.1.prev_ref = bf16[256,4096]{1,0:T(8,128)(2,1)} custom-call(bf16[256,4096]{1,0:T(8,128)(2,1)} %attend_0.1.prev_ref, s32[16]{0:T(128)S(1)} %select_reduce_fusion.2.refs_0_.where_ref, s32[16,16]{1,0:T(8,128)S(1)} %bitcast.19, bf16[256,4096]{1,0:T(8,128)(2,1)S(1)} %convolution_convert_fusion.refs_2_.q_ref, ...), custom_call_target="tpu_custom_call", output_to_operand_aliasing={{}: (0, {})} | custom-call | flops 201326592 | bytes 8388608 | tf_op jit(solution)/shard_map/attend_2/pallas_call | solution.py:87
  161.0 4.2 %attend_4.1.prev_ref = bf16[256,4096]{1,0:T(8,128)(2,1)} custom-call(bf16[256,4096]{1,0:T(8,128)(2,1)} %attend_2.1.prev_ref, s32[16]{0:T(128)S(1)} %select_reduce_fusion.2.refs_0_.where_ref, s32[16,16]{1,0:T(8,128)S(1)} %bitcast.20, bf16[256,4096]{1,0:T(8,128)(2,1)S(1)} %convolution_convert_fusion.refs_2_.q_ref, ...), custom_call_target="tpu_custom_call", output_to_operand_aliasing={{}: (0, {})} | custom-call | flops 201326592 | bytes 8388608 | tf_op jit(solution)/shard_map/attend_4/pallas_call | solution.py:87
  165.2 4.2 %attend_6.1.prev_ref = bf16[256,4096]{1,0:T(8,128)(2,1)} custom-call(bf16[256,4096]{1,0:T(8,128)(2,1)} %attend_4.1.prev_ref, s32[16]{0:T(128)S(1)} %select_reduce_fusion.2.refs_0_.where_ref, s32[16,16]{1,0:T(8,128)S(1)} %bitcast.21, bf16[256,4096]{1,0:T(8,128)(2,1)S(1)} %convolution_convert_fusion.refs_2_.q_ref, ...), custom_call_target="tpu_custom_call", output_to_operand_aliasing={{}: (0, {})} | custom-call | flops 201326592 | bytes 8388608 | tf_op jit(solution)/shard_map/attend_6/pallas_call | solution.py:87
  169.5 4.2 %attend_8.1.prev_ref = bf16[256,4096]{1,0:T(8,128)(2,1)} custom-call(bf16[256,4096]{1,0:T(8,128)(2,1)} %attend_6.1.prev_ref, s32[16]{0:T(128)S(1)} %select_reduce_fusion.2.refs_0_.where_ref, s32[16,16]{1,0:T(8,128)S(1)} %bitcast.22, bf16[256,4096]{1,0:T(8,128)(2,1)S(1)} %convolution_convert_fusion.refs_2_.q_ref, ...), custom_call_target="tpu_custom_call", output_to_operand_aliasing={{}: (0, {})} | custom-call | flops 201326592 | bytes 8388608 | tf_op jit(solution)/shard_map/attend_8/pallas_call | solution.py:87
  173.7 4.2 %attend_10.1.prev_ref = bf16[256,4096]{1,0:T(8,128)(2,1)} custom-call(bf16[256,4096]{1,0:T(8,128)(2,1)} %attend_8.1.prev_ref, s32[16]{0:T(128)S(1)} %select_reduce_fusion.2.refs_0_.where_ref, s32[16,16]{1,0:T(8,128)S(1)} %bitcast.23, bf16[256,4096]{1,0:T(8,128)(2,1)S(1)} %convolution_convert_fusion.refs_2_.q_ref, ...), custom_call_target="tpu_custom_call", output_to_operand_aliasing={{}: (0, {})} | custom-call | flops 201326592 | bytes 8388608 | tf_op jit(solution)/shard_map/attend_10/pallas_call | solution.py:87
  178.0 4.2 %attend_12.1.prev_ref = bf16[256,4096]{1,0:T(8,128)(2,1)} custom-call(bf16[256,4096]{1,0:T(8,128)(2,1)} %attend_10.1.prev_ref, s32[16]{0:T(128)S(1)} %select_reduce_fusion.2.refs_0_.where_ref, s32[16,16]{1,0:T(8,128)S(1)} %bitcast.24, bf16[256,4096]{1,0:T(8,128)(2,1)S(1)} %convolution_convert_fusion.refs_2_.q_ref, ...), custom_call_target="tpu_custom_call", output_to_operand_aliasing={{}: (0, {})} | custom-call | flops 201326592 | bytes 8388608 | tf_op jit(solution)/shard_map/attend_12/pallas_call | solution.py:87
  182.2 3.0 %attend_14.1 = bf16[256,4096]{1,0:T(8,128)(2,1)} custom-call(bf16[256,4096]{1,0:T(8,128)(2,1)} %attend_12.1.prev_ref, s32[16]{0:T(128)S(1)} %select_reduce_fusion.2.refs_0_.where_ref, s32[16,16]{1,0:T(8,128)S(1)} %bitcast.25, bf16[256,4096]{1,0:T(8,128)(2,1)S(1)} %convolution_convert_fusion.refs_2_.q_ref, ...), custom_call_target="tpu_custom_call", output_to_operand_aliasing={{}: (0, {})} | custom-call | flops 100663296 | bytes 8388608 | tf_op jit(solution)/shard_map/attend_14/pallas_call | solution.py:87
  (53 shorter events, 9.9 us)
Async XLA Ops:
  0.0 50.1 %copy-start = (bf16[1,1,256,4096]{3,2,1,0:T(8,128)(2,1)S(1)}, bf16[1,1,256,4096]{3,2,1,0:T(8,128)(2,1)}, u32[]{:S(2)}) copy-start(bf16[1,1,256,4096]{3,2,1,0:T(8,128)(2,1)} %param.6) | copy-start | bytes 6291460
  0.0 50.1 %copy-start.3 = (s32[1,1,256]{2,1,0:T(1,128)S(1)}, s32[1,1,256]{2,1,0:T(1,128)}, u32[]{:S(2)}) copy-start(s32[1,1,256]{2,1,0:T(1,128)} %param.7) | copy-start | bytes 3076
  1.5 21.3 %collective-permute-start = (bf16[384,512]{1,0:T(8,128)(2,1)S(1)}, bf16[384,512]{1,0:T(8,128)(2,1)S(1)}, u32[]{:S(2)}, u32[]{:S(2)}) collective-permute-start(bf16[384,512]{1,0:T(8,128)(2,1)S(1)} %pad_maximum_fusion.refs_3_), channel_id=1, source_target_pairs={{0,1},{1,2},{2,3},{3,4},{4,5},{5,6},{6,7},{7,8},{8,9},{9,10},{10,1... | collective-permute-start | bytes 1179656 | tf_op jit(solution)/shard_map/ppermute | solution.py:132
  5.3 25.9 %collective-permute-start.1 = (bf16[384,512]{1,0:T(8,128)(2,1)S(1)}, bf16[384,512]{1,0:T(8,128)(2,1)S(1)}, u32[]{:S(2)}, u32[]{:S(2)}) collective-permute-start(bf16[384,512]{1,0:T(8,128)(2,1)S(1)} %pad_maximum_fusion.1.refs_4_), channel_id=1, source_target_pairs={{0,1},{1,2},{2,3},{3,4},{4,5},{5,6},{6,7},{7,8},{8,9},{9,10},{10,1... | collective-permute-start | bytes 1179656 | tf_op jit(solution)/shard_map/ppermute | solution.py:132
  9.2 24.7 %collective-permute-start.2 = (bf16[384,512]{1,0:T(8,128)(2,1)S(1)}, bf16[384,512]{1,0:T(8,128)(2,1)}, u32[]{:S(2)}, u32[]{:S(2)}) collective-permute-start(bf16[384,512]{1,0:T(8,128)(2,1)S(1)} %pad_maximum_fusion.refs_3_), channel_id=1, source_target_pairs={{0,15},{1,0},{2,1},{3,2},{4,3},{5,4},{6,5},{7,6},{8,7},{9,8},{10,9... | collective-permute-start | bytes 1179656 | tf_op jit(solution)/shard_map/ppermute | solution.py:134
  16.8 22.3 %collective-permute-start.3 = (bf16[384,512]{1,0:T(8,128)(2,1)S(1)}, bf16[384,512]{1,0:T(8,128)(2,1)}, u32[]{:S(2)}, u32[]{:S(2)}) collective-permute-start(bf16[384,512]{1,0:T(8,128)(2,1)S(1)} %pad_maximum_fusion.1.refs_4_), channel_id=1, source_target_pairs={{0,15},{1,0},{2,1},{3,2},{4,3},{5,4},{6,5},{7,6},{8,7},{9,8},{10,9... | collective-permute-start | bytes 1179656 | tf_op jit(solution)/shard_map/ppermute | solution.py:134
  22.8 19.0 %collective-permute-start.4 = (bf16[384,512]{1,0:T(8,128)(2,1)S(1)}, bf16[384,512]{1,0:T(8,128)(2,1)}, u32[]{:S(2)}, u32[]{:S(2)}) collective-permute-start(bf16[384,512]{1,0:T(8,128)(2,1)S(1)} %collective-permute-done.refs_0_), channel_id=1, source_target_pairs={{0,1},{1,2},{2,3},{3,4},{4,5},{5,6},{6,7},{7,8},{8,9},{9,10},{10,1... | collective-permute-start | bytes 1179656 | tf_op jit(solution)/shard_map/ppermute | solution.py:132
  31.2 17.0 %collective-permute-start.5 = (bf16[384,512]{1,0:T(8,128)(2,1)S(1)}, bf16[384,512]{1,0:T(8,128)(2,1)}, u32[]{:S(2)}, u32[]{:S(2)}) collective-permute-start(bf16[384,512]{1,0:T(8,128)(2,1)S(1)} %collective-permute-done.1.refs_1_), channel_id=1, source_target_pairs={{0,1},{1,2},{2,3},{3,4},{4,5},{5,6},{6,7},{7,8},{8,9},{9,10},{10,1... | collective-permute-start | bytes 1179656 | tf_op jit(solution)/shard_map/ppermute | solution.py:132
  33.1 0.8 copy-start.1
  33.9 26.1 %collective-permute-start.6 = (bf16[384,512]{1,0:T(8,128)(2,1)}, bf16[384,512]{1,0:T(8,128)(2,1)}, u32[]{:S(2)}, u32[]{:S(2)}) collective-permute-start(bf16[384,512]{1,0:T(8,128)(2,1)} %collective-permute-done.2.refs_2_), channel_id=1, source_target_pairs={{0,15},{1,0},{2,1},{3,2},{4,3},{5,4},{6,5},{7,6},{8,7},{9,8},{10,9... | collective-permute-start | bytes 1179656 | tf_op jit(solution)/shard_map/ppermute | solution.py:134
  39.1 26.1 %collective-permute-start.7 = (bf16[384,512]{1,0:T(8,128)(2,1)}, bf16[384,512]{1,0:T(8,128)(2,1)}, u32[]{:S(2)}, u32[]{:S(2)}) collective-permute-start(bf16[384,512]{1,0:T(8,128)(2,1)} %collective-permute-done.3.refs_3_), channel_id=1, source_target_pairs={{0,15},{1,0},{2,1},{3,2},{4,3},{5,4},{6,5},{7,6},{8,7},{9,8},{10,9... | collective-permute-start | bytes 1179656 | tf_op jit(solution)/shard_map/ppermute | solution.py:134
  41.8 26.1 %collective-permute-start.8 = (bf16[384,512]{1,0:T(8,128)(2,1)}, bf16[384,512]{1,0:T(8,128)(2,1)}, u32[]{:S(2)}, u32[]{:S(2)}) collective-permute-start(bf16[384,512]{1,0:T(8,128)(2,1)} %collective-permute-done.4.refs_0_), channel_id=1, source_target_pairs={{0,1},{1,2},{2,3},{3,4},{4,5},{5,6},{6,7},{7,8},{8,9},{9,10},{10,1... | collective-permute-start | bytes 1179656 | tf_op jit(solution)/shard_map/ppermute | solution.py:132
  48.2 22.8 %collective-permute-start.9 = (bf16[384,512]{1,0:T(8,128)(2,1)}, bf16[384,512]{1,0:T(8,128)(2,1)}, u32[]{:S(2)}, u32[]{:S(2)}) collective-permute-start(bf16[384,512]{1,0:T(8,128)(2,1)} %collective-permute-done.5.refs_1_), channel_id=1, source_target_pairs={{0,1},{1,2},{2,3},{3,4},{4,5},{5,6},{6,7},{7,8},{8,9},{9,10},{10,1... | collective-permute-start | bytes 1179656 | tf_op jit(solution)/shard_map/ppermute | solution.py:132
  52.2 40.7 %copy-start.6 = (s32[1,1,16]{2,1,0:T(1,128)S(1)}, s32[1,1,16]{2,1,0:T(1,128)}, u32[]{:S(2)}) copy-start(s32[1,1,16]{2,1,0:T(1,128)} %param.10) | copy-start | bytes 196
  52.2 60.3 %copy-start.5 = (s32[1,1,256]{2,1,0:T(1,128)S(1)}, s32[1,1,256]{2,1,0:T(1,128)}, u32[]{:S(2)}) copy-start(s32[1,1,256]{2,1,0:T(1,128)} %param.9) | copy-start | bytes 3076
  52.2 61.2 %copy-start.4 = (s32[1,1,256]{2,1,0:T(1,128)S(1)}, s32[1,1,256]{2,1,0:T(1,128)}, u32[]{:S(2)}) copy-start(s32[1,1,256]{2,1,0:T(1,128)} %param.8) | copy-start | bytes 3076
  52.2 95.9 %all-to-all-start = ((bf16[32,8,4096]{2,1,0:T(8,128)(2,1)}), bf16[32,8,4096]{2,1,0:T(8,128)(2,1)}, u32[]{:S(2)}, u32[]{:S(2)}) async-start(bf16[32,8,4096]{2,1,0:T(8,128)(2,1)} %fusion), calls=%async_computation | async-start | bytes 4194304 | tf_op jit(solution)/shard_map/all_to_all | solution.py:138
  60.0 14.9 %collective-permute-start.10 = (bf16[384,512]{1,0:T(8,128)(2,1)}, bf16[384,512]{1,0:T(8,128)(2,1)}, u32[]{:S(2)}, u32[]{:S(2)}) collective-permute-start(bf16[384,512]{1,0:T(8,128)(2,1)} %collective-permute-done.6.refs_2_), channel_id=1, source_target_pairs={{0,15},{1,0},{2,1},{3,2},{4,3},{5,4},{6,5},{7,6},{8,7},{9,8},{10,9... | collective-permute-start | bytes 1179656 | tf_op jit(solution)/shard_map/ppermute | solution.py:134
  65.1 18.2 %collective-permute-start.11 = (bf16[384,512]{1,0:T(8,128)(2,1)}, bf16[384,512]{1,0:T(8,128)(2,1)}, u32[]{:S(2)}, u32[]{:S(2)}) collective-permute-start(bf16[384,512]{1,0:T(8,128)(2,1)} %collective-permute-done.7.refs_3_), channel_id=1, source_target_pairs={{0,15},{1,0},{2,1},{3,2},{4,3},{5,4},{6,5},{7,6},{8,7},{9,8},{10,9... | collective-permute-start | bytes 1179656 | tf_op jit(solution)/shard_map/ppermute | solution.py:134
  67.9 21.0 %collective-permute-start.12 = (bf16[384,512]{1,0:T(8,128)(2,1)}, bf16[384,512]{1,0:T(8,128)(2,1)}, u32[]{:S(2)}, u32[]{:S(2)}) collective-permute-start(bf16[384,512]{1,0:T(8,128)(2,1)} %collective-permute-done.8.refs_0_), channel_id=1, source_target_pairs={{0,1},{1,2},{2,3},{3,4},{4,5},{5,6},{6,7},{7,8},{8,9},{9,10},{10,1... | collective-permute-start | bytes 1179656 | tf_op jit(solution)/shard_map/ppermute | solution.py:132
  71.0 19.8 %collective-permute-start.13 = (bf16[384,512]{1,0:T(8,128)(2,1)}, bf16[384,512]{1,0:T(8,128)(2,1)}, u32[]{:S(2)}, u32[]{:S(2)}) collective-permute-start(bf16[384,512]{1,0:T(8,128)(2,1)} %collective-permute-done.9.refs_1_), channel_id=1, source_target_pairs={{0,1},{1,2},{2,3},{3,4},{4,5},{5,6},{6,7},{7,8},{8,9},{9,10},{10,1... | collective-permute-start | bytes 1179656 | tf_op jit(solution)/shard_map/ppermute | solution.py:132
  74.9 17.9 %collective-permute-start.14 = (bf16[384,512]{1,0:T(8,128)(2,1)}, bf16[384,512]{1,0:T(8,128)(2,1)}, u32[]{:S(2)}, u32[]{:S(2)}) collective-permute-start(bf16[384,512]{1,0:T(8,128)(2,1)} %collective-permute-done.10.refs_2_), channel_id=1, source_target_pairs={{0,15},{1,0},{2,1},{3,2},{4,3},{5,4},{6,5},{7,6},{8,7},{9,8},{10,9... | collective-permute-start | bytes 1179656 | tf_op jit(solution)/shard_map/ppermute | solution.py:134
  83.3 16.9 %collective-permute-start.15 = (bf16[384,512]{1,0:T(8,128)(2,1)}, bf16[384,512]{1,0:T(8,128)(2,1)}, u32[]{:S(2)}, u32[]{:S(2)}) collective-permute-start(bf16[384,512]{1,0:T(8,128)(2,1)} %collective-permute-done.11.refs_3_), channel_id=1, source_target_pairs={{0,15},{1,0},{2,1},{3,2},{4,3},{5,4},{6,5},{7,6},{8,7},{9,8},{10,9... | collective-permute-start | bytes 1179656 | tf_op jit(solution)/shard_map/ppermute | solution.py:134
  88.9 16.8 %collective-permute-start.16 = (bf16[384,512]{1,0:T(8,128)(2,1)}, bf16[384,512]{1,0:T(8,128)(2,1)}, u32[]{:S(2)}, u32[]{:S(2)}) collective-permute-start(bf16[384,512]{1,0:T(8,128)(2,1)} %collective-permute-done.12.refs_0_), channel_id=1, source_target_pairs={{0,1},{1,2},{2,3},{3,4},{4,5},{5,6},{6,7},{7,8},{8,9},{9,10},{10,1... | collective-permute-start | bytes 1179656 | tf_op jit(solution)/shard_map/ppermute | solution.py:132
  90.9 19.2 %collective-permute-start.17 = (bf16[384,512]{1,0:T(8,128)(2,1)}, bf16[384,512]{1,0:T(8,128)(2,1)}, u32[]{:S(2)}, u32[]{:S(2)}) collective-permute-start(bf16[384,512]{1,0:T(8,128)(2,1)} %collective-permute-done.13.refs_1_), channel_id=1, source_target_pairs={{0,1},{1,2},{2,3},{3,4},{4,5},{5,6},{6,7},{7,8},{8,9},{9,10},{10,1... | collective-permute-start | bytes 1179656 | tf_op jit(solution)/shard_map/ppermute | solution.py:132
  92.9 20.5 %collective-permute-start.18 = (bf16[384,512]{1,0:T(8,128)(2,1)}, bf16[384,512]{1,0:T(8,128)(2,1)}, u32[]{:S(2)}, u32[]{:S(2)}) collective-permute-start(bf16[384,512]{1,0:T(8,128)(2,1)} %collective-permute-done.14.refs_2_), channel_id=1, source_target_pairs={{0,15},{1,0},{2,1},{3,2},{4,3},{5,4},{6,5},{7,6},{8,7},{9,8},{10,9... | collective-permute-start | bytes 1179656 | tf_op jit(solution)/shard_map/ppermute | solution.py:134
  100.2 18.4 %collective-permute-start.19 = (bf16[384,512]{1,0:T(8,128)(2,1)}, bf16[384,512]{1,0:T(8,128)(2,1)}, u32[]{:S(2)}, u32[]{:S(2)}) collective-permute-start(bf16[384,512]{1,0:T(8,128)(2,1)} %collective-permute-done.15.refs_3_), channel_id=1, source_target_pairs={{0,15},{1,0},{2,1},{3,2},{4,3},{5,4},{6,5},{7,6},{8,7},{9,8},{10,9... | collective-permute-start | bytes 1179656 | tf_op jit(solution)/shard_map/ppermute | solution.py:134
  105.8 16.2 %collective-permute-start.20 = (bf16[384,512]{1,0:T(8,128)(2,1)}, bf16[384,512]{1,0:T(8,128)(2,1)}, u32[]{:S(2)}, u32[]{:S(2)}) collective-permute-start(bf16[384,512]{1,0:T(8,128)(2,1)} %collective-permute-done.16.refs_0_), channel_id=1, source_target_pairs={{0,1},{1,2},{2,3},{3,4},{4,5},{5,6},{6,7},{7,8},{8,9},{9,10},{10,1... | collective-permute-start | bytes 1179656 | tf_op jit(solution)/shard_map/ppermute | solution.py:132
  110.1 16.9 %collective-permute-start.21 = (bf16[384,512]{1,0:T(8,128)(2,1)}, bf16[384,512]{1,0:T(8,128)(2,1)}, u32[]{:S(2)}, u32[]{:S(2)}) collective-permute-start(bf16[384,512]{1,0:T(8,128)(2,1)} %collective-permute-done.17.refs_1_), channel_id=1, source_target_pairs={{0,1},{1,2},{2,3},{3,4},{4,5},{5,6},{6,7},{7,8},{8,9},{9,10},{10,1... | collective-permute-start | bytes 1179656 | tf_op jit(solution)/shard_map/ppermute | solution.py:132
  113.4 15.7 %collective-permute-start.22 = (bf16[384,512]{1,0:T(8,128)(2,1)}, bf16[384,512]{1,0:T(8,128)(2,1)}, u32[]{:S(2)}, u32[]{:S(2)}) collective-permute-start(bf16[384,512]{1,0:T(8,128)(2,1)} %collective-permute-done.18.refs_2_), channel_id=1, source_target_pairs={{0,15},{1,0},{2,1},{3,2},{4,3},{5,4},{6,5},{7,6},{8,7},{9,8},{10,9... | collective-permute-start | bytes 1179656 | tf_op jit(solution)/shard_map/ppermute | solution.py:134
  118.5 15.9 %collective-permute-start.23 = (bf16[384,512]{1,0:T(8,128)(2,1)}, bf16[384,512]{1,0:T(8,128)(2,1)}, u32[]{:S(2)}, u32[]{:S(2)}) collective-permute-start(bf16[384,512]{1,0:T(8,128)(2,1)} %collective-permute-done.19.refs_3_), channel_id=1, source_target_pairs={{0,15},{1,0},{2,1},{3,2},{4,3},{5,4},{6,5},{7,6},{8,7},{9,8},{10,9... | collective-permute-start | bytes 1179656 | tf_op jit(solution)/shard_map/ppermute | solution.py:134
  122.0 18.0 %collective-permute-start.24 = (bf16[384,512]{1,0:T(8,128)(2,1)}, bf16[384,512]{1,0:T(8,128)(2,1)}, u32[]{:S(2)}, u32[]{:S(2)}) collective-permute-start(bf16[384,512]{1,0:T(8,128)(2,1)} %collective-permute-done.20.refs_0_), channel_id=1, source_target_pairs={{0,1},{1,2},{2,3},{3,4},{4,5},{5,6},{6,7},{7,8},{8,9},{9,10},{10,1... | collective-permute-start | bytes 1179656 | tf_op jit(solution)/shard_map/ppermute | solution.py:132
  126.9 19.0 %collective-permute-start.25 = (bf16[384,512]{1,0:T(8,128)(2,1)}, bf16[384,512]{1,0:T(8,128)(2,1)}, u32[]{:S(2)}, u32[]{:S(2)}) collective-permute-start(bf16[384,512]{1,0:T(8,128)(2,1)} %collective-permute-done.21.refs_1_), channel_id=1, source_target_pairs={{0,1},{1,2},{2,3},{3,4},{4,5},{5,6},{6,7},{7,8},{8,9},{9,10},{10,1... | collective-permute-start | bytes 1179656 | tf_op jit(solution)/shard_map/ppermute | solution.py:132
  129.1 48.8 %collective-permute-start.26 = (bf16[384,512]{1,0:T(8,128)(2,1)}, bf16[384,512]{1,0:T(8,128)(2,1)}, u32[]{:S(2)}, u32[]{:S(2)}) collective-permute-start(bf16[384,512]{1,0:T(8,128)(2,1)} %collective-permute-done.22.refs_2_), channel_id=1, source_target_pairs={{0,15},{1,0},{2,1},{3,2},{4,3},{5,4},{6,5},{7,6},{8,7},{9,8},{10,9... | collective-permute-start | bytes 1179656 | tf_op jit(solution)/shard_map/ppermute | solution.py:134
  134.4 43.5 %collective-permute-start.27 = (bf16[384,512]{1,0:T(8,128)(2,1)}, bf16[384,512]{1,0:T(8,128)(2,1)}, u32[]{:S(2)}, u32[]{:S(2)}) collective-permute-start(bf16[384,512]{1,0:T(8,128)(2,1)} %collective-permute-done.23.refs_3_), channel_id=1, source_target_pairs={{0,15},{1,0},{2,1},{3,2},{4,3},{5,4},{6,5},{7,6},{8,7},{9,8},{10,9... | collective-permute-start | bytes 1179656 | tf_op jit(solution)/shard_map/ppermute | solution.py:134
  140.0 42.2 %collective-permute-start.28 = (bf16[384,512]{1,0:T(8,128)(2,1)}, bf16[384,512]{1,0:T(8,128)(2,1)}, u32[]{:S(2)}, u32[]{:S(2)}) collective-permute-start(bf16[384,512]{1,0:T(8,128)(2,1)} %collective-permute-done.24.refs_0_), channel_id=1, source_target_pairs={{0,1},{1,2},{2,3},{3,4},{4,5},{5,6},{6,7},{7,8},{8,9},{9,10},{10,1... | collective-permute-start | bytes 1179656 | tf_op jit(solution)/shard_map/ppermute | solution.py:132
  145.9 36.3 %collective-permute-start.29 = (bf16[384,512]{1,0:T(8,128)(2,1)}, bf16[384,512]{1,0:T(8,128)(2,1)}, u32[]{:S(2)}, u32[]{:S(2)}) collective-permute-start(bf16[384,512]{1,0:T(8,128)(2,1)} %collective-permute-done.25.refs_1_), channel_id=1, source_target_pairs={{0,1},{1,2},{2,3},{3,4},{4,5},{5,6},{6,7},{7,8},{8,9},{9,10},{10,1... | collective-permute-start | bytes 1179656 | tf_op jit(solution)/shard_map/ppermute | solution.py:132
  150.4 2.4 %copy-start.2 = (bf16[384,512]{1,0:T(8,128)(2,1)S(1)}, bf16[384,512]{1,0:T(8,128)(2,1)}, u32[]{:S(2)}) copy-start(bf16[384,512]{1,0:T(8,128)(2,1)} %copy-done.1) | copy-start | bytes 1179652

commit v2 on v0

v2 whole, which is shorter than its diff:
```python
import functools
import math

import jax
import jax.numpy as jnp
from jax import lax
from jax.experimental import pallas as pl
from jax.experimental.pallas import tpu as pltpu
from jax.sharding import PartitionSpec as P

HD = 128
QH = 32
KVH = 4
GROUPS = QH // KVH
SCALE = math.log2(math.e) / math.sqrt(HD)


PARTS = 2
HEADS = KVH // PARTS


def score_group(query_ref, row, rows, blocks, limits, out_ref, out_row):
    cache_len = blocks[0].shape[0]
    visible = lax.broadcasted_iota(jnp.int32, (cache_len, GROUPS * rows), 0) <= limits
    for k in range(KVH):
        block, at = blocks[k // HEADS], k % HEADS
        heads = [slice((k * GROUPS + g) * HD, (k * GROUPS + g + 1) * HD) for g in range(GROUPS)]
        query = jnp.concatenate([query_ref[row : row + rows, h] for h in heads], axis=0)
        scores = lax.dot_general(
            block[:, at * HD : (at + 1) * HD],
            query,
            (((1,), (1,)), ((), ())),
            preferred_element_type=jnp.float32,
        )
        scores = jnp.where(visible, scores, -jnp.inf)
        row_max = jnp.max(scores, axis=0, keepdims=True)
        exponent = jnp.exp2((scores - row_max) * SCALE)
        row_total = jnp.sum(exponent, axis=0, keepdims=True)
        mixed = lax.dot_general(
            exponent.astype(jnp.bfloat16),
            block[:, (HEADS + at) * HD : (HEADS + at + 1) * HD],
            (((0,), (0,)), ((), ())),
            preferred_element_type=jnp.float32,
        )
        mixed = (mixed / row_total.reshape(GROUPS * rows, 1)).astype(jnp.bfloat16)
        for g in range(GROUPS):
            out_ref[out_row : out_row + rows, heads[g]] = mixed[g * rows : (g + 1) * rows]


def step_kernel(spots, rows, limits_ref, query_ref, *refs):
    blocks, out_ref = refs[:-1], refs[-1]
    for i, spot in enumerate(spots):
        group = blocks[PARTS * i : PARTS * (i + 1)]
        score_group(query_ref, spot * rows, rows, group, limits_ref[spot : spot + 1, :], out_ref, i * rows)


def guest_kernel(count, rows, *refs):
    blocks, refs = refs[:PARTS], refs[PARTS:]
    for guest_ref, out_ref in zip(refs[:count], refs[count:]):
        width = out_ref.shape[1]
        parts = guest_ref[:, width:].astype(jnp.float32)
        limits = (parts[0:1] * 16.0 + parts[1:2]).astype(jnp.int32)
        score_group(guest_ref, 0, rows, blocks, limits, out_ref, 0)


def place_kernel(ref_spots, rows, again, where_ref, *refs):
    if again:
        refs = refs[1:]
    held, out_ref, sems = refs[: len(ref_spots)], refs[-2], refs[-1]
    copies = []
    for ref, spots in zip(held, ref_spots):
        for i, spot in enumerate(spots):
            start = pl.multiple_of(where_ref[spot] * rows, rows)
            copy = pltpu.make_async_copy(
                ref.at[pl.ds(i * rows, rows), :], out_ref.at[pl.ds(start, rows), :], sems.at[len(copies)]
            )
            copy.start()
            copies.append(copy)
    for copy in copies:
        copy.wait()


def cost(spots, rows, cache_len):
    work = len(spots) * rows * QH * cache_len
    return pl.CostEstimate(flops=4 * work * HD, bytes_accessed=2**20, transcendentals=work)


VMEM = pl.BlockSpec(memory_space=pltpu.VMEM)
SMEM = pl.BlockSpec(memory_space=pltpu.SMEM)
ANY = pl.BlockSpec(memory_space=pl.ANY)
PARAMS = pltpu.CompilerParams(vmem_limit_bytes=10 * 2**20)


def attend_step(limits, packed, spots, blocks, rows):
    return pl.pallas_call(
        functools.partial(step_kernel, spots, rows),
        out_shape=jax.ShapeDtypeStruct((len(spots) * rows, packed.shape[1]), packed.dtype),
        in_specs=[VMEM] * (2 + len(blocks)),
        out_specs=VMEM,
        compiler_params=PARAMS,
        cost_estimate=cost(spots, rows, blocks[0].shape[0]),
        name="attend_%d" % spots[0],
    )(limits, packed, *blocks)


def attend_guests(guests, blocks, rows):
    width = guests[0].shape[1] - HD
    return pl.pallas_call(
        functools.partial(guest_kernel, len(guests), rows),
        out_shape=[jax.ShapeDtypeStruct((rows, width), g.dtype) for g in guests],
        in_specs=[VMEM] * (PARTS + len(guests)),
        out_specs=[VMEM] * len(guests),
        compiler_params=PARAMS,
        cost_estimate=cost(guests, rows, blocks[0].shape[0]),
        name="attend_guests",
    )(*blocks, *guests)


def place_rows(where, held, held_spots, rows, out, shape):
    again = out is not None
    return pl.pallas_call(
        functools.partial(place_kernel, tuple(held_spots), rows, again),
        out_shape=jax.ShapeDtypeStruct(shape, held[0].dtype),
        in_specs=[SMEM] + [ANY] * (again + len(held)),
        out_specs=ANY,
        scratch_shapes=[pltpu.SemaphoreType.DMA((sum(len(s) for s in held_spots),))],
        input_output_aliases={1: 0} if again else {},
        compiler_params=PARAMS,
        cost_estimate=pl.CostEstimate(flops=0, bytes_accessed=2 * held[0].size, transcendentals=0),
        name="place_last" if again else "place_held",
    )(where, *([out] if again else []), *held)


def move_rows(targets, rows):
    count = rows.shape[0]
    pick = (jnp.arange(count, dtype=jnp.int32)[:, None] == targets[None, :]).astype(rows.dtype)
    return jnp.dot(pick, rows, preferred_element_type=jnp.float32).astype(rows.dtype)


def tie(values, after):
    return lax.optimization_barrier((values, after))


def body(queries, send_list, recv_list, slot_pos, pack_seq, seq_kv):
    query_rows = queries[0, 0]
    row_count, width = query_rows.shape
    dp_count = lax.axis_size("dp")
    ring = lax.axis_size("prompt")
    group_rows = row_count // ring
    me = lax.axis_index("prompt")
    kv = seq_kv[0, 0]
    steps = ring // 2

    span, part = KVH * HD, HEADS * HD
    own = tuple(
        jnp.concatenate([kv[:, lo : lo + part], kv[:, span + lo : span + lo + part]], axis=1)
        for lo in range(0, span, part)
    )

    def shifted(x, by):
        return lax.ppermute(x, "prompt", [(i, (i + by) % ring) for i in range(ring)])

    def tie_first(parts, after):
        first, after = tie(parts[0], after)
        return (first, *parts[1:]), after

    up = tuple(shifted(x, 1) for x in own)
    down = tuple(shifted(x, -1) for x in own)
    blocks_of = [(*up, *down)]

    send, _ = tie(send_list[0, 0], up[0])
    ordered = move_rows(send, query_rows)
    arrived = lax.all_to_all(
        ordered.reshape(dp_count, row_count // dp_count, width), "dp", split_axis=0, concat_axis=0, tiled=True
    ).reshape(row_count, width)

    sequences = pack_seq[0, 0]
    behind = (me - sequences) % ring
    place = jnp.where(
        behind == 0,
        ring - 1,
        jnp.where(behind <= steps, 2 * (behind - 1), 2 * (ring - behind - 1) + 1),
    )
    spots = jnp.arange(ring, dtype=jnp.int32)
    at_place = place[None, :] == spots[:, None]
    where = jnp.sum(jnp.where(at_place, spots[None, :], 0), axis=1)
    grouped_pos = slot_pos[0, 0].reshape(ring, group_rows)
    limits = jnp.sum(jnp.where(at_place[:, :, None], grouped_pos[None], 0), axis=1)
    limits = jnp.tile(limits, (1, GROUPS))
    slot = recv_list[0, 0]
    of_group = (slot // group_rows)[:, None] == spots[None, :]
    target = jnp.sum(jnp.where(of_group, place[None, :], 0), axis=1) * group_rows + slot % group_rows
    packed = move_rows(target, arrived)

    far = steps - 2
    mine, behind_far, ahead_far, opposite = (ring - 1,), (2 * far,), (2 * far + 1,), (2 * far + 2,)

    def payload(spot):
        rows = packed[spot * group_rows : (spot + 1) * group_rows]
        parts = jnp.stack([limits[spot] // 16, limits[spot] % 16]).astype(rows.dtype)
        beside = jnp.pad(parts, ((0, group_rows - 2), (0, 0)))
        return jnp.concatenate([rows, beside], axis=1)

    held, held_spots = [], []

    def score(spot_list, blocks):
        held.append(attend_step(limits, packed, spot_list, blocks, group_rows))
        held_spots.append(spot_list)

    for step in range(1, far):
        if step == 2:
            up, ordered = tie_first(up, ordered)
        if step == 3:
            guests = [payload(s[0]) for s in (behind_far, opposite, ahead_far)]
            up, guests = tie_first(up, guests)
            guests = [shifted(g, by) for g, by in zip(guests, (-1, -2, 1))]
        if step == 4:
            score(mine, own)
            score((0, 1), blocks_of[0])
            up, (guests, held) = tie_first(up, (guests, held))
        if step == 5:
            score((2, 3), blocks_of[1])
            score((4, 5), blocks_of[2])
            up, held = tie_first(up, held)
        up = tuple(shifted(x, 1) for x in up)
        down = tuple(shifted(x, -1) for x in down)
        blocks_of.append((*up, *down))
    score((6, 7), blocks_of[3])
    score((8, 9), blocks_of[4])
    out = place_rows(where, held, held_spots, group_rows, None, packed.shape)
    up, out = tie_first(up, out)
    behind_out, opposite_out = attend_guests(guests[:2], up, group_rows)
    behind_out, opposite_out = shifted(behind_out, 1), shifted(opposite_out, 2)
    (ahead_out,) = attend_guests(guests[2:], down, group_rows)
    ahead_out = shifted(ahead_out, -1)
    held, held_spots = [], []
    score((2 * far - 2, 2 * far - 1), (*up, *down))
    out = place_rows(
        where,
        [*held, behind_out, opposite_out, ahead_out],
        [*held_spots, behind_far, opposite, ahead_far],
        group_rows,
        out,
        packed.shape,
    )
    return out[None, None]


def solution(mesh):
    return jax.shard_map(
        body,
        mesh=mesh,
        in_specs=(
            P("prompt", "dp", None, None),
            P("prompt", "dp", None),
            P("prompt", "dp", None),
            P("prompt", "dp", None),
            P("prompt", "dp", None),
            P("dp", "prompt", None, None),
        ),
        out_specs=P("prompt", "dp", None, None),
        check_vma=False,
    )
```

time: 309 us -> 162 us (0.52)
  the two profiles are of different devices: /device:TPU:1 before, /device:TPU:2 now
where the time goes in v2:
time: 162 us; the launch traced here: 160 us
  starting transfers between devices  113 us (70%)
  Pallas kernels  18.2 us (11%)
  waiting for transfers between devices  13.9 us (9%)
  local copies, waits for them, and re-layouts  8.27 us (5%)
  matrix products  4.34 us (3%)
  other arithmetic  1.82 us (1%)
    ppermute x30, starting transfers between devices, shifted(): lax.ppermute(x, 'prompt', [(i, (i + by) % ring) for i in range(ring)])  105 us
    ppermute x30, waiting for transfers between devices, shifted(): lax.ppermute(x, 'prompt', [(i, (i + by) % ring) for i in range(ring)])  13.9 us
    pallas_call x7, Pallas kernels, attend_step(): pl.pallas_call(functools.partial(step_kernel, spots, rows), out_shape=jax...  12.6 us
    all_to_all x1, starting transfers between devices, body(): lax.all_to_all(ordered.reshape(dp_count, row_count // dp_count, width), '...  7.81 us
    unnamed x29, local copies, waits for them, and re-layouts  4.94 us
    dot_general x2, matrix products, move_rows(): jnp.dot(pick, rows, preferred_element_type=jnp.float32).astype(rows.dtype)  4.34 us
  transfers between devices with their start and end apart: 31, of which 6 were waited for; matrix products, arithmetic and copies ran while one was open for 5% of the time, Pallas kernels for 10%

profile of v2, /device:TPU:2, one launch (start us, length us, event | category | flops | bytes accessed | tf_op | source)
XLA Modules:
  0.0 160.5 jit_solution(15975248153419037769)
XLA Ops:
  0.0 1.4 fusion.22
  1.5 3.8 %collective-permute-start = (bf16[384,512]{1,0:T(8,128)(2,1)S(1)}, bf16[384,512]{1,0:T(8,128)(2,1)S(1)}, u32[]{:S(2)}, u32[]{:S(2)}) collective-permute-start(bf16[384,512]{1,0:T(8,128)(2,1)S(1)} %pad_maximum_fusion.refs_0_), channel_id=1, source_target_pairs={{0,1},{1,2},{2,3},{3,4},{4,5},{5,6},{6,7},{7,8},{8,9},{9,10},{10,1... | collective-permute-start | bytes 1179656 | tf_op jit(solution)/shard_map/ppermute | solution.py:161
  5.3 9.5 %collective-permute-start.8 = (bf16[384,512]{1,0:T(8,128)(2,1)S(1)}, bf16[384,512]{1,0:T(8,128)(2,1)}, u32[]{:S(2)}, u32[]{:S(2)}) collective-permute-start(bf16[384,512]{1,0:T(8,128)(2,1)S(1)} %pad_maximum_fusion.refs_0_), channel_id=1, source_target_pairs={{0,15},{1,0},{2,1},{3,2},{4,3},{5,4},{6,5},{7,6},{8,7},{9,8},{10,9... | collective-permute-start | bytes 1179656 | tf_op jit(solution)/shard_map/ppermute | solution.py:161
  14.9 1.9 %collective-permute-start.7 = (bf16[384,512]{1,0:T(8,128)(2,1)S(1)}, bf16[384,512]{1,0:T(8,128)(2,1)}, u32[]{:S(2)}, u32[]{:S(2)}) collective-permute-start(bf16[384,512]{1,0:T(8,128)(2,1)S(1)} %pad_maximum_fusion.1.refs_1_), channel_id=1, source_target_pairs={{0,1},{1,2},{2,3},{3,4},{4,5},{5,6},{6,7},{7,8},{8,9},{9,10},{10,1... | collective-permute-start | bytes 1179656 | tf_op jit(solution)/shard_map/ppermute | solution.py:161
  16.8 5.1 %collective-permute-start.9 = (bf16[384,512]{1,0:T(8,128)(2,1)S(1)}, bf16[384,512]{1,0:T(8,128)(2,1)}, u32[]{:S(2)}, u32[]{:S(2)}) collective-permute-start(bf16[384,512]{1,0:T(8,128)(2,1)S(1)} %pad_maximum_fusion.1.refs_1_), channel_id=1, source_target_pairs={{0,15},{1,0},{2,1},{3,2},{4,3},{5,4},{6,5},{7,6},{8,7},{9,8},{10,9... | collective-permute-start | bytes 1179656 | tf_op jit(solution)/shard_map/ppermute | solution.py:161
  23.3 2.0 %convolution_convert_fusion.1 = bf16[256,4096]{1,0:T(8,128)(2,1)} fusion(bf16[1,1,256,4096]{3,2,1,0:T(8,128)(2,1)S(1)} %copy-done, s32[256]{0:T(256)S(1)} %bitcast.23), kind=kOutput, calls=%fused_computation.1 | convolution fusion | flops 537985024 | bytes 4195328 | tf_op jit(solution)/shard_map/dot_general | solution.py:137
  25.3 7.8 %all-to-all-start = ((bf16[32,8,4096]{2,1,0:T(8,128)(2,1)}), bf16[32,8,4096]{2,1,0:T(8,128)(2,1)}, u32[]{:S(2)}, u32[]{:S(2)}) async-start(bf16[32,8,4096]{2,1,0:T(8,128)(2,1)} %bitcast.21), calls=%async_computation | async-start | bytes 4194304 | tf_op jit(solution)/shard_map/all_to_all | solution.py:173
  33.6 3.5 %collective-permute-start.12 = (bf16[384,512]{1,0:T(8,128)(2,1)}, bf16[384,512]{1,0:T(8,128)(2,1)S(1)}, u32[]{:S(2)}, u32[]{:S(2)}) collective-permute-start(bf16[384,512]{1,0:T(8,128)(2,1)} %collective-permute-done.8.refs_2_), channel_id=1, source_target_pairs={{0,15},{1,0},{2,1},{3,2},{4,3},{5,4},{6,5},{7,6},{8,7},{9,8},{10,9... | collective-permute-start | bytes 1179656 | tf_op jit(solution)/shard_map/ppermute | solution.py:161
  37.1 2.9 %collective-permute-start.13 = (bf16[384,512]{1,0:T(8,128)(2,1)}, bf16[384,512]{1,0:T(8,128)(2,1)S(1)}, u32[]{:S(2)}, u32[]{:S(2)}) collective-permute-start(bf16[384,512]{1,0:T(8,128)(2,1)} %collective-permute-done.9.refs_3_), channel_id=1, source_target_pairs={{0,15},{1,0},{2,1},{3,2},{4,3},{5,4},{6,5},{7,6},{8,7},{9,8},{10,9... | collective-permute-start | bytes 1179656 | tf_op jit(solution)/shard_map/ppermute | solution.py:161
  40.1 2.9 %collective-permute-start.1 = (bf16[384,512]{1,0:T(8,128)(2,1)S(1)}, bf16[384,512]{1,0:T(8,128)(2,1)}, u32[]{:S(2)}, u32[]{:S(2)}) collective-permute-start(bf16[384,512]{1,0:T(8,128)(2,1)S(1)} %collective-permute-done.refs_0_), channel_id=1, source_target_pairs={{0,1},{1,2},{2,3},{3,4},{4,5},{5,6},{6,7},{7,8},{8,9},{9,10},{10,1... | collective-permute-start | bytes 1179656 | tf_op jit(solution)/shard_map/ppermute | solution.py:161
  43.1 2.3 %collective-permute-start.11 = (bf16[384,512]{1,0:T(8,128)(2,1)}, bf16[384,512]{1,0:T(8,128)(2,1)}, u32[]{:S(2)}, u32[]{:S(2)}) collective-permute-start(bf16[384,512]{1,0:T(8,128)(2,1)} %collective-permute-done.7.refs_1_), channel_id=1, source_target_pairs={{0,1},{1,2},{2,3},{3,4},{4,5},{5,6},{6,7},{7,8},{8,9},{9,10},{10,1... | collective-permute-start | bytes 1179656 | tf_op jit(solution)/shard_map/ppermute | solution.py:161
  45.4 2.3 %collective-permute-done.12.refs_2_ = bf16[384,512]{1,0:T(8,128)(2,1)S(1)} collective-permute-done((bf16[384,512]{1,0:T(8,128)(2,1)}, bf16[384,512]{1,0:T(8,128)(2,1)S(1)}, u32[]{:S(2)}, u32[]{:S(2)}) %collective-permute-start.12) | collective-permute-done | bytes 393248 | tf_op jit(solution)/shard_map/ppermute | solution.py:161
  47.7 4.7 %collective-permute-start.15 = (bf16[384,512]{1,0:T(8,128)(2,1)S(1)}, bf16[384,512]{1,0:T(8,128)(2,1)}, u32[]{:S(2)}, u32[]{:S(2)}) collective-permute-start(bf16[384,512]{1,0:T(8,128)(2,1)S(1)} %collective-permute-done.12.refs_2_), channel_id=1, source_target_pairs={{0,15},{1,0},{2,1},{3,2},{4,3},{5,4},{6,5},{7,6},{8,7},{9,8},{10,9... | collective-permute-start | bytes 1179656 | tf_op jit(solution)/shard_map/ppermute | solution.py:161
  53.2 2.9 %collective-permute-done.13.refs_3_ = bf16[384,512]{1,0:T(8,128)(2,1)S(1)} collective-permute-done((bf16[384,512]{1,0:T(8,128)(2,1)}, bf16[384,512]{1,0:T(8,128)(2,1)S(1)}, u32[]{:S(2)}, u32[]{:S(2)}) %collective-permute-start.13) | collective-permute-done | bytes 393248 | tf_op jit(solution)/shard_map/ppermute | solution.py:161
  56.1 4.7 %collective-permute-start.16 = (bf16[384,512]{1,0:T(8,128)(2,1)S(1)}, bf16[384,512]{1,0:T(8,128)(2,1)}, u32[]{:S(2)}, u32[]{:S(2)}) collective-permute-start(bf16[384,512]{1,0:T(8,128)(2,1)S(1)} %collective-permute-done.13.refs_3_), channel_id=1, source_target_pairs={{0,15},{1,0},{2,1},{3,2},{4,3},{5,4},{6,5},{7,6},{8,7},{9,8},{10,9... | collective-permute-start | bytes 1179656 | tf_op jit(solution)/shard_map/ppermute | solution.py:161
  61.7 1.9 %collective-permute-start.2 = (bf16[384,512]{1,0:T(8,128)(2,1)}, bf16[384,512]{1,0:T(8,128)(2,1)}, u32[]{:S(2)}, u32[]{:S(2)}) collective-permute-start(bf16[384,512]{1,0:T(8,128)(2,1)} %collective-permute-done.1.refs_0_), channel_id=1, source_target_pairs={{0,1},{1,2},{2,3},{3,4},{4,5},{5,6},{6,7},{7,8},{8,9},{9,10},{10,1... | collective-permute-start | bytes 1179656 | tf_op jit(solution)/shard_map/ppermute | solution.py:161
  63.6 1.9 %collective-permute-start.14 = (bf16[384,512]{1,0:T(8,128)(2,1)}, bf16[384,512]{1,0:T(8,128)(2,1)}, u32[]{:S(2)}, u32[]{:S(2)}) collective-permute-start(bf16[384,512]{1,0:T(8,128)(2,1)} %collective-permute-done.11.refs_1_), channel_id=1, source_target_pairs={{0,1},{1,2},{2,3},{3,4},{4,5},{5,6},{6,7},{7,8},{8,9},{9,10},{10,1... | collective-permute-start | bytes 1179656 | tf_op jit(solution)/shard_map/ppermute | solution.py:161
  65.6 5.1 %collective-permute-start.19 = (bf16[384,512]{1,0:T(8,128)(2,1)}, bf16[384,512]{1,0:T(8,128)(2,1)}, u32[]{:S(2)}, u32[]{:S(2)}) collective-permute-start(bf16[384,512]{1,0:T(8,128)(2,1)} %collective-permute-done.15.refs_2_), channel_id=1, source_target_pairs={{0,15},{1,0},{2,1},{3,2},{4,3},{5,4},{6,5},{7,6},{8,7},{9,8},{10,9... | collective-permute-start | bytes 1179656 | tf_op jit(solution)/shard_map/ppermute | solution.py:161
  70.7 2.3 %collective-permute-done.16.refs_3_ = bf16[384,512]{1,0:T(8,128)(2,1)} collective-permute-done((bf16[384,512]{1,0:T(8,128)(2,1)S(1)}, bf16[384,512]{1,0:T(8,128)(2,1)}, u32[]{:S(2)}, u32[]{:S(2)}) %collective-permute-start.16) | collective-permute-done | bytes 393248 | tf_op jit(solution)/shard_map/ppermute | solution.py:161
  73.0 4.7 %collective-permute-start.20 = (bf16[384,512]{1,0:T(8,128)(2,1)}, bf16[384,512]{1,0:T(8,128)(2,1)}, u32[]{:S(2)}, u32[]{:S(2)}) collective-permute-start(bf16[384,512]{1,0:T(8,128)(2,1)} %collective-permute-done.16.refs_3_), channel_id=1, source_target_pairs={{0,15},{1,0},{2,1},{3,2},{4,3},{5,4},{6,5},{7,6},{8,7},{9,8},{10,9... | collective-permute-start | bytes 1179656 | tf_op jit(solution)/shard_map/ppermute | solution.py:161
  77.8 2.3 %convolution_convert_fusion.query_ref = bf16[256,4096]{1,0:T(8,128)(2,1)S(1)} fusion(bf16[32,8,4096]{2,1,0:T(8,128)(2,1)} %all-to-all-done, s32[256]{0:T(256)S(1)} %fusion.13), kind=kOutput, calls=%fused_computation | convolution fusion | flops 537985024 | bytes 4195328 | tf_op jit(solution)/shard_map/dot_general | solution.py:137
  82.1 1.9 %collective-permute-start.3 = (bf16[384,512]{1,0:T(8,128)(2,1)}, bf16[384,512]{1,0:T(8,128)(2,1)}, u32[]{:S(2)}, u32[]{:S(2)}) collective-permute-start(bf16[384,512]{1,0:T(8,128)(2,1)} %collective-permute-done.2.refs_0_), channel_id=1, source_target_pairs={{0,1},{1,2},{2,3},{3,4},{4,5},{5,6},{6,7},{7,8},{8,9},{9,10},{10,1... | collective-permute-start | bytes 1179656 | tf_op jit(solution)/shard_map/ppermute | solution.py:161
  84.1 1.9 %collective-permute-start.18 = (bf16[384,512]{1,0:T(8,128)(2,1)}, bf16[384,512]{1,0:T(8,128)(2,1)}, u32[]{:S(2)}, u32[]{:S(2)}) collective-permute-start(bf16[384,512]{1,0:T(8,128)(2,1)} %collective-permute-done.14.refs_1_), channel_id=1, source_target_pairs={{0,1},{1,2},{2,3},{3,4},{4,5},{5,6},{6,7},{7,8},{8,9},{9,10},{10,1... | collective-permute-start | bytes 1179656 | tf_op jit(solution)/shard_map/ppermute | solution.py:161
  86.0 5.1 %collective-permute-start.4 = (bf16[16,4224]{1,0:T(8,128)(2,1)S(1)}, bf16[16,4224]{1,0:T(8,128)(2,1)S(1)}, u32[]{:S(2)}, u32[]{:S(2)}) collective-permute-start(bf16[16,4224]{1,0:T(8,128)(2,1)S(1)} %get-tuple-element.29), channel_id=1, source_target_pairs={{0,15},{1,0},{2,1},{3,2},{4,3},{5,4},{6,5},{7,6},{8,7},{9,8},{10,9... | collective-permute-start | bytes 405512 | tf_op jit(solution)/shard_map/ppermute | solution.py:161
  91.2 3.4 %collective-permute-start.5 = (bf16[16,4224]{1,0:T(8,128)(2,1)S(1)}, bf16[16,4224]{1,0:T(8,128)(2,1)S(1)}, u32[]{:S(2)}, u32[]{:S(2)}) collective-permute-start(bf16[16,4224]{1,0:T(8,128)(2,1)S(1)} %get-tuple-element.30), channel_id=1, source_target_pairs={{0,14},{1,15},{2,0},{3,1},{4,2},{5,3},{6,4},{7,5},{8,6},{9,7},{10,... | collective-permute-start | bytes 405512 | tf_op jit(solution)/shard_map/ppermute | solution.py:161
  94.5 3.9 %collective-permute-start.6 = (bf16[16,4224]{1,0:T(8,128)(2,1)}, bf16[16,4224]{1,0:T(8,128)(2,1)}, u32[]{:S(2)}, u32[]{:S(2)}) collective-permute-start(bf16[16,4224]{1,0:T(8,128)(2,1)} %pad_maximum_fusion.4), channel_id=1, source_target_pairs={{0,1},{1,2},{2,3},{3,4},{4,5},{5,6},{6,7},{7,8},{8,9},{9,10},{10,1... | collective-permute-start | bytes 405512 | tf_op jit(solution)/shard_map/ppermute | solution.py:161
  98.5 3.5 %collective-permute-start.22 = (bf16[384,512]{1,0:T(8,128)(2,1)}, bf16[384,512]{1,0:T(8,128)(2,1)}, u32[]{:S(2)}, u32[]{:S(2)}) collective-permute-start(bf16[384,512]{1,0:T(8,128)(2,1)} %collective-permute-done.19.refs_2_), channel_id=1, source_target_pairs={{0,15},{1,0},{2,1},{3,2},{4,3},{5,4},{6,5},{7,6},{8,7},{9,8},{10,9... | collective-permute-start | bytes 1179656 | tf_op jit(solution)/shard_map/ppermute | solution.py:161
  102.1 4.3 %collective-permute-start.23 = (bf16[384,512]{1,0:T(8,128)(2,1)}, bf16[384,512]{1,0:T(8,128)(2,1)}, u32[]{:S(2)}, u32[]{:S(2)}) collective-permute-start(bf16[384,512]{1,0:T(8,128)(2,1)} %collective-permute-done.20.refs_3_), channel_id=1, source_target_pairs={{0,15},{1,0},{2,1},{3,2},{4,3},{5,4},{6,5},{7,6},{8,7},{9,8},{10,9... | collective-permute-start | bytes 1179656 | tf_op jit(solution)/shard_map/ppermute | solution.py:161
  107.9 1.6 copy-done.2
  110.1 2.2 %attend_0.1.refs_1_ = bf16[32,4096]{1,0:T(8,128)(2,1)S(1)} custom-call(s32[16,128]{1,0:T(8,128)S(1)} %tile.28.limits_ref, bf16[256,4096]{1,0:T(8,128)(2,1)S(1)} %copy-done.2, bf16[384,512]{1,0:T(8,128)(2,1)S(1)} %collective-permute-done.refs_0_, bf16[384,512]{1,0:T(8,128)(2,1)} %collective-permute-done.7.refs_1_, ...), custom_call_target="tpu_custom_call" | custom-call | flops 201326592 | bytes 1048576 | tf_op jit(solution)/shard_map/attend_0/pallas_call | solution.py:95
  112.4 1.9 %collective-permute-start.10 = (bf16[384,512]{1,0:T(8,128)(2,1)}, bf16[384,512]{1,0:T(8,128)(2,1)S(1)}, u32[]{:S(2)}, u32[]{:S(2)}) collective-permute-start(bf16[384,512]{1,0:T(8,128)(2,1)} %collective-permute-done.3.refs_0_), channel_id=1, source_target_pairs={{0,1},{1,2},{2,3},{3,4},{4,5},{5,6},{6,7},{7,8},{8,9},{9,10},{10,1... | collective-permute-start | bytes 1179656 | tf_op jit(solution)/shard_map/ppermute | solution.py:161
  114.3 2.0 %collective-permute-start.21 = (bf16[384,512]{1,0:T(8,128)(2,1)}, bf16[384,512]{1,0:T(8,128)(2,1)S(1)}, u32[]{:S(2)}, u32[]{:S(2)}) collective-permute-start(bf16[384,512]{1,0:T(8,128)(2,1)} %collective-permute-done.18.refs_1_), channel_id=1, source_target_pairs={{0,1},{1,2},{2,3},{3,4},{4,5},{5,6},{6,7},{7,8},{8,9},{9,10},{10,1... | collective-permute-start | bytes 1179656 | tf_op jit(solution)/shard_map/ppermute | solution.py:161
  116.3 5.1 %collective-permute-start.25 = (bf16[384,512]{1,0:T(8,128)(2,1)}, bf16[384,512]{1,0:T(8,128)(2,1)S(1)}, u32[]{:S(2)}, u32[]{:S(2)}) collective-permute-start(bf16[384,512]{1,0:T(8,128)(2,1)} %collective-permute-done.22.refs_2_), channel_id=1, source_target_pairs={{0,15},{1,0},{2,1},{3,2},{4,3},{5,4},{6,5},{7,6},{8,7},{9,8},{10,9... | collective-permute-start | bytes 1179656 | tf_op jit(solution)/shard_map/ppermute | solution.py:161
  121.4 3.9 %collective-permute-start.26 = (bf16[384,512]{1,0:T(8,128)(2,1)}, bf16[384,512]{1,0:T(8,128)(2,1)S(1)}, u32[]{:S(2)}, u32[]{:S(2)}) collective-permute-start(bf16[384,512]{1,0:T(8,128)(2,1)} %collective-permute-done.23.refs_3_), channel_id=1, source_target_pairs={{0,15},{1,0},{2,1},{3,2},{4,3},{5,4},{6,5},{7,6},{8,7},{9,8},{10,9... | collective-permute-start | bytes 1179656 | tf_op jit(solution)/shard_map/ppermute | solution.py:161
  125.4 2.0 %attend_2.1.refs_2_ = bf16[32,4096]{1,0:T(8,128)(2,1)S(1)} custom-call(s32[16,128]{1,0:T(8,128)S(1)} %tile.28.limits_ref, bf16[256,4096]{1,0:T(8,128)(2,1)S(1)} %copy-done.2, bf16[384,512]{1,0:T(8,128)(2,1)} %collective-permute-done.1.refs_0_, bf16[384,512]{1,0:T(8,128)(2,1)} %collective-permute-done.11.refs_1_, bf16[384,512]{1,0:T(8,128)(2,1)S(1)} %copy-done.5, ...), custom_call_target="tpu_custom_call" | custom-call | flops 201326592 | bytes 1048576 | tf_op jit(solution)/shard_map/attend_2/pallas_call | solution.py:95
  127.4 2.4 %attend_4.1.refs_3_ = bf16[32,4096]{1,0:T(8,128)(2,1)S(1)} custom-call(s32[16,128]{1,0:T(8,128)S(1)} %tile.28.limits_ref, bf16[256,4096]{1,0:T(8,128)(2,1)S(1)} %copy-done.2, bf16[384,512]{1,0:T(8,128)(2,1)} %collective-permute-done.2.refs_0_, bf16[384,512]{1,0:T(8,128)(2,1)} %collective-permute-done.14.refs_1_, ...), custom_call_target="tpu_custom_call" | custom-call | flops 201326592 | bytes 1048576 | tf_op jit(solution)/shard_map/attend_4/pallas_call | solution.py:95
  129.9 1.9 %collective-permute-start.17 = (bf16[384,512]{1,0:T(8,128)(2,1)S(1)}, bf16[384,512]{1,0:T(8,128)(2,1)S(1)}, u32[]{:S(2)}, u32[]{:S(2)}) collective-permute-start(bf16[384,512]{1,0:T(8,128)(2,1)S(1)} %collective-permute-done.10.refs_0_), channel_id=1, source_target_pairs={{0,1},{1,2},{2,3},{3,4},{4,5},{5,6},{6,7},{7,8},{8,9},{9,10},{10,1... | collective-permute-start | bytes 1179656 | tf_op jit(solution)/shard_map/ppermute | solution.py:161
  131.8 1.9 %collective-permute-start.24 = (bf16[384,512]{1,0:T(8,128)(2,1)S(1)}, bf16[384,512]{1,0:T(8,128)(2,1)S(1)}, u32[]{:S(2)}, u32[]{:S(2)}) collective-permute-start(bf16[384,512]{1,0:T(8,128)(2,1)S(1)} %collective-permute-done.21.refs_1_), channel_id=1, source_target_pairs={{0,1},{1,2},{2,3},{3,4},{4,5},{5,6},{6,7},{7,8},{8,9},{9,10},{10,1... | collective-permute-start | bytes 1179656 | tf_op jit(solution)/shard_map/ppermute | solution.py:161
  134.6 1.5 attend_guests.3
  136.2 4.8 %collective-permute-start.29 = (bf16[16,4096]{1,0:T(8,128)(2,1)S(1)}, bf16[16,4096]{1,0:T(8,128)(2,1)S(1)}, u32[]{:S(2)}, u32[]{:S(2)}) collective-permute-start(bf16[16,4096]{1,0:T(8,128)(2,1)S(1)} %attend_guests.3), channel_id=1, source_target_pairs={{0,15},{1,0},{2,1},{3,2},{4,3},{5,4},{6,5},{7,6},{8,7},{9,8},{10,9... | collective-permute-start | bytes 393224 | tf_op jit(solution)/shard_map/ppermute | solution.py:161
  141.0 2.3 %attend_6.1.refs_4_ = bf16[32,4096]{1,0:T(8,128)(2,1)S(1)} custom-call(s32[16,128]{1,0:T(8,128)S(1)} %tile.28.limits_ref, bf16[256,4096]{1,0:T(8,128)(2,1)S(1)} %copy-done.3, bf16[384,512]{1,0:T(8,128)(2,1)} %collective-permute-done.3.refs_0_, bf16[384,512]{1,0:T(8,128)(2,1)} %collective-permute-done.18.refs_1_, ...), custom_call_target="tpu_custom_call" | custom-call | flops 201326592 | bytes 1048576 | tf_op jit(solution)/shard_map/attend_6/pallas_call | solution.py:95
  143.2 2.1 %attend_8.1.refs_5_ = bf16[32,4096]{1,0:T(8,128)(2,1)S(1)} custom-call(s32[16,128]{1,0:T(8,128)S(1)} %tile.28.limits_ref, bf16[256,4096]{1,0:T(8,128)(2,1)S(1)} %copy-done.3, bf16[384,512]{1,0:T(8,128)(2,1)S(1)} %collective-permute-done.10.refs_0_, bf16[384,512]{1,0:T(8,128)(2,1)S(1)} %collective-permute-done.21.refs_1_, ...), custom_call_target="tpu_custom_call" | custom-call | flops 201326592 | bytes 1048576 | tf_op jit(solution)/shard_map/attend_8/pallas_call | solution.py:95
  145.3 1.7 %place_held.1.refs_0_ = bf16[256,4096]{1,0:T(8,128)(2,1)} custom-call(s32[16]{0:T(128)S(1)} %select_reduce_fusion.2.where_ref, bf16[16,4096]{1,0:T(8,128)(2,1)S(1)} %attend_15.1.refs_0_, bf16[32,4096]{1,0:T(8,128)(2,1)S(1)} %attend_0.1.refs_1_, bf16[32,4096]{1,0:T(8,128)(2,1)S(1)} %attend_2.1.refs_2_, bf16[32,4096]{1,0:T(8,128)(2,1)S(1)} %attend_4.1.refs_3_, ...), custom_call_target="tpu_custom_call" | custom-call | bytes 131072 | tf_op jit(solution)/shard_map/place_held/pallas_call | solution.py:121
  148.1 1.9 %collective-permute-start.27 = (bf16[16,4096]{1,0:T(8,128)(2,1)S(1)}, bf16[16,4096]{1,0:T(8,128)(2,1)S(1)}, u32[]{:S(2)}, u32[]{:S(2)}) collective-permute-start(bf16[16,4096]{1,0:T(8,128)(2,1)S(1)} %get-tuple-element.44), channel_id=1, source_target_pairs={{0,1},{1,2},{2,3},{3,4},{4,5},{5,6},{6,7},{7,8},{8,9},{9,10},{10,1... | collective-permute-start | bytes 393224 | tf_op jit(solution)/shard_map/ppermute | solution.py:161
  150.0 2.6 %collective-permute-start.28 = (bf16[16,4096]{1,0:T(8,128)(2,1)S(1)}, bf16[16,4096]{1,0:T(8,128)(2,1)S(1)}, u32[]{:S(2)}, u32[]{:S(2)}) collective-permute-start(bf16[16,4096]{1,0:T(8,128)(2,1)S(1)} %get-tuple-element.45), channel_id=1, source_target_pairs={{0,2},{1,3},{2,4},{3,5},{4,6},{5,7},{6,8},{7,9},{8,10},{9,11},{10,... | collective-permute-start | bytes 393224 | tf_op jit(solution)/shard_map/ppermute | solution.py:161
  153.6 2.6 %collective-permute-done.27.refs_2_ = bf16[16,4096]{1,0:T(8,128)(2,1)S(1)} collective-permute-done((bf16[16,4096]{1,0:T(8,128)(2,1)S(1)}, bf16[16,4096]{1,0:T(8,128)(2,1)S(1)}, u32[]{:S(2)}, u32[]{:S(2)}) %collective-permute-start.27) | collective-permute-done | bytes 131104 | tf_op jit(solution)/shard_map/ppermute | solution.py:161
  156.1 2.9 %collective-permute-done.28.refs_3_ = bf16[16,4096]{1,0:T(8,128)(2,1)S(1)} collective-permute-done((bf16[16,4096]{1,0:T(8,128)(2,1)S(1)}, bf16[16,4096]{1,0:T(8,128)(2,1)S(1)}, u32[]{:S(2)}, u32[]{:S(2)}) %collective-permute-start.28) | collective-permute-done | bytes 131104 | tf_op jit(solution)/shard_map/ppermute | solution.py:161
  159.1 1.4 place_last.1
  (86 shorter events, 10.5 us)
Async XLA Ops:
  0.0 23.2 %copy-start = (bf16[1,1,256,4096]{3,2,1,0:T(8,128)(2,1)S(1)}, bf16[1,1,256,4096]{3,2,1,0:T(8,128)(2,1)}, u32[]{:S(2)}) copy-start(bf16[1,1,256,4096]{3,2,1,0:T(8,128)(2,1)} %param.6) | copy-start | bytes 6291460
  0.0 22.4 %copy-start.12 = (s32[1,1,256]{2,1,0:T(1,128)S(1)}, s32[1,1,256]{2,1,0:T(1,128)}, u32[]{:S(2)}) copy-start(s32[1,1,256]{2,1,0:T(1,128)} %param.9) | copy-start | bytes 3076
  0.0 23.2 %copy-start.13 = (s32[1,1,16]{2,1,0:T(1,128)S(1)}, s32[1,1,16]{2,1,0:T(1,128)}, u32[]{:S(2)}) copy-start(s32[1,1,16]{2,1,0:T(1,128)} %param.10) | copy-start | bytes 196
  0.0 23.2 %copy-start.8 = (s32[1,1,256]{2,1,0:T(1,128)S(1)}, s32[1,1,256]{2,1,0:T(1,128)}, u32[]{:S(2)}) copy-start(s32[1,1,256]{2,1,0:T(1,128)} %param.7) | copy-start | bytes 3076
  1.5 21.7 %collective-permute-start = (bf16[384,512]{1,0:T(8,128)(2,1)S(1)}, bf16[384,512]{1,0:T(8,128)(2,1)S(1)}, u32[]{:S(2)}, u32[]{:S(2)}) collective-permute-start(bf16[384,512]{1,0:T(8,128)(2,1)S(1)} %pad_maximum_fusion.refs_0_), channel_id=1, source_target_pairs={{0,1},{1,2},{2,3},{3,4},{4,5},{5,6},{6,7},{7,8},{8,9},{9,10},{10,1... | collective-permute-start | bytes 1179656 | tf_op jit(solution)/shard_map/ppermute | solution.py:161
  5.3 28.3 %collective-permute-start.8 = (bf16[384,512]{1,0:T(8,128)(2,1)S(1)}, bf16[384,512]{1,0:T(8,128)(2,1)}, u32[]{:S(2)}, u32[]{:S(2)}) collective-permute-start(bf16[384,512]{1,0:T(8,128)(2,1)S(1)} %pad_maximum_fusion.refs_0_), channel_id=1, source_target_pairs={{0,15},{1,0},{2,1},{3,2},{4,3},{5,4},{6,5},{7,6},{8,7},{9,8},{10,9... | collective-permute-start | bytes 1179656 | tf_op jit(solution)/shard_map/ppermute | solution.py:161
  14.9 28.2 %collective-permute-start.7 = (bf16[384,512]{1,0:T(8,128)(2,1)S(1)}, bf16[384,512]{1,0:T(8,128)(2,1)}, u32[]{:S(2)}, u32[]{:S(2)}) collective-permute-start(bf16[384,512]{1,0:T(8,128)(2,1)S(1)} %pad_maximum_fusion.1.refs_1_), channel_id=1, source_target_pairs={{0,1},{1,2},{2,3},{3,4},{4,5},{5,6},{6,7},{7,8},{8,9},{9,10},{10,1... | collective-permute-start | bytes 1179656 | tf_op jit(solution)/shard_map/ppermute | solution.py:161
  16.8 20.4 %collective-permute-start.9 = (bf16[384,512]{1,0:T(8,128)(2,1)S(1)}, bf16[384,512]{1,0:T(8,128)(2,1)}, u32[]{:S(2)}, u32[]{:S(2)}) collective-permute-start(bf16[384,512]{1,0:T(8,128)(2,1)S(1)} %pad_maximum_fusion.1.refs_1_), channel_id=1, source_target_pairs={{0,15},{1,0},{2,1},{3,2},{4,3},{5,4},{6,5},{7,6},{8,7},{9,8},{10,9... | collective-permute-start | bytes 1179656 | tf_op jit(solution)/shard_map/ppermute | solution.py:161
  23.2 38.4 %copy-start.10 = (s32[16]{0:T(128)}, s32[16]{0:T(128)S(1)}, u32[]{:S(2)}) copy-start(s32[16]{0:T(128)S(1)} %compare_select_fusion.3) | copy-start | bytes 196
  25.3 14.8 %copy-start.9 = (s32[1,1,256]{2,1,0:T(1,128)S(1)}, s32[1,1,256]{2,1,0:T(1,128)}, u32[]{:S(2)}) copy-start(s32[1,1,256]{2,1,0:T(1,128)} %param.8) | copy-start | bytes 3076
  25.3 52.5 %all-to-all-start = ((bf16[32,8,4096]{2,1,0:T(8,128)(2,1)}), bf16[32,8,4096]{2,1,0:T(8,128)(2,1)}, u32[]{:S(2)}, u32[]{:S(2)}) async-start(bf16[32,8,4096]{2,1,0:T(8,128)(2,1)} %bitcast.21), calls=%async_computation | async-start | bytes 4194304 | tf_op jit(solution)/shard_map/all_to_all | solution.py:173
  33.6 14.1 %collective-permute-start.12 = (bf16[384,512]{1,0:T(8,128)(2,1)}, bf16[384,512]{1,0:T(8,128)(2,1)S(1)}, u32[]{:S(2)}, u32[]{:S(2)}) collective-permute-start(bf16[384,512]{1,0:T(8,128)(2,1)} %collective-permute-done.8.refs_2_), channel_id=1, source_target_pairs={{0,15},{1,0},{2,1},{3,2},{4,3},{5,4},{6,5},{7,6},{8,7},{9,8},{10,9... | collective-permute-start | bytes 1179656 | tf_op jit(solution)/shard_map/ppermute | solution.py:161
  37.1 18.9 %collective-permute-start.13 = (bf16[384,512]{1,0:T(8,128)(2,1)}, bf16[384,512]{1,0:T(8,128)(2,1)S(1)}, u32[]{:S(2)}, u32[]{:S(2)}) collective-permute-start(bf16[384,512]{1,0:T(8,128)(2,1)} %collective-permute-done.9.refs_3_), channel_id=1, source_target_pairs={{0,15},{1,0},{2,1},{3,2},{4,3},{5,4},{6,5},{7,6},{8,7},{9,8},{10,9... | collective-permute-start | bytes 1179656 | tf_op jit(solution)/shard_map/ppermute | solution.py:161
  40.1 21.6 %collective-permute-start.1 = (bf16[384,512]{1,0:T(8,128)(2,1)S(1)}, bf16[384,512]{1,0:T(8,128)(2,1)}, u32[]{:S(2)}, u32[]{:S(2)}) collective-permute-start(bf16[384,512]{1,0:T(8,128)(2,1)S(1)} %collective-permute-done.refs_0_), channel_id=1, source_target_pairs={{0,1},{1,2},{2,3},{3,4},{4,5},{5,6},{6,7},{7,8},{8,9},{9,10},{10,1... | collective-permute-start | bytes 1179656 | tf_op jit(solution)/shard_map/ppermute | solution.py:161
  43.1 20.6 %collective-permute-start.11 = (bf16[384,512]{1,0:T(8,128)(2,1)}, bf16[384,512]{1,0:T(8,128)(2,1)}, u32[]{:S(2)}, u32[]{:S(2)}) collective-permute-start(bf16[384,512]{1,0:T(8,128)(2,1)} %collective-permute-done.7.refs_1_), channel_id=1, source_target_pairs={{0,1},{1,2},{2,3},{3,4},{4,5},{5,6},{6,7},{7,8},{8,9},{9,10},{10,1... | collective-permute-start | bytes 1179656 | tf_op jit(solution)/shard_map/ppermute | solution.py:161
  47.7 17.9 %collective-permute-start.15 = (bf16[384,512]{1,0:T(8,128)(2,1)S(1)}, bf16[384,512]{1,0:T(8,128)(2,1)}, u32[]{:S(2)}, u32[]{:S(2)}) collective-permute-start(bf16[384,512]{1,0:T(8,128)(2,1)S(1)} %collective-permute-done.12.refs_2_), channel_id=1, source_target_pairs={{0,15},{1,0},{2,1},{3,2},{4,3},{5,4},{6,5},{7,6},{8,7},{9,8},{10,9... | collective-permute-start | bytes 1179656 | tf_op jit(solution)/shard_map/ppermute | solution.py:161
  52.4 0.8 copy-start.4
  56.1 17.0 %collective-permute-start.16 = (bf16[384,512]{1,0:T(8,128)(2,1)S(1)}, bf16[384,512]{1,0:T(8,128)(2,1)}, u32[]{:S(2)}, u32[]{:S(2)}) collective-permute-start(bf16[384,512]{1,0:T(8,128)(2,1)S(1)} %collective-permute-done.13.refs_3_), channel_id=1, source_target_pairs={{0,15},{1,0},{2,1},{3,2},{4,3},{5,4},{6,5},{7,6},{8,7},{9,8},{10,9... | collective-permute-start | bytes 1179656 | tf_op jit(solution)/shard_map/ppermute | solution.py:161
  60.8 0.7 copy-start.6
  61.7 20.5 %collective-permute-start.2 = (bf16[384,512]{1,0:T(8,128)(2,1)}, bf16[384,512]{1,0:T(8,128)(2,1)}, u32[]{:S(2)}, u32[]{:S(2)}) collective-permute-start(bf16[384,512]{1,0:T(8,128)(2,1)} %collective-permute-done.1.refs_0_), channel_id=1, source_target_pairs={{0,1},{1,2},{2,3},{3,4},{4,5},{5,6},{6,7},{7,8},{8,9},{9,10},{10,1... | collective-permute-start | bytes 1179656 | tf_op jit(solution)/shard_map/ppermute | solution.py:161
  63.6 20.4 %collective-permute-start.14 = (bf16[384,512]{1,0:T(8,128)(2,1)}, bf16[384,512]{1,0:T(8,128)(2,1)}, u32[]{:S(2)}, u32[]{:S(2)}) collective-permute-start(bf16[384,512]{1,0:T(8,128)(2,1)} %collective-permute-done.11.refs_1_), channel_id=1, source_target_pairs={{0,1},{1,2},{2,3},{3,4},{4,5},{5,6},{6,7},{7,8},{8,9},{9,10},{10,1... | collective-permute-start | bytes 1179656 | tf_op jit(solution)/shard_map/ppermute | solution.py:161
  65.6 25.6 %collective-permute-start.19 = (bf16[384,512]{1,0:T(8,128)(2,1)}, bf16[384,512]{1,0:T(8,128)(2,1)}, u32[]{:S(2)}, u32[]{:S(2)}) collective-permute-start(bf16[384,512]{1,0:T(8,128)(2,1)} %collective-permute-done.15.refs_2_), channel_id=1, source_target_pairs={{0,15},{1,0},{2,1},{3,2},{4,3},{5,4},{6,5},{7,6},{8,7},{9,8},{10,9... | collective-permute-start | bytes 1179656 | tf_op jit(solution)/shard_map/ppermute | solution.py:161
  73.0 21.5 %collective-permute-start.20 = (bf16[384,512]{1,0:T(8,128)(2,1)}, bf16[384,512]{1,0:T(8,128)(2,1)}, u32[]{:S(2)}, u32[]{:S(2)}) collective-permute-start(bf16[384,512]{1,0:T(8,128)(2,1)} %collective-permute-done.16.refs_3_), channel_id=1, source_target_pairs={{0,15},{1,0},{2,1},{3,2},{4,3},{5,4},{6,5},{7,6},{8,7},{9,8},{10,9... | collective-permute-start | bytes 1179656 | tf_op jit(solution)/shard_map/ppermute | solution.py:161
  80.1 1.3 copy-start.1
  82.1 30.2 %collective-permute-start.3 = (bf16[384,512]{1,0:T(8,128)(2,1)}, bf16[384,512]{1,0:T(8,128)(2,1)}, u32[]{:S(2)}, u32[]{:S(2)}) collective-permute-start(bf16[384,512]{1,0:T(8,128)(2,1)} %collective-permute-done.2.refs_0_), channel_id=1, source_target_pairs={{0,1},{1,2},{2,3},{3,4},{4,5},{5,6},{6,7},{7,8},{8,9},{9,10},{10,1... | collective-permute-start | bytes 1179656 | tf_op jit(solution)/shard_map/ppermute | solution.py:161
  84.1 30.2 %collective-permute-start.18 = (bf16[384,512]{1,0:T(8,128)(2,1)}, bf16[384,512]{1,0:T(8,128)(2,1)}, u32[]{:S(2)}, u32[]{:S(2)}) collective-permute-start(bf16[384,512]{1,0:T(8,128)(2,1)} %collective-permute-done.14.refs_1_), channel_id=1, source_target_pairs={{0,1},{1,2},{2,3},{3,4},{4,5},{5,6},{6,7},{7,8},{8,9},{9,10},{10,1... | collective-permute-start | bytes 1179656 | tf_op jit(solution)/shard_map/ppermute | solution.py:161
  86.0 12.5 %collective-permute-start.4 = (bf16[16,4224]{1,0:T(8,128)(2,1)S(1)}, bf16[16,4224]{1,0:T(8,128)(2,1)S(1)}, u32[]{:S(2)}, u32[]{:S(2)}) collective-permute-start(bf16[16,4224]{1,0:T(8,128)(2,1)S(1)} %get-tuple-element.29), channel_id=1, source_target_pairs={{0,15},{1,0},{2,1},{3,2},{4,3},{5,4},{6,5},{7,6},{8,7},{9,8},{10,9... | collective-permute-start | bytes 405512 | tf_op jit(solution)/shard_map/ppermute | solution.py:161
  91.2 10.9 %collective-permute-start.5 = (bf16[16,4224]{1,0:T(8,128)(2,1)S(1)}, bf16[16,4224]{1,0:T(8,128)(2,1)S(1)}, u32[]{:S(2)}, u32[]{:S(2)}) collective-permute-start(bf16[16,4224]{1,0:T(8,128)(2,1)S(1)} %get-tuple-element.30), channel_id=1, source_target_pairs={{0,14},{1,15},{2,0},{3,1},{4,2},{5,3},{6,4},{7,5},{8,6},{9,7},{10,... | collective-permute-start | bytes 405512 | tf_op jit(solution)/shard_map/ppermute | solution.py:161
  94.5 17.8 %collective-permute-start.6 = (bf16[16,4224]{1,0:T(8,128)(2,1)}, bf16[16,4224]{1,0:T(8,128)(2,1)}, u32[]{:S(2)}, u32[]{:S(2)}) collective-permute-start(bf16[16,4224]{1,0:T(8,128)(2,1)} %pad_maximum_fusion.4), channel_id=1, source_target_pairs={{0,1},{1,2},{2,3},{3,4},{4,5},{5,6},{6,7},{7,8},{8,9},{9,10},{10,1... | collective-permute-start | bytes 405512 | tf_op jit(solution)/shard_map/ppermute | solution.py:161
  98.5 17.8 %collective-permute-start.22 = (bf16[384,512]{1,0:T(8,128)(2,1)}, bf16[384,512]{1,0:T(8,128)(2,1)}, u32[]{:S(2)}, u32[]{:S(2)}) collective-permute-start(bf16[384,512]{1,0:T(8,128)(2,1)} %collective-permute-done.19.refs_2_), channel_id=1, source_target_pairs={{0,15},{1,0},{2,1},{3,2},{4,3},{5,4},{6,5},{7,6},{8,7},{9,8},{10,9... | collective-permute-start | bytes 1179656 | tf_op jit(solution)/shard_map/ppermute | solution.py:161
  102.1 19.4 %collective-permute-start.23 = (bf16[384,512]{1,0:T(8,128)(2,1)}, bf16[384,512]{1,0:T(8,128)(2,1)}, u32[]{:S(2)}, u32[]{:S(2)}) collective-permute-start(bf16[384,512]{1,0:T(8,128)(2,1)} %collective-permute-done.20.refs_3_), channel_id=1, source_target_pairs={{0,15},{1,0},{2,1},{3,2},{4,3},{5,4},{6,5},{7,6},{8,7},{9,8},{10,9... | collective-permute-start | bytes 1179656 | tf_op jit(solution)/shard_map/ppermute | solution.py:161
  107.9 1.6 copy-start.2
  110.1 15.2 %copy-start.5 = (bf16[384,512]{1,0:T(8,128)(2,1)S(1)}, bf16[384,512]{1,0:T(8,128)(2,1)}, u32[]{:S(2)}) copy-start(bf16[384,512]{1,0:T(8,128)(2,1)} %copy-done.4) | copy-start | bytes 1179652
  110.1 15.2 %copy-start.7 = (bf16[384,512]{1,0:T(8,128)(2,1)S(1)}, bf16[384,512]{1,0:T(8,128)(2,1)}, u32[]{:S(2)}) copy-start(bf16[384,512]{1,0:T(8,128)(2,1)} %copy-done.6) | copy-start | bytes 1179652
  112.4 17.5 %collective-permute-start.10 = (bf16[384,512]{1,0:T(8,128)(2,1)}, bf16[384,512]{1,0:T(8,128)(2,1)S(1)}, u32[]{:S(2)}, u32[]{:S(2)}) collective-permute-start(bf16[384,512]{1,0:T(8,128)(2,1)} %collective-permute-done.3.refs_0_), channel_id=1, source_target_pairs={{0,1},{1,2},{2,3},{3,4},{4,5},{5,6},{6,7},{7,8},{8,9},{9,10},{10,1... | collective-permute-start | bytes 1179656 | tf_op jit(solution)/shard_map/ppermute | solution.py:161
  114.3 17.5 %collective-permute-start.21 = (bf16[384,512]{1,0:T(8,128)(2,1)}, bf16[384,512]{1,0:T(8,128)(2,1)S(1)}, u32[]{:S(2)}, u32[]{:S(2)}) collective-permute-start(bf16[384,512]{1,0:T(8,128)(2,1)} %collective-permute-done.18.refs_1_), channel_id=1, source_target_pairs={{0,1},{1,2},{2,3},{3,4},{4,5},{5,6},{6,7},{7,8},{8,9},{9,10},{10,1... | collective-permute-start | bytes 1179656 | tf_op jit(solution)/shard_map/ppermute | solution.py:161
  116.3 17.6 %collective-permute-start.25 = (bf16[384,512]{1,0:T(8,128)(2,1)}, bf16[384,512]{1,0:T(8,128)(2,1)S(1)}, u32[]{:S(2)}, u32[]{:S(2)}) collective-permute-start(bf16[384,512]{1,0:T(8,128)(2,1)} %collective-permute-done.22.refs_2_), channel_id=1, source_target_pairs={{0,15},{1,0},{2,1},{3,2},{4,3},{5,4},{6,5},{7,6},{8,7},{9,8},{10,9... | collective-permute-start | bytes 1179656 | tf_op jit(solution)/shard_map/ppermute | solution.py:161
  121.4 13.2 %collective-permute-start.26 = (bf16[384,512]{1,0:T(8,128)(2,1)}, bf16[384,512]{1,0:T(8,128)(2,1)S(1)}, u32[]{:S(2)}, u32[]{:S(2)}) collective-permute-start(bf16[384,512]{1,0:T(8,128)(2,1)} %collective-permute-done.23.refs_3_), channel_id=1, source_target_pairs={{0,15},{1,0},{2,1},{3,2},{4,3},{5,4},{6,5},{7,6},{8,7},{9,8},{10,9... | collective-permute-start | bytes 1179656 | tf_op jit(solution)/shard_map/ppermute | solution.py:161
  127.4 6.3 %copy-start.11 = (s32[16]{0:T(128)S(1)}, s32[16]{0:T(128)}, u32[]{:S(2)}) copy-start(s32[16]{0:T(128)} %copy-done.10) | copy-start | bytes 196
  127.4 13.5 %copy-start.3 = (bf16[256,4096]{1,0:T(8,128)(2,1)S(1)}, bf16[256,4096]{1,0:T(8,128)(2,1)}, u32[]{:S(2)}) copy-start(bf16[256,4096]{1,0:T(8,128)(2,1)} %copy-done.1) | copy-start | bytes 6291460
  129.9 17.2 %collective-permute-start.17 = (bf16[384,512]{1,0:T(8,128)(2,1)S(1)}, bf16[384,512]{1,0:T(8,128)(2,1)S(1)}, u32[]{:S(2)}, u32[]{:S(2)}) collective-permute-start(bf16[384,512]{1,0:T(8,128)(2,1)S(1)} %collective-permute-done.10.refs_0_), channel_id=1, source_target_pairs={{0,1},{1,2},{2,3},{3,4},{4,5},{5,6},{6,7},{7,8},{8,9},{9,10},{10,1... | collective-permute-start | bytes 1179656 | tf_op jit(solution)/shard_map/ppermute | solution.py:161
  131.8 15.3 %collective-permute-start.24 = (bf16[384,512]{1,0:T(8,128)(2,1)S(1)}, bf16[384,512]{1,0:T(8,128)(2,1)S(1)}, u32[]{:S(2)}, u32[]{:S(2)}) collective-permute-start(bf16[384,512]{1,0:T(8,128)(2,1)S(1)} %collective-permute-done.21.refs_1_), channel_id=1, source_target_pairs={{0,1},{1,2},{2,3},{3,4},{4,5},{5,6},{6,7},{7,8},{8,9},{9,10},{10,1... | collective-permute-start | bytes 1179656 | tf_op jit(solution)/shard_map/ppermute | solution.py:161
  136.2 17.4 %collective-permute-start.29 = (bf16[16,4096]{1,0:T(8,128)(2,1)S(1)}, bf16[16,4096]{1,0:T(8,128)(2,1)S(1)}, u32[]{:S(2)}, u32[]{:S(2)}) collective-permute-start(bf16[16,4096]{1,0:T(8,128)(2,1)S(1)} %attend_guests.3), channel_id=1, source_target_pairs={{0,15},{1,0},{2,1},{3,2},{4,3},{5,4},{6,5},{7,6},{8,7},{9,8},{10,9... | collective-permute-start | bytes 393224 | tf_op jit(solution)/shard_map/ppermute | solution.py:161
  148.1 8.1 %collective-permute-start.27 = (bf16[16,4096]{1,0:T(8,128)(2,1)S(1)}, bf16[16,4096]{1,0:T(8,128)(2,1)S(1)}, u32[]{:S(2)}, u32[]{:S(2)}) collective-permute-start(bf16[16,4096]{1,0:T(8,128)(2,1)S(1)} %get-tuple-element.44), channel_id=1, source_target_pairs={{0,1},{1,2},{2,3},{3,4},{4,5},{5,6},{6,7},{7,8},{8,9},{9,10},{10,1... | collective-permute-start | bytes 393224 | tf_op jit(solution)/shard_map/ppermute | solution.py:161
  150.0 9.1 %collective-permute-start.28 = (bf16[16,4096]{1,0:T(8,128)(2,1)S(1)}, bf16[16,4096]{1,0:T(8,128)(2,1)S(1)}, u32[]{:S(2)}, u32[]{:S(2)}) collective-permute-start(bf16[16,4096]{1,0:T(8,128)(2,1)S(1)} %get-tuple-element.45), channel_id=1, source_target_pairs={{0,2},{1,3},{2,4},{3,5},{4,6},{5,7},{6,8},{7,9},{8,10},{9,11},{10,... | collective-permute-start | bytes 393224 | tf_op jit(solution)/shard_map/ppermute | solution.py:161

commit v3 on v2

--- a/solution.py
+++ b/solution.py
@@ -15,19 +15,14 @@
 SCALE = math.log2(math.e) / math.sqrt(HD)
 
 
-PARTS = 2
-HEADS = KVH // PARTS
-
-
-def score_group(query_ref, row, rows, blocks, limits, out_ref, out_row):
-    cache_len = blocks[0].shape[0]
+def score_group(query_ref, row, rows, block, limits, out_ref, out_row):
+    cache_len = block.shape[0]
     visible = lax.broadcasted_iota(jnp.int32, (cache_len, GROUPS * rows), 0) <= limits
     for k in range(KVH):
-        block, at = blocks[k // HEADS], k % HEADS
         heads = [slice((k * GROUPS + g) * HD, (k * GROUPS + g + 1) * HD) for g in range(GROUPS)]
         query = jnp.concatenate([query_ref[row : row + rows, h] for h in heads], axis=0)
         scores = lax.dot_general(
-            block[:, at * HD : (at + 1) * HD],
+            block[:, k * HD : (k + 1) * HD],
             query,
             (((1,), (1,)), ((), ())),
             preferred_element_type=jnp.float32,
@@ -38,7 +33,7 @@
         row_total = jnp.sum(exponent, axis=0, keepdims=True)
         mixed = lax.dot_general(
             exponent.astype(jnp.bfloat16),
-            block[:, (HEADS + at) * HD : (HEADS + at + 1) * HD],
+            block[:, (KVH + k) * HD : (KVH + k + 1) * HD],
             (((0,), (0,)), ((), ())),
             preferred_element_type=jnp.float32,
         )
@@ -50,17 +45,15 @@
 def step_kernel(spots, rows, limits_ref, query_ref, *refs):
     blocks, out_ref = refs[:-1], refs[-1]
     for i, spot in enumerate(spots):
-        group = blocks[PARTS * i : PARTS * (i + 1)]
-        score_group(query_ref, spot * rows, rows, group, limits_ref[spot : spot + 1, :], out_ref, i * rows)
-
-
-def guest_kernel(count, rows, *refs):
-    blocks, refs = refs[:PARTS], refs[PARTS:]
+        score_group(query_ref, spot * rows, rows, blocks[i], limits_ref[spot : spot + 1, :], out_ref, i * rows)
+
+
+def guest_kernel(count, rows, block, *refs):
     for guest_ref, out_ref in zip(refs[:count], refs[count:]):
         width = out_ref.shape[1]
         parts = guest_ref[:, width:].astype(jnp.float32)
         limits = (parts[0:1] * 16.0 + parts[1:2]).astype(jnp.int32)
-        score_group(guest_ref, 0, rows, blocks, limits, out_ref, 0)
+        score_group(guest_ref, 0, rows, block, limits, out_ref, 0)
 
 
 def place_kernel(ref_spots, rows, again, where_ref, *refs):
@@ -95,7 +88,7 @@
     return pl.pallas_call(
         functools.partial(step_kernel, spots, rows),
         out_shape=jax.ShapeDtypeStruct((len(spots) * rows, packed.shape[1]), packed.dtype),
-        in_specs=[VMEM] * (2 + len(blocks)),
+        in_specs=[VMEM] * (2 + len(spots)),
         out_specs=VMEM,
         compiler_params=PARAMS,
         cost_estimate=cost(spots, rows, blocks[0].shape[0]),
@@ -103,17 +96,17 @@
     )(limits, packed, *blocks)
 
 
-def attend_guests(guests, blocks, rows):
+def attend_guests(guests, block, rows):
     width = guests[0].shape[1] - HD
     return pl.pallas_call(
         functools.partial(guest_kernel, len(guests), rows),
         out_shape=[jax.ShapeDtypeStruct((rows, width), g.dtype) for g in guests],
-        in_specs=[VMEM] * (PARTS + len(guests)),
+        in_specs=[VMEM] * (1 + len(guests)),
         out_specs=[VMEM] * len(guests),
         compiler_params=PARAMS,
-        cost_estimate=cost(guests, rows, blocks[0].shape[0]),
+        cost_estimate=cost(guests, rows, block.shape[0]),
         name="attend_guests",
-    )(*blocks, *guests)
+    )(block, *guests)
 
 
 def place_rows(where, held, held_spots, rows, out, shape):
@@ -149,37 +142,23 @@
     group_rows = row_count // ring
     me = lax.axis_index("prompt")
     kv = seq_kv[0, 0]
-    steps = ring // 2
-
-    span, part = KVH * HD, HEADS * HD
-    own = tuple(
-        jnp.concatenate([kv[:, lo : lo + part], kv[:, span + lo : span + lo + part]], axis=1)
-        for lo in range(0, span, part)
-    )
 
     def shifted(x, by):
         return lax.ppermute(x, "prompt", [(i, (i + by) % ring) for i in range(ring)])
 
-    def tie_first(parts, after):
-        first, after = tie(parts[0], after)
-        return (first, *parts[1:]), after
-
-    up = tuple(shifted(x, 1) for x in own)
-    down = tuple(shifted(x, -1) for x in own)
-    blocks_of = [(*up, *down)]
-
-    send, _ = tie(send_list[0, 0], up[0])
-    ordered = move_rows(send, query_rows)
+    steps = ring // 2
+
+    ordered = move_rows(send_list[0, 0], query_rows)
     arrived = lax.all_to_all(
         ordered.reshape(dp_count, row_count // dp_count, width), "dp", split_axis=0, concat_axis=0, tiled=True
     ).reshape(row_count, width)
 
     sequences = pack_seq[0, 0]
-    behind = (me - sequences) % ring
+    offset = (me - sequences) % ring
     place = jnp.where(
-        behind == 0,
+        offset == 0,
         ring - 1,
-        jnp.where(behind <= steps, 2 * (behind - 1), 2 * (ring - behind - 1) + 1),
+        jnp.where(offset <= steps, 2 * (offset - 1), 2 * (ring - offset - 1) + 1),
     )
     spots = jnp.arange(ring, dtype=jnp.int32)
     at_place = place[None, :] == spots[:, None]
@@ -192,8 +171,11 @@
     target = jnp.sum(jnp.where(of_group, place[None, :], 0), axis=1) * group_rows + slot % group_rows
     packed = move_rows(target, arrived)
 
-    far = steps - 2
-    mine, behind_far, ahead_far, opposite = (ring - 1,), (2 * far,), (2 * far + 1,), (2 * far + 2,)
+    far = steps - 4
+    behind = [2 * (d - 1) for d in range(steps, far, -1)]
+    ahead = [2 * (d - 1) + 1 for d in range(steps - 1, far, -1)]
+    behind_hops = [d - far for d in range(steps, far, -1)]
+    ahead_hops = [d - far for d in range(steps - 1, far, -1)]
 
     def payload(spot):
         rows = packed[spot * group_rows : (spot + 1) * group_rows]
@@ -207,38 +189,37 @@
         held.append(attend_step(limits, packed, spot_list, blocks, group_rows))
         held_spots.append(spot_list)
 
-    for step in range(1, far):
-        if step == 2:
-            up, ordered = tie_first(up, ordered)
-        if step == 3:
-            guests = [payload(s[0]) for s in (behind_far, opposite, ahead_far)]
-            up, guests = tie_first(up, guests)
-            guests = [shifted(g, by) for g, by in zip(guests, (-1, -2, 1))]
-        if step == 4:
-            score(mine, own)
+    up, down = kv, kv
+    blocks_of = []
+    for step in range(far):
+        if step == 0:
+            down, ordered = tie(down, ordered)
+        if step == far - 2:
+            from_behind, from_ahead = [payload(s) for s in behind], [payload(s) for s in ahead]
+            up, (from_behind, from_ahead) = tie(up, (from_behind, from_ahead))
+            from_behind = [shifted(g, -by) for g, by in zip(from_behind, behind_hops)]
+            from_ahead = [shifted(g, by) for g, by in zip(from_ahead, ahead_hops)]
+        if step == far - 1:
+            score((ring - 1,), (kv,))
             score((0, 1), blocks_of[0])
-            up, (guests, held) = tie_first(up, (guests, held))
-        if step == 5:
-            score((2, 3), blocks_of[1])
-            score((4, 5), blocks_of[2])
-            up, held = tie_first(up, held)
-        up = tuple(shifted(x, 1) for x in up)
-        down = tuple(shifted(x, -1) for x in down)
-        blocks_of.append((*up, *down))
-    score((6, 7), blocks_of[3])
-    score((8, 9), blocks_of[4])
+            up, (held, from_behind) = tie(up, (held, from_behind))
+        up = shifted(up, 1)
+        down = shifted(down, -1)
+        blocks_of.append((up, down))
+    for step in range(1, far - 1):
+        score((2 * step, 2 * step + 1), blocks_of[step])
     out = place_rows(where, held, held_spots, group_rows, None, packed.shape)
-    up, out = tie_first(up, out)
-    behind_out, opposite_out = attend_guests(guests[:2], up, group_rows)
-    behind_out, opposite_out = shifted(behind_out, 1), shifted(opposite_out, 2)
-    (ahead_out,) = attend_guests(guests[2:], down, group_rows)
-    ahead_out = shifted(ahead_out, -1)
+    up, out = tie(up, out)
+    from_behind = attend_guests(from_behind, up, group_rows)
+    from_behind = [shifted(g, by) for g, by in zip(from_behind, behind_hops)]
+    from_ahead = attend_guests(from_ahead, down, group_rows)
+    from_ahead = [shifted(g, -by) for g, by in zip(from_ahead, ahead_hops)]
     held, held_spots = [], []
-    score((2 * far - 2, 2 * far - 1), (*up, *down))
+    score((2 * far - 2, 2 * far - 1), (up, down))
     out = place_rows(
         where,
-        [*held, behind_out, opposite_out, ahead_out],
-        [*held_spots, behind_far, opposite, ahead_far],
+        [*held, *from_behind, *from_ahead],
+        [*held_spots, *((s,) for s in behind), *((s,) for s in ahead)],
         group_rows,
         out,
         packed.shape,

time: 162 us -> 219 us (1.35)
  waiting for transfers between devices: 13.9 us -> 83.4 us
  starting transfers between devices: 113 us -> 105 us
  Pallas kernels: 18.2 us -> 15.1 us
  local copies, waits for them, and re-layouts: 8.27 us -> 5.41 us
    ppermute x30 -> x22, waiting for transfers between devices: 13.9 us -> 83.4 us  [shifted(): lax.ppermute(x, 'prompt', [(i, (i + by) % ring) for i in range(ring)])]
    ppermute x30 -> x22, starting transfers between devices: 105 us -> 96.6 us  [shifted(): lax.ppermute(x, 'prompt', [(i, (i + by) % ring) for i in range(ring)])]
    pallas_call x7 -> x5, Pallas kernels: 12.6 us -> 8.67 us  [attend_step(): pl.pallas_call(functools.partial(step_kernel, spots, rows), out_shape=jax...]
  transfers between devices with their start and end apart: 31 -> 23, of which waited for: 6 -> 12; matrix products, arithmetic and copies ran while one was open for 5% -> 5% of each run, Pallas kernels for 10% -> 6%
where the time goes in v3:
time: 219 us; the launch traced here: 218 us
  starting transfers between devices  105 us (48%)
  waiting for transfers between devices  83.4 us (38%)
  Pallas kernels  15.1 us (7%)
  local copies, waits for them, and re-layouts  5.41 us (2%)
  matrix products  5.02 us (2%)
  other arithmetic  3.9 us (2%)
    ppermute x22, starting transfers between devices, shifted(): lax.ppermute(x, 'prompt', [(i, (i + by) % ring) for i in range(ring)])  96.6 us
    ppermute x22, waiting for transfers between devices, shifted(): lax.ppermute(x, 'prompt', [(i, (i + by) % ring) for i in range(ring)])  83.4 us
    pallas_call x5, Pallas kernels, attend_step(): pl.pallas_call(functools.partial(step_kernel, spots, rows), out_shape=jax...  8.67 us
    all_to_all x1, starting transfers between devices, body(): lax.all_to_all(ordered.reshape(dp_count, row_count // dp_count, width), '...  8.5 us
    dot_general x2, matrix products, move_rows(): jnp.dot(pick, rows, preferred_element_type=jnp.float32).astype(rows.dtype)  5.02 us
    unnamed x29, local copies, waits for them, and re-layouts  4.6 us
  transfers between devices with their start and end apart: 23, of which 12 were waited for; matrix products, arithmetic and copies ran while one was open for 5% of the time, Pallas kernels for 6%

profile of v3, /device:TPU:2, one launch (start us, length us, event | category | flops | bytes accessed | tf_op | source)
XLA Modules:
  0.0 218.5 jit_solution(3888395619963153908)
XLA Ops:
  0.0 3.9 %collective-permute-start = (bf16[384,1024]{1,0:T(8,128)(2,1)}, bf16[384,1024]{1,0:T(8,128)(2,1)}, u32[]{:S(2)}, u32[]{:S(2)}) collective-permute-start(bf16[384,1024]{1,0:T(8,128)(2,1)} %bitcast.29), channel_id=1, source_target_pairs={{0,1},{1,2},{2,3},{3,4},{4,5},{5,6},{6,7},{7,8},{8,9},{9,10},{10,1... | collective-permute-start | bytes 2359304 | tf_op jit(solution)/shard_map/ppermute | solution.py:147
  4.0 2.7 %convolution_convert_fusion.1 = bf16[256,4096]{1,0:T(8,128)(2,1)} fusion(bf16[1,1,256,4096]{3,2,1,0:T(8,128)(2,1)S(1)} %copy-done, s32[256]{0:T(256)} %bitcast.33), kind=kOutput, calls=%fused_computation.1 | convolution fusion | flops 537985024 | bytes 4195328 | tf_op jit(solution)/shard_map/dot_general | solution.py:130
  6.7 8.5 %all-to-all-start = ((bf16[32,8,4096]{2,1,0:T(8,128)(2,1)}), bf16[32,8,4096]{2,1,0:T(8,128)(2,1)}, u32[]{:S(2)}, u32[]{:S(2)}) async-start(bf16[32,8,4096]{2,1,0:T(8,128)(2,1)} %bitcast.32), calls=%async_computation | async-start | bytes 4194304 | tf_op jit(solution)/shard_map/all_to_all | solution.py:152
  15.2 8.8 %collective-permute-start.3 = (bf16[384,1024]{1,0:T(8,128)(2,1)S(1)}, bf16[384,1024]{1,0:T(8,128)(2,1)}, u32[]{:S(2)}, u32[]{:S(2)}) collective-permute-start(bf16[384,1024]{1,0:T(8,128)(2,1)S(1)} %bitcast.30), channel_id=1, source_target_pairs={{0,15},{1,0},{2,1},{3,2},{4,3},{5,4},{6,5},{7,6},{8,7},{9,8},{10,9... | collective-permute-start | bytes 2359304 | tf_op jit(solution)/shard_map/ppermute | solution.py:147
  26.2 14.9 %collective-permute-done.3.refs_1_ = bf16[384,1024]{1,0:T(8,128)(2,1)} collective-permute-done((bf16[384,1024]{1,0:T(8,128)(2,1)S(1)}, bf16[384,1024]{1,0:T(8,128)(2,1)}, u32[]{:S(2)}, u32[]{:S(2)}) %collective-permute-start.3) | collective-permute-done | bytes 786464 | tf_op jit(solution)/shard_map/ppermute | solution.py:147
  41.1 5.7 %collective-permute-start.9 = (bf16[384,1024]{1,0:T(8,128)(2,1)}, bf16[384,1024]{1,0:T(8,128)(2,1)S(1)}, u32[]{:S(2)}, u32[]{:S(2)}) collective-permute-start(bf16[384,1024]{1,0:T(8,128)(2,1)} %collective-permute-done.3.refs_1_), channel_id=1, source_target_pairs={{0,15},{1,0},{2,1},{3,2},{4,3},{5,4},{6,5},{7,6},{8,7},{9,8},{10,9... | collective-permute-start | bytes 2359304 | tf_op jit(solution)/shard_map/ppermute | solution.py:147
  47.0 1.9 collective-permute-start.1
  48.9 14.5 %collective-permute-done.9.refs_1_ = bf16[384,1024]{1,0:T(8,128)(2,1)S(1)} collective-permute-done((bf16[384,1024]{1,0:T(8,128)(2,1)}, bf16[384,1024]{1,0:T(8,128)(2,1)S(1)}, u32[]{:S(2)}, u32[]{:S(2)}) %collective-permute-start.9) | collective-permute-done | bytes 786464 | tf_op jit(solution)/shard_map/ppermute | solution.py:147
  63.4 5.5 %collective-permute-start.10 = (bf16[384,1024]{1,0:T(8,128)(2,1)S(1)}, bf16[384,1024]{1,0:T(8,128)(2,1)}, u32[]{:S(2)}, u32[]{:S(2)}) collective-permute-start(bf16[384,1024]{1,0:T(8,128)(2,1)S(1)} %collective-permute-done.9.refs_1_), channel_id=1, source_target_pairs={{0,15},{1,0},{2,1},{3,2},{4,3},{5,4},{6,5},{7,6},{8,7},{9,8},{10,9... | collective-permute-start | bytes 2359304 | tf_op jit(solution)/shard_map/ppermute | solution.py:147
  68.9 2.3 %convolution_convert_fusion.query_ref = bf16[256,4096]{1,0:T(8,128)(2,1)S(1)} fusion(bf16[32,8,4096]{2,1,0:T(8,128)(2,1)} %all-to-all-done, s32[256]{0:T(256)S(1)} %fusion.25), kind=kOutput, calls=%fused_computation | convolution fusion | flops 537985024 | bytes 4195328 | tf_op jit(solution)/shard_map/dot_general | solution.py:130
  71.3 1.3 copy-done.1
  75.4 1.9 collective-permute-start.2
  77.3 6.5 %collective-permute-start.4 = (bf16[16,4224]{1,0:T(8,128)(2,1)S(1)}, bf16[16,4224]{1,0:T(8,128)(2,1)S(1)}, u32[]{:S(2)}, u32[]{:S(2)}) collective-permute-start(bf16[16,4224]{1,0:T(8,128)(2,1)S(1)} %get-tuple-element.32), channel_id=1, source_target_pairs={{0,12},{1,13},{2,14},{3,15},{4,0},{5,1},{6,2},{7,3},{8,4},{9,5},{1... | collective-permute-start | bytes 405512 | tf_op jit(solution)/shard_map/ppermute | solution.py:147
  83.8 11.6 %collective-permute-done.10.refs_1_ = bf16[384,1024]{1,0:T(8,128)(2,1)} collective-permute-done((bf16[384,1024]{1,0:T(8,128)(2,1)S(1)}, bf16[384,1024]{1,0:T(8,128)(2,1)}, u32[]{:S(2)}, u32[]{:S(2)}) %collective-permute-start.10) | collective-permute-done | bytes 786464 | tf_op jit(solution)/shard_map/ppermute | solution.py:147
  95.4 5.8 %collective-permute-start.11 = (bf16[384,1024]{1,0:T(8,128)(2,1)}, bf16[384,1024]{1,0:T(8,128)(2,1)S(1)}, u32[]{:S(2)}, u32[]{:S(2)}) collective-permute-start(bf16[384,1024]{1,0:T(8,128)(2,1)} %collective-permute-done.10.refs_1_), channel_id=1, source_target_pairs={{0,15},{1,0},{2,1},{3,2},{4,3},{5,4},{6,5},{7,6},{8,7},{9,8},{10,9... | collective-permute-start | bytes 2359304 | tf_op jit(solution)/shard_map/ppermute | solution.py:147
  101.3 3.2 %collective-permute-start.5 = (bf16[16,4224]{1,0:T(8,128)(2,1)}, bf16[16,4224]{1,0:T(8,128)(2,1)S(1)}, u32[]{:S(2)}, u32[]{:S(2)}) collective-permute-start(bf16[16,4224]{1,0:T(8,128)(2,1)} %get-tuple-element.33), channel_id=1, source_target_pairs={{0,13},{1,14},{2,15},{3,0},{4,1},{5,2},{6,3},{7,4},{8,5},{9,6},{10... | collective-permute-start | bytes 405512 | tf_op jit(solution)/shard_map/ppermute | solution.py:147
  104.5 5.2 %collective-permute-start.6 = (bf16[16,4224]{1,0:T(8,128)(2,1)}, bf16[16,4224]{1,0:T(8,128)(2,1)S(1)}, u32[]{:S(2)}, u32[]{:S(2)}) collective-permute-start(bf16[16,4224]{1,0:T(8,128)(2,1)} %get-tuple-element.34), channel_id=1, source_target_pairs={{0,14},{1,15},{2,0},{3,1},{4,2},{5,3},{6,4},{7,5},{8,6},{9,7},{10,... | collective-permute-start | bytes 405512 | tf_op jit(solution)/shard_map/ppermute | solution.py:147
  109.7 2.5 %collective-permute-start.7 = (bf16[16,4224]{1,0:T(8,128)(2,1)}, bf16[16,4224]{1,0:T(8,128)(2,1)S(1)}, u32[]{:S(2)}, u32[]{:S(2)}) collective-permute-start(bf16[16,4224]{1,0:T(8,128)(2,1)} %get-tuple-element.35), channel_id=1, source_target_pairs={{0,15},{1,0},{2,1},{3,2},{4,3},{5,4},{6,5},{7,6},{8,7},{9,8},{10,9... | collective-permute-start | bytes 405512 | tf_op jit(solution)/shard_map/ppermute | solution.py:147
  112.3 1.6 copy-done.2
  113.9 1.1 copy-done.5
  115.7 2.5 %attend_0.1.refs_1_ = bf16[32,4096]{1,0:T(8,128)(2,1)S(1)} custom-call(s32[16,128]{1,0:T(8,128)S(1)} %tile.52.limits_ref, bf16[256,4096]{1,0:T(8,128)(2,1)S(1)} %copy-done.2, bf16[384,1024]{1,0:T(8,128)(2,1)} %collective-permute-done.refs_0_, bf16[384,1024]{1,0:T(8,128)(2,1)} %collective-permute-done.3.refs_1_), custom_call_target="tpu_custom_call" | custom-call | flops 201326592 | bytes 1048576 | tf_op jit(solution)/shard_map/attend_0/pallas_call | solution.py:88
  118.2 9.2 %collective-permute-done.5.refs_1_ = bf16[16,4224]{1,0:T(8,128)(2,1)S(1)} collective-permute-done((bf16[16,4224]{1,0:T(8,128)(2,1)}, bf16[16,4224]{1,0:T(8,128)(2,1)S(1)}, u32[]{:S(2)}, u32[]{:S(2)}) %collective-permute-start.5) | collective-permute-done | bytes 135200 | tf_op jit(solution)/shard_map/ppermute | solution.py:147
  127.3 1.4 collective-permute-done.6.refs_2_
  128.8 1.4 collective-permute-done.7.refs_3_
  130.2 1.9 collective-permute-start.8
  132.1 4.9 %collective-permute-start.16 = (bf16[16,4224]{1,0:T(8,128)(2,1)S(1)}, bf16[16,4224]{1,0:T(8,128)(2,1)S(1)}, u32[]{:S(2)}, u32[]{:S(2)}) collective-permute-start(bf16[16,4224]{1,0:T(8,128)(2,1)S(1)} %copy-done.10), channel_id=1, source_target_pairs={{0,3},{1,4},{2,5},{3,6},{4,7},{5,8},{6,9},{7,10},{8,11},{9,12},{10... | collective-permute-start | bytes 405512 | tf_op jit(solution)/shard_map/ppermute | solution.py:147
  137.0 7.0 %collective-permute-start.17 = (bf16[16,4224]{1,0:T(8,128)(2,1)S(1)}, bf16[16,4224]{1,0:T(8,128)(2,1)S(1)}, u32[]{:S(2)}, u32[]{:S(2)}) collective-permute-start(bf16[16,4224]{1,0:T(8,128)(2,1)S(1)} %copy-done.9), channel_id=1, source_target_pairs={{0,2},{1,3},{2,4},{3,5},{4,6},{5,7},{6,8},{7,9},{8,10},{9,11},{10,... | collective-permute-start | bytes 405512 | tf_op jit(solution)/shard_map/ppermute | solution.py:147
  144.1 3.9 %collective-permute-start.18 = (bf16[16,4224]{1,0:T(8,128)(2,1)S(1)}, bf16[16,4224]{1,0:T(8,128)(2,1)S(1)}, u32[]{:S(2)}, u32[]{:S(2)}) collective-permute-start(bf16[16,4224]{1,0:T(8,128)(2,1)S(1)} %copy-done.8), channel_id=1, source_target_pairs={{0,1},{1,2},{2,3},{3,4},{4,5},{5,6},{6,7},{7,8},{8,9},{9,10},{10,1... | collective-permute-start | bytes 405512 | tf_op jit(solution)/shard_map/ppermute | solution.py:147
  148.0 13.7 %collective-permute-done.16.refs_0_ = bf16[16,4224]{1,0:T(8,128)(2,1)S(1)} collective-permute-done((bf16[16,4224]{1,0:T(8,128)(2,1)S(1)}, bf16[16,4224]{1,0:T(8,128)(2,1)S(1)}, u32[]{:S(2)}, u32[]{:S(2)}) %collective-permute-start.16) | collective-permute-done | bytes 135200 | tf_op jit(solution)/shard_map/ppermute | solution.py:147
  161.7 1.1 collective-permute-done.18.refs_2_
  162.8 1.4 attend_guests.3
  164.2 8.4 %collective-permute-start.19 = (bf16[16,4096]{1,0:T(8,128)(2,1)S(1)}, bf16[16,4096]{1,0:T(8,128)(2,1)S(1)}, u32[]{:S(2)}, u32[]{:S(2)}) collective-permute-start(bf16[16,4096]{1,0:T(8,128)(2,1)S(1)} %get-tuple-element.52), channel_id=1, source_target_pairs={{0,13},{1,14},{2,15},{3,0},{4,1},{5,2},{6,3},{7,4},{8,5},{9,6},{10... | collective-permute-start | bytes 393224 | tf_op jit(solution)/shard_map/ppermute | solution.py:147
  172.6 1.9 collective-permute-start.20
  174.6 2.2 attend_2.1.refs_2_
  176.8 2.4 %attend_4.1.refs_3_ = bf16[32,4096]{1,0:T(8,128)(2,1)S(1)} custom-call(s32[16,128]{1,0:T(8,128)S(1)} %tile.52.limits_ref, bf16[256,4096]{1,0:T(8,128)(2,1)S(1)} %copy-done.3, bf16[384,1024]{1,0:T(8,128)(2,1)} %collective-permute-done.2.refs_0_, bf16[384,1024]{1,0:T(8,128)(2,1)} %collective-permute-done.10.refs_1_), custom_call_target="tpu_custom_call" | custom-call | flops 201326592 | bytes 1048576 | tf_op jit(solution)/shard_map/attend_4/pallas_call | solution.py:88
  179.2 1.5 place_held.1.refs_0_
  180.7 2.5 %collective-permute-start.21 = (bf16[16,4096]{1,0:T(8,128)(2,1)S(1)}, bf16[16,4096]{1,0:T(8,128)(2,1)S(1)}, u32[]{:S(2)}, u32[]{:S(2)}) collective-permute-start(bf16[16,4096]{1,0:T(8,128)(2,1)S(1)} %get-tuple-element.54), channel_id=1, source_target_pairs={{0,15},{1,0},{2,1},{3,2},{4,3},{5,4},{6,5},{7,6},{8,7},{9,8},{10,9... | collective-permute-start | bytes 393224 | tf_op jit(solution)/shard_map/ppermute | solution.py:147
  183.2 1.9 attend_guests.2
  185.1 6.6 %collective-permute-start.12 = (bf16[16,4096]{1,0:T(8,128)(2,1)S(1)}, bf16[16,4096]{1,0:T(8,128)(2,1)S(1)}, u32[]{:S(2)}, u32[]{:S(2)}) collective-permute-start(bf16[16,4096]{1,0:T(8,128)(2,1)S(1)} %get-tuple-element.45), channel_id=1, source_target_pairs={{0,4},{1,5},{2,6},{3,7},{4,8},{5,9},{6,10},{7,11},{8,12},{9,13},{1... | collective-permute-start | bytes 393224 | tf_op jit(solution)/shard_map/ppermute | solution.py:147
  191.7 1.9 collective-permute-start.13
  193.7 4.5 %collective-permute-start.14 = (bf16[16,4096]{1,0:T(8,128)(2,1)S(1)}, bf16[16,4096]{1,0:T(8,128)(2,1)S(1)}, u32[]{:S(2)}, u32[]{:S(2)}) collective-permute-start(bf16[16,4096]{1,0:T(8,128)(2,1)S(1)} %get-tuple-element.47), channel_id=1, source_target_pairs={{0,2},{1,3},{2,4},{3,5},{4,6},{5,7},{6,8},{7,9},{8,10},{9,11},{10,... | collective-permute-start | bytes 393224 | tf_op jit(solution)/shard_map/ppermute | solution.py:147
  198.2 2.1 collective-permute-start.15
  200.3 1.0 attend_6.1.refs_1_
  201.3 3.7 %collective-permute-done.12.refs_2_ = bf16[16,4096]{1,0:T(8,128)(2,1)S(1)} collective-permute-done((bf16[16,4096]{1,0:T(8,128)(2,1)S(1)}, bf16[16,4096]{1,0:T(8,128)(2,1)S(1)}, u32[]{:S(2)}, u32[]{:S(2)}) %collective-permute-start.12) | collective-permute-done | bytes 131104 | tf_op jit(solution)/shard_map/ppermute | solution.py:147
  205.0 6.1 %collective-permute-done.13.refs_3_ = bf16[16,4096]{1,0:T(8,128)(2,1)S(1)} collective-permute-done((bf16[16,4096]{1,0:T(8,128)(2,1)S(1)}, bf16[16,4096]{1,0:T(8,128)(2,1)S(1)}, u32[]{:S(2)}, u32[]{:S(2)}) %collective-permute-start.13) | collective-permute-done | bytes 131104 | tf_op jit(solution)/shard_map/ppermute | solution.py:147
  211.1 4.3 %collective-permute-done.14.refs_4_ = bf16[16,4096]{1,0:T(8,128)(2,1)S(1)} collective-permute-done((bf16[16,4096]{1,0:T(8,128)(2,1)S(1)}, bf16[16,4096]{1,0:T(8,128)(2,1)S(1)}, u32[]{:S(2)}, u32[]{:S(2)}) %collective-permute-start.14) | collective-permute-done | bytes 131104 | tf_op jit(solution)/shard_map/ppermute | solution.py:147
  215.4 1.4 collective-permute-done.15.refs_5_
  216.8 1.6 place_last.1
  (83 shorter events, 6.0 us)
Async XLA Ops:
  0.0 4.0 %copy-start = (bf16[1,1,256,4096]{3,2,1,0:T(8,128)(2,1)S(1)}, bf16[1,1,256,4096]{3,2,1,0:T(8,128)(2,1)}, u32[]{:S(2)}) copy-start(bf16[1,1,256,4096]{3,2,1,0:T(8,128)(2,1)} %param.6) | copy-start | bytes 6291460
  0.0 47.0 %collective-permute-start = (bf16[384,1024]{1,0:T(8,128)(2,1)}, bf16[384,1024]{1,0:T(8,128)(2,1)}, u32[]{:S(2)}, u32[]{:S(2)}) collective-permute-start(bf16[384,1024]{1,0:T(8,128)(2,1)} %bitcast.29), channel_id=1, source_target_pairs={{0,1},{1,2},{2,3},{3,4},{4,5},{5,6},{6,7},{7,8},{8,9},{9,10},{10,1... | collective-permute-start | bytes 2359304 | tf_op jit(solution)/shard_map/ppermute | solution.py:147
  6.7 8.5 %copy-start.4 = (bf16[1,1,384,1024]{3,2,1,0:T(8,128)(2,1)S(1)}, bf16[1,1,384,1024]{3,2,1,0:T(8,128)(2,1)}, u32[]{:S(2)}) copy-start(bf16[1,1,384,1024]{3,2,1,0:T(8,128)(2,1)} %param.11) | copy-start | bytes 2359300
  6.7 17.4 %copy-start.13 = (s32[1,1,16]{2,1,0:T(1,128)S(1)}, s32[1,1,16]{2,1,0:T(1,128)}, u32[]{:S(2)}) copy-start(s32[1,1,16]{2,1,0:T(1,128)} %param.10) | copy-start | bytes 196
  6.7 17.9 %copy-start.12 = (s32[1,1,256]{2,1,0:T(1,128)S(1)}, s32[1,1,256]{2,1,0:T(1,128)}, u32[]{:S(2)}) copy-start(s32[1,1,256]{2,1,0:T(1,128)} %param.9) | copy-start | bytes 3076
  6.7 40.2 %copy-start.11 = (s32[1,1,256]{2,1,0:T(1,128)S(1)}, s32[1,1,256]{2,1,0:T(1,128)}, u32[]{:S(2)}) copy-start(s32[1,1,256]{2,1,0:T(1,128)} %param.8) | copy-start | bytes 3076
  6.7 62.2 %all-to-all-start = ((bf16[32,8,4096]{2,1,0:T(8,128)(2,1)}), bf16[32,8,4096]{2,1,0:T(8,128)(2,1)}, u32[]{:S(2)}, u32[]{:S(2)}) async-start(bf16[32,8,4096]{2,1,0:T(8,128)(2,1)} %bitcast.32), calls=%async_computation | async-start | bytes 4194304 | tf_op jit(solution)/shard_map/all_to_all | solution.py:152
  15.2 25.9 %collective-permute-start.3 = (bf16[384,1024]{1,0:T(8,128)(2,1)S(1)}, bf16[384,1024]{1,0:T(8,128)(2,1)}, u32[]{:S(2)}, u32[]{:S(2)}) collective-permute-start(bf16[384,1024]{1,0:T(8,128)(2,1)S(1)} %bitcast.30), channel_id=1, source_target_pairs={{0,15},{1,0},{2,1},{3,2},{4,3},{5,4},{6,5},{7,6},{8,7},{9,8},{10,9... | collective-permute-start | bytes 2359304 | tf_op jit(solution)/shard_map/ppermute | solution.py:147
  41.1 22.3 %collective-permute-start.9 = (bf16[384,1024]{1,0:T(8,128)(2,1)}, bf16[384,1024]{1,0:T(8,128)(2,1)S(1)}, u32[]{:S(2)}, u32[]{:S(2)}) collective-permute-start(bf16[384,1024]{1,0:T(8,128)(2,1)} %collective-permute-done.3.refs_1_), channel_id=1, source_target_pairs={{0,15},{1,0},{2,1},{3,2},{4,3},{5,4},{6,5},{7,6},{8,7},{9,8},{10,9... | collective-permute-start | bytes 2359304 | tf_op jit(solution)/shard_map/ppermute | solution.py:147
  47.0 28.4 %collective-permute-start.1 = (bf16[384,1024]{1,0:T(8,128)(2,1)}, bf16[384,1024]{1,0:T(8,128)(2,1)}, u32[]{:S(2)}, u32[]{:S(2)}) collective-permute-start(bf16[384,1024]{1,0:T(8,128)(2,1)} %collective-permute-done.refs_0_), channel_id=1, source_target_pairs={{0,1},{1,2},{2,3},{3,4},{4,5},{5,6},{6,7},{7,8},{8,9},{9,10},{10,1... | collective-permute-start | bytes 2359304 | tf_op jit(solution)/shard_map/ppermute | solution.py:147
  63.4 7.8 %copy-start.6 = (bf16[384,1024]{1,0:T(8,128)(2,1)}, bf16[384,1024]{1,0:T(8,128)(2,1)S(1)}, u32[]{:S(2)}) copy-start(bf16[384,1024]{1,0:T(8,128)(2,1)S(1)} %collective-permute-done.9.refs_1_) | copy-start | bytes 2359300
  63.4 32.0 %collective-permute-start.10 = (bf16[384,1024]{1,0:T(8,128)(2,1)S(1)}, bf16[384,1024]{1,0:T(8,128)(2,1)}, u32[]{:S(2)}, u32[]{:S(2)}) collective-permute-start(bf16[384,1024]{1,0:T(8,128)(2,1)S(1)} %collective-permute-done.9.refs_1_), channel_id=1, source_target_pairs={{0,15},{1,0},{2,1},{3,2},{4,3},{5,4},{6,5},{7,6},{8,7},{9,8},{10,9... | collective-permute-start | bytes 2359304 | tf_op jit(solution)/shard_map/ppermute | solution.py:147
  71.3 1.3 copy-start.1
  75.4 54.8 %collective-permute-start.2 = (bf16[384,1024]{1,0:T(8,128)(2,1)}, bf16[384,1024]{1,0:T(8,128)(2,1)}, u32[]{:S(2)}, u32[]{:S(2)}) collective-permute-start(bf16[384,1024]{1,0:T(8,128)(2,1)} %collective-permute-done.1.refs_0_), channel_id=1, source_target_pairs={{0,1},{1,2},{2,3},{3,4},{4,5},{5,6},{6,7},{7,8},{8,9},{9,10},{10,1... | collective-permute-start | bytes 2359304 | tf_op jit(solution)/shard_map/ppermute | solution.py:147
  77.3 32.3 %collective-permute-start.4 = (bf16[16,4224]{1,0:T(8,128)(2,1)S(1)}, bf16[16,4224]{1,0:T(8,128)(2,1)S(1)}, u32[]{:S(2)}, u32[]{:S(2)}) collective-permute-start(bf16[16,4224]{1,0:T(8,128)(2,1)S(1)} %get-tuple-element.32), channel_id=1, source_target_pairs={{0,12},{1,13},{2,14},{3,15},{4,0},{5,1},{6,2},{7,3},{8,4},{9,5},{1... | collective-permute-start | bytes 405512 | tf_op jit(solution)/shard_map/ppermute | solution.py:147
  95.4 67.4 %collective-permute-start.11 = (bf16[384,1024]{1,0:T(8,128)(2,1)}, bf16[384,1024]{1,0:T(8,128)(2,1)S(1)}, u32[]{:S(2)}, u32[]{:S(2)}) collective-permute-start(bf16[384,1024]{1,0:T(8,128)(2,1)} %collective-permute-done.10.refs_1_), channel_id=1, source_target_pairs={{0,15},{1,0},{2,1},{3,2},{4,3},{5,4},{6,5},{7,6},{8,7},{9,8},{10,9... | collective-permute-start | bytes 2359304 | tf_op jit(solution)/shard_map/ppermute | solution.py:147
  101.3 26.1 %collective-permute-start.5 = (bf16[16,4224]{1,0:T(8,128)(2,1)}, bf16[16,4224]{1,0:T(8,128)(2,1)S(1)}, u32[]{:S(2)}, u32[]{:S(2)}) collective-permute-start(bf16[16,4224]{1,0:T(8,128)(2,1)} %get-tuple-element.33), channel_id=1, source_target_pairs={{0,13},{1,14},{2,15},{3,0},{4,1},{5,2},{6,3},{7,4},{8,5},{9,6},{10... | collective-permute-start | bytes 405512 | tf_op jit(solution)/shard_map/ppermute | solution.py:147
  104.5 24.3 %collective-permute-start.6 = (bf16[16,4224]{1,0:T(8,128)(2,1)}, bf16[16,4224]{1,0:T(8,128)(2,1)S(1)}, u32[]{:S(2)}, u32[]{:S(2)}) collective-permute-start(bf16[16,4224]{1,0:T(8,128)(2,1)} %get-tuple-element.34), channel_id=1, source_target_pairs={{0,14},{1,15},{2,0},{3,1},{4,2},{5,3},{6,4},{7,5},{8,6},{9,7},{10,... | collective-permute-start | bytes 405512 | tf_op jit(solution)/shard_map/ppermute | solution.py:147
  109.7 20.5 %collective-permute-start.7 = (bf16[16,4224]{1,0:T(8,128)(2,1)}, bf16[16,4224]{1,0:T(8,128)(2,1)S(1)}, u32[]{:S(2)}, u32[]{:S(2)}) collective-permute-start(bf16[16,4224]{1,0:T(8,128)(2,1)} %get-tuple-element.35), channel_id=1, source_target_pairs={{0,15},{1,0},{2,1},{3,2},{4,3},{5,4},{6,5},{7,6},{8,7},{9,8},{10,9... | collective-permute-start | bytes 405512 | tf_op jit(solution)/shard_map/ppermute | solution.py:147
  112.3 1.6 copy-start.2
  113.8 1.1 copy-start.5
  115.6 16.5 %copy-start.10 = (bf16[16,4224]{1,0:T(8,128)(2,1)S(1)}, bf16[16,4224]{1,0:T(8,128)(2,1)}, u32[]{:S(2)}) copy-start(bf16[16,4224]{1,0:T(8,128)(2,1)} %get-tuple-element.49) | copy-start | bytes 405508
  115.6 21.4 %copy-start.9 = (bf16[16,4224]{1,0:T(8,128)(2,1)S(1)}, bf16[16,4224]{1,0:T(8,128)(2,1)}, u32[]{:S(2)}) copy-start(bf16[16,4224]{1,0:T(8,128)(2,1)} %get-tuple-element.50) | copy-start | bytes 405508
  115.7 28.4 %copy-start.8 = (bf16[16,4224]{1,0:T(8,128)(2,1)S(1)}, bf16[16,4224]{1,0:T(8,128)(2,1)}, u32[]{:S(2)}) copy-start(bf16[16,4224]{1,0:T(8,128)(2,1)} %pad_maximum_fusion.6) | copy-start | bytes 405508
  115.7 59.0 %copy-start.3 = (bf16[256,4096]{1,0:T(8,128)(2,1)S(1)}, bf16[256,4096]{1,0:T(8,128)(2,1)}, u32[]{:S(2)}) copy-start(bf16[256,4096]{1,0:T(8,128)(2,1)} %copy-done.1) | copy-start | bytes 6291460
  115.7 59.0 %copy-start.7 = (bf16[384,1024]{1,0:T(8,128)(2,1)S(1)}, bf16[384,1024]{1,0:T(8,128)(2,1)}, u32[]{:S(2)}) copy-start(bf16[384,1024]{1,0:T(8,128)(2,1)} %copy-done.6) | copy-start | bytes 2359300
  130.2 53.0 %collective-permute-start.8 = (bf16[384,1024]{1,0:T(8,128)(2,1)}, bf16[384,1024]{1,0:T(8,128)(2,1)S(1)}, u32[]{:S(2)}, u32[]{:S(2)}) collective-permute-start(bf16[384,1024]{1,0:T(8,128)(2,1)} %collective-permute-done.2.refs_0_), channel_id=1, source_target_pairs={{0,1},{1,2},{2,3},{3,4},{4,5},{5,6},{6,7},{7,8},{8,9},{9,10},{10,1... | collective-permute-start | bytes 2359304 | tf_op jit(solution)/shard_map/ppermute | solution.py:147
  132.1 29.6 %collective-permute-start.16 = (bf16[16,4224]{1,0:T(8,128)(2,1)S(1)}, bf16[16,4224]{1,0:T(8,128)(2,1)S(1)}, u32[]{:S(2)}, u32[]{:S(2)}) collective-permute-start(bf16[16,4224]{1,0:T(8,128)(2,1)S(1)} %copy-done.10), channel_id=1, source_target_pairs={{0,3},{1,4},{2,5},{3,6},{4,7},{5,8},{6,9},{7,10},{8,11},{9,12},{10... | collective-permute-start | bytes 405512 | tf_op jit(solution)/shard_map/ppermute | solution.py:147
  137.0 24.7 %collective-permute-start.17 = (bf16[16,4224]{1,0:T(8,128)(2,1)S(1)}, bf16[16,4224]{1,0:T(8,128)(2,1)S(1)}, u32[]{:S(2)}, u32[]{:S(2)}) collective-permute-start(bf16[16,4224]{1,0:T(8,128)(2,1)S(1)} %copy-done.9), channel_id=1, source_target_pairs={{0,2},{1,3},{2,4},{3,5},{4,6},{5,7},{6,8},{7,9},{8,10},{9,11},{10,... | collective-permute-start | bytes 405512 | tf_op jit(solution)/shard_map/ppermute | solution.py:147
  144.1 18.7 %collective-permute-start.18 = (bf16[16,4224]{1,0:T(8,128)(2,1)S(1)}, bf16[16,4224]{1,0:T(8,128)(2,1)S(1)}, u32[]{:S(2)}, u32[]{:S(2)}) collective-permute-start(bf16[16,4224]{1,0:T(8,128)(2,1)S(1)} %copy-done.8), channel_id=1, source_target_pairs={{0,1},{1,2},{2,3},{3,4},{4,5},{5,6},{6,7},{7,8},{8,9},{9,10},{10,1... | collective-permute-start | bytes 405512 | tf_op jit(solution)/shard_map/ppermute | solution.py:147
  164.2 29.5 %collective-permute-start.19 = (bf16[16,4096]{1,0:T(8,128)(2,1)S(1)}, bf16[16,4096]{1,0:T(8,128)(2,1)S(1)}, u32[]{:S(2)}, u32[]{:S(2)}) collective-permute-start(bf16[16,4096]{1,0:T(8,128)(2,1)S(1)} %get-tuple-element.52), channel_id=1, source_target_pairs={{0,13},{1,14},{2,15},{3,0},{4,1},{5,2},{6,3},{7,4},{8,5},{9,6},{10... | collective-permute-start | bytes 393224 | tf_op jit(solution)/shard_map/ppermute | solution.py:147
  172.6 25.6 %collective-permute-start.20 = (bf16[16,4096]{1,0:T(8,128)(2,1)S(1)}, bf16[16,4096]{1,0:T(8,128)(2,1)S(1)}, u32[]{:S(2)}, u32[]{:S(2)}) collective-permute-start(bf16[16,4096]{1,0:T(8,128)(2,1)S(1)} %get-tuple-element.53), channel_id=1, source_target_pairs={{0,14},{1,15},{2,0},{3,1},{4,2},{5,3},{6,4},{7,5},{8,6},{9,7},{10,... | collective-permute-start | bytes 393224 | tf_op jit(solution)/shard_map/ppermute | solution.py:147
  180.7 20.6 %collective-permute-start.21 = (bf16[16,4096]{1,0:T(8,128)(2,1)S(1)}, bf16[16,4096]{1,0:T(8,128)(2,1)S(1)}, u32[]{:S(2)}, u32[]{:S(2)}) collective-permute-start(bf16[16,4096]{1,0:T(8,128)(2,1)S(1)} %get-tuple-element.54), channel_id=1, source_target_pairs={{0,15},{1,0},{2,1},{3,2},{4,3},{5,4},{6,5},{7,6},{8,7},{9,8},{10,9... | collective-permute-start | bytes 393224 | tf_op jit(solution)/shard_map/ppermute | solution.py:147
  185.1 19.9 %collective-permute-start.12 = (bf16[16,4096]{1,0:T(8,128)(2,1)S(1)}, bf16[16,4096]{1,0:T(8,128)(2,1)S(1)}, u32[]{:S(2)}, u32[]{:S(2)}) collective-permute-start(bf16[16,4096]{1,0:T(8,128)(2,1)S(1)} %get-tuple-element.45), channel_id=1, source_target_pairs={{0,4},{1,5},{2,6},{3,7},{4,8},{5,9},{6,10},{7,11},{8,12},{9,13},{1... | collective-permute-start | bytes 393224 | tf_op jit(solution)/shard_map/ppermute | solution.py:147
  191.7 19.4 %collective-permute-start.13 = (bf16[16,4096]{1,0:T(8,128)(2,1)S(1)}, bf16[16,4096]{1,0:T(8,128)(2,1)S(1)}, u32[]{:S(2)}, u32[]{:S(2)}) collective-permute-start(bf16[16,4096]{1,0:T(8,128)(2,1)S(1)} %get-tuple-element.46), channel_id=1, source_target_pairs={{0,3},{1,4},{2,5},{3,6},{4,7},{5,8},{6,9},{7,10},{8,11},{9,12},{10... | collective-permute-start | bytes 393224 | tf_op jit(solution)/shard_map/ppermute | solution.py:147
  193.7 21.7 %collective-permute-start.14 = (bf16[16,4096]{1,0:T(8,128)(2,1)S(1)}, bf16[16,4096]{1,0:T(8,128)(2,1)S(1)}, u32[]{:S(2)}, u32[]{:S(2)}) collective-permute-start(bf16[16,4096]{1,0:T(8,128)(2,1)S(1)} %get-tuple-element.47), channel_id=1, source_target_pairs={{0,2},{1,3},{2,4},{3,5},{4,6},{5,7},{6,8},{7,9},{8,10},{9,11},{10,... | collective-permute-start | bytes 393224 | tf_op jit(solution)/shard_map/ppermute | solution.py:147
  198.2 18.7 %collective-permute-start.15 = (bf16[16,4096]{1,0:T(8,128)(2,1)S(1)}, bf16[16,4096]{1,0:T(8,128)(2,1)S(1)}, u32[]{:S(2)}, u32[]{:S(2)}) collective-permute-start(bf16[16,4096]{1,0:T(8,128)(2,1)S(1)} %get-tuple-element.48), channel_id=1, source_target_pairs={{0,1},{1,2},{2,3},{3,4},{4,5},{5,6},{6,7},{7,8},{8,9},{9,10},{10,1... | collective-permute-start | bytes 393224 | tf_op jit(solution)/shard_map/ppermute | solution.py:147

commit v4 on v3

--- a/solution.py
+++ b/solution.py
@@ -48,12 +48,14 @@
         score_group(query_ref, spot * rows, rows, blocks[i], limits_ref[spot : spot + 1, :], out_ref, i * rows)
 
 
-def guest_kernel(count, rows, block, *refs):
-    for guest_ref, out_ref in zip(refs[:count], refs[count:]):
+def guest_kernel(sources, rows, *refs):
+    count = len(sources)
+    blocks, guests, outs = refs[: -2 * count], refs[-2 * count : -count], refs[-count:]
+    for source, guest_ref, out_ref in zip(sources, guests, outs):
         width = out_ref.shape[1]
         parts = guest_ref[:, width:].astype(jnp.float32)
         limits = (parts[0:1] * 16.0 + parts[1:2]).astype(jnp.int32)
-        score_group(guest_ref, 0, rows, block, limits, out_ref, 0)
+        score_group(guest_ref, 0, rows, blocks[source], limits, out_ref, 0)
 
 
 def place_kernel(ref_spots, rows, again, where_ref, *refs):
@@ -96,17 +98,17 @@
     )(limits, packed, *blocks)
 
 
-def attend_guests(guests, block, rows):
+def attend_guests(guests, sources, blocks, rows):
     width = guests[0].shape[1] - HD
     return pl.pallas_call(
-        functools.partial(guest_kernel, len(guests), rows),
+        functools.partial(guest_kernel, sources, rows),
         out_shape=[jax.ShapeDtypeStruct((rows, width), g.dtype) for g in guests],
-        in_specs=[VMEM] * (1 + len(guests)),
+        in_specs=[VMEM] * (len(blocks) + len(guests)),
         out_specs=[VMEM] * len(guests),
         compiler_params=PARAMS,
-        cost_estimate=cost(guests, rows, block.shape[0]),
+        cost_estimate=cost(guests, rows, blocks[0].shape[0]),
         name="attend_guests",
-    )(block, *guests)
+    )(*blocks, *guests)
 
 
 def place_rows(where, held, held_spots, rows, out, shape):
@@ -154,11 +156,11 @@
     ).reshape(row_count, width)
 
     sequences = pack_seq[0, 0]
-    offset = (me - sequences) % ring
+    behind = (me - sequences) % ring
     place = jnp.where(
-        offset == 0,
+        behind == 0,
         ring - 1,
-        jnp.where(offset <= steps, 2 * (offset - 1), 2 * (ring - offset - 1) + 1),
+        jnp.where(behind <= steps, 2 * (behind - 1), 2 * (ring - behind - 1) + 1),
     )
     spots = jnp.arange(ring, dtype=jnp.int32)
     at_place = place[None, :] == spots[:, None]
@@ -171,11 +173,8 @@
     target = jnp.sum(jnp.where(of_group, place[None, :], 0), axis=1) * group_rows + slot % group_rows
     packed = move_rows(target, arrived)
 
-    far = steps - 4
-    behind = [2 * (d - 1) for d in range(steps, far, -1)]
-    ahead = [2 * (d - 1) + 1 for d in range(steps - 1, far, -1)]
-    behind_hops = [d - far for d in range(steps, far, -1)]
-    ahead_hops = [d - far for d in range(steps - 1, far, -1)]
+    far = steps - 2
+    mine, behind_far, ahead_far, opposite = (ring - 1,), (2 * far,), (2 * far + 1,), (2 * far + 2,)
 
     def payload(spot):
         rows = packed[spot * group_rows : (spot + 1) * group_rows]
@@ -183,46 +182,42 @@
         beside = jnp.pad(parts, ((0, group_rows - 2), (0, 0)))
         return jnp.concatenate([rows, beside], axis=1)
 
+    up, down = kv, kv
     held, held_spots = [], []
+    blocks_of = []
 
     def score(spot_list, blocks):
         held.append(attend_step(limits, packed, spot_list, blocks, group_rows))
         held_spots.append(spot_list)
 
-    up, down = kv, kv
-    blocks_of = []
     for step in range(far):
-        if step == 0:
-            down, ordered = tie(down, ordered)
-        if step == far - 2:
-            from_behind, from_ahead = [payload(s) for s in behind], [payload(s) for s in ahead]
-            up, (from_behind, from_ahead) = tie(up, (from_behind, from_ahead))
-            from_behind = [shifted(g, -by) for g, by in zip(from_behind, behind_hops)]
-            from_ahead = [shifted(g, by) for g, by in zip(from_ahead, ahead_hops)]
-        if step == far - 1:
-            score((ring - 1,), (kv,))
+        if step == 2:
+            up, ordered = tie(up, ordered)
+        if step == 3:
+            guests = [payload(s[0]) for s in (opposite, behind_far, ahead_far)]
+            up, guests = tie(up, guests)
+            guests = [shifted(g, by) for g, by in zip(guests, (-2, -1, 1))]
+        if step == 4:
+            score(mine, (kv,))
             score((0, 1), blocks_of[0])
-            up, (held, from_behind) = tie(up, (held, from_behind))
+            up, (guests, held) = tie(up, (guests, held))
+        if step == 5:
+            score((2, 3), blocks_of[1])
+            score((4, 5), blocks_of[2])
+            up, held = tie(up, held)
         up = shifted(up, 1)
         down = shifted(down, -1)
         blocks_of.append((up, down))
-    for step in range(1, far - 1):
-        score((2 * step, 2 * step + 1), blocks_of[step])
+    score((6, 7), blocks_of[3])
+    score((8, 9), blocks_of[4])
     out = place_rows(where, held, held_spots, group_rows, None, packed.shape)
     up, out = tie(up, out)
-    from_behind = attend_guests(from_behind, up, group_rows)
-    from_behind = [shifted(g, by) for g, by in zip(from_behind, behind_hops)]
-    from_ahead = attend_guests(from_ahead, down, group_rows)
-    from_ahead = [shifted(g, -by) for g, by in zip(from_ahead, ahead_hops)]
+    back = attend_guests(guests, (0, 0, 1), (up, down), group_rows)
+    back = [shifted(g, by) for g, by in zip(back, (2, 1, -1))]
     held, held_spots = [], []
     score((2 * far - 2, 2 * far - 1), (up, down))
     out = place_rows(
-        where,
-        [*held, *from_behind, *from_ahead],
-        [*held_spots, *((s,) for s in behind), *((s,) for s in ahead)],
-        group_rows,
-        out,
-        packed.shape,
+        where, [*held, *back], [*held_spots, opposite, behind_far, ahead_far], group_rows, out, packed.shape
     )
     return out[None, None]
 

time: 219 us -> 157 us (0.72)
  the two profiles are of different devices: /device:TPU:2 before, /device:TPU:126 now
where the time goes in v4:
time: 157 us
  starting transfers between devices  73.7 us (47%)
  waiting for transfers between devices  54.8 us (35%)
  Pallas kernels  16.8 us (11%)
  matrix products  5.03 us (3%)
  local copies, waits for them, and re-layouts  3.95 us (3%)
  other arithmetic  1.83 us (1%)
    ppermute x18, starting transfers between devices, shifted(): lax.ppermute(x, 'prompt', [(i, (i + by) % ring) for i in range(ring)])  66.2 us
    ppermute x18, waiting for transfers between devices, shifted(): lax.ppermute(x, 'prompt', [(i, (i + by) % ring) for i in range(ring)])  54.8 us
    pallas_call x7, Pallas kernels, attend_step(): pl.pallas_call(functools.partial(step_kernel, spots, rows), out_shape=jax...  12.3 us
    all_to_all x1, starting transfers between devices, body(): lax.all_to_all(ordered.reshape(dp_count, row_count // dp_count, width), '...  7.49 us
    dot_general x2, matrix products, move_rows(): jnp.dot(pick, rows, preferred_element_type=jnp.float32).astype(rows.dtype)  5.03 us
    unnamed x17, local copies, waits for them, and re-layouts  3.5 us
  transfers between devices with their start and end apart: 19, of which 9 were waited for; matrix products, arithmetic and copies ran while one was open for 5% of the time, Pallas kernels for 9%

profile of v4, /device:TPU:126, one launch (start us, length us, event | category | flops | bytes accessed | tf_op | source)
XLA Modules:
  0.0 156.6 jit_solution(13155569928341255841)
XLA Ops:
  0.0 5.2 %collective-permute-start = (bf16[384,1024]{1,0:T(8,128)(2,1)}, bf16[384,1024]{1,0:T(8,128)(2,1)}, u32[]{:S(2)}, u32[]{:S(2)}) collective-permute-start(bf16[384,1024]{1,0:T(8,128)(2,1)} %bitcast.21), channel_id=1, source_target_pairs={{0,1},{1,2},{2,3},{3,4},{4,5},{5,6},{6,7},{7,8},{8,9},{9,10},{10,1... | collective-permute-start | bytes 2359304 | tf_op jit(solution)/shard_map/ppermute | solution.py:149
  5.2 1.9 %collective-permute-start.7 = (bf16[384,1024]{1,0:T(8,128)(2,1)}, bf16[384,1024]{1,0:T(8,128)(2,1)}, u32[]{:S(2)}, u32[]{:S(2)}) collective-permute-start(bf16[384,1024]{1,0:T(8,128)(2,1)} %bitcast.22), channel_id=1, source_target_pairs={{0,15},{1,0},{2,1},{3,2},{4,3},{5,4},{6,5},{7,6},{8,7},{9,8},{10,9... | collective-permute-start | bytes 2359304 | tf_op jit(solution)/shard_map/ppermute | solution.py:149
  7.1 2.7 %convolution_convert_fusion.1 = bf16[256,4096]{1,0:T(8,128)(2,1)} fusion(bf16[1,1,256,4096]{3,2,1,0:T(8,128)(2,1)S(1)} %copy-done, s32[256]{0:T(256)} %bitcast.25), kind=kOutput, calls=%fused_computation.1 | convolution fusion | flops 537985024 | bytes 4195328 | tf_op jit(solution)/shard_map/dot_general | solution.py:132
  9.8 7.5 %all-to-all-start = ((bf16[32,8,4096]{2,1,0:T(8,128)(2,1)}), bf16[32,8,4096]{2,1,0:T(8,128)(2,1)}, u32[]{:S(2)}, u32[]{:S(2)}) async-start(bf16[32,8,4096]{2,1,0:T(8,128)(2,1)} %bitcast.24), calls=%async_computation | async-start | bytes 4194304 | tf_op jit(solution)/shard_map/all_to_all | solution.py:154
  17.3 0.6 broadcast.561
  17.9 0.6 reduce.3
  18.7 0.1 select_reduce_fusion
  19.2 3.1 %collective-permute-done.refs_0_ = bf16[384,1024]{1,0:T(8,128)(2,1)} collective-permute-done((bf16[384,1024]{1,0:T(8,128)(2,1)}, bf16[384,1024]{1,0:T(8,128)(2,1)}, u32[]{:S(2)}, u32[]{:S(2)}) %collective-permute-start) | collective-permute-done | bytes 786464 | tf_op jit(solution)/shard_map/ppermute | solution.py:149
  22.3 5.6 %collective-permute-start.1 = (bf16[384,1024]{1,0:T(8,128)(2,1)}, bf16[384,1024]{1,0:T(8,128)(2,1)}, u32[]{:S(2)}, u32[]{:S(2)}) collective-permute-start(bf16[384,1024]{1,0:T(8,128)(2,1)} %collective-permute-done.refs_0_), channel_id=1, source_target_pairs={{0,1},{1,2},{2,3},{3,4},{4,5},{5,6},{6,7},{7,8},{8,9},{9,10},{10,1... | collective-permute-start | bytes 2359304 | tf_op jit(solution)/shard_map/ppermute | solution.py:149
  27.9 1.9 %collective-permute-start.9 = (bf16[384,1024]{1,0:T(8,128)(2,1)}, bf16[384,1024]{1,0:T(8,128)(2,1)}, u32[]{:S(2)}, u32[]{:S(2)}) collective-permute-start(bf16[384,1024]{1,0:T(8,128)(2,1)} %collective-permute-done.7.refs_1_), channel_id=1, source_target_pairs={{0,15},{1,0},{2,1},{3,2},{4,3},{5,4},{6,5},{7,6},{8,7},{9,8},{10,9... | collective-permute-start | bytes 2359304 | tf_op jit(solution)/shard_map/ppermute | solution.py:149
  29.9 0.1 select_reduce_fusion.1
  30.0 14.1 %collective-permute-done.1.refs_0_ = bf16[384,1024]{1,0:T(8,128)(2,1)} collective-permute-done((bf16[384,1024]{1,0:T(8,128)(2,1)}, bf16[384,1024]{1,0:T(8,128)(2,1)}, u32[]{:S(2)}, u32[]{:S(2)}) %collective-permute-start.1) | collective-permute-done | bytes 786464 | tf_op jit(solution)/shard_map/ppermute | solution.py:149
  44.1 5.6 %collective-permute-start.2 = (bf16[384,1024]{1,0:T(8,128)(2,1)}, bf16[384,1024]{1,0:T(8,128)(2,1)}, u32[]{:S(2)}, u32[]{:S(2)}) collective-permute-start(bf16[384,1024]{1,0:T(8,128)(2,1)} %collective-permute-done.1.refs_0_), channel_id=1, source_target_pairs={{0,1},{1,2},{2,3},{3,4},{4,5},{5,6},{6,7},{7,8},{8,9},{9,10},{10,1... | collective-permute-start | bytes 2359304 | tf_op jit(solution)/shard_map/ppermute | solution.py:149
  49.7 1.9 %collective-permute-start.10 = (bf16[384,1024]{1,0:T(8,128)(2,1)}, bf16[384,1024]{1,0:T(8,128)(2,1)}, u32[]{:S(2)}, u32[]{:S(2)}) collective-permute-start(bf16[384,1024]{1,0:T(8,128)(2,1)} %collective-permute-done.9.refs_1_), channel_id=1, source_target_pairs={{0,15},{1,0},{2,1},{3,2},{4,3},{5,4},{6,5},{7,6},{8,7},{9,8},{10,9... | collective-permute-start | bytes 2359304 | tf_op jit(solution)/shard_map/ppermute | solution.py:149
  51.6 2.3 %convolution_convert_fusion.query_ref = bf16[256,4096]{1,0:T(8,128)(2,1)S(1)} fusion(bf16[32,8,4096]{2,1,0:T(8,128)(2,1)} %all-to-all-done, s32[256]{0:T(256)S(1)} %fusion.13), kind=kOutput, calls=%fused_computation | convolution fusion | flops 537985024 | bytes 4195328 | tf_op jit(solution)/shard_map/dot_general | solution.py:132
  54.0 1.3 copy-done.1
  55.3 0.7 pad_maximum_fusion
  56.1 8.9 %collective-permute-done.2.refs_0_ = bf16[384,1024]{1,0:T(8,128)(2,1)} collective-permute-done((bf16[384,1024]{1,0:T(8,128)(2,1)}, bf16[384,1024]{1,0:T(8,128)(2,1)}, u32[]{:S(2)}, u32[]{:S(2)}) %collective-permute-start.2) | collective-permute-done | bytes 786464 | tf_op jit(solution)/shard_map/ppermute | solution.py:149
  65.0 5.6 %collective-permute-start.3 = (bf16[384,1024]{1,0:T(8,128)(2,1)}, bf16[384,1024]{1,0:T(8,128)(2,1)}, u32[]{:S(2)}, u32[]{:S(2)}) collective-permute-start(bf16[384,1024]{1,0:T(8,128)(2,1)} %collective-permute-done.2.refs_0_), channel_id=1, source_target_pairs={{0,1},{1,2},{2,3},{3,4},{4,5},{5,6},{6,7},{7,8},{8,9},{9,10},{10,1... | collective-permute-start | bytes 2359304 | tf_op jit(solution)/shard_map/ppermute | solution.py:149
  70.6 1.9 %collective-permute-start.12 = (bf16[384,1024]{1,0:T(8,128)(2,1)}, bf16[384,1024]{1,0:T(8,128)(2,1)}, u32[]{:S(2)}, u32[]{:S(2)}) collective-permute-start(bf16[384,1024]{1,0:T(8,128)(2,1)} %collective-permute-done.10.refs_1_), channel_id=1, source_target_pairs={{0,15},{1,0},{2,1},{3,2},{4,3},{5,4},{6,5},{7,6},{8,7},{9,8},{10,9... | collective-permute-start | bytes 2359304 | tf_op jit(solution)/shard_map/ppermute | solution.py:149
  72.5 5.7 %collective-permute-start.4 = (bf16[16,4224]{1,0:T(8,128)(2,1)}, bf16[16,4224]{1,0:T(8,128)(2,1)S(1)}, u32[]{:S(2)}, u32[]{:S(2)}) collective-permute-start(bf16[16,4224]{1,0:T(8,128)(2,1)} %get-tuple-element.28), channel_id=1, source_target_pairs={{0,14},{1,15},{2,0},{3,1},{4,2},{5,3},{6,4},{7,5},{8,6},{9,7},{10,... | collective-permute-start | bytes 405512 | tf_op jit(solution)/shard_map/ppermute | solution.py:149
  78.3 5.1 %collective-permute-start.5 = (bf16[16,4224]{1,0:T(8,128)(2,1)}, bf16[16,4224]{1,0:T(8,128)(2,1)S(1)}, u32[]{:S(2)}, u32[]{:S(2)}) collective-permute-start(bf16[16,4224]{1,0:T(8,128)(2,1)} %get-tuple-element.29), channel_id=1, source_target_pairs={{0,15},{1,0},{2,1},{3,2},{4,3},{5,4},{6,5},{7,6},{8,7},{9,8},{10,9... | collective-permute-start | bytes 405512 | tf_op jit(solution)/shard_map/ppermute | solution.py:149
  83.4 1.9 %collective-permute-start.6 = (bf16[16,4224]{1,0:T(8,128)(2,1)S(1)}, bf16[16,4224]{1,0:T(8,128)(2,1)S(1)}, u32[]{:S(2)}, u32[]{:S(2)}) collective-permute-start(bf16[16,4224]{1,0:T(8,128)(2,1)S(1)} %pad_maximum_fusion.2), channel_id=1, source_target_pairs={{0,1},{1,2},{2,3},{3,4},{4,5},{5,6},{6,7},{7,8},{8,9},{9,10},{10,1... | collective-permute-start | bytes 405512 | tf_op jit(solution)/shard_map/ppermute | solution.py:149
  85.4 1.6 %copy-done.2 = bf16[256,4096]{1,0:T(8,128)(2,1)S(1)} copy-done((bf16[256,4096]{1,0:T(8,128)(2,1)S(1)}, bf16[256,4096]{1,0:T(8,128)(2,1)}, u32[]{:S(2)}) %copy-start.2) | copy-done | bytes 2097176
  87.0 0.6 attend_15.1.refs_0_
  87.7 2.4 %attend_0.1.refs_1_ = bf16[32,4096]{1,0:T(8,128)(2,1)S(1)} custom-call(s32[16,128]{1,0:T(8,128)S(1)} %tile.28.limits_ref, bf16[256,4096]{1,0:T(8,128)(2,1)S(1)} %copy-done.2, bf16[384,1024]{1,0:T(8,128)(2,1)} %collective-permute-done.refs_0_, bf16[384,1024]{1,0:T(8,128)(2,1)} %collective-permute-done.7.refs_1_), custom_call_target="tpu_custom_call" | custom-call | flops 201326592 | bytes 1048576 | tf_op jit(solution)/shard_map/attend_0/pallas_call | solution.py:90
  90.0 5.8 %collective-permute-done.4.refs_2_ = bf16[16,4224]{1,0:T(8,128)(2,1)S(1)} collective-permute-done((bf16[16,4224]{1,0:T(8,128)(2,1)}, bf16[16,4224]{1,0:T(8,128)(2,1)S(1)}, u32[]{:S(2)}, u32[]{:S(2)}) %collective-permute-start.4) | collective-permute-done | bytes 135200 | tf_op jit(solution)/shard_map/ppermute | solution.py:149
  95.9 3.0 %collective-permute-done.5.refs_3_ = bf16[16,4224]{1,0:T(8,128)(2,1)S(1)} collective-permute-done((bf16[16,4224]{1,0:T(8,128)(2,1)}, bf16[16,4224]{1,0:T(8,128)(2,1)S(1)}, u32[]{:S(2)}, u32[]{:S(2)}) %collective-permute-start.5) | collective-permute-done | bytes 135200 | tf_op jit(solution)/shard_map/ppermute | solution.py:149
  98.9 2.3 %collective-permute-start.8 = (bf16[384,1024]{1,0:T(8,128)(2,1)}, bf16[384,1024]{1,0:T(8,128)(2,1)S(1)}, u32[]{:S(2)}, u32[]{:S(2)}) collective-permute-start(bf16[384,1024]{1,0:T(8,128)(2,1)} %collective-permute-done.3.refs_0_), channel_id=1, source_target_pairs={{0,1},{1,2},{2,3},{3,4},{4,5},{5,6},{6,7},{7,8},{8,9},{9,10},{10,1... | collective-permute-start | bytes 2359304 | tf_op jit(solution)/shard_map/ppermute | solution.py:149
  101.2 3.6 %collective-permute-start.13 = (bf16[384,1024]{1,0:T(8,128)(2,1)}, bf16[384,1024]{1,0:T(8,128)(2,1)S(1)}, u32[]{:S(2)}, u32[]{:S(2)}) collective-permute-start(bf16[384,1024]{1,0:T(8,128)(2,1)} %collective-permute-done.12.refs_1_), channel_id=1, source_target_pairs={{0,15},{1,0},{2,1},{3,2},{4,3},{5,4},{6,5},{7,6},{8,7},{9,8},{10,9... | collective-permute-start | bytes 2359304 | tf_op jit(solution)/shard_map/ppermute | solution.py:149
  104.7 2.4 %attend_2.1.refs_2_ = bf16[32,4096]{1,0:T(8,128)(2,1)S(1)} custom-call(s32[16,128]{1,0:T(8,128)S(1)} %tile.28.limits_ref, bf16[256,4096]{1,0:T(8,128)(2,1)S(1)} %copy-done.2, bf16[384,1024]{1,0:T(8,128)(2,1)} %collective-permute-done.1.refs_0_, bf16[384,1024]{1,0:T(8,128)(2,1)} %collective-permute-done.9.refs_1_), custom_call_target="tpu_custom_call" | custom-call | flops 201326592 | bytes 1048576 | tf_op jit(solution)/shard_map/attend_2/pallas_call | solution.py:90
  107.1 2.5 %attend_4.1.refs_3_ = bf16[32,4096]{1,0:T(8,128)(2,1)S(1)} custom-call(s32[16,128]{1,0:T(8,128)S(1)} %tile.28.limits_ref, bf16[256,4096]{1,0:T(8,128)(2,1)S(1)} %copy-done.2, bf16[384,1024]{1,0:T(8,128)(2,1)} %collective-permute-done.2.refs_0_, bf16[384,1024]{1,0:T(8,128)(2,1)} %collective-permute-done.10.refs_1_), custom_call_target="tpu_custom_call" | custom-call | flops 201326592 | bytes 1048576 | tf_op jit(solution)/shard_map/attend_4/pallas_call | solution.py:90
  109.6 5.5 %collective-permute-done.8.refs_0_ = bf16[384,1024]{1,0:T(8,128)(2,1)S(1)} collective-permute-done((bf16[384,1024]{1,0:T(8,128)(2,1)}, bf16[384,1024]{1,0:T(8,128)(2,1)S(1)}, u32[]{:S(2)}, u32[]{:S(2)}) %collective-permute-start.8) | collective-permute-done | bytes 786464 | tf_op jit(solution)/shard_map/ppermute | solution.py:149
  115.1 4.2 %collective-permute-start.11 = (bf16[384,1024]{1,0:T(8,128)(2,1)S(1)}, bf16[384,1024]{1,0:T(8,128)(2,1)S(1)}, u32[]{:S(2)}, u32[]{:S(2)}) collective-permute-start(bf16[384,1024]{1,0:T(8,128)(2,1)S(1)} %collective-permute-done.8.refs_0_), channel_id=1, source_target_pairs={{0,1},{1,2},{2,3},{3,4},{4,5},{5,6},{6,7},{7,8},{8,9},{9,10},{10,1... | collective-permute-start | bytes 2359304 | tf_op jit(solution)/shard_map/ppermute | solution.py:149
  119.4 1.9 %collective-permute-start.14 = (bf16[384,1024]{1,0:T(8,128)(2,1)S(1)}, bf16[384,1024]{1,0:T(8,128)(2,1)S(1)}, u32[]{:S(2)}, u32[]{:S(2)}) collective-permute-start(bf16[384,1024]{1,0:T(8,128)(2,1)S(1)} %collective-permute-done.13.refs_1_), channel_id=1, source_target_pairs={{0,15},{1,0},{2,1},{3,2},{4,3},{5,4},{6,5},{7,6},{8,7},{9,8},{10,9... | collective-permute-start | bytes 2359304 | tf_op jit(solution)/shard_map/ppermute | solution.py:149
  121.3 0.1 select_reduce_fusion.2.where_ref
  121.4 2.4 %attend_6.1.refs_4_ = bf16[32,4096]{1,0:T(8,128)(2,1)S(1)} custom-call(s32[16,128]{1,0:T(8,128)S(1)} %tile.28.limits_ref, bf16[256,4096]{1,0:T(8,128)(2,1)S(1)} %copy-done.3, bf16[384,1024]{1,0:T(8,128)(2,1)} %collective-permute-done.3.refs_0_, bf16[384,1024]{1,0:T(8,128)(2,1)} %collective-permute-done.12.refs_1_), custom_call_target="tpu_custom_call" | custom-call | flops 201326592 | bytes 1048576 | tf_op jit(solution)/shard_map/attend_6/pallas_call | solution.py:90
  123.8 1.0 attend_8.1.refs_5_
  124.8 1.7 %place_held.1.refs_0_ = bf16[256,4096]{1,0:T(8,128)(2,1)} custom-call(s32[16]{0:T(128)S(1)} %select_reduce_fusion.2.where_ref, bf16[16,4096]{1,0:T(8,128)(2,1)S(1)} %attend_15.1.refs_0_, bf16[32,4096]{1,0:T(8,128)(2,1)S(1)} %attend_0.1.refs_1_, bf16[32,4096]{1,0:T(8,128)(2,1)S(1)} %attend_2.1.refs_2_, bf16[32,4096]{1,0:T(8,128)(2,1)S(1)} %attend_4.1.refs_3_, ...), custom_call_target="tpu_custom_call" | custom-call | bytes 131072 | tf_op jit(solution)/shard_map/place_held/pallas_call | solution.py:116
  126.6 5.3 %collective-permute-done.11.refs_0_ = bf16[384,1024]{1,0:T(8,128)(2,1)S(1)} collective-permute-done((bf16[384,1024]{1,0:T(8,128)(2,1)S(1)}, bf16[384,1024]{1,0:T(8,128)(2,1)S(1)}, u32[]{:S(2)}, u32[]{:S(2)}) %collective-permute-start.11) | collective-permute-done | bytes 786464 | tf_op jit(solution)/shard_map/ppermute | solution.py:149
  131.9 4.2 %collective-permute-done.14.refs_1_ = bf16[384,1024]{1,0:T(8,128)(2,1)S(1)} collective-permute-done((bf16[384,1024]{1,0:T(8,128)(2,1)S(1)}, bf16[384,1024]{1,0:T(8,128)(2,1)S(1)}, u32[]{:S(2)}, u32[]{:S(2)}) %collective-permute-start.14) | collective-permute-done | bytes 786464 | tf_op jit(solution)/shard_map/ppermute | solution.py:149
  136.0 1.5 attend_guests.1
  137.5 6.0 %collective-permute-start.15 = (bf16[16,4096]{1,0:T(8,128)(2,1)S(1)}, bf16[16,4096]{1,0:T(8,128)(2,1)S(1)}, u32[]{:S(2)}, u32[]{:S(2)}) collective-permute-start(bf16[16,4096]{1,0:T(8,128)(2,1)S(1)} %get-tuple-element.44), channel_id=1, source_target_pairs={{0,2},{1,3},{2,4},{3,5},{4,6},{5,7},{6,8},{7,9},{8,10},{9,11},{10,... | collective-permute-start | bytes 393224 | tf_op jit(solution)/shard_map/ppermute | solution.py:149
  143.5 3.6 %collective-permute-start.16 = (bf16[16,4096]{1,0:T(8,128)(2,1)S(1)}, bf16[16,4096]{1,0:T(8,128)(2,1)S(1)}, u32[]{:S(2)}, u32[]{:S(2)}) collective-permute-start(bf16[16,4096]{1,0:T(8,128)(2,1)S(1)} %get-tuple-element.45), channel_id=1, source_target_pairs={{0,1},{1,2},{2,3},{3,4},{4,5},{5,6},{6,7},{7,8},{8,9},{9,10},{10,1... | collective-permute-start | bytes 393224 | tf_op jit(solution)/shard_map/ppermute | solution.py:149
  147.1 2.2 %collective-permute-start.17 = (bf16[16,4096]{1,0:T(8,128)(2,1)S(1)}, bf16[16,4096]{1,0:T(8,128)(2,1)S(1)}, u32[]{:S(2)}, u32[]{:S(2)}) collective-permute-start(bf16[16,4096]{1,0:T(8,128)(2,1)S(1)} %get-tuple-element.46), channel_id=1, source_target_pairs={{0,15},{1,0},{2,1},{3,2},{4,3},{5,4},{6,5},{7,6},{8,7},{9,8},{10,9... | collective-permute-start | bytes 393224 | tf_op jit(solution)/shard_map/ppermute | solution.py:149
  149.3 1.0 attend_10.1.refs_1_
  150.4 4.8 %collective-permute-done.17.refs_4_ = bf16[16,4096]{1,0:T(8,128)(2,1)S(1)} collective-permute-done((bf16[16,4096]{1,0:T(8,128)(2,1)S(1)}, bf16[16,4096]{1,0:T(8,128)(2,1)S(1)}, u32[]{:S(2)}, u32[]{:S(2)}) %collective-permute-start.17) | collective-permute-done | bytes 131104 | tf_op jit(solution)/shard_map/ppermute | solution.py:149
  155.2 1.4 place_last.1
  (46 shorter events, 0.6 us)
Async XLA Ops:
  0.0 7.1 %copy-start = (bf16[1,1,256,4096]{3,2,1,0:T(8,128)(2,1)S(1)}, bf16[1,1,256,4096]{3,2,1,0:T(8,128)(2,1)}, u32[]{:S(2)}) copy-start(bf16[1,1,256,4096]{3,2,1,0:T(8,128)(2,1)} %param.6) | copy-start | bytes 6291460
  0.0 22.3 %collective-permute-start = (bf16[384,1024]{1,0:T(8,128)(2,1)}, bf16[384,1024]{1,0:T(8,128)(2,1)}, u32[]{:S(2)}, u32[]{:S(2)}) collective-permute-start(bf16[384,1024]{1,0:T(8,128)(2,1)} %bitcast.21), channel_id=1, source_target_pairs={{0,1},{1,2},{2,3},{3,4},{4,5},{5,6},{6,7},{7,8},{8,9},{9,10},{10,1... | collective-permute-start | bytes 2359304 | tf_op jit(solution)/shard_map/ppermute | solution.py:149
  5.2 22.7 %collective-permute-start.7 = (bf16[384,1024]{1,0:T(8,128)(2,1)}, bf16[384,1024]{1,0:T(8,128)(2,1)}, u32[]{:S(2)}, u32[]{:S(2)}) collective-permute-start(bf16[384,1024]{1,0:T(8,128)(2,1)} %bitcast.22), channel_id=1, source_target_pairs={{0,15},{1,0},{2,1},{3,2},{4,3},{5,4},{6,5},{7,6},{8,7},{9,8},{10,9... | collective-permute-start | bytes 2359304 | tf_op jit(solution)/shard_map/ppermute | solution.py:149
  9.8 8.1 %copy-start.6 = (s32[1,1,256]{2,1,0:T(1,128)S(1)}, s32[1,1,256]{2,1,0:T(1,128)}, u32[]{:S(2)}) copy-start(s32[1,1,256]{2,1,0:T(1,128)} %param.9) | copy-start | bytes 3076
  9.8 8.8 %copy-start.7 = (s32[1,1,16]{2,1,0:T(1,128)S(1)}, s32[1,1,16]{2,1,0:T(1,128)}, u32[]{:S(2)}) copy-start(s32[1,1,16]{2,1,0:T(1,128)} %param.10) | copy-start | bytes 196
  9.8 20.0 %copy-start.5 = (s32[1,1,256]{2,1,0:T(1,128)S(1)}, s32[1,1,256]{2,1,0:T(1,128)}, u32[]{:S(2)}) copy-start(s32[1,1,256]{2,1,0:T(1,128)} %param.8) | copy-start | bytes 3076
  9.8 41.8 %all-to-all-start = ((bf16[32,8,4096]{2,1,0:T(8,128)(2,1)}), bf16[32,8,4096]{2,1,0:T(8,128)(2,1)}, u32[]{:S(2)}, u32[]{:S(2)}) async-start(bf16[32,8,4096]{2,1,0:T(8,128)(2,1)} %bitcast.24), calls=%async_computation | async-start | bytes 4194304 | tf_op jit(solution)/shard_map/all_to_all | solution.py:154
  22.3 21.8 %collective-permute-start.1 = (bf16[384,1024]{1,0:T(8,128)(2,1)}, bf16[384,1024]{1,0:T(8,128)(2,1)}, u32[]{:S(2)}, u32[]{:S(2)}) collective-permute-start(bf16[384,1024]{1,0:T(8,128)(2,1)} %collective-permute-done.refs_0_), channel_id=1, source_target_pairs={{0,1},{1,2},{2,3},{3,4},{4,5},{5,6},{6,7},{7,8},{8,9},{9,10},{10,1... | collective-permute-start | bytes 2359304 | tf_op jit(solution)/shard_map/ppermute | solution.py:149
  27.9 21.8 %collective-permute-start.9 = (bf16[384,1024]{1,0:T(8,128)(2,1)}, bf16[384,1024]{1,0:T(8,128)(2,1)}, u32[]{:S(2)}, u32[]{:S(2)}) collective-permute-start(bf16[384,1024]{1,0:T(8,128)(2,1)} %collective-permute-done.7.refs_1_), channel_id=1, source_target_pairs={{0,15},{1,0},{2,1},{3,2},{4,3},{5,4},{6,5},{7,6},{8,7},{9,8},{10,9... | collective-permute-start | bytes 2359304 | tf_op jit(solution)/shard_map/ppermute | solution.py:149
  30.0 55.5 %copy-start.4 = (bf16[1,1,384,1024]{3,2,1,0:T(8,128)(2,1)S(1)}, bf16[1,1,384,1024]{3,2,1,0:T(8,128)(2,1)}, u32[]{:S(2)}) copy-start(bf16[1,1,384,1024]{3,2,1,0:T(8,128)(2,1)} %param.11) | copy-start | bytes 2359300
  44.1 20.9 %collective-permute-start.2 = (bf16[384,1024]{1,0:T(8,128)(2,1)}, bf16[384,1024]{1,0:T(8,128)(2,1)}, u32[]{:S(2)}, u32[]{:S(2)}) collective-permute-start(bf16[384,1024]{1,0:T(8,128)(2,1)} %collective-permute-done.1.refs_0_), channel_id=1, source_target_pairs={{0,1},{1,2},{2,3},{3,4},{4,5},{5,6},{6,7},{7,8},{8,9},{9,10},{10,1... | collective-permute-start | bytes 2359304 | tf_op jit(solution)/shard_map/ppermute | solution.py:149
  49.7 20.9 %collective-permute-start.10 = (bf16[384,1024]{1,0:T(8,128)(2,1)}, bf16[384,1024]{1,0:T(8,128)(2,1)}, u32[]{:S(2)}, u32[]{:S(2)}) collective-permute-start(bf16[384,1024]{1,0:T(8,128)(2,1)} %collective-permute-done.9.refs_1_), channel_id=1, source_target_pairs={{0,15},{1,0},{2,1},{3,2},{4,3},{5,4},{6,5},{7,6},{8,7},{9,8},{10,9... | collective-permute-start | bytes 2359304 | tf_op jit(solution)/shard_map/ppermute | solution.py:149
  54.0 1.3 copy-start.1
  65.0 33.9 %collective-permute-start.3 = (bf16[384,1024]{1,0:T(8,128)(2,1)}, bf16[384,1024]{1,0:T(8,128)(2,1)}, u32[]{:S(2)}, u32[]{:S(2)}) collective-permute-start(bf16[384,1024]{1,0:T(8,128)(2,1)} %collective-permute-done.2.refs_0_), channel_id=1, source_target_pairs={{0,1},{1,2},{2,3},{3,4},{4,5},{5,6},{6,7},{7,8},{8,9},{9,10},{10,1... | collective-permute-start | bytes 2359304 | tf_op jit(solution)/shard_map/ppermute | solution.py:149
  70.6 30.6 %collective-permute-start.12 = (bf16[384,1024]{1,0:T(8,128)(2,1)}, bf16[384,1024]{1,0:T(8,128)(2,1)}, u32[]{:S(2)}, u32[]{:S(2)}) collective-permute-start(bf16[384,1024]{1,0:T(8,128)(2,1)} %collective-permute-done.10.refs_1_), channel_id=1, source_target_pairs={{0,15},{1,0},{2,1},{3,2},{4,3},{5,4},{6,5},{7,6},{8,7},{9,8},{10,9... | collective-permute-start | bytes 2359304 | tf_op jit(solution)/shard_map/ppermute | solution.py:149
  72.5 23.3 %collective-permute-start.4 = (bf16[16,4224]{1,0:T(8,128)(2,1)}, bf16[16,4224]{1,0:T(8,128)(2,1)S(1)}, u32[]{:S(2)}, u32[]{:S(2)}) collective-permute-start(bf16[16,4224]{1,0:T(8,128)(2,1)} %get-tuple-element.28), channel_id=1, source_target_pairs={{0,14},{1,15},{2,0},{3,1},{4,2},{5,3},{6,4},{7,5},{8,6},{9,7},{10,... | collective-permute-start | bytes 405512 | tf_op jit(solution)/shard_map/ppermute | solution.py:149
  78.3 20.6 %collective-permute-start.5 = (bf16[16,4224]{1,0:T(8,128)(2,1)}, bf16[16,4224]{1,0:T(8,128)(2,1)S(1)}, u32[]{:S(2)}, u32[]{:S(2)}) collective-permute-start(bf16[16,4224]{1,0:T(8,128)(2,1)} %get-tuple-element.29), channel_id=1, source_target_pairs={{0,15},{1,0},{2,1},{3,2},{4,3},{5,4},{6,5},{7,6},{8,7},{9,8},{10,9... | collective-permute-start | bytes 405512 | tf_op jit(solution)/shard_map/ppermute | solution.py:149
  83.4 15.5 %collective-permute-start.6 = (bf16[16,4224]{1,0:T(8,128)(2,1)S(1)}, bf16[16,4224]{1,0:T(8,128)(2,1)S(1)}, u32[]{:S(2)}, u32[]{:S(2)}) collective-permute-start(bf16[16,4224]{1,0:T(8,128)(2,1)S(1)} %pad_maximum_fusion.2), channel_id=1, source_target_pairs={{0,1},{1,2},{2,3},{3,4},{4,5},{5,6},{6,7},{7,8},{8,9},{9,10},{10,1... | collective-permute-start | bytes 405512 | tf_op jit(solution)/shard_map/ppermute | solution.py:149
  85.4 1.6 %copy-start.2 = (bf16[256,4096]{1,0:T(8,128)(2,1)S(1)}, bf16[256,4096]{1,0:T(8,128)(2,1)}, u32[]{:S(2)}) copy-start(bf16[256,4096]{1,0:T(8,128)(2,1)} %copy-done.1) | copy-start | bytes 6291460
  98.9 16.3 %collective-permute-start.8 = (bf16[384,1024]{1,0:T(8,128)(2,1)}, bf16[384,1024]{1,0:T(8,128)(2,1)S(1)}, u32[]{:S(2)}, u32[]{:S(2)}) collective-permute-start(bf16[384,1024]{1,0:T(8,128)(2,1)} %collective-permute-done.3.refs_0_), channel_id=1, source_target_pairs={{0,1},{1,2},{2,3},{3,4},{4,5},{5,6},{6,7},{7,8},{8,9},{9,10},{10,1... | collective-permute-start | bytes 2359304 | tf_op jit(solution)/shard_map/ppermute | solution.py:149
  101.2 18.2 %collective-permute-start.13 = (bf16[384,1024]{1,0:T(8,128)(2,1)}, bf16[384,1024]{1,0:T(8,128)(2,1)S(1)}, u32[]{:S(2)}, u32[]{:S(2)}) collective-permute-start(bf16[384,1024]{1,0:T(8,128)(2,1)} %collective-permute-done.12.refs_1_), channel_id=1, source_target_pairs={{0,15},{1,0},{2,1},{3,2},{4,3},{5,4},{6,5},{7,6},{8,7},{9,8},{10,9... | collective-permute-start | bytes 2359304 | tf_op jit(solution)/shard_map/ppermute | solution.py:149
  107.1 14.3 %copy-start.3 = (bf16[256,4096]{1,0:T(8,128)(2,1)S(1)}, bf16[256,4096]{1,0:T(8,128)(2,1)}, u32[]{:S(2)}) copy-start(bf16[256,4096]{1,0:T(8,128)(2,1)} %copy-done.1) | copy-start | bytes 6291460
  115.1 16.7 %collective-permute-start.11 = (bf16[384,1024]{1,0:T(8,128)(2,1)S(1)}, bf16[384,1024]{1,0:T(8,128)(2,1)S(1)}, u32[]{:S(2)}, u32[]{:S(2)}) collective-permute-start(bf16[384,1024]{1,0:T(8,128)(2,1)S(1)} %collective-permute-done.8.refs_0_), channel_id=1, source_target_pairs={{0,1},{1,2},{2,3},{3,4},{4,5},{5,6},{6,7},{7,8},{8,9},{9,10},{10,1... | collective-permute-start | bytes 2359304 | tf_op jit(solution)/shard_map/ppermute | solution.py:149
  119.4 16.6 %collective-permute-start.14 = (bf16[384,1024]{1,0:T(8,128)(2,1)S(1)}, bf16[384,1024]{1,0:T(8,128)(2,1)S(1)}, u32[]{:S(2)}, u32[]{:S(2)}) collective-permute-start(bf16[384,1024]{1,0:T(8,128)(2,1)S(1)} %collective-permute-done.13.refs_1_), channel_id=1, source_target_pairs={{0,15},{1,0},{2,1},{3,2},{4,3},{5,4},{6,5},{7,6},{8,7},{9,8},{10,9... | collective-permute-start | bytes 2359304 | tf_op jit(solution)/shard_map/ppermute | solution.py:149
  137.5 12.9 %collective-permute-start.15 = (bf16[16,4096]{1,0:T(8,128)(2,1)S(1)}, bf16[16,4096]{1,0:T(8,128)(2,1)S(1)}, u32[]{:S(2)}, u32[]{:S(2)}) collective-permute-start(bf16[16,4096]{1,0:T(8,128)(2,1)S(1)} %get-tuple-element.44), channel_id=1, source_target_pairs={{0,2},{1,3},{2,4},{3,5},{4,6},{5,7},{6,8},{7,9},{8,10},{9,11},{10,... | collective-permute-start | bytes 393224 | tf_op jit(solution)/shard_map/ppermute | solution.py:149
  143.5 6.9 %collective-permute-start.16 = (bf16[16,4096]{1,0:T(8,128)(2,1)S(1)}, bf16[16,4096]{1,0:T(8,128)(2,1)S(1)}, u32[]{:S(2)}, u32[]{:S(2)}) collective-permute-start(bf16[16,4096]{1,0:T(8,128)(2,1)S(1)} %get-tuple-element.45), channel_id=1, source_target_pairs={{0,1},{1,2},{2,3},{3,4},{4,5},{5,6},{6,7},{7,8},{8,9},{9,10},{10,1... | collective-permute-start | bytes 393224 | tf_op jit(solution)/shard_map/ppermute | solution.py:149
  147.1 8.1 %collective-permute-start.17 = (bf16[16,4096]{1,0:T(8,128)(2,1)S(1)}, bf16[16,4096]{1,0:T(8,128)(2,1)S(1)}, u32[]{:S(2)}, u32[]{:S(2)}) collective-permute-start(bf16[16,4096]{1,0:T(8,128)(2,1)S(1)} %get-tuple-element.46), channel_id=1, source_target_pairs={{0,15},{1,0},{2,1},{3,2},{4,3},{5,4},{6,5},{7,6},{8,7},{9,8},{10,9... | collective-permute-start | bytes 393224 | tf_op jit(solution)/shard_map/ppermute | solution.py:149

commit v5 on v4

--- a/solution.py
+++ b/solution.py
@@ -15,10 +15,13 @@
 SCALE = math.log2(math.e) / math.sqrt(HD)
 
 
+HALF = KVH // 2
+
+
 def score_group(query_ref, row, rows, block, limits, out_ref, out_row):
     cache_len = block.shape[0]
     visible = lax.broadcasted_iota(jnp.int32, (cache_len, GROUPS * rows), 0) <= limits
-    for k in range(KVH):
+    for k in range(HALF):
         heads = [slice((k * GROUPS + g) * HD, (k * GROUPS + g + 1) * HD) for g in range(GROUPS)]
         query = jnp.concatenate([query_ref[row : row + rows, h] for h in heads], axis=0)
         scores = lax.dot_general(
@@ -33,7 +36,7 @@
         row_total = jnp.sum(exponent, axis=0, keepdims=True)
         mixed = lax.dot_general(
             exponent.astype(jnp.bfloat16),
-            block[:, (KVH + k) * HD : (KVH + k + 1) * HD],
+            block[:, (HALF + k) * HD : (HALF + k + 1) * HD],
             (((0,), (0,)), ((), ())),
             preferred_element_type=jnp.float32,
         )
@@ -63,16 +66,24 @@
         refs = refs[1:]
     held, out_ref, sems = refs[: len(ref_spots)], refs[-2], refs[-1]
     copies = []
+    width = held[0].shape[1]
     for ref, spots in zip(held, ref_spots):
         for i, spot in enumerate(spots):
             start = pl.multiple_of(where_ref[spot] * rows, rows)
             copy = pltpu.make_async_copy(
-                ref.at[pl.ds(i * rows, rows), :], out_ref.at[pl.ds(start, rows), :], sems.at[len(copies)]
+                ref.at[pl.ds(i * rows, rows), :], out_ref.at[pl.ds(start, rows), pl.ds(width, width)], sems.at[len(copies)]
             )
             copy.start()
             copies.append(copy)
     for copy in copies:
         copy.wait()
+
+
+def gathered_kernel(rows, place_ref, seq_ref, prev_ref, limits_ref, query_a, query_b, block_a, block_b, out_ref):
+    del seq_ref, prev_ref
+    for i, (query_ref, block) in enumerate(((query_a, block_a), (query_b, block_b))):
+        spot = place_ref[2 * pl.program_id(0) + i]
+        score_group(query_ref, 0, rows, block.at[0], limits_ref[pl.ds(spot, 1), :], out_ref, i * rows)
 
 
 def cost(spots, rows, cache_len):
@@ -124,6 +135,43 @@
         cost_estimate=pl.CostEstimate(flops=0, bytes_accessed=2 * held[0].size, transcendentals=0),
         name="place_last" if again else "place_held",
     )(where, *([out] if again else []), *held)
+
+
+def attend_gathered(place, sequences, limits, packed, gathered, out, rows):
+    count, cache_len, span = gathered.shape
+    width = packed.shape[1]
+
+    def query_spec(i):
+        return pl.BlockSpec((rows, width), lambda g, place, seq: (place[2 * g + i], 0))
+
+    def block_spec(i):
+        return pl.BlockSpec((1, cache_len, span), lambda g, place, seq: (seq[2 * g + i], 0, 0))
+
+    return pl.pallas_call(
+        functools.partial(gathered_kernel, rows),
+        out_shape=jax.ShapeDtypeStruct(out.shape, out.dtype),
+        grid_spec=pltpu.PrefetchScalarGridSpec(
+            num_scalar_prefetch=2,
+            grid=(count // 2,),
+            in_specs=[
+                ANY,
+                pl.BlockSpec(limits.shape, lambda g, place, seq: (0, 0)),
+                query_spec(0),
+                query_spec(1),
+                block_spec(0),
+                block_spec(1),
+            ],
+            out_specs=pl.BlockSpec((2 * rows, width), lambda g, place, seq: (g, 0)),
+        ),
+        input_output_aliases={2: 0},
+        compiler_params=PARAMS,
+        cost_estimate=pl.CostEstimate(
+            flops=2 * count * rows * QH * cache_len * HD,
+            bytes_accessed=2 * gathered.size + 4 * packed.size,
+            transcendentals=count * rows * QH * cache_len // 2,
+        ),
+        name="attend_gathered",
+    )(place, sequences, out, limits, packed, packed, gathered, gathered)
 
 
 def move_rows(targets, rows):
@@ -149,6 +197,12 @@
         return lax.ppermute(x, "prompt", [(i, (i + by) % ring) for i in range(ring)])
 
     steps = ring // 2
+
+    span, half = KVH * HD, HALF * HD
+    first_half, second_half = (
+        jnp.concatenate([kv[:, lo : lo + half], kv[:, span + lo : span + lo + half]], axis=1) for lo in (0, half)
+    )
+    gathered = lax.all_gather(first_half, "prompt", axis=0)
 
     ordered = move_rows(send_list[0, 0], query_rows)
     arrived = lax.all_to_all(
@@ -171,7 +225,8 @@
     slot = recv_list[0, 0]
     of_group = (slot // group_rows)[:, None] == spots[None, :]
     target = jnp.sum(jnp.where(of_group, place[None, :], 0), axis=1) * group_rows + slot % group_rows
-    packed = move_rows(target, arrived)
+    packed_first = move_rows(target, arrived[:, : width // 2])
+    packed = move_rows(target, arrived[:, width // 2 :])
 
     far = steps - 2
     mine, behind_far, ahead_far, opposite = (ring - 1,), (2 * far,), (2 * far + 1,), (2 * far + 2,)
@@ -182,7 +237,7 @@
         beside = jnp.pad(parts, ((0, group_rows - 2), (0, 0)))
         return jnp.concatenate([rows, beside], axis=1)
 
-    up, down = kv, kv
+    up, down = second_half, second_half
     held, held_spots = [], []
     blocks_of = []
 
@@ -198,7 +253,7 @@
             up, guests = tie(up, guests)
             guests = [shifted(g, by) for g, by in zip(guests, (-2, -1, 1))]
         if step == 4:
-            score(mine, (kv,))
+            score(mine, (second_half,))
             score((0, 1), blocks_of[0])
             up, (guests, held) = tie(up, (guests, held))
         if step == 5:
@@ -210,14 +265,16 @@
         blocks_of.append((up, down))
     score((6, 7), blocks_of[3])
     score((8, 9), blocks_of[4])
-    out = place_rows(where, held, held_spots, group_rows, None, packed.shape)
+    out = place_rows(where, held, held_spots, group_rows, None, query_rows.shape)
     up, out = tie(up, out)
     back = attend_guests(guests, (0, 0, 1), (up, down), group_rows)
+    out, back = tie(out, back)
     back = [shifted(g, by) for g, by in zip(back, (2, 1, -1))]
+    out = attend_gathered(place, sequences, limits, packed_first, gathered, out, group_rows)
     held, held_spots = [], []
     score((2 * far - 2, 2 * far - 1), (up, down))
     out = place_rows(
-        where, [*held, *back], [*held_spots, opposite, behind_far, ahead_far], group_rows, out, packed.shape
+        where, [*held, *back], [*held_spots, opposite, behind_far, ahead_far], group_rows, out, query_rows.shape
     )
     return out[None, None]
 

time: 157 us -> 179 us (1.14)
  the two profiles are of different devices: /device:TPU:126 before, /device:TPU:2 now
where the time goes in v5:
time: 179 us; the launch traced here: 177 us
  starting transfers between devices  77 us (43%)
  waiting for transfers between devices  42.8 us (24%)
  Pallas kernels  20.3 us (11%)
  between operations  13.9 us (8%)
  local copies, waits for them, and re-layouts  12.1 us (7%)
  matrix products  6.35 us (4%)
  other arithmetic  4.93 us (3%)
    ppermute x18, starting transfers between devices, shifted(): lax.ppermute(x, 'prompt', [(i, (i + by) % ring) for i in range(ring)])  69.2 us
    ppermute x18, waiting for transfers between devices, shifted(): lax.ppermute(x, 'prompt', [(i, (i + by) % ring) for i in range(ring)])  42.7 us
    unnamed x35, local copies, waits for them, and re-layouts  8.83 us
    pallas_call x7, Pallas kernels, attend_step(): pl.pallas_call(functools.partial(step_kernel, spots, rows), out_shape=jax...  8.61 us
    all_to_all x1, starting transfers between devices, body(): lax.all_to_all(ordered.reshape(dp_count, row_count // dp_count, width), '...  7.81 us
    pallas_call x1, Pallas kernels, attend_gathered(): pl.pallas_call(functools.partial(gathered_kernel, rows), out_shape=jax.Sh...  6.55 us
    dot_general x3, matrix products, move_rows(): jnp.dot(pick, rows, preferred_element_type=jnp.float32).astype(rows.dtype)  6.35 us
  transfers between devices with their start and end apart: 20, of which 5 were waited for; matrix products, arithmetic and copies ran while one was open for 7% of the time, Pallas kernels for 11%

profile of v5, /device:TPU:2, one launch (start us, length us, event | category | flops | bytes accessed | tf_op | source)
XLA Modules:
  0.0 177.5 jit_solution(4648417207584000602)
XLA Ops:
  6.5 1.4 fusion.24
  8.0 0.8 pad_maximum_fusion.1
  8.8 3.8 %collective-permute-start = (bf16[384,512]{1,0:T(8,128)(2,1)S(1)}, bf16[384,512]{1,0:T(8,128)(2,1)S(1)}, u32[]{:S(2)}, u32[]{:S(2)}) collective-permute-start(bf16[384,512]{1,0:T(8,128)(2,1)S(1)} %pad_maximum_fusion.refs_0_), channel_id=1, source_target_pairs={{0,1},{1,2},{2,3},{3,4},{4,5},{5,6},{6,7},{7,8},{8,9},{9,10},{10,1... | collective-permute-start | bytes 1179656 | tf_op jit(solution)/shard_map/ppermute | solution.py:197
  12.6 9.5 %collective-permute-start.7 = (bf16[384,512]{1,0:T(8,128)(2,1)S(1)}, bf16[384,512]{1,0:T(8,128)(2,1)S(1)}, u32[]{:S(2)}, u32[]{:S(2)}) collective-permute-start(bf16[384,512]{1,0:T(8,128)(2,1)S(1)} %pad_maximum_fusion.refs_0_), channel_id=1, source_target_pairs={{0,15},{1,0},{2,1},{3,2},{4,3},{5,4},{6,5},{7,6},{8,7},{9,8},{10,9... | collective-permute-start | bytes 1179656 | tf_op jit(solution)/shard_map/ppermute | solution.py:197
  22.2 2.0 %convolution_convert_fusion = bf16[256,4096]{1,0:T(8,128)(2,1)} fusion(bf16[1,1,256,4096]{3,2,1,0:T(8,128)(2,1)S(1)} %copy-done, s32[256]{0:T(256)S(1)} %bitcast.23), kind=kOutput, calls=%fused_computation | convolution fusion | flops 537985024 | bytes 4195328 | tf_op jit(solution)/shard_map/dot_general | solution.py:180
  24.2 7.8 %all-to-all-start = ((bf16[32,8,4096]{2,1,0:T(8,128)(2,1)}), bf16[32,8,4096]{2,1,0:T(8,128)(2,1)}, u32[]{:S(2)}, u32[]{:S(2)}) async-start(bf16[32,8,4096]{2,1,0:T(8,128)(2,1)} %bitcast.21), calls=%async_computation | async-start | bytes 4194304 | tf_op jit(solution)/shard_map/all_to_all | solution.py:208
  32.6 0.7 reduce.3
  34.5 3.9 %collective-permute-start.9 = (bf16[384,512]{1,0:T(8,128)(2,1)S(1)}, bf16[384,512]{1,0:T(8,128)(2,1)S(1)}, u32[]{:S(2)}, u32[]{:S(2)}) collective-permute-start(bf16[384,512]{1,0:T(8,128)(2,1)S(1)} %collective-permute-done.7.refs_1_), channel_id=1, source_target_pairs={{0,15},{1,0},{2,1},{3,2},{4,3},{5,4},{6,5},{7,6},{8,7},{9,8},{10,9... | collective-permute-start | bytes 1179656 | tf_op jit(solution)/shard_map/ppermute | solution.py:197
  38.4 0.7 copy-done.5
  39.2 1.9 %collective-permute-start.1 = (bf16[384,512]{1,0:T(8,128)(2,1)S(1)}, bf16[384,512]{1,0:T(8,128)(2,1)}, u32[]{:S(2)}, u32[]{:S(2)}) collective-permute-start(bf16[384,512]{1,0:T(8,128)(2,1)S(1)} %collective-permute-done.refs_0_), channel_id=1, source_target_pairs={{0,1},{1,2},{2,3},{3,4},{4,5},{5,6},{6,7},{7,8},{8,9},{9,10},{10,1... | collective-permute-start | bytes 1179656 | tf_op jit(solution)/shard_map/ppermute | solution.py:197
  41.1 0.7 copy-done.3
  41.8 14.1 %collective-permute-done.9.refs_1_ = bf16[384,512]{1,0:T(8,128)(2,1)S(1)} collective-permute-done((bf16[384,512]{1,0:T(8,128)(2,1)S(1)}, bf16[384,512]{1,0:T(8,128)(2,1)S(1)}, u32[]{:S(2)}, u32[]{:S(2)}) %collective-permute-start.9) | collective-permute-done | bytes 393248 | tf_op jit(solution)/shard_map/ppermute | solution.py:197
  55.9 5.4 %collective-permute-start.10 = (bf16[384,512]{1,0:T(8,128)(2,1)S(1)}, bf16[384,512]{1,0:T(8,128)(2,1)}, u32[]{:S(2)}, u32[]{:S(2)}) collective-permute-start(bf16[384,512]{1,0:T(8,128)(2,1)S(1)} %collective-permute-done.9.refs_1_), channel_id=1, source_target_pairs={{0,15},{1,0},{2,1},{3,2},{4,3},{5,4},{6,5},{7,6},{8,7},{9,8},{10,9... | collective-permute-start | bytes 1179656 | tf_op jit(solution)/shard_map/ppermute | solution.py:197
  61.3 0.8 copy-done.7
  63.3 1.9 %collective-permute-start.2 = (bf16[384,512]{1,0:T(8,128)(2,1)}, bf16[384,512]{1,0:T(8,128)(2,1)}, u32[]{:S(2)}, u32[]{:S(2)}) collective-permute-start(bf16[384,512]{1,0:T(8,128)(2,1)} %collective-permute-done.1.refs_0_), channel_id=1, source_target_pairs={{0,1},{1,2},{2,3},{3,4},{4,5},{5,6},{6,7},{7,8},{8,9},{9,10},{10,1... | collective-permute-start | bytes 1179656 | tf_op jit(solution)/shard_map/ppermute | solution.py:197
  65.2 13.5 %collective-permute-done.10.refs_1_ = bf16[384,512]{1,0:T(8,128)(2,1)} collective-permute-done((bf16[384,512]{1,0:T(8,128)(2,1)S(1)}, bf16[384,512]{1,0:T(8,128)(2,1)}, u32[]{:S(2)}, u32[]{:S(2)}) %collective-permute-start.10) | collective-permute-done | bytes 393248 | tf_op jit(solution)/shard_map/ppermute | solution.py:197
  78.7 5.7 %collective-permute-start.12 = (bf16[384,512]{1,0:T(8,128)(2,1)}, bf16[384,512]{1,0:T(8,128)(2,1)}, u32[]{:S(2)}, u32[]{:S(2)}) collective-permute-start(bf16[384,512]{1,0:T(8,128)(2,1)} %collective-permute-done.10.refs_1_), channel_id=1, source_target_pairs={{0,15},{1,0},{2,1},{3,2},{4,3},{5,4},{6,5},{7,6},{8,7},{9,8},{10,9... | collective-permute-start | bytes 1179656 | tf_op jit(solution)/shard_map/ppermute | solution.py:197
  84.5 1.7 convolution_convert_fusion.2.query_ref
  86.2 0.7 pad_maximum_fusion.2
  87.5 1.9 %collective-permute-start.3 = (bf16[384,512]{1,0:T(8,128)(2,1)}, bf16[384,512]{1,0:T(8,128)(2,1)}, u32[]{:S(2)}, u32[]{:S(2)}) collective-permute-start(bf16[384,512]{1,0:T(8,128)(2,1)} %collective-permute-done.2.refs_0_), channel_id=1, source_target_pairs={{0,1},{1,2},{2,3},{3,4},{4,5},{5,6},{6,7},{7,8},{8,9},{9,10},{10,1... | collective-permute-start | bytes 1179656 | tf_op jit(solution)/shard_map/ppermute | solution.py:197
  89.4 3.4 %collective-permute-start.4 = (bf16[16,2176]{1,0:T(8,128)(2,1)}, bf16[16,2176]{1,0:T(8,128)(2,1)}, u32[]{:S(2)}, u32[]{:S(2)}) collective-permute-start(bf16[16,2176]{1,0:T(8,128)(2,1)} %get-tuple-element.32), channel_id=1, source_target_pairs={{0,14},{1,15},{2,0},{3,1},{4,2},{5,3},{6,4},{7,5},{8,6},{9,7},{10,... | collective-permute-start | bytes 208904 | tf_op jit(solution)/shard_map/ppermute | solution.py:197
  92.8 3.7 %collective-permute-start.5 = (bf16[16,2176]{1,0:T(8,128)(2,1)}, bf16[16,2176]{1,0:T(8,128)(2,1)}, u32[]{:S(2)}, u32[]{:S(2)}) collective-permute-start(bf16[16,2176]{1,0:T(8,128)(2,1)} %get-tuple-element.33), channel_id=1, source_target_pairs={{0,15},{1,0},{2,1},{3,2},{4,3},{5,4},{6,5},{7,6},{8,7},{9,8},{10,9... | collective-permute-start | bytes 208904 | tf_op jit(solution)/shard_map/ppermute | solution.py:197
  96.5 3.4 %collective-permute-start.6 = (bf16[16,2176]{1,0:T(8,128)(2,1)}, bf16[16,2176]{1,0:T(8,128)(2,1)}, u32[]{:S(2)}, u32[]{:S(2)}) collective-permute-start(bf16[16,2176]{1,0:T(8,128)(2,1)} %pad_maximum_fusion.4), channel_id=1, source_target_pairs={{0,1},{1,2},{2,3},{3,4},{4,5},{5,6},{6,7},{7,8},{8,9},{9,10},{10,1... | collective-permute-start | bytes 208904 | tf_op jit(solution)/shard_map/ppermute | solution.py:197
  99.8 3.3 %collective-permute-done.12.refs_1_ = bf16[384,512]{1,0:T(8,128)(2,1)} collective-permute-done((bf16[384,512]{1,0:T(8,128)(2,1)}, bf16[384,512]{1,0:T(8,128)(2,1)}, u32[]{:S(2)}, u32[]{:S(2)}) %collective-permute-start.12) | collective-permute-done | bytes 393248 | tf_op jit(solution)/shard_map/ppermute | solution.py:197
  103.2 6.3 %collective-permute-start.13 = (bf16[384,512]{1,0:T(8,128)(2,1)}, bf16[384,512]{1,0:T(8,128)(2,1)}, u32[]{:S(2)}, u32[]{:S(2)}) collective-permute-start(bf16[384,512]{1,0:T(8,128)(2,1)} %collective-permute-done.12.refs_1_), channel_id=1, source_target_pairs={{0,15},{1,0},{2,1},{3,2},{4,3},{5,4},{6,5},{7,6},{8,7},{9,8},{10,9... | collective-permute-start | bytes 1179656 | tf_op jit(solution)/shard_map/ppermute | solution.py:197
  110.1 0.9 tile.28.limits_ref
  111.6 1.0 copy-done.4
  112.6 1.0 copy-done.6
  114.3 1.9 %collective-permute-start.8 = (bf16[384,512]{1,0:T(8,128)(2,1)}, bf16[384,512]{1,0:T(8,128)(2,1)S(1)}, u32[]{:S(2)}, u32[]{:S(2)}) collective-permute-start(bf16[384,512]{1,0:T(8,128)(2,1)} %collective-permute-done.3.refs_0_), channel_id=1, source_target_pairs={{0,1},{1,2},{2,3},{3,4},{4,5},{5,6},{6,7},{7,8},{8,9},{9,10},{10,1... | collective-permute-start | bytes 1179656 | tf_op jit(solution)/shard_map/ppermute | solution.py:197
  116.2 10.5 %collective-permute-done.13.refs_1_ = bf16[384,512]{1,0:T(8,128)(2,1)} collective-permute-done((bf16[384,512]{1,0:T(8,128)(2,1)}, bf16[384,512]{1,0:T(8,128)(2,1)}, u32[]{:S(2)}, u32[]{:S(2)}) %collective-permute-start.13) | collective-permute-done | bytes 393248 | tf_op jit(solution)/shard_map/ppermute | solution.py:197
  126.7 5.6 %collective-permute-start.14 = (bf16[384,512]{1,0:T(8,128)(2,1)}, bf16[384,512]{1,0:T(8,128)(2,1)S(1)}, u32[]{:S(2)}, u32[]{:S(2)}) collective-permute-start(bf16[384,512]{1,0:T(8,128)(2,1)} %collective-permute-done.13.refs_1_), channel_id=1, source_target_pairs={{0,15},{1,0},{2,1},{3,2},{4,3},{5,4},{6,5},{7,6},{8,7},{9,8},{10,9... | collective-permute-start | bytes 1179656 | tf_op jit(solution)/shard_map/ppermute | solution.py:197
  132.3 1.8 attend_4.1.refs_3_
  134.1 1.6 attend_2.1.refs_2_
  135.7 1.9 %collective-permute-start.11 = (bf16[384,512]{1,0:T(8,128)(2,1)S(1)}, bf16[384,512]{1,0:T(8,128)(2,1)S(1)}, u32[]{:S(2)}, u32[]{:S(2)}) collective-permute-start(bf16[384,512]{1,0:T(8,128)(2,1)S(1)} %collective-permute-done.8.refs_0_), channel_id=1, source_target_pairs={{0,1},{1,2},{2,3},{3,4},{4,5},{5,6},{6,7},{7,8},{8,9},{9,10},{10,1... | collective-permute-start | bytes 1179656 | tf_op jit(solution)/shard_map/ppermute | solution.py:197
  137.8 2.6 %convolution_convert_fusion.1.query_a.query_b = bf16[256,2048]{1,0:T(8,128)(2,1)} fusion(bf16[256,4096]{1,0:T(8,128)(2,1)} %bitcast.6, s32[256]{0:T(256)S(1)} %copy-done.13), kind=kOutput, calls=%fused_computation.1 | convolution fusion | flops 269025280 | bytes 2098176 | tf_op jit(solution)/shard_map/dot_general | solution.py:180
  140.4 1.8 attend_6.1.refs_4_
  142.2 1.6 attend_8.1.refs_5_
  143.8 1.5 place_held.1.prev_ref
  145.3 1.3 collective-permute-done.11.refs_0_
  146.7 2.4 %attend_guests.1 = (bf16[16,2048]{1,0:T(8,128)(2,1)}, bf16[16,2048]{1,0:T(8,128)(2,1)}, bf16[16,2048]{1,0:T(8,128)(2,1)}) custom-call(bf16[384,512]{1,0:T(8,128)(2,1)S(1)} %collective-permute-done.11.refs_0_, bf16[384,512]{1,0:T(8,128)(2,1)S(1)} %collective-permute-done.14.refs_1_, bf16[16,2176]{1,0:T(8,128)(2,1)} %collective-permute-done.4.refs_2_, ...), custom_call_target="tpu_custom_call" | custom-call | flops 301989888 | bytes 1048576 | tf_op jit(solution)/shard_map/attend_guests/pallas_call | solution.py:114
  149.1 1.9 %collective-permute-start.15 = (bf16[16,2048]{1,0:T(8,128)(2,1)}, bf16[16,2048]{1,0:T(8,128)(2,1)S(1)}, u32[]{:S(2)}, u32[]{:S(2)}) collective-permute-start(bf16[16,2048]{1,0:T(8,128)(2,1)} %get-tuple-element.52), channel_id=1, source_target_pairs={{0,2},{1,3},{2,4},{3,5},{4,6},{5,7},{6,8},{7,9},{8,10},{9,11},{10,... | collective-permute-start | bytes 196616 | tf_op jit(solution)/shard_map/ppermute | solution.py:197
  151.0 2.5 %collective-permute-start.16 = (bf16[16,2048]{1,0:T(8,128)(2,1)}, bf16[16,2048]{1,0:T(8,128)(2,1)S(1)}, u32[]{:S(2)}, u32[]{:S(2)}) collective-permute-start(bf16[16,2048]{1,0:T(8,128)(2,1)} %get-tuple-element.53), channel_id=1, source_target_pairs={{0,1},{1,2},{2,3},{3,4},{4,5},{5,6},{6,7},{7,8},{8,9},{9,10},{10,1... | collective-permute-start | bytes 196616 | tf_op jit(solution)/shard_map/ppermute | solution.py:197
  153.5 4.5 %collective-permute-start.17 = (bf16[16,2048]{1,0:T(8,128)(2,1)}, bf16[16,2048]{1,0:T(8,128)(2,1)S(1)}, u32[]{:S(2)}, u32[]{:S(2)}) collective-permute-start(bf16[16,2048]{1,0:T(8,128)(2,1)} %get-tuple-element.54), channel_id=1, source_target_pairs={{0,15},{1,0},{2,1},{3,2},{4,3},{5,4},{6,5},{7,6},{8,7},{9,8},{10,9... | collective-permute-start | bytes 196616 | tf_op jit(solution)/shard_map/ppermute | solution.py:197
  158.0 0.7 attend_10.1.refs_1_
  158.7 2.8 %copy-done.1 = bf16[6144,512]{1,0:T(8,128)(2,1)S(1)} copy-done((bf16[6144,512]{1,0:T(8,128)(2,1)S(1)}, bf16[6144,512]{1,0:T(8,128)(2,1)}, u32[]{:S(2)}) %copy-start.1) | copy-done | bytes 6291480
  161.5 1.2 copy-done.2
  162.7 6.6 %attend_gathered.1.refs_0_ = bf16[256,4096]{1,0:T(8,128)(2,1)} custom-call(s32[16]{0:T(128)S(1)} %compare_select_fusion.3.place_ref, s32[16]{0:T(128)S(1)} %bitcast.20, bf16[256,4096]{1,0:T(8,128)(2,1)} %place_held.1.prev_ref, s32[16,128]{1,0:T(8,128)S(1)} %tile.28.limits_ref, bf16[256,2048]{1,0:T(8,128)(2,1)S(1)} %copy-done.2, ...), custom_call_target="tpu_custom_call", output_to_operand_aliasing={{}: (2, {})} | custom-call | flops 805306368 | bytes 8388608 | tf_op jit(solution)/shard_map/attend_gathered/pallas_call | solution.py:150
  169.3 1.3 place_last.1
  (72 shorter events, 5.6 us)
Async XLA Ops:
  6.5 15.6 %copy-start = (bf16[1,1,256,4096]{3,2,1,0:T(8,128)(2,1)S(1)}, bf16[1,1,256,4096]{3,2,1,0:T(8,128)(2,1)}, u32[]{:S(2)}) copy-start(bf16[1,1,256,4096]{3,2,1,0:T(8,128)(2,1)} %param.6) | copy-start | bytes 6291460
  6.5 15.6 %copy-start.14 = (s32[1,1,256]{2,1,0:T(1,128)S(1)}, s32[1,1,256]{2,1,0:T(1,128)}, u32[]{:S(2)}) copy-start(s32[1,1,256]{2,1,0:T(1,128)} %param.7) | copy-start | bytes 3076
  6.5 152.2 %all-gather.3.cloned.1.call-start = ((), (), s32[]{:S(2)}) async-start(), calls=%async_computation.1 | async-start | bytes 6684672 | tf_op jit(solution)/shard_map/all_gather | solution.py:205
  8.8 30.4 %collective-permute-start = (bf16[384,512]{1,0:T(8,128)(2,1)S(1)}, bf16[384,512]{1,0:T(8,128)(2,1)S(1)}, u32[]{:S(2)}, u32[]{:S(2)}) collective-permute-start(bf16[384,512]{1,0:T(8,128)(2,1)S(1)} %pad_maximum_fusion.refs_0_), channel_id=1, source_target_pairs={{0,1},{1,2},{2,3},{3,4},{4,5},{5,6},{6,7},{7,8},{8,9},{9,10},{10,1... | collective-permute-start | bytes 1179656 | tf_op jit(solution)/shard_map/ppermute | solution.py:197
  12.6 21.8 %collective-permute-start.7 = (bf16[384,512]{1,0:T(8,128)(2,1)S(1)}, bf16[384,512]{1,0:T(8,128)(2,1)S(1)}, u32[]{:S(2)}, u32[]{:S(2)}) collective-permute-start(bf16[384,512]{1,0:T(8,128)(2,1)S(1)} %pad_maximum_fusion.refs_0_), channel_id=1, source_target_pairs={{0,15},{1,0},{2,1},{3,2},{4,3},{5,4},{6,5},{7,6},{8,7},{9,8},{10,9... | collective-permute-start | bytes 1179656 | tf_op jit(solution)/shard_map/ppermute | solution.py:197
  24.2 8.4 %copy-start.16 = (s32[1,1,256]{2,1,0:T(1,128)S(1)}, s32[1,1,256]{2,1,0:T(1,128)}, u32[]{:S(2)}) copy-start(s32[1,1,256]{2,1,0:T(1,128)} %param.9) | copy-start | bytes 3076
  24.2 9.2 %copy-start.9 = (s32[1,1,16]{2,1,0:T(1,128)S(1)}, s32[1,1,16]{2,1,0:T(1,128)}, u32[]{:S(2)}) copy-start(s32[1,1,16]{2,1,0:T(1,128)} %param.10) | copy-start | bytes 196
  24.2 14.9 %copy-start.15 = (s32[1,1,256]{2,1,0:T(1,128)S(1)}, s32[1,1,256]{2,1,0:T(1,128)}, u32[]{:S(2)}) copy-start(s32[1,1,256]{2,1,0:T(1,128)} %param.8) | copy-start | bytes 3076
  24.2 60.2 %all-to-all-start = ((bf16[32,8,4096]{2,1,0:T(8,128)(2,1)}), bf16[32,8,4096]{2,1,0:T(8,128)(2,1)}, u32[]{:S(2)}, u32[]{:S(2)}) async-start(bf16[32,8,4096]{2,1,0:T(8,128)(2,1)} %bitcast.21), calls=%async_computation | async-start | bytes 4194304 | tf_op jit(solution)/shard_map/all_to_all | solution.py:208
  34.5 21.5 %collective-permute-start.9 = (bf16[384,512]{1,0:T(8,128)(2,1)S(1)}, bf16[384,512]{1,0:T(8,128)(2,1)S(1)}, u32[]{:S(2)}, u32[]{:S(2)}) collective-permute-start(bf16[384,512]{1,0:T(8,128)(2,1)S(1)} %collective-permute-done.7.refs_1_), channel_id=1, source_target_pairs={{0,15},{1,0},{2,1},{3,2},{4,3},{5,4},{6,5},{7,6},{8,7},{9,8},{10,9... | collective-permute-start | bytes 1179656 | tf_op jit(solution)/shard_map/ppermute | solution.py:197
  38.4 0.8 copy-start.5
  39.2 24.1 %collective-permute-start.1 = (bf16[384,512]{1,0:T(8,128)(2,1)S(1)}, bf16[384,512]{1,0:T(8,128)(2,1)}, u32[]{:S(2)}, u32[]{:S(2)}) collective-permute-start(bf16[384,512]{1,0:T(8,128)(2,1)S(1)} %collective-permute-done.refs_0_), channel_id=1, source_target_pairs={{0,1},{1,2},{2,3},{3,4},{4,5},{5,6},{6,7},{7,8},{8,9},{9,10},{10,1... | collective-permute-start | bytes 1179656 | tf_op jit(solution)/shard_map/ppermute | solution.py:197
  41.1 0.7 copy-start.3
  55.9 22.8 %collective-permute-start.10 = (bf16[384,512]{1,0:T(8,128)(2,1)S(1)}, bf16[384,512]{1,0:T(8,128)(2,1)}, u32[]{:S(2)}, u32[]{:S(2)}) collective-permute-start(bf16[384,512]{1,0:T(8,128)(2,1)S(1)} %collective-permute-done.9.refs_1_), channel_id=1, source_target_pairs={{0,15},{1,0},{2,1},{3,2},{4,3},{5,4},{6,5},{7,6},{8,7},{9,8},{10,9... | collective-permute-start | bytes 1179656 | tf_op jit(solution)/shard_map/ppermute | solution.py:197
  61.3 0.8 copy-start.7
  63.3 24.2 %collective-permute-start.2 = (bf16[384,512]{1,0:T(8,128)(2,1)}, bf16[384,512]{1,0:T(8,128)(2,1)}, u32[]{:S(2)}, u32[]{:S(2)}) collective-permute-start(bf16[384,512]{1,0:T(8,128)(2,1)} %collective-permute-done.1.refs_0_), channel_id=1, source_target_pairs={{0,1},{1,2},{2,3},{3,4},{4,5},{5,6},{6,7},{7,8},{8,9},{9,10},{10,1... | collective-permute-start | bytes 1179656 | tf_op jit(solution)/shard_map/ppermute | solution.py:197
  78.7 24.5 %collective-permute-start.12 = (bf16[384,512]{1,0:T(8,128)(2,1)}, bf16[384,512]{1,0:T(8,128)(2,1)}, u32[]{:S(2)}, u32[]{:S(2)}) collective-permute-start(bf16[384,512]{1,0:T(8,128)(2,1)} %collective-permute-done.10.refs_1_), channel_id=1, source_target_pairs={{0,15},{1,0},{2,1},{3,2},{4,3},{5,4},{6,5},{7,6},{8,7},{9,8},{10,9... | collective-permute-start | bytes 1179656 | tf_op jit(solution)/shard_map/ppermute | solution.py:197
  84.4 1.7 copy-start.11
  84.4 2.4 %copy-start.12 = (bf16[16,128]{1,0:T(8,128)(2,1)S(1)}, bf16[16,128]{1,0:T(8,128)(2,1)}, u32[]{:S(2)}) copy-start(bf16[16,128]{1,0:T(8,128)(2,1)} %fusion.14) | copy-start | bytes 12292
  87.5 26.8 %collective-permute-start.3 = (bf16[384,512]{1,0:T(8,128)(2,1)}, bf16[384,512]{1,0:T(8,128)(2,1)}, u32[]{:S(2)}, u32[]{:S(2)}) collective-permute-start(bf16[384,512]{1,0:T(8,128)(2,1)} %collective-permute-done.2.refs_0_), channel_id=1, source_target_pairs={{0,1},{1,2},{2,3},{3,4},{4,5},{5,6},{6,7},{7,8},{8,9},{9,10},{10,1... | collective-permute-start | bytes 1179656 | tf_op jit(solution)/shard_map/ppermute | solution.py:197
  89.4 24.9 %collective-permute-start.4 = (bf16[16,2176]{1,0:T(8,128)(2,1)}, bf16[16,2176]{1,0:T(8,128)(2,1)}, u32[]{:S(2)}, u32[]{:S(2)}) collective-permute-start(bf16[16,2176]{1,0:T(8,128)(2,1)} %get-tuple-element.32), channel_id=1, source_target_pairs={{0,14},{1,15},{2,0},{3,1},{4,2},{5,3},{6,4},{7,5},{8,6},{9,7},{10,... | collective-permute-start | bytes 208904 | tf_op jit(solution)/shard_map/ppermute | solution.py:197
  92.8 21.5 %collective-permute-start.5 = (bf16[16,2176]{1,0:T(8,128)(2,1)}, bf16[16,2176]{1,0:T(8,128)(2,1)}, u32[]{:S(2)}, u32[]{:S(2)}) collective-permute-start(bf16[16,2176]{1,0:T(8,128)(2,1)} %get-tuple-element.33), channel_id=1, source_target_pairs={{0,15},{1,0},{2,1},{3,2},{4,3},{5,4},{6,5},{7,6},{8,7},{9,8},{10,9... | collective-permute-start | bytes 208904 | tf_op jit(solution)/shard_map/ppermute | solution.py:197
  96.5 17.8 %collective-permute-start.6 = (bf16[16,2176]{1,0:T(8,128)(2,1)}, bf16[16,2176]{1,0:T(8,128)(2,1)}, u32[]{:S(2)}, u32[]{:S(2)}) collective-permute-start(bf16[16,2176]{1,0:T(8,128)(2,1)} %pad_maximum_fusion.4), channel_id=1, source_target_pairs={{0,1},{1,2},{2,3},{3,4},{4,5},{5,6},{6,7},{7,8},{8,9},{9,10},{10,1... | collective-permute-start | bytes 208904 | tf_op jit(solution)/shard_map/ppermute | solution.py:197
  103.2 23.5 %collective-permute-start.13 = (bf16[384,512]{1,0:T(8,128)(2,1)}, bf16[384,512]{1,0:T(8,128)(2,1)}, u32[]{:S(2)}, u32[]{:S(2)}) collective-permute-start(bf16[384,512]{1,0:T(8,128)(2,1)} %collective-permute-done.12.refs_1_), channel_id=1, source_target_pairs={{0,15},{1,0},{2,1},{3,2},{4,3},{5,4},{6,5},{7,6},{8,7},{9,8},{10,9... | collective-permute-start | bytes 1179656 | tf_op jit(solution)/shard_map/ppermute | solution.py:197
  111.6 1.0 copy-start.4
  112.6 1.0 copy-start.6
  113.6 20.5 %copy-start.8 = (bf16[384,512]{1,0:T(8,128)(2,1)S(1)}, bf16[384,512]{1,0:T(8,128)(2,1)}, u32[]{:S(2)}) copy-start(bf16[384,512]{1,0:T(8,128)(2,1)} %copy-done.7) | copy-start | bytes 1179652
  114.2 23.5 %copy-start.13 = (s32[256]{0:T(256)S(1)}, s32[256]{0:T(256)}, u32[]{:S(2)}) copy-start(s32[256]{0:T(256)} %fusion.15) | copy-start | bytes 3076
  114.3 21.4 %collective-permute-start.8 = (bf16[384,512]{1,0:T(8,128)(2,1)}, bf16[384,512]{1,0:T(8,128)(2,1)S(1)}, u32[]{:S(2)}, u32[]{:S(2)}) collective-permute-start(bf16[384,512]{1,0:T(8,128)(2,1)} %collective-permute-done.3.refs_0_), channel_id=1, source_target_pairs={{0,1},{1,2},{2,3},{3,4},{4,5},{5,6},{6,7},{7,8},{8,9},{9,10},{10,1... | collective-permute-start | bytes 1179656 | tf_op jit(solution)/shard_map/ppermute | solution.py:197
  126.7 20.0 %collective-permute-start.14 = (bf16[384,512]{1,0:T(8,128)(2,1)}, bf16[384,512]{1,0:T(8,128)(2,1)S(1)}, u32[]{:S(2)}, u32[]{:S(2)}) collective-permute-start(bf16[384,512]{1,0:T(8,128)(2,1)} %collective-permute-done.13.refs_1_), channel_id=1, source_target_pairs={{0,15},{1,0},{2,1},{3,2},{4,3},{5,4},{6,5},{7,6},{8,7},{9,8},{10,9... | collective-permute-start | bytes 1179656 | tf_op jit(solution)/shard_map/ppermute | solution.py:197
  135.7 10.9 %collective-permute-start.11 = (bf16[384,512]{1,0:T(8,128)(2,1)S(1)}, bf16[384,512]{1,0:T(8,128)(2,1)S(1)}, u32[]{:S(2)}, u32[]{:S(2)}) collective-permute-start(bf16[384,512]{1,0:T(8,128)(2,1)S(1)} %collective-permute-done.8.refs_0_), channel_id=1, source_target_pairs={{0,1},{1,2},{2,3},{3,4},{4,5},{5,6},{6,7},{7,8},{8,9},{9,10},{10,1... | collective-permute-start | bytes 1179656 | tf_op jit(solution)/shard_map/ppermute | solution.py:197
  145.3 13.4 %copy-start.10 = (s32[1,1,16]{2,1,0:T(1,128)S(1)}, s32[1,1,16]{2,1,0:T(1,128)}, u32[]{:S(2)}) copy-start(s32[1,1,16]{2,1,0:T(1,128)} %param.10) | copy-start | bytes 196
  149.1 20.2 %collective-permute-start.15 = (bf16[16,2048]{1,0:T(8,128)(2,1)}, bf16[16,2048]{1,0:T(8,128)(2,1)S(1)}, u32[]{:S(2)}, u32[]{:S(2)}) collective-permute-start(bf16[16,2048]{1,0:T(8,128)(2,1)} %get-tuple-element.52), channel_id=1, source_target_pairs={{0,2},{1,3},{2,4},{3,5},{4,6},{5,7},{6,8},{7,9},{8,10},{9,11},{10,... | collective-permute-start | bytes 196616 | tf_op jit(solution)/shard_map/ppermute | solution.py:197
  151.0 18.3 %collective-permute-start.16 = (bf16[16,2048]{1,0:T(8,128)(2,1)}, bf16[16,2048]{1,0:T(8,128)(2,1)S(1)}, u32[]{:S(2)}, u32[]{:S(2)}) collective-permute-start(bf16[16,2048]{1,0:T(8,128)(2,1)} %get-tuple-element.53), channel_id=1, source_target_pairs={{0,1},{1,2},{2,3},{3,4},{4,5},{5,6},{6,7},{7,8},{8,9},{9,10},{10,1... | collective-permute-start | bytes 196616 | tf_op jit(solution)/shard_map/ppermute | solution.py:197
  153.5 15.8 %collective-permute-start.17 = (bf16[16,2048]{1,0:T(8,128)(2,1)}, bf16[16,2048]{1,0:T(8,128)(2,1)S(1)}, u32[]{:S(2)}, u32[]{:S(2)}) collective-permute-start(bf16[16,2048]{1,0:T(8,128)(2,1)} %get-tuple-element.54), channel_id=1, source_target_pairs={{0,15},{1,0},{2,1},{3,2},{4,3},{5,4},{6,5},{7,6},{8,7},{9,8},{10,9... | collective-permute-start | bytes 196616 | tf_op jit(solution)/shard_map/ppermute | solution.py:197
  158.7 2.8 %copy-start.1 = (bf16[6144,512]{1,0:T(8,128)(2,1)S(1)}, bf16[6144,512]{1,0:T(8,128)(2,1)}, u32[]{:S(2)}) copy-start(bf16[6144,512]{1,0:T(8,128)(2,1)} %all-gather.3.cloned.1.call-done) | copy-start | bytes 18874372
  161.5 1.2 copy-start.2
Sparse Core Ops, SparseCore 0:
  9.4 132.7 all-gather.2

commit v6 on v4

--- a/solution.py
+++ b/solution.py
@@ -15,14 +15,26 @@
 SCALE = math.log2(math.e) / math.sqrt(HD)
 
 
-def score_group(query_ref, row, rows, block, limits, out_ref, out_row):
-    cache_len = block.shape[0]
+HALF = KVH // 2
+
+
+def head_of(parts, k):
+    kind, refs = parts
+    at, half = k % HALF, k // HALF
+    if kind == "cached":
+        return refs[0], k * HD, (KVH + k) * HD
+    if kind == "halves":
+        return refs[half], at * HD, (HALF + at) * HD
+    return refs[0], (2 * half * HALF + at) * HD, ((2 * half + 1) * HALF + at) * HD
+
+
+def score_group(query_of, rows, parts, cache_len, limits, out_ref, out_row):
     visible = lax.broadcasted_iota(jnp.int32, (cache_len, GROUPS * rows), 0) <= limits
     for k in range(KVH):
-        heads = [slice((k * GROUPS + g) * HD, (k * GROUPS + g + 1) * HD) for g in range(GROUPS)]
-        query = jnp.concatenate([query_ref[row : row + rows, h] for h in heads], axis=0)
+        block, key_at, value_at = head_of(parts, k)
+        query = jnp.concatenate([query_of(k, g) for g in range(GROUPS)], axis=0)
         scores = lax.dot_general(
-            block[:, k * HD : (k + 1) * HD],
+            block[:cache_len, key_at : key_at + HD],
             query,
             (((1,), (1,)), ((), ())),
             preferred_element_type=jnp.float32,
@@ -33,29 +45,44 @@
         row_total = jnp.sum(exponent, axis=0, keepdims=True)
         mixed = lax.dot_general(
             exponent.astype(jnp.bfloat16),
-            block[:, (KVH + k) * HD : (KVH + k + 1) * HD],
+            block[:cache_len, value_at : value_at + HD],
             (((0,), (0,)), ((), ())),
             preferred_element_type=jnp.float32,
         )
         mixed = (mixed / row_total.reshape(GROUPS * rows, 1)).astype(jnp.bfloat16)
         for g in range(GROUPS):
-            out_ref[out_row : out_row + rows, heads[g]] = mixed[g * rows : (g + 1) * rows]
-
-
-def step_kernel(spots, rows, limits_ref, query_ref, *refs):
-    blocks, out_ref = refs[:-1], refs[-1]
+            column = (k * GROUPS + g) * HD
+            out_ref[out_row : out_row + rows, column : column + HD] = mixed[g * rows : (g + 1) * rows]
+
+
+def take(kinds, refs):
+    refs, blocks = list(refs), []
+    for kind in kinds:
+        count = 2 if kind == "halves" else 1
+        blocks.append((kind, refs[:count]))
+        del refs[:count]
+    return blocks
+
+
+def step_kernel(spots, kinds, rows, cache_len, limits_ref, query_ref, *refs):
+    blocks, out_ref = take(kinds, refs[:-1]), refs[-1]
     for i, spot in enumerate(spots):
-        score_group(query_ref, spot * rows, rows, blocks[i], limits_ref[spot : spot + 1, :], out_ref, i * rows)
-
-
-def guest_kernel(sources, rows, *refs):
-    count = len(sources)
-    blocks, guests, outs = refs[: -2 * count], refs[-2 * count : -count], refs[-count:]
-    for source, guest_ref, out_ref in zip(sources, guests, outs):
-        width = out_ref.shape[1]
-        parts = guest_ref[:, width:].astype(jnp.float32)
-        limits = (parts[0:1] * 16.0 + parts[1:2]).astype(jnp.int32)
-        score_group(guest_ref, 0, rows, blocks[source], limits, out_ref, 0)
+
+        def query_of(k, g, row=spot * rows):
+            return query_ref[row : row + rows, (k * GROUPS + g) * HD : (k * GROUPS + g + 1) * HD]
+
+        score_group(query_of, rows, blocks[i], cache_len, limits_ref[spot : spot + 1, :], out_ref, i * rows)
+
+
+def guest_kernel(count, rows, cache_len, block, *refs):
+    for guest_ref, out_ref in zip(refs[:count], refs[count:]):
+        places = guest_ref[KVH * rows : (KVH + 1) * rows, :HD].astype(jnp.float32)
+        limits = (places[0:1] * 16.0 + places[1:2]).astype(jnp.int32)
+
+        def query_of(k, g, guest_ref=guest_ref):
+            return guest_ref[k * rows : (k + 1) * rows, g * HD : (g + 1) * HD]
+
+        score_group(query_of, rows, ("joined", [block]), cache_len, limits, out_ref, 0)
 
 
 def place_kernel(ref_spots, rows, again, where_ref, *refs):
@@ -75,6 +102,23 @@
         copy.wait()
 
 
+def join_kernel(spots, rows, limits_ref, query_ref, first_ref, second_ref, out_ref):
+    cache_len, width = first_ref.shape
+    out_ref[:cache_len, :width] = first_ref[...]
+    out_ref[:cache_len, width:] = second_ref[...]
+    for i, spot in enumerate(spots):
+        base = cache_len + i * (KVH + 1) * rows
+        for k in range(KVH):
+            heads = query_ref[spot * rows : (spot + 1) * rows, 2 * k * width : 2 * (k + 1) * width]
+            out_ref[base + k * rows : base + (k + 1) * rows, :] = heads
+        places = jnp.broadcast_to(limits_ref[spot : spot + 1, :], (rows, limits_ref.shape[1]))
+        row = lax.broadcasted_iota(jnp.int32, places.shape, 0)
+        places = jnp.where(row == 0, places >> 4, jnp.where(row == 1, places & 15, 0))
+        below = base + KVH * rows
+        out_ref[below : below + rows, :] = jnp.zeros((rows, 2 * width), out_ref.dtype)
+        out_ref[below : below + rows, : places.shape[1]] = places.astype(jnp.float32).astype(out_ref.dtype)
+
+
 def cost(spots, rows, cache_len):
     work = len(spots) * rows * QH * cache_len
     return pl.CostEstimate(flops=4 * work * HD, bytes_accessed=2**20, transcendentals=work)
@@ -86,29 +130,45 @@
 PARAMS = pltpu.CompilerParams(vmem_limit_bytes=10 * 2**20)
 
 
-def attend_step(limits, packed, spots, blocks, rows):
+def join(limits, packed, halves, spots, rows):
+    cache_len, width = halves[0].shape
+    shape = (cache_len + len(spots) * (KVH + 1) * rows, 2 * width)
     return pl.pallas_call(
-        functools.partial(step_kernel, spots, rows),
-        out_shape=jax.ShapeDtypeStruct((len(spots) * rows, packed.shape[1]), packed.dtype),
-        in_specs=[VMEM] * (2 + len(spots)),
+        functools.partial(join_kernel, spots, rows),
+        out_shape=jax.ShapeDtypeStruct(shape, packed.dtype),
+        in_specs=[VMEM] * 4,
         out_specs=VMEM,
         compiler_params=PARAMS,
-        cost_estimate=cost(spots, rows, blocks[0].shape[0]),
+        cost_estimate=pl.CostEstimate(flops=0, bytes_accessed=4 * shape[0] * shape[1], transcendentals=0),
+        name="join",
+    )(limits, packed, *halves)
+
+
+def attend_step(limits, packed, spots, blocks, rows, cache_len):
+    kinds = tuple(kind for kind, _ in blocks)
+    arrays = [a for _, arrays in blocks for a in arrays]
+    return pl.pallas_call(
+        functools.partial(step_kernel, spots, kinds, rows, cache_len),
+        out_shape=jax.ShapeDtypeStruct((len(spots) * rows, packed.shape[1]), packed.dtype),
+        in_specs=[VMEM] * (2 + len(arrays)),
+        out_specs=VMEM,
+        compiler_params=PARAMS,
+        cost_estimate=cost(spots, rows, cache_len),
         name="attend_%d" % spots[0],
-    )(limits, packed, *blocks)
-
-
-def attend_guests(guests, sources, blocks, rows):
-    width = guests[0].shape[1] - HD
+    )(limits, packed, *arrays)
+
+
+def attend_guests(guests, block, rows, cache_len):
+    width = QH * HD
     return pl.pallas_call(
-        functools.partial(guest_kernel, sources, rows),
+        functools.partial(guest_kernel, len(guests), rows, cache_len),
         out_shape=[jax.ShapeDtypeStruct((rows, width), g.dtype) for g in guests],
-        in_specs=[VMEM] * (len(blocks) + len(guests)),
+        in_specs=[VMEM] * (1 + len(guests)),
         out_specs=[VMEM] * len(guests),
         compiler_params=PARAMS,
-        cost_estimate=cost(guests, rows, blocks[0].shape[0]),
+        cost_estimate=cost(guests, rows, cache_len),
         name="attend_guests",
-    )(*blocks, *guests)
+    )(block, *guests)
 
 
 def place_rows(where, held, held_spots, rows, out, shape):
@@ -174,50 +234,66 @@
     packed = move_rows(target, arrived)
 
     far = steps - 2
+    cache_len = kv.shape[0]
     mine, behind_far, ahead_far, opposite = (ring - 1,), (2 * far,), (2 * far + 1,), (2 * far + 2,)
-
-    def payload(spot):
-        rows = packed[spot * group_rows : (spot + 1) * group_rows]
-        parts = jnp.stack([limits[spot] // 16, limits[spot] % 16]).astype(rows.dtype)
-        beside = jnp.pad(parts, ((0, group_rows - 2), (0, 0)))
-        return jnp.concatenate([rows, beside], axis=1)
-
-    up, down = kv, kv
+    guest_rows = (KVH + 1) * group_rows
+
+    span, half = KVH * HD, HALF * HD
+
+    def halves_of(block):
+        return tuple(
+            jnp.concatenate([block[:, lo : lo + half], block[:, span + lo : span + lo + half]], axis=1)
+            for lo in (0, half)
+        )
+
     held, held_spots = [], []
-    blocks_of = []
 
     def score(spot_list, blocks):
-        held.append(attend_step(limits, packed, spot_list, blocks, group_rows))
+        held.append(attend_step(limits, packed, spot_list, blocks, group_rows, cache_len))
         held_spots.append(spot_list)
 
-    for step in range(far):
+    up, down = shifted(kv, 1), shifted(kv, -1)
+    blocks_of = [[("cached", [up]), ("cached", [down])]]
+    up, down = halves_of(up), halves_of(down)
+    for step in (1, 2):
         if step == 2:
-            up, ordered = tie(up, ordered)
-        if step == 3:
-            guests = [payload(s[0]) for s in (opposite, behind_far, ahead_far)]
-            up, guests = tie(up, guests)
-            guests = [shifted(g, by) for g, by in zip(guests, (-2, -1, 1))]
-        if step == 4:
-            score(mine, (kv,))
-            score((0, 1), blocks_of[0])
-            up, (guests, held) = tie(up, (guests, held))
-        if step == 5:
-            score((2, 3), blocks_of[1])
-            score((4, 5), blocks_of[2])
-            up, held = tie(up, held)
-        up = shifted(up, 1)
-        down = shifted(down, -1)
-        blocks_of.append((up, down))
+            first, ordered = tie(up[0], ordered)
+            up = (first, up[1])
+        up = tuple(shifted(x, 1) for x in up)
+        down = tuple(shifted(x, -1) for x in down)
+        blocks_of.append([("halves", list(up)), ("halves", list(down))])
+    up = join(limits, packed, up, ahead_far, group_rows)
+    down = join(limits, packed, down, opposite + behind_far, group_rows)
+    up, down = shifted(up, 1), shifted(down, -1)
+    blocks_of.append([("joined", [up]), ("joined", [down])])
+    ahead_guest, behind_guest = up[cache_len:], down[cache_len + guest_rows :]
+    score(mine, [("cached", [kv])])
+    score((0, 1), blocks_of[0])
+    score((2, 3), blocks_of[1])
+    up, held = tie(up[:cache_len], held)
+    up, down = shifted(up, 1), shifted(down[: cache_len + guest_rows], -1)
+    blocks_of.append([("joined", [up]), ("joined", [down])])
+    opposite_guest = down[cache_len:]
+    score((4, 5), blocks_of[2])
+    up, held = tie(up, held)
+    up, down = shifted(up, 1), shifted(down[:cache_len], -1)
     score((6, 7), blocks_of[3])
     score((8, 9), blocks_of[4])
     out = place_rows(where, held, held_spots, group_rows, None, packed.shape)
     up, out = tie(up, out)
-    back = attend_guests(guests, (0, 0, 1), (up, down), group_rows)
-    back = [shifted(g, by) for g, by in zip(back, (2, 1, -1))]
+    opposite_out, behind_out = attend_guests([opposite_guest, behind_guest], up, group_rows, cache_len)
+    opposite_out, behind_out = shifted(opposite_out, 2), shifted(behind_out, 1)
+    (ahead_out,) = attend_guests([ahead_guest], down, group_rows, cache_len)
+    ahead_out = shifted(ahead_out, -1)
     held, held_spots = [], []
-    score((2 * far - 2, 2 * far - 1), (up, down))
+    score((2 * far - 2, 2 * far - 1), [("joined", [up]), ("joined", [down])])
     out = place_rows(
-        where, [*held, *back], [*held_spots, opposite, behind_far, ahead_far], group_rows, out, packed.shape
+        where,
+        [*held, opposite_out, behind_out, ahead_out],
+        [*held_spots, opposite, behind_far, ahead_far],
+        group_rows,
+        out,
+        packed.shape,
     )
     return out[None, None]
 

time: 157 us -> 158 us (level)
  the two profiles are of different devices: /device:TPU:126 before, /device:TPU:4 now
where the time goes in v6:
time: 158 us; the launch traced here: 157 us
  starting transfers between devices  81 us (51%)
  waiting for transfers between devices  47.5 us (30%)
  Pallas kernels  17.3 us (11%)
  matrix products  5.03 us (3%)
  other arithmetic  3.46 us (2%)
  local copies, waits for them, and re-layouts  2.3 us (1%)
    ppermute x19, starting transfers between devices, shifted(): lax.ppermute(x, 'prompt', [(i, (i + by) % ring) for i in range(ring)])  73.2 us
    ppermute x19, waiting for transfers between devices, shifted(): lax.ppermute(x, 'prompt', [(i, (i + by) % ring) for i in range(ring)])  47.5 us
    pallas_call x7, Pallas kernels, attend_step(): pl.pallas_call(functools.partial(step_kernel, spots, kinds, rows, cache_l...  10.3 us
    all_to_all x1, starting transfers between devices, body(): lax.all_to_all(ordered.reshape(dp_count, row_count // dp_count, width), '...  7.77 us
    dot_general x2, matrix products, move_rows(): jnp.dot(pick, rows, preferred_element_type=jnp.float32).astype(rows.dtype)  5.03 us
  transfers between devices with their start and end apart: 20, of which 7 were waited for; matrix products, arithmetic and copies ran while one was open for 7% of the time, Pallas kernels for 10%

profile of v6, /device:TPU:4, one launch (start us, length us, event | category | flops | bytes accessed | tf_op | source)
XLA Modules:
  0.0 157.1 jit_solution(4714338781142060865)
XLA Ops:
  0.0 11.5 %collective-permute-start.6 = (bf16[384,1024]{1,0:T(8,128)(2,1)}, bf16[384,1024]{1,0:T(8,128)(2,1)S(1)}, u32[]{:S(2)}, u32[]{:S(2)}) collective-permute-start(bf16[384,1024]{1,0:T(8,128)(2,1)} %bitcast.15), channel_id=1, source_target_pairs={{0,15},{1,0},{2,1},{3,2},{4,3},{5,4},{6,5},{7,6},{8,7},{9,8},{10,9... | collective-permute-start | bytes 2359304 | tf_op jit(solution)/shard_map/ppermute | solution.py:209
  11.5 1.9 %collective-permute-start = (bf16[384,1024]{1,0:T(8,128)(2,1)}, bf16[384,1024]{1,0:T(8,128)(2,1)}, u32[]{:S(2)}, u32[]{:S(2)}) collective-permute-start(bf16[384,1024]{1,0:T(8,128)(2,1)} %bitcast.16), channel_id=1, source_target_pairs={{0,1},{1,2},{2,3},{3,4},{4,5},{5,6},{6,7},{7,8},{8,9},{9,10},{10,1... | collective-permute-start | bytes 2359304 | tf_op jit(solution)/shard_map/ppermute | solution.py:209
  13.5 2.7 %convolution_convert_fusion.1 = bf16[256,4096]{1,0:T(8,128)(2,1)} fusion(bf16[1,1,256,4096]{3,2,1,0:T(8,128)(2,1)S(1)} %copy-done, s32[256]{0:T(256)} %bitcast.19), kind=kOutput, calls=%fused_computation.1 | convolution fusion | flops 537985024 | bytes 4195328 | tf_op jit(solution)/shard_map/dot_general | solution.py:192
  16.2 7.8 %all-to-all-start = ((bf16[32,8,4096]{2,1,0:T(8,128)(2,1)}), bf16[32,8,4096]{2,1,0:T(8,128)(2,1)}, u32[]{:S(2)}, u32[]{:S(2)}) async-start(bf16[32,8,4096]{2,1,0:T(8,128)(2,1)} %bitcast.18), calls=%async_computation | async-start | bytes 4194304 | tf_op jit(solution)/shard_map/all_to_all | solution.py:214
  24.1 4.6 %collective-permute-done.6.refs_1_ = bf16[384,1024]{1,0:T(8,128)(2,1)S(1)} collective-permute-done((bf16[384,1024]{1,0:T(8,128)(2,1)}, bf16[384,1024]{1,0:T(8,128)(2,1)S(1)}, u32[]{:S(2)}, u32[]{:S(2)}) %collective-permute-start.6) | collective-permute-done | bytes 786464 | tf_op jit(solution)/shard_map/ppermute | solution.py:209
  28.7 5.5 %collective-permute-start.7 = (bf16[384,512]{1,0:T(8,128)(2,1)S(1)}, bf16[384,512]{1,0:T(8,128)(2,1)}, u32[]{:S(2)}, u32[]{:S(2)}) collective-permute-start(bf16[384,512]{1,0:T(8,128)(2,1)S(1)} %pad_maximum_fusion.2), channel_id=1, source_target_pairs={{0,15},{1,0},{2,1},{3,2},{4,3},{5,4},{6,5},{7,6},{8,7},{9,8},{10,9... | collective-permute-start | bytes 1179656 | tf_op jit(solution)/shard_map/ppermute | solution.py:209
  34.2 0.8 pad_maximum_fusion.3
  35.0 1.9 %collective-permute-start.8 = (bf16[384,512]{1,0:T(8,128)(2,1)}, bf16[384,512]{1,0:T(8,128)(2,1)}, u32[]{:S(2)}, u32[]{:S(2)}) collective-permute-start(bf16[384,512]{1,0:T(8,128)(2,1)} %pad_maximum_fusion.3), channel_id=1, source_target_pairs={{0,15},{1,0},{2,1},{3,2},{4,3},{5,4},{6,5},{7,6},{8,7},{9,8},{10,9... | collective-permute-start | bytes 1179656 | tf_op jit(solution)/shard_map/ppermute | solution.py:209
  37.0 1.3 fusion.7
  38.2 0.8 pad_maximum_fusion
  39.1 3.9 %collective-permute-start.1 = (bf16[384,512]{1,0:T(8,128)(2,1)}, bf16[384,512]{1,0:T(8,128)(2,1)}, u32[]{:S(2)}, u32[]{:S(2)}) collective-permute-start(bf16[384,512]{1,0:T(8,128)(2,1)} %pad_maximum_fusion), channel_id=1, source_target_pairs={{0,1},{1,2},{2,3},{3,4},{4,5},{5,6},{6,7},{7,8},{8,9},{9,10},{10,1... | collective-permute-start | bytes 1179656 | tf_op jit(solution)/shard_map/ppermute | solution.py:209
  43.0 0.8 pad_maximum_fusion.1
  43.8 1.9 %collective-permute-start.3 = (bf16[384,512]{1,0:T(8,128)(2,1)}, bf16[384,512]{1,0:T(8,128)(2,1)}, u32[]{:S(2)}, u32[]{:S(2)}) collective-permute-start(bf16[384,512]{1,0:T(8,128)(2,1)} %pad_maximum_fusion.1), channel_id=1, source_target_pairs={{0,1},{1,2},{2,3},{3,4},{4,5},{5,6},{6,7},{7,8},{8,9},{9,10},{10,1... | collective-permute-start | bytes 1179656 | tf_op jit(solution)/shard_map/ppermute | solution.py:209
  45.8 0.6 broadcast.191
  46.3 0.7 reduce.3
  47.1 5.1 %collective-permute-start.10 = (bf16[384,512]{1,0:T(8,128)(2,1)}, bf16[384,512]{1,0:T(8,128)(2,1)}, u32[]{:S(2)}, u32[]{:S(2)}) collective-permute-start(bf16[384,512]{1,0:T(8,128)(2,1)} %collective-permute-done.7.refs_2_), channel_id=1, source_target_pairs={{0,15},{1,0},{2,1},{3,2},{4,3},{5,4},{6,5},{7,6},{8,7},{9,8},{10,9... | collective-permute-start | bytes 1179656 | tf_op jit(solution)/shard_map/ppermute | solution.py:209
  52.3 3.7 %collective-permute-start.11 = (bf16[384,512]{1,0:T(8,128)(2,1)}, bf16[384,512]{1,0:T(8,128)(2,1)}, u32[]{:S(2)}, u32[]{:S(2)}) collective-permute-start(bf16[384,512]{1,0:T(8,128)(2,1)} %collective-permute-done.8.refs_3_), channel_id=1, source_target_pairs={{0,15},{1,0},{2,1},{3,2},{4,3},{5,4},{6,5},{7,6},{8,7},{9,8},{10,9... | collective-permute-start | bytes 1179656 | tf_op jit(solution)/shard_map/ppermute | solution.py:209
  56.2 2.2 %collective-permute-start.2 = (bf16[384,512]{1,0:T(8,128)(2,1)}, bf16[384,512]{1,0:T(8,128)(2,1)S(1)}, u32[]{:S(2)}, u32[]{:S(2)}) collective-permute-start(bf16[384,512]{1,0:T(8,128)(2,1)} %collective-permute-done.1.refs_0_), channel_id=1, source_target_pairs={{0,1},{1,2},{2,3},{3,4},{4,5},{5,6},{6,7},{7,8},{8,9},{9,10},{10,1... | collective-permute-start | bytes 1179656 | tf_op jit(solution)/shard_map/ppermute | solution.py:209
  58.4 2.9 %collective-permute-done.3.refs_1_ = bf16[384,512]{1,0:T(8,128)(2,1)} collective-permute-done((bf16[384,512]{1,0:T(8,128)(2,1)}, bf16[384,512]{1,0:T(8,128)(2,1)}, u32[]{:S(2)}, u32[]{:S(2)}) %collective-permute-start.3) | collective-permute-done | bytes 393248 | tf_op jit(solution)/shard_map/ppermute | solution.py:209
  61.3 3.9 %collective-permute-start.4 = (bf16[384,512]{1,0:T(8,128)(2,1)}, bf16[384,512]{1,0:T(8,128)(2,1)}, u32[]{:S(2)}, u32[]{:S(2)}) collective-permute-start(bf16[384,512]{1,0:T(8,128)(2,1)} %collective-permute-done.3.refs_1_), channel_id=1, source_target_pairs={{0,1},{1,2},{2,3},{3,4},{4,5},{5,6},{6,7},{7,8},{8,9},{9,10},{10,1... | collective-permute-start | bytes 1179656 | tf_op jit(solution)/shard_map/ppermute | solution.py:209
  65.2 2.3 %convolution_convert_fusion.query_ref = bf16[256,4096]{1,0:T(8,128)(2,1)S(1)} fusion(bf16[32,8,4096]{2,1,0:T(8,128)(2,1)} %all-to-all-done, s32[256]{0:T(256)S(1)} %fusion.4), kind=kOutput, calls=%fused_computation | convolution fusion | flops 537985024 | bytes 4195328 | tf_op jit(solution)/shard_map/dot_general | solution.py:192
  67.5 1.2 join.3
  68.7 5.7 %collective-permute-start.13 = (bf16[544,1024]{1,0:T(8,128)(2,1)S(1)}, bf16[544,1024]{1,0:T(8,128)(2,1)S(1)}, u32[]{:S(2)}, u32[]{:S(2)}) collective-permute-start(bf16[544,1024]{1,0:T(8,128)(2,1)S(1)} %join.3), channel_id=1, source_target_pairs={{0,15},{1,0},{2,1},{3,2},{4,3},{5,4},{6,5},{7,6},{8,7},{9,8},{10,9... | collective-permute-start | bytes 3342344 | tf_op jit(solution)/shard_map/ppermute | solution.py:209
  74.4 3.1 %collective-permute-done.4.second_ref.refs_1_ = bf16[384,512]{1,0:T(8,128)(2,1)} collective-permute-done((bf16[384,512]{1,0:T(8,128)(2,1)}, bf16[384,512]{1,0:T(8,128)(2,1)}, u32[]{:S(2)}, u32[]{:S(2)}) %collective-permute-start.4) | collective-permute-done | bytes 393248 | tf_op jit(solution)/shard_map/ppermute | solution.py:209
  77.6 1.1 join.2
  78.6 2.4 %collective-permute-start.5 = (bf16[464,1024]{1,0:T(8,128)(2,1)S(1)}, bf16[464,1024]{1,0:T(8,128)(2,1)S(1)}, u32[]{:S(2)}, u32[]{:S(2)}) collective-permute-start(bf16[464,1024]{1,0:T(8,128)(2,1)S(1)} %join.2), channel_id=1, source_target_pairs={{0,1},{1,2},{2,3},{3,4},{4,5},{5,6},{6,7},{7,8},{8,9},{9,10},{10,1... | collective-permute-start | bytes 2850824 | tf_op jit(solution)/shard_map/ppermute | solution.py:209
  81.1 14.4 %collective-permute-done.13.refs_1_ = bf16[544,1024]{1,0:T(8,128)(2,1)S(1)} collective-permute-done((bf16[544,1024]{1,0:T(8,128)(2,1)S(1)}, bf16[544,1024]{1,0:T(8,128)(2,1)S(1)}, u32[]{:S(2)}, u32[]{:S(2)}) %collective-permute-start.13) | collective-permute-done | bytes 1114144 | tf_op jit(solution)/shard_map/ppermute | solution.py:209
  95.5 5.6 %collective-permute-start.14 = (bf16[464,1024]{1,0:T(8,128)(2,1)S(1)}, bf16[464,1024]{1,0:T(8,128)(2,1)S(1)}, u32[]{:S(2)}, u32[]{:S(2)}) collective-permute-start(bf16[464,1024]{1,0:T(8,128)(2,1)S(1)} %slice.65), channel_id=1, source_target_pairs={{0,15},{1,0},{2,1},{3,2},{4,3},{5,4},{6,5},{7,6},{8,7},{9,8},{10,9... | collective-permute-start | bytes 2850824 | tf_op jit(solution)/shard_map/ppermute | solution.py:209
  101.1 0.6 attend_15.1.refs_0_
  101.8 2.1 %attend_0.1.refs_1_ = bf16[32,4096]{1,0:T(8,128)(2,1)S(1)} custom-call(s32[16,128]{1,0:T(8,128)S(1)} %tile.10.limits_ref, bf16[256,4096]{1,0:T(8,128)(2,1)S(1)} %convolution_convert_fusion.query_ref, bf16[384,1024]{1,0:T(8,128)(2,1)} %collective-permute-done.refs_0_, bf16[384,1024]{1,0:T(8,128)(2,1)S(1)} %collective-permute-done.6.refs_1_), custom_call_target="tpu_custom_call" | custom-call | flops 201326592 | bytes 1048576 | tf_op jit(solution)/shard_map/attend_0/pallas_call | solution.py:150
  103.9 2.3 %attend_2.1.refs_2_ = bf16[32,4096]{1,0:T(8,128)(2,1)S(1)} custom-call(s32[16,128]{1,0:T(8,128)S(1)} %tile.10.limits_ref, bf16[256,4096]{1,0:T(8,128)(2,1)S(1)} %convolution_convert_fusion.query_ref, bf16[384,512]{1,0:T(8,128)(2,1)} %collective-permute-done.1.refs_0_, bf16[384,512]{1,0:T(8,128)(2,1)} %collective-permute-done.3.refs_1_, ...), custom_call_target="tpu_custom_call" | custom-call | flops 201326592 | bytes 1048576 | tf_op jit(solution)/shard_map/attend_2/pallas_call | solution.py:150
  106.2 1.9 %collective-permute-start.9 = (bf16[384,1024]{1,0:T(8,128)(2,1)S(1)}, bf16[384,1024]{1,0:T(8,128)(2,1)S(1)}, u32[]{:S(2)}, u32[]{:S(2)}) collective-permute-start(bf16[384,1024]{1,0:T(8,128)(2,1)S(1)} %slice.60), channel_id=1, source_target_pairs={{0,1},{1,2},{2,3},{3,4},{4,5},{5,6},{6,7},{7,8},{8,9},{9,10},{10,1... | collective-permute-start | bytes 2359304 | tf_op jit(solution)/shard_map/ppermute | solution.py:209
  108.2 2.2 %attend_4.1.refs_3_ = bf16[32,4096]{1,0:T(8,128)(2,1)S(1)} custom-call(s32[16,128]{1,0:T(8,128)S(1)} %tile.10.limits_ref, bf16[256,4096]{1,0:T(8,128)(2,1)S(1)} %convolution_convert_fusion.query_ref, bf16[384,512]{1,0:T(8,128)(2,1)S(1)} %collective-permute-done.2.first_ref.refs_0_, bf16[384,512]{1,0:T(8,128)(2,1)} %collective-permute-done.4.second_ref.refs_1_, ...), custom_call_target="tpu_custom_call" | custom-call | flops 201326592 | bytes 1048576 | tf_op jit(solution)/shard_map/attend_4/pallas_call | solution.py:150
  110.3 14.3 %collective-permute-done.9.refs_0_ = bf16[384,1024]{1,0:T(8,128)(2,1)S(1)} collective-permute-done((bf16[384,1024]{1,0:T(8,128)(2,1)S(1)}, bf16[384,1024]{1,0:T(8,128)(2,1)S(1)}, u32[]{:S(2)}, u32[]{:S(2)}) %collective-permute-start.9) | collective-permute-done | bytes 786464 | tf_op jit(solution)/shard_map/ppermute | solution.py:209
  124.6 1.9 %collective-permute-start.12 = (bf16[384,1024]{1,0:T(8,128)(2,1)S(1)}, bf16[384,1024]{1,0:T(8,128)(2,1)S(1)}, u32[]{:S(2)}, u32[]{:S(2)}) collective-permute-start(bf16[384,1024]{1,0:T(8,128)(2,1)S(1)} %collective-permute-done.9.refs_0_), channel_id=1, source_target_pairs={{0,1},{1,2},{2,3},{3,4},{4,5},{5,6},{6,7},{7,8},{8,9},{9,10},{10,1... | collective-permute-start | bytes 2359304 | tf_op jit(solution)/shard_map/ppermute | solution.py:209
  126.6 5.1 %collective-permute-start.15 = (bf16[384,1024]{1,0:T(8,128)(2,1)S(1)}, bf16[384,1024]{1,0:T(8,128)(2,1)S(1)}, u32[]{:S(2)}, u32[]{:S(2)}) collective-permute-start(bf16[384,1024]{1,0:T(8,128)(2,1)S(1)} %slice.66), channel_id=1, source_target_pairs={{0,15},{1,0},{2,1},{3,2},{4,3},{5,4},{6,5},{7,6},{8,7},{9,8},{10,9... | collective-permute-start | bytes 2359304 | tf_op jit(solution)/shard_map/ppermute | solution.py:209
  131.9 1.0 attend_6.1.refs_4_
  132.9 1.0 attend_8.1.refs_5_
  133.9 1.7 %place_held.1.refs_0_ = bf16[256,4096]{1,0:T(8,128)(2,1)} custom-call(s32[16]{0:T(128)S(1)} %select_reduce_fusion.2.where_ref, bf16[16,4096]{1,0:T(8,128)(2,1)S(1)} %attend_15.1.refs_0_, bf16[32,4096]{1,0:T(8,128)(2,1)S(1)} %attend_0.1.refs_1_, bf16[32,4096]{1,0:T(8,128)(2,1)S(1)} %attend_2.1.refs_2_, bf16[32,4096]{1,0:T(8,128)(2,1)S(1)} %attend_4.1.refs_3_, ...), custom_call_target="tpu_custom_call" | custom-call | bytes 131072 | tf_op jit(solution)/shard_map/place_held/pallas_call | solution.py:176
  135.7 6.8 %collective-permute-done.12.refs_0_.block = bf16[384,1024]{1,0:T(8,128)(2,1)S(1)} collective-permute-done((bf16[384,1024]{1,0:T(8,128)(2,1)S(1)}, bf16[384,1024]{1,0:T(8,128)(2,1)S(1)}, u32[]{:S(2)}, u32[]{:S(2)}) %collective-permute-start.12) | collective-permute-done | bytes 786464 | tf_op jit(solution)/shard_map/ppermute | solution.py:209
  142.5 1.0 attend_guests.2
  143.5 1.9 %collective-permute-start.16 = (bf16[16,4096]{1,0:T(8,128)(2,1)S(1)}, bf16[16,4096]{1,0:T(8,128)(2,1)S(1)}, u32[]{:S(2)}, u32[]{:S(2)}) collective-permute-start(bf16[16,4096]{1,0:T(8,128)(2,1)S(1)} %get-tuple-element.31), channel_id=1, source_target_pairs={{0,2},{1,3},{2,4},{3,5},{4,6},{5,7},{6,8},{7,9},{8,10},{9,11},{10,... | collective-permute-start | bytes 393224 | tf_op jit(solution)/shard_map/ppermute | solution.py:209
  145.4 1.9 %collective-permute-start.17 = (bf16[16,4096]{1,0:T(8,128)(2,1)S(1)}, bf16[16,4096]{1,0:T(8,128)(2,1)S(1)}, u32[]{:S(2)}, u32[]{:S(2)}) collective-permute-start(bf16[16,4096]{1,0:T(8,128)(2,1)S(1)} %get-tuple-element.32), channel_id=1, source_target_pairs={{0,1},{1,2},{2,3},{3,4},{4,5},{5,6},{6,7},{7,8},{8,9},{9,10},{10,1... | collective-permute-start | bytes 393224 | tf_op jit(solution)/shard_map/ppermute | solution.py:209
  147.4 0.6 attend_guests.3
  148.0 5.1 %collective-permute-start.18 = (bf16[16,4096]{1,0:T(8,128)(2,1)S(1)}, bf16[16,4096]{1,0:T(8,128)(2,1)S(1)}, u32[]{:S(2)}, u32[]{:S(2)}) collective-permute-start(bf16[16,4096]{1,0:T(8,128)(2,1)S(1)} %attend_guests.3), channel_id=1, source_target_pairs={{0,15},{1,0},{2,1},{3,2},{4,3},{5,4},{6,5},{7,6},{8,7},{9,8},{10,9... | collective-permute-start | bytes 393224 | tf_op jit(solution)/shard_map/ppermute | solution.py:209
  153.2 1.0 attend_10.1.refs_1_
  154.2 1.4 collective-permute-done.18.refs_4_
  155.7 1.4 place_last.1
  (41 shorter events, 0.9 us)
Async XLA Ops:
  0.0 13.5 %copy-start = (bf16[1,1,256,4096]{3,2,1,0:T(8,128)(2,1)S(1)}, bf16[1,1,256,4096]{3,2,1,0:T(8,128)(2,1)}, u32[]{:S(2)}) copy-start(bf16[1,1,256,4096]{3,2,1,0:T(8,128)(2,1)} %param.6) | copy-start | bytes 6291460
  0.0 28.6 %collective-permute-start.6 = (bf16[384,1024]{1,0:T(8,128)(2,1)}, bf16[384,1024]{1,0:T(8,128)(2,1)S(1)}, u32[]{:S(2)}, u32[]{:S(2)}) collective-permute-start(bf16[384,1024]{1,0:T(8,128)(2,1)} %bitcast.15), channel_id=1, source_target_pairs={{0,15},{1,0},{2,1},{3,2},{4,3},{5,4},{6,5},{7,6},{8,7},{9,8},{10,9... | collective-permute-start | bytes 2359304 | tf_op jit(solution)/shard_map/ppermute | solution.py:209
  11.5 25.4 %collective-permute-start = (bf16[384,1024]{1,0:T(8,128)(2,1)}, bf16[384,1024]{1,0:T(8,128)(2,1)}, u32[]{:S(2)}, u32[]{:S(2)}) collective-permute-start(bf16[384,1024]{1,0:T(8,128)(2,1)} %bitcast.16), channel_id=1, source_target_pairs={{0,1},{1,2},{2,3},{3,4},{4,5},{5,6},{6,7},{7,8},{8,9},{9,10},{10,1... | collective-permute-start | bytes 2359304 | tf_op jit(solution)/shard_map/ppermute | solution.py:209
  16.2 7.8 %copy-start.2 = (s32[1,1,256]{2,1,0:T(1,128)S(1)}, s32[1,1,256]{2,1,0:T(1,128)}, u32[]{:S(2)}) copy-start(s32[1,1,256]{2,1,0:T(1,128)} %param.8) | copy-start | bytes 3076
  16.2 7.8 %copy-start.4 = (s32[1,1,16]{2,1,0:T(1,128)S(1)}, s32[1,1,16]{2,1,0:T(1,128)}, u32[]{:S(2)}) copy-start(s32[1,1,16]{2,1,0:T(1,128)} %param.10) | copy-start | bytes 196
  16.2 48.9 %all-to-all-start = ((bf16[32,8,4096]{2,1,0:T(8,128)(2,1)}), bf16[32,8,4096]{2,1,0:T(8,128)(2,1)}, u32[]{:S(2)}, u32[]{:S(2)}) async-start(bf16[32,8,4096]{2,1,0:T(8,128)(2,1)} %bitcast.18), calls=%async_computation | async-start | bytes 4194304 | tf_op jit(solution)/shard_map/all_to_all | solution.py:214
  28.7 17.6 %copy-start.3 = (s32[1,1,256]{2,1,0:T(1,128)S(1)}, s32[1,1,256]{2,1,0:T(1,128)}, u32[]{:S(2)}) copy-start(s32[1,1,256]{2,1,0:T(1,128)} %param.9) | copy-start | bytes 3076
  28.7 18.4 %collective-permute-start.7 = (bf16[384,512]{1,0:T(8,128)(2,1)S(1)}, bf16[384,512]{1,0:T(8,128)(2,1)}, u32[]{:S(2)}, u32[]{:S(2)}) collective-permute-start(bf16[384,512]{1,0:T(8,128)(2,1)S(1)} %pad_maximum_fusion.2), channel_id=1, source_target_pairs={{0,15},{1,0},{2,1},{3,2},{4,3},{5,4},{6,5},{7,6},{8,7},{9,8},{10,9... | collective-permute-start | bytes 1179656 | tf_op jit(solution)/shard_map/ppermute | solution.py:209
  35.0 17.2 %collective-permute-start.8 = (bf16[384,512]{1,0:T(8,128)(2,1)}, bf16[384,512]{1,0:T(8,128)(2,1)}, u32[]{:S(2)}, u32[]{:S(2)}) collective-permute-start(bf16[384,512]{1,0:T(8,128)(2,1)} %pad_maximum_fusion.3), channel_id=1, source_target_pairs={{0,15},{1,0},{2,1},{3,2},{4,3},{5,4},{6,5},{7,6},{8,7},{9,8},{10,9... | collective-permute-start | bytes 1179656 | tf_op jit(solution)/shard_map/ppermute | solution.py:209
  39.1 17.1 %collective-permute-start.1 = (bf16[384,512]{1,0:T(8,128)(2,1)}, bf16[384,512]{1,0:T(8,128)(2,1)}, u32[]{:S(2)}, u32[]{:S(2)}) collective-permute-start(bf16[384,512]{1,0:T(8,128)(2,1)} %pad_maximum_fusion), channel_id=1, source_target_pairs={{0,1},{1,2},{2,3},{3,4},{4,5},{5,6},{6,7},{7,8},{8,9},{9,10},{10,1... | collective-permute-start | bytes 1179656 | tf_op jit(solution)/shard_map/ppermute | solution.py:209
  43.8 17.5 %collective-permute-start.3 = (bf16[384,512]{1,0:T(8,128)(2,1)}, bf16[384,512]{1,0:T(8,128)(2,1)}, u32[]{:S(2)}, u32[]{:S(2)}) collective-permute-start(bf16[384,512]{1,0:T(8,128)(2,1)} %pad_maximum_fusion.1), channel_id=1, source_target_pairs={{0,1},{1,2},{2,3},{3,4},{4,5},{5,6},{6,7},{7,8},{8,9},{9,10},{10,1... | collective-permute-start | bytes 1179656 | tf_op jit(solution)/shard_map/ppermute | solution.py:209
  47.1 20.3 %collective-permute-start.10 = (bf16[384,512]{1,0:T(8,128)(2,1)}, bf16[384,512]{1,0:T(8,128)(2,1)}, u32[]{:S(2)}, u32[]{:S(2)}) collective-permute-start(bf16[384,512]{1,0:T(8,128)(2,1)} %collective-permute-done.7.refs_2_), channel_id=1, source_target_pairs={{0,15},{1,0},{2,1},{3,2},{4,3},{5,4},{6,5},{7,6},{8,7},{9,8},{10,9... | collective-permute-start | bytes 1179656 | tf_op jit(solution)/shard_map/ppermute | solution.py:209
  52.3 15.2 %collective-permute-start.11 = (bf16[384,512]{1,0:T(8,128)(2,1)}, bf16[384,512]{1,0:T(8,128)(2,1)}, u32[]{:S(2)}, u32[]{:S(2)}) collective-permute-start(bf16[384,512]{1,0:T(8,128)(2,1)} %collective-permute-done.8.refs_3_), channel_id=1, source_target_pairs={{0,15},{1,0},{2,1},{3,2},{4,3},{5,4},{6,5},{7,6},{8,7},{9,8},{10,9... | collective-permute-start | bytes 1179656 | tf_op jit(solution)/shard_map/ppermute | solution.py:209
  56.2 21.4 %collective-permute-start.2 = (bf16[384,512]{1,0:T(8,128)(2,1)}, bf16[384,512]{1,0:T(8,128)(2,1)S(1)}, u32[]{:S(2)}, u32[]{:S(2)}) collective-permute-start(bf16[384,512]{1,0:T(8,128)(2,1)} %collective-permute-done.1.refs_0_), channel_id=1, source_target_pairs={{0,1},{1,2},{2,3},{3,4},{4,5},{5,6},{6,7},{7,8},{8,9},{9,10},{10,1... | collective-permute-start | bytes 1179656 | tf_op jit(solution)/shard_map/ppermute | solution.py:209
  61.3 16.3 %collective-permute-start.4 = (bf16[384,512]{1,0:T(8,128)(2,1)}, bf16[384,512]{1,0:T(8,128)(2,1)}, u32[]{:S(2)}, u32[]{:S(2)}) collective-permute-start(bf16[384,512]{1,0:T(8,128)(2,1)} %collective-permute-done.3.refs_1_), channel_id=1, source_target_pairs={{0,1},{1,2},{2,3},{3,4},{4,5},{5,6},{6,7},{7,8},{8,9},{9,10},{10,1... | collective-permute-start | bytes 1179656 | tf_op jit(solution)/shard_map/ppermute | solution.py:209
  68.7 32.4 %copy-start.1 = (bf16[1,1,384,1024]{3,2,1,0:T(8,128)(2,1)S(1)}, bf16[1,1,384,1024]{3,2,1,0:T(8,128)(2,1)}, u32[]{:S(2)}) copy-start(bf16[1,1,384,1024]{3,2,1,0:T(8,128)(2,1)} %param.11) | copy-start | bytes 2359300
  68.7 26.7 %collective-permute-start.13 = (bf16[544,1024]{1,0:T(8,128)(2,1)S(1)}, bf16[544,1024]{1,0:T(8,128)(2,1)S(1)}, u32[]{:S(2)}, u32[]{:S(2)}) collective-permute-start(bf16[544,1024]{1,0:T(8,128)(2,1)S(1)} %join.3), channel_id=1, source_target_pairs={{0,15},{1,0},{2,1},{3,2},{4,3},{5,4},{6,5},{7,6},{8,7},{9,8},{10,9... | collective-permute-start | bytes 3342344 | tf_op jit(solution)/shard_map/ppermute | solution.py:209
  78.6 27.5 %collective-permute-start.5 = (bf16[464,1024]{1,0:T(8,128)(2,1)S(1)}, bf16[464,1024]{1,0:T(8,128)(2,1)S(1)}, u32[]{:S(2)}, u32[]{:S(2)}) collective-permute-start(bf16[464,1024]{1,0:T(8,128)(2,1)S(1)} %join.2), channel_id=1, source_target_pairs={{0,1},{1,2},{2,3},{3,4},{4,5},{5,6},{6,7},{7,8},{8,9},{9,10},{10,1... | collective-permute-start | bytes 2850824 | tf_op jit(solution)/shard_map/ppermute | solution.py:209
  95.5 31.0 %collective-permute-start.14 = (bf16[464,1024]{1,0:T(8,128)(2,1)S(1)}, bf16[464,1024]{1,0:T(8,128)(2,1)S(1)}, u32[]{:S(2)}, u32[]{:S(2)}) collective-permute-start(bf16[464,1024]{1,0:T(8,128)(2,1)S(1)} %slice.65), channel_id=1, source_target_pairs={{0,15},{1,0},{2,1},{3,2},{4,3},{5,4},{6,5},{7,6},{8,7},{9,8},{10,9... | collective-permute-start | bytes 2850824 | tf_op jit(solution)/shard_map/ppermute | solution.py:209
  106.2 18.4 %collective-permute-start.9 = (bf16[384,1024]{1,0:T(8,128)(2,1)S(1)}, bf16[384,1024]{1,0:T(8,128)(2,1)S(1)}, u32[]{:S(2)}, u32[]{:S(2)}) collective-permute-start(bf16[384,1024]{1,0:T(8,128)(2,1)S(1)} %slice.60), channel_id=1, source_target_pairs={{0,1},{1,2},{2,3},{3,4},{4,5},{5,6},{6,7},{7,8},{8,9},{9,10},{10,1... | collective-permute-start | bytes 2359304 | tf_op jit(solution)/shard_map/ppermute | solution.py:209
  124.6 17.9 %collective-permute-start.12 = (bf16[384,1024]{1,0:T(8,128)(2,1)S(1)}, bf16[384,1024]{1,0:T(8,128)(2,1)S(1)}, u32[]{:S(2)}, u32[]{:S(2)}) collective-permute-start(bf16[384,1024]{1,0:T(8,128)(2,1)S(1)} %collective-permute-done.9.refs_0_), channel_id=1, source_target_pairs={{0,1},{1,2},{2,3},{3,4},{4,5},{5,6},{6,7},{7,8},{8,9},{9,10},{10,1... | collective-permute-start | bytes 2359304 | tf_op jit(solution)/shard_map/ppermute | solution.py:209
  126.6 20.8 %collective-permute-start.15 = (bf16[384,1024]{1,0:T(8,128)(2,1)S(1)}, bf16[384,1024]{1,0:T(8,128)(2,1)S(1)}, u32[]{:S(2)}, u32[]{:S(2)}) collective-permute-start(bf16[384,1024]{1,0:T(8,128)(2,1)S(1)} %slice.66), channel_id=1, source_target_pairs={{0,15},{1,0},{2,1},{3,2},{4,3},{5,4},{6,5},{7,6},{8,7},{9,8},{10,9... | collective-permute-start | bytes 2359304 | tf_op jit(solution)/shard_map/ppermute | solution.py:209
  143.5 10.7 %collective-permute-start.16 = (bf16[16,4096]{1,0:T(8,128)(2,1)S(1)}, bf16[16,4096]{1,0:T(8,128)(2,1)S(1)}, u32[]{:S(2)}, u32[]{:S(2)}) collective-permute-start(bf16[16,4096]{1,0:T(8,128)(2,1)S(1)} %get-tuple-element.31), channel_id=1, source_target_pairs={{0,2},{1,3},{2,4},{3,5},{4,6},{5,7},{6,8},{7,9},{8,10},{9,11},{10,... | collective-permute-start | bytes 393224 | tf_op jit(solution)/shard_map/ppermute | solution.py:209
  145.4 8.8 %collective-permute-start.17 = (bf16[16,4096]{1,0:T(8,128)(2,1)S(1)}, bf16[16,4096]{1,0:T(8,128)(2,1)S(1)}, u32[]{:S(2)}, u32[]{:S(2)}) collective-permute-start(bf16[16,4096]{1,0:T(8,128)(2,1)S(1)} %get-tuple-element.32), channel_id=1, source_target_pairs={{0,1},{1,2},{2,3},{3,4},{4,5},{5,6},{6,7},{7,8},{8,9},{9,10},{10,1... | collective-permute-start | bytes 393224 | tf_op jit(solution)/shard_map/ppermute | solution.py:209
  148.0 7.6 %collective-permute-start.18 = (bf16[16,4096]{1,0:T(8,128)(2,1)S(1)}, bf16[16,4096]{1,0:T(8,128)(2,1)S(1)}, u32[]{:S(2)}, u32[]{:S(2)}) collective-permute-start(bf16[16,4096]{1,0:T(8,128)(2,1)S(1)} %attend_guests.3), channel_id=1, source_target_pairs={{0,15},{1,0},{2,1},{3,2},{4,3},{5,4},{6,5},{7,6},{8,7},{9,8},{10,9... | collective-permute-start | bytes 393224 | tf_op jit(solution)/shard_map/ppermute | solution.py:209

commit v7 on v4

--- a/solution.py
+++ b/solution.py
@@ -145,8 +145,13 @@
     me = lax.axis_index("prompt")
     kv = seq_kv[0, 0]
 
+    turn = 1 - 2 * (lax.axis_index("dp") % 2)
+
     def shifted(x, by):
-        return lax.ppermute(x, "prompt", [(i, (i + by) % ring) for i in range(ring)])
+        pairs = [
+            (d * ring + i, d * ring + (i + by * (1 - 2 * (d % 2))) % ring) for d in range(dp_count) for i in range(ring)
+        ]
+        return lax.ppermute(x, ("dp", "prompt"), pairs)
 
     steps = ring // 2
 
@@ -156,7 +161,7 @@
     ).reshape(row_count, width)
 
     sequences = pack_seq[0, 0]
-    behind = (me - sequences) % ring
+    behind = (turn * (me - sequences)) % ring
     place = jnp.where(
         behind == 0,
         ring - 1,
@@ -196,15 +201,16 @@
         if step == 3:
             guests = [payload(s[0]) for s in (opposite, behind_far, ahead_far)]
             up, guests = tie(up, guests)
-            guests = [shifted(g, by) for g, by in zip(guests, (-2, -1, 1))]
+            guests[0] = shifted(guests[0], -2)
         if step == 4:
             score(mine, (kv,))
             score((0, 1), blocks_of[0])
             up, (guests, held) = tie(up, (guests, held))
+            guests[1], guests[2] = shifted(guests[1], -1), shifted(guests[2], 1)
         if step == 5:
             score((2, 3), blocks_of[1])
             score((4, 5), blocks_of[2])
-            up, held = tie(up, held)
+            up, (guests, held) = tie(up, (guests, held))
         up = shifted(up, 1)
         down = shifted(down, -1)
         blocks_of.append((up, down))

time: 157 us -> 165 us (1.051)
  the two profiles are of different devices: /device:TPU:126 before, /device:TPU:48 now
where the time goes in v7:
time: 165 us; the launch traced here: 164 us
  starting transfers between devices  80.8 us (49%)
  waiting for transfers between devices  55.5 us (34%)
  Pallas kernels  16.8 us (10%)
  matrix products  5.03 us (3%)
  local copies, waits for them, and re-layouts  3.95 us (2%)
    ppermute x18, starting transfers between devices, shifted(): return lax.ppermute(x, ('dp', 'prompt'), pairs)  72.5 us
    ppermute x18, waiting for transfers between devices, shifted(): return lax.ppermute(x, ('dp', 'prompt'), pairs)  55.5 us
    pallas_call x7, Pallas kernels, attend_step(): pl.pallas_call(functools.partial(step_kernel, spots, rows), out_shape=jax...  12.3 us
    all_to_all x1, starting transfers between devices, body(): lax.all_to_all(ordered.reshape(dp_count, row_count // dp_count, width), '...  8.38 us
    dot_general x2, matrix products, move_rows(): jnp.dot(pick, rows, preferred_element_type=jnp.float32).astype(rows.dtype)  5.03 us
    unnamed x17, local copies, waits for them, and re-layouts  3.5 us
  transfers between devices with their start and end apart: 19, of which 9 were waited for; matrix products, arithmetic and copies ran while one was open for 4% of the time, Pallas kernels for 9%

profile of v7, /device:TPU:48, one launch (start us, length us, event | category | flops | bytes accessed | tf_op | source)
XLA Modules:
  0.0 163.7 jit_solution(2376673174614376136)
XLA Ops:
  0.0 3.9 %collective-permute-start = (bf16[384,1024]{1,0:T(8,128)(2,1)}, bf16[384,1024]{1,0:T(8,128)(2,1)}, u32[]{:S(2)}, u32[]{:S(2)}) collective-permute-start(bf16[384,1024]{1,0:T(8,128)(2,1)} %bitcast.21), channel_id=1, source_target_pairs={{0,1},{1,2},{2,3},{3,4},{4,5},{5,6},{6,7},{7,8},{8,9},{9,10},{10,1... | collective-permute-start | bytes 2359304 | tf_op jit(solution)/shard_map/ppermute | solution.py:154
  4.0 2.0 %collective-permute-start.5 = (bf16[384,1024]{1,0:T(8,128)(2,1)}, bf16[384,1024]{1,0:T(8,128)(2,1)}, u32[]{:S(2)}, u32[]{:S(2)}) collective-permute-start(bf16[384,1024]{1,0:T(8,128)(2,1)} %bitcast.22), channel_id=1, source_target_pairs={{0,15},{1,0},{2,1},{3,2},{4,3},{5,4},{6,5},{7,6},{8,7},{9,8},{10,9... | collective-permute-start | bytes 2359304 | tf_op jit(solution)/shard_map/ppermute | solution.py:154
  6.0 2.7 %convolution_convert_fusion.1 = bf16[256,4096]{1,0:T(8,128)(2,1)} fusion(bf16[1,1,256,4096]{3,2,1,0:T(8,128)(2,1)S(1)} %copy-done, s32[256]{0:T(256)} %bitcast.25), kind=kOutput, calls=%fused_computation.1 | convolution fusion | flops 537985024 | bytes 4195328 | tf_op jit(solution)/shard_map/dot_general | solution.py:132
  8.7 8.4 %all-to-all-start = ((bf16[32,8,4096]{2,1,0:T(8,128)(2,1)}), bf16[32,8,4096]{2,1,0:T(8,128)(2,1)}, u32[]{:S(2)}, u32[]{:S(2)}) async-start(bf16[32,8,4096]{2,1,0:T(8,128)(2,1)} %bitcast.24), calls=%async_computation | async-start | bytes 4194304 | tf_op jit(solution)/shard_map/all_to_all | solution.py:159
  17.1 0.6 broadcast.568
  17.7 0.6 reduce.3
  18.5 0.1 select_reduce_fusion
  18.7 0.1 tile.24
  18.9 2.5 %collective-permute-done.refs_0_ = bf16[384,1024]{1,0:T(8,128)(2,1)} collective-permute-done((bf16[384,1024]{1,0:T(8,128)(2,1)}, bf16[384,1024]{1,0:T(8,128)(2,1)}, u32[]{:S(2)}, u32[]{:S(2)}) %collective-permute-start) | collective-permute-done | bytes 786464 | tf_op jit(solution)/shard_map/ppermute | solution.py:154
  21.4 4.4 %collective-permute-start.1 = (bf16[384,1024]{1,0:T(8,128)(2,1)}, bf16[384,1024]{1,0:T(8,128)(2,1)}, u32[]{:S(2)}, u32[]{:S(2)}) collective-permute-start(bf16[384,1024]{1,0:T(8,128)(2,1)} %collective-permute-done.refs_0_), channel_id=1, source_target_pairs={{0,1},{1,2},{2,3},{3,4},{4,5},{5,6},{6,7},{7,8},{8,9},{9,10},{10,1... | collective-permute-start | bytes 2359304 | tf_op jit(solution)/shard_map/ppermute | solution.py:154
  25.8 4.8 %collective-permute-start.9 = (bf16[384,1024]{1,0:T(8,128)(2,1)}, bf16[384,1024]{1,0:T(8,128)(2,1)}, u32[]{:S(2)}, u32[]{:S(2)}) collective-permute-start(bf16[384,1024]{1,0:T(8,128)(2,1)} %collective-permute-done.5.refs_1_), channel_id=1, source_target_pairs={{0,15},{1,0},{2,1},{3,2},{4,3},{5,4},{6,5},{7,6},{8,7},{9,8},{10,9... | collective-permute-start | bytes 2359304 | tf_op jit(solution)/shard_map/ppermute | solution.py:154
  30.7 0.1 select_reduce_fusion.1
  30.8 12.4 %collective-permute-done.1.refs_0_ = bf16[384,1024]{1,0:T(8,128)(2,1)} collective-permute-done((bf16[384,1024]{1,0:T(8,128)(2,1)}, bf16[384,1024]{1,0:T(8,128)(2,1)}, u32[]{:S(2)}, u32[]{:S(2)}) %collective-permute-start.1) | collective-permute-done | bytes 786464 | tf_op jit(solution)/shard_map/ppermute | solution.py:154
  43.3 5.2 %collective-permute-start.2 = (bf16[384,1024]{1,0:T(8,128)(2,1)}, bf16[384,1024]{1,0:T(8,128)(2,1)}, u32[]{:S(2)}, u32[]{:S(2)}) collective-permute-start(bf16[384,1024]{1,0:T(8,128)(2,1)} %collective-permute-done.1.refs_0_), channel_id=1, source_target_pairs={{0,1},{1,2},{2,3},{3,4},{4,5},{5,6},{6,7},{7,8},{8,9},{9,10},{10,1... | collective-permute-start | bytes 2359304 | tf_op jit(solution)/shard_map/ppermute | solution.py:154
  48.4 4.2 %collective-permute-start.10 = (bf16[384,1024]{1,0:T(8,128)(2,1)}, bf16[384,1024]{1,0:T(8,128)(2,1)}, u32[]{:S(2)}, u32[]{:S(2)}) collective-permute-start(bf16[384,1024]{1,0:T(8,128)(2,1)} %collective-permute-done.9.refs_1_), channel_id=1, source_target_pairs={{0,15},{1,0},{2,1},{3,2},{4,3},{5,4},{6,5},{7,6},{8,7},{9,8},{10,9... | collective-permute-start | bytes 2359304 | tf_op jit(solution)/shard_map/ppermute | solution.py:154
  52.6 2.3 %convolution_convert_fusion.query_ref = bf16[256,4096]{1,0:T(8,128)(2,1)S(1)} fusion(bf16[32,8,4096]{2,1,0:T(8,128)(2,1)} %all-to-all-done, s32[256]{0:T(256)S(1)} %fusion.13), kind=kOutput, calls=%fused_computation | convolution fusion | flops 537985024 | bytes 4195328 | tf_op jit(solution)/shard_map/dot_general | solution.py:132
  55.0 1.3 copy-done.1
  56.3 10.9 %collective-permute-done.2.refs_0_ = bf16[384,1024]{1,0:T(8,128)(2,1)} collective-permute-done((bf16[384,1024]{1,0:T(8,128)(2,1)}, bf16[384,1024]{1,0:T(8,128)(2,1)}, u32[]{:S(2)}, u32[]{:S(2)}) %collective-permute-start.2) | collective-permute-done | bytes 786464 | tf_op jit(solution)/shard_map/ppermute | solution.py:154
  67.3 4.0 %collective-permute-start.3 = (bf16[384,1024]{1,0:T(8,128)(2,1)}, bf16[384,1024]{1,0:T(8,128)(2,1)}, u32[]{:S(2)}, u32[]{:S(2)}) collective-permute-start(bf16[384,1024]{1,0:T(8,128)(2,1)} %collective-permute-done.2.refs_0_), channel_id=1, source_target_pairs={{0,1},{1,2},{2,3},{3,4},{4,5},{5,6},{6,7},{7,8},{8,9},{9,10},{10,1... | collective-permute-start | bytes 2359304 | tf_op jit(solution)/shard_map/ppermute | solution.py:154
  71.3 4.8 %collective-permute-start.12 = (bf16[384,1024]{1,0:T(8,128)(2,1)}, bf16[384,1024]{1,0:T(8,128)(2,1)}, u32[]{:S(2)}, u32[]{:S(2)}) collective-permute-start(bf16[384,1024]{1,0:T(8,128)(2,1)} %collective-permute-done.10.refs_1_), channel_id=1, source_target_pairs={{0,15},{1,0},{2,1},{3,2},{4,3},{5,4},{6,5},{7,6},{8,7},{9,8},{10,9... | collective-permute-start | bytes 2359304 | tf_op jit(solution)/shard_map/ppermute | solution.py:154
  76.1 6.3 %collective-permute-start.4 = (bf16[16,4224]{1,0:T(8,128)(2,1)S(1)}, bf16[16,4224]{1,0:T(8,128)(2,1)S(1)}, u32[]{:S(2)}, u32[]{:S(2)}) collective-permute-start(bf16[16,4224]{1,0:T(8,128)(2,1)S(1)} %get-tuple-element.31), channel_id=1, source_target_pairs={{0,14},{1,15},{2,0},{3,1},{4,2},{5,3},{6,4},{7,5},{8,6},{9,7},{10,... | collective-permute-start | bytes 405512 | tf_op jit(solution)/shard_map/ppermute | solution.py:154
  82.5 1.6 copy-done.2
  84.1 0.6 attend_15.1.refs_0_
  84.7 2.3 %attend_0.1.refs_1_ = bf16[32,4096]{1,0:T(8,128)(2,1)S(1)} custom-call(s32[16,128]{1,0:T(8,128)S(1)} %tile.28.limits_ref, bf16[256,4096]{1,0:T(8,128)(2,1)S(1)} %copy-done.2, bf16[384,1024]{1,0:T(8,128)(2,1)} %collective-permute-done.refs_0_, bf16[384,1024]{1,0:T(8,128)(2,1)} %collective-permute-done.5.refs_1_), custom_call_target="tpu_custom_call" | custom-call | flops 201326592 | bytes 1048576 | tf_op jit(solution)/shard_map/attend_0/pallas_call | solution.py:90
  87.1 4.6 %collective-permute-done.4.refs_2_ = bf16[16,4224]{1,0:T(8,128)(2,1)S(1)} collective-permute-done((bf16[16,4224]{1,0:T(8,128)(2,1)S(1)}, bf16[16,4224]{1,0:T(8,128)(2,1)S(1)}, u32[]{:S(2)}, u32[]{:S(2)}) %collective-permute-start.4) | collective-permute-done | bytes 135200 | tf_op jit(solution)/shard_map/ppermute | solution.py:154
  91.7 1.0 collective-permute-done.3.refs_0_
  92.7 5.6 %collective-permute-start.6 = (bf16[384,1024]{1,0:T(8,128)(2,1)}, bf16[384,1024]{1,0:T(8,128)(2,1)S(1)}, u32[]{:S(2)}, u32[]{:S(2)}) collective-permute-start(bf16[384,1024]{1,0:T(8,128)(2,1)} %collective-permute-done.3.refs_0_), channel_id=1, source_target_pairs={{0,1},{1,2},{2,3},{3,4},{4,5},{5,6},{6,7},{7,8},{8,9},{9,10},{10,1... | collective-permute-start | bytes 2359304 | tf_op jit(solution)/shard_map/ppermute | solution.py:154
  98.3 2.1 %collective-permute-start.13 = (bf16[384,1024]{1,0:T(8,128)(2,1)}, bf16[384,1024]{1,0:T(8,128)(2,1)S(1)}, u32[]{:S(2)}, u32[]{:S(2)}) collective-permute-start(bf16[384,1024]{1,0:T(8,128)(2,1)} %collective-permute-done.12.refs_1_), channel_id=1, source_target_pairs={{0,15},{1,0},{2,1},{3,2},{4,3},{5,4},{6,5},{7,6},{8,7},{9,8},{10,9... | collective-permute-start | bytes 2359304 | tf_op jit(solution)/shard_map/ppermute | solution.py:154
  100.4 5.1 %collective-permute-start.7 = (bf16[16,4224]{1,0:T(8,128)(2,1)S(1)}, bf16[16,4224]{1,0:T(8,128)(2,1)S(1)}, u32[]{:S(2)}, u32[]{:S(2)}) collective-permute-start(bf16[16,4224]{1,0:T(8,128)(2,1)S(1)} %get-tuple-element.36), channel_id=1, source_target_pairs={{0,15},{1,0},{2,1},{3,2},{4,3},{5,4},{6,5},{7,6},{8,7},{9,8},{10,9... | collective-permute-start | bytes 405512 | tf_op jit(solution)/shard_map/ppermute | solution.py:154
  105.5 1.9 %collective-permute-start.8 = (bf16[16,4224]{1,0:T(8,128)(2,1)S(1)}, bf16[16,4224]{1,0:T(8,128)(2,1)S(1)}, u32[]{:S(2)}, u32[]{:S(2)}) collective-permute-start(bf16[16,4224]{1,0:T(8,128)(2,1)S(1)} %pad_maximum_fusion.2), channel_id=1, source_target_pairs={{0,1},{1,2},{2,3},{3,4},{4,5},{5,6},{6,7},{7,8},{8,9},{9,10},{10,1... | collective-permute-start | bytes 405512 | tf_op jit(solution)/shard_map/ppermute | solution.py:154
  107.4 2.3 %attend_2.1.refs_2_ = bf16[32,4096]{1,0:T(8,128)(2,1)S(1)} custom-call(s32[16,128]{1,0:T(8,128)S(1)} %tile.28.limits_ref, bf16[256,4096]{1,0:T(8,128)(2,1)S(1)} %copy-done.2, bf16[384,1024]{1,0:T(8,128)(2,1)} %collective-permute-done.1.refs_0_, bf16[384,1024]{1,0:T(8,128)(2,1)} %collective-permute-done.9.refs_1_), custom_call_target="tpu_custom_call" | custom-call | flops 201326592 | bytes 1048576 | tf_op jit(solution)/shard_map/attend_2/pallas_call | solution.py:90
  109.8 2.5 %attend_4.1.refs_3_ = bf16[32,4096]{1,0:T(8,128)(2,1)S(1)} custom-call(s32[16,128]{1,0:T(8,128)S(1)} %tile.28.limits_ref, bf16[256,4096]{1,0:T(8,128)(2,1)S(1)} %copy-done.2, bf16[384,1024]{1,0:T(8,128)(2,1)} %collective-permute-done.2.refs_0_, bf16[384,1024]{1,0:T(8,128)(2,1)} %collective-permute-done.10.refs_1_), custom_call_target="tpu_custom_call" | custom-call | flops 201326592 | bytes 1048576 | tf_op jit(solution)/shard_map/attend_4/pallas_call | solution.py:90
  112.3 10.2 %collective-permute-done.7.refs_3_ = bf16[16,4224]{1,0:T(8,128)(2,1)S(1)} collective-permute-done((bf16[16,4224]{1,0:T(8,128)(2,1)S(1)}, bf16[16,4224]{1,0:T(8,128)(2,1)S(1)}, u32[]{:S(2)}, u32[]{:S(2)}) %collective-permute-start.7) | collective-permute-done | bytes 135200 | tf_op jit(solution)/shard_map/ppermute | solution.py:154
  122.5 1.9 %collective-permute-start.11 = (bf16[384,1024]{1,0:T(8,128)(2,1)S(1)}, bf16[384,1024]{1,0:T(8,128)(2,1)S(1)}, u32[]{:S(2)}, u32[]{:S(2)}) collective-permute-start(bf16[384,1024]{1,0:T(8,128)(2,1)S(1)} %collective-permute-done.6.refs_0_), channel_id=1, source_target_pairs={{0,1},{1,2},{2,3},{3,4},{4,5},{5,6},{6,7},{7,8},{8,9},{9,10},{10,1... | collective-permute-start | bytes 2359304 | tf_op jit(solution)/shard_map/ppermute | solution.py:154
  124.4 3.9 %collective-permute-start.14 = (bf16[384,1024]{1,0:T(8,128)(2,1)S(1)}, bf16[384,1024]{1,0:T(8,128)(2,1)S(1)}, u32[]{:S(2)}, u32[]{:S(2)}) collective-permute-start(bf16[384,1024]{1,0:T(8,128)(2,1)S(1)} %collective-permute-done.13.refs_1_), channel_id=1, source_target_pairs={{0,15},{1,0},{2,1},{3,2},{4,3},{5,4},{6,5},{7,6},{8,7},{9,8},{10,9... | collective-permute-start | bytes 2359304 | tf_op jit(solution)/shard_map/ppermute | solution.py:154
  128.3 0.1 select_reduce_fusion.2.where_ref
  128.5 2.4 %attend_6.1.refs_4_ = bf16[32,4096]{1,0:T(8,128)(2,1)S(1)} custom-call(s32[16,128]{1,0:T(8,128)S(1)} %tile.28.limits_ref, bf16[256,4096]{1,0:T(8,128)(2,1)S(1)} %copy-done.3, bf16[384,1024]{1,0:T(8,128)(2,1)} %collective-permute-done.3.refs_0_, bf16[384,1024]{1,0:T(8,128)(2,1)} %collective-permute-done.12.refs_1_), custom_call_target="tpu_custom_call" | custom-call | flops 201326592 | bytes 1048576 | tf_op jit(solution)/shard_map/attend_6/pallas_call | solution.py:90
  130.8 1.0 attend_8.1.refs_5_
  131.8 1.7 %place_held.1.refs_0_ = bf16[256,4096]{1,0:T(8,128)(2,1)} custom-call(s32[16]{0:T(128)S(1)} %select_reduce_fusion.2.where_ref, bf16[16,4096]{1,0:T(8,128)(2,1)S(1)} %attend_15.1.refs_0_, bf16[32,4096]{1,0:T(8,128)(2,1)S(1)} %attend_0.1.refs_1_, bf16[32,4096]{1,0:T(8,128)(2,1)S(1)} %attend_2.1.refs_2_, bf16[32,4096]{1,0:T(8,128)(2,1)S(1)} %attend_4.1.refs_3_, ...), custom_call_target="tpu_custom_call" | custom-call | bytes 131072 | tf_op jit(solution)/shard_map/place_held/pallas_call | solution.py:116
  133.6 10.0 %collective-permute-done.11.refs_0_ = bf16[384,1024]{1,0:T(8,128)(2,1)S(1)} collective-permute-done((bf16[384,1024]{1,0:T(8,128)(2,1)S(1)}, bf16[384,1024]{1,0:T(8,128)(2,1)S(1)}, u32[]{:S(2)}, u32[]{:S(2)}) %collective-permute-start.11) | collective-permute-done | bytes 786464 | tf_op jit(solution)/shard_map/ppermute | solution.py:154
  143.6 1.4 attend_guests.1
  145.0 5.5 %collective-permute-start.15 = (bf16[16,4096]{1,0:T(8,128)(2,1)S(1)}, bf16[16,4096]{1,0:T(8,128)(2,1)S(1)}, u32[]{:S(2)}, u32[]{:S(2)}) collective-permute-start(bf16[16,4096]{1,0:T(8,128)(2,1)S(1)} %get-tuple-element.50), channel_id=1, source_target_pairs={{0,2},{1,3},{2,4},{3,5},{4,6},{5,7},{6,8},{7,9},{8,10},{9,11},{10,... | collective-permute-start | bytes 393224 | tf_op jit(solution)/shard_map/ppermute | solution.py:154
  150.5 5.0 %collective-permute-start.16 = (bf16[16,4096]{1,0:T(8,128)(2,1)S(1)}, bf16[16,4096]{1,0:T(8,128)(2,1)S(1)}, u32[]{:S(2)}, u32[]{:S(2)}) collective-permute-start(bf16[16,4096]{1,0:T(8,128)(2,1)S(1)} %get-tuple-element.51), channel_id=1, source_target_pairs={{0,1},{1,2},{2,3},{3,4},{4,5},{5,6},{6,7},{7,8},{8,9},{9,10},{10,1... | collective-permute-start | bytes 393224 | tf_op jit(solution)/shard_map/ppermute | solution.py:154
  155.5 1.9 %collective-permute-start.17 = (bf16[16,4096]{1,0:T(8,128)(2,1)S(1)}, bf16[16,4096]{1,0:T(8,128)(2,1)S(1)}, u32[]{:S(2)}, u32[]{:S(2)}) collective-permute-start(bf16[16,4096]{1,0:T(8,128)(2,1)S(1)} %get-tuple-element.52), channel_id=1, source_target_pairs={{0,15},{1,0},{2,1},{3,2},{4,3},{5,4},{6,5},{7,6},{8,7},{9,8},{10,9... | collective-permute-start | bytes 393224 | tf_op jit(solution)/shard_map/ppermute | solution.py:154
  157.4 1.0 attend_10.1.refs_1_
  158.5 0.1 collective-permute-done.16.refs_3_
  158.6 3.8 %collective-permute-done.17.refs_4_ = bf16[16,4096]{1,0:T(8,128)(2,1)S(1)} collective-permute-done((bf16[16,4096]{1,0:T(8,128)(2,1)S(1)}, bf16[16,4096]{1,0:T(8,128)(2,1)S(1)}, u32[]{:S(2)}, u32[]{:S(2)}) %collective-permute-start.17) | collective-permute-done | bytes 131104 | tf_op jit(solution)/shard_map/ppermute | solution.py:154
  162.3 1.4 place_last.1
  (46 shorter events, 0.6 us)
Async XLA Ops:
  0.0 6.0 %copy-start = (bf16[1,1,256,4096]{3,2,1,0:T(8,128)(2,1)S(1)}, bf16[1,1,256,4096]{3,2,1,0:T(8,128)(2,1)}, u32[]{:S(2)}) copy-start(bf16[1,1,256,4096]{3,2,1,0:T(8,128)(2,1)} %param.6) | copy-start | bytes 6291460
  0.0 21.4 %collective-permute-start = (bf16[384,1024]{1,0:T(8,128)(2,1)}, bf16[384,1024]{1,0:T(8,128)(2,1)}, u32[]{:S(2)}, u32[]{:S(2)}) collective-permute-start(bf16[384,1024]{1,0:T(8,128)(2,1)} %bitcast.21), channel_id=1, source_target_pairs={{0,1},{1,2},{2,3},{3,4},{4,5},{5,6},{6,7},{7,8},{8,9},{9,10},{10,1... | collective-permute-start | bytes 2359304 | tf_op jit(solution)/shard_map/ppermute | solution.py:154
  4.0 21.9 %collective-permute-start.5 = (bf16[384,1024]{1,0:T(8,128)(2,1)}, bf16[384,1024]{1,0:T(8,128)(2,1)}, u32[]{:S(2)}, u32[]{:S(2)}) collective-permute-start(bf16[384,1024]{1,0:T(8,128)(2,1)} %bitcast.22), channel_id=1, source_target_pairs={{0,15},{1,0},{2,1},{3,2},{4,3},{5,4},{6,5},{7,6},{8,7},{9,8},{10,9... | collective-permute-start | bytes 2359304 | tf_op jit(solution)/shard_map/ppermute | solution.py:154
  8.7 9.0 %copy-start.6 = (s32[1,1,256]{2,1,0:T(1,128)S(1)}, s32[1,1,256]{2,1,0:T(1,128)}, u32[]{:S(2)}) copy-start(s32[1,1,256]{2,1,0:T(1,128)} %param.9) | copy-start | bytes 3076
  8.7 9.7 %copy-start.7 = (s32[1,1,16]{2,1,0:T(1,128)S(1)}, s32[1,1,16]{2,1,0:T(1,128)}, u32[]{:S(2)}) copy-start(s32[1,1,16]{2,1,0:T(1,128)} %param.10) | copy-start | bytes 196
  8.7 22.0 %copy-start.5 = (s32[1,1,256]{2,1,0:T(1,128)S(1)}, s32[1,1,256]{2,1,0:T(1,128)}, u32[]{:S(2)}) copy-start(s32[1,1,256]{2,1,0:T(1,128)} %param.8) | copy-start | bytes 3076
  8.7 43.9 %all-to-all-start = ((bf16[32,8,4096]{2,1,0:T(8,128)(2,1)}), bf16[32,8,4096]{2,1,0:T(8,128)(2,1)}, u32[]{:S(2)}, u32[]{:S(2)}) async-start(bf16[32,8,4096]{2,1,0:T(8,128)(2,1)} %bitcast.24), calls=%async_computation | async-start | bytes 4194304 | tf_op jit(solution)/shard_map/all_to_all | solution.py:159
  21.4 21.8 %collective-permute-start.1 = (bf16[384,1024]{1,0:T(8,128)(2,1)}, bf16[384,1024]{1,0:T(8,128)(2,1)}, u32[]{:S(2)}, u32[]{:S(2)}) collective-permute-start(bf16[384,1024]{1,0:T(8,128)(2,1)} %collective-permute-done.refs_0_), channel_id=1, source_target_pairs={{0,1},{1,2},{2,3},{3,4},{4,5},{5,6},{6,7},{7,8},{8,9},{9,10},{10,1... | collective-permute-start | bytes 2359304 | tf_op jit(solution)/shard_map/ppermute | solution.py:154
  25.8 22.6 %collective-permute-start.9 = (bf16[384,1024]{1,0:T(8,128)(2,1)}, bf16[384,1024]{1,0:T(8,128)(2,1)}, u32[]{:S(2)}, u32[]{:S(2)}) collective-permute-start(bf16[384,1024]{1,0:T(8,128)(2,1)} %collective-permute-done.5.refs_1_), channel_id=1, source_target_pairs={{0,15},{1,0},{2,1},{3,2},{4,3},{5,4},{6,5},{7,6},{8,7},{9,8},{10,9... | collective-permute-start | bytes 2359304 | tf_op jit(solution)/shard_map/ppermute | solution.py:154
  30.8 51.7 %copy-start.4 = (bf16[1,1,384,1024]{3,2,1,0:T(8,128)(2,1)S(1)}, bf16[1,1,384,1024]{3,2,1,0:T(8,128)(2,1)}, u32[]{:S(2)}) copy-start(bf16[1,1,384,1024]{3,2,1,0:T(8,128)(2,1)} %param.11) | copy-start | bytes 2359300
  43.3 24.0 %collective-permute-start.2 = (bf16[384,1024]{1,0:T(8,128)(2,1)}, bf16[384,1024]{1,0:T(8,128)(2,1)}, u32[]{:S(2)}, u32[]{:S(2)}) collective-permute-start(bf16[384,1024]{1,0:T(8,128)(2,1)} %collective-permute-done.1.refs_0_), channel_id=1, source_target_pairs={{0,1},{1,2},{2,3},{3,4},{4,5},{5,6},{6,7},{7,8},{8,9},{9,10},{10,1... | collective-permute-start | bytes 2359304 | tf_op jit(solution)/shard_map/ppermute | solution.py:154
  48.4 22.9 %collective-permute-start.10 = (bf16[384,1024]{1,0:T(8,128)(2,1)}, bf16[384,1024]{1,0:T(8,128)(2,1)}, u32[]{:S(2)}, u32[]{:S(2)}) collective-permute-start(bf16[384,1024]{1,0:T(8,128)(2,1)} %collective-permute-done.9.refs_1_), channel_id=1, source_target_pairs={{0,15},{1,0},{2,1},{3,2},{4,3},{5,4},{6,5},{7,6},{8,7},{9,8},{10,9... | collective-permute-start | bytes 2359304 | tf_op jit(solution)/shard_map/ppermute | solution.py:154
  55.0 1.3 copy-start.1
  67.3 25.4 %collective-permute-start.3 = (bf16[384,1024]{1,0:T(8,128)(2,1)}, bf16[384,1024]{1,0:T(8,128)(2,1)}, u32[]{:S(2)}, u32[]{:S(2)}) collective-permute-start(bf16[384,1024]{1,0:T(8,128)(2,1)} %collective-permute-done.2.refs_0_), channel_id=1, source_target_pairs={{0,1},{1,2},{2,3},{3,4},{4,5},{5,6},{6,7},{7,8},{8,9},{9,10},{10,1... | collective-permute-start | bytes 2359304 | tf_op jit(solution)/shard_map/ppermute | solution.py:154
  71.3 26.9 %collective-permute-start.12 = (bf16[384,1024]{1,0:T(8,128)(2,1)}, bf16[384,1024]{1,0:T(8,128)(2,1)}, u32[]{:S(2)}, u32[]{:S(2)}) collective-permute-start(bf16[384,1024]{1,0:T(8,128)(2,1)} %collective-permute-done.10.refs_1_), channel_id=1, source_target_pairs={{0,15},{1,0},{2,1},{3,2},{4,3},{5,4},{6,5},{7,6},{8,7},{9,8},{10,9... | collective-permute-start | bytes 2359304 | tf_op jit(solution)/shard_map/ppermute | solution.py:154
  76.1 15.6 %collective-permute-start.4 = (bf16[16,4224]{1,0:T(8,128)(2,1)S(1)}, bf16[16,4224]{1,0:T(8,128)(2,1)S(1)}, u32[]{:S(2)}, u32[]{:S(2)}) collective-permute-start(bf16[16,4224]{1,0:T(8,128)(2,1)S(1)} %get-tuple-element.31), channel_id=1, source_target_pairs={{0,14},{1,15},{2,0},{3,1},{4,2},{5,3},{6,4},{7,5},{8,6},{9,7},{10,... | collective-permute-start | bytes 405512 | tf_op jit(solution)/shard_map/ppermute | solution.py:154
  82.5 1.6 copy-start.2
  92.7 29.8 %collective-permute-start.6 = (bf16[384,1024]{1,0:T(8,128)(2,1)}, bf16[384,1024]{1,0:T(8,128)(2,1)S(1)}, u32[]{:S(2)}, u32[]{:S(2)}) collective-permute-start(bf16[384,1024]{1,0:T(8,128)(2,1)} %collective-permute-done.3.refs_0_), channel_id=1, source_target_pairs={{0,1},{1,2},{2,3},{3,4},{4,5},{5,6},{6,7},{7,8},{8,9},{9,10},{10,1... | collective-permute-start | bytes 2359304 | tf_op jit(solution)/shard_map/ppermute | solution.py:154
  98.3 26.1 %collective-permute-start.13 = (bf16[384,1024]{1,0:T(8,128)(2,1)}, bf16[384,1024]{1,0:T(8,128)(2,1)S(1)}, u32[]{:S(2)}, u32[]{:S(2)}) collective-permute-start(bf16[384,1024]{1,0:T(8,128)(2,1)} %collective-permute-done.12.refs_1_), channel_id=1, source_target_pairs={{0,15},{1,0},{2,1},{3,2},{4,3},{5,4},{6,5},{7,6},{8,7},{9,8},{10,9... | collective-permute-start | bytes 2359304 | tf_op jit(solution)/shard_map/ppermute | solution.py:154
  100.4 22.1 %collective-permute-start.7 = (bf16[16,4224]{1,0:T(8,128)(2,1)S(1)}, bf16[16,4224]{1,0:T(8,128)(2,1)S(1)}, u32[]{:S(2)}, u32[]{:S(2)}) collective-permute-start(bf16[16,4224]{1,0:T(8,128)(2,1)S(1)} %get-tuple-element.36), channel_id=1, source_target_pairs={{0,15},{1,0},{2,1},{3,2},{4,3},{5,4},{6,5},{7,6},{8,7},{9,8},{10,9... | collective-permute-start | bytes 405512 | tf_op jit(solution)/shard_map/ppermute | solution.py:154
  105.5 17.0 %collective-permute-start.8 = (bf16[16,4224]{1,0:T(8,128)(2,1)S(1)}, bf16[16,4224]{1,0:T(8,128)(2,1)S(1)}, u32[]{:S(2)}, u32[]{:S(2)}) collective-permute-start(bf16[16,4224]{1,0:T(8,128)(2,1)S(1)} %pad_maximum_fusion.2), channel_id=1, source_target_pairs={{0,1},{1,2},{2,3},{3,4},{4,5},{5,6},{6,7},{7,8},{8,9},{9,10},{10,1... | collective-permute-start | bytes 405512 | tf_op jit(solution)/shard_map/ppermute | solution.py:154
  109.8 18.7 %copy-start.3 = (bf16[256,4096]{1,0:T(8,128)(2,1)S(1)}, bf16[256,4096]{1,0:T(8,128)(2,1)}, u32[]{:S(2)}) copy-start(bf16[256,4096]{1,0:T(8,128)(2,1)} %copy-done.1) | copy-start | bytes 6291460
  122.5 21.1 %collective-permute-start.11 = (bf16[384,1024]{1,0:T(8,128)(2,1)S(1)}, bf16[384,1024]{1,0:T(8,128)(2,1)S(1)}, u32[]{:S(2)}, u32[]{:S(2)}) collective-permute-start(bf16[384,1024]{1,0:T(8,128)(2,1)S(1)} %collective-permute-done.6.refs_0_), channel_id=1, source_target_pairs={{0,1},{1,2},{2,3},{3,4},{4,5},{5,6},{6,7},{7,8},{8,9},{9,10},{10,1... | collective-permute-start | bytes 2359304 | tf_op jit(solution)/shard_map/ppermute | solution.py:154
  124.4 19.2 %collective-permute-start.14 = (bf16[384,1024]{1,0:T(8,128)(2,1)S(1)}, bf16[384,1024]{1,0:T(8,128)(2,1)S(1)}, u32[]{:S(2)}, u32[]{:S(2)}) collective-permute-start(bf16[384,1024]{1,0:T(8,128)(2,1)S(1)} %collective-permute-done.13.refs_1_), channel_id=1, source_target_pairs={{0,15},{1,0},{2,1},{3,2},{4,3},{5,4},{6,5},{7,6},{8,7},{9,8},{10,9... | collective-permute-start | bytes 2359304 | tf_op jit(solution)/shard_map/ppermute | solution.py:154
  145.0 13.4 %collective-permute-start.15 = (bf16[16,4096]{1,0:T(8,128)(2,1)S(1)}, bf16[16,4096]{1,0:T(8,128)(2,1)S(1)}, u32[]{:S(2)}, u32[]{:S(2)}) collective-permute-start(bf16[16,4096]{1,0:T(8,128)(2,1)S(1)} %get-tuple-element.50), channel_id=1, source_target_pairs={{0,2},{1,3},{2,4},{3,5},{4,6},{5,7},{6,8},{7,9},{8,10},{9,11},{10,... | collective-permute-start | bytes 393224 | tf_op jit(solution)/shard_map/ppermute | solution.py:154
  150.5 8.1 %collective-permute-start.16 = (bf16[16,4096]{1,0:T(8,128)(2,1)S(1)}, bf16[16,4096]{1,0:T(8,128)(2,1)S(1)}, u32[]{:S(2)}, u32[]{:S(2)}) collective-permute-start(bf16[16,4096]{1,0:T(8,128)(2,1)S(1)} %get-tuple-element.51), channel_id=1, source_target_pairs={{0,1},{1,2},{2,3},{3,4},{4,5},{5,6},{6,7},{7,8},{8,9},{9,10},{10,1... | collective-permute-start | bytes 393224 | tf_op jit(solution)/shard_map/ppermute | solution.py:154
  155.5 6.9 %collective-permute-start.17 = (bf16[16,4096]{1,0:T(8,128)(2,1)S(1)}, bf16[16,4096]{1,0:T(8,128)(2,1)S(1)}, u32[]{:S(2)}, u32[]{:S(2)}) collective-permute-start(bf16[16,4096]{1,0:T(8,128)(2,1)S(1)} %get-tuple-element.52), channel_id=1, source_target_pairs={{0,15},{1,0},{2,1},{3,2},{4,3},{5,4},{6,5},{7,6},{8,7},{9,8},{10,9... | collective-permute-start | bytes 393224 | tf_op jit(solution)/shard_map/ppermute | solution.py:154

commit v8 on v6

--- a/solution.py
+++ b/solution.py
@@ -15,23 +15,10 @@
 SCALE = math.log2(math.e) / math.sqrt(HD)
 
 
-HALF = KVH // 2
-
-
-def head_of(parts, k):
-    kind, refs = parts
-    at, half = k % HALF, k // HALF
-    if kind == "cached":
-        return refs[0], k * HD, (KVH + k) * HD
-    if kind == "halves":
-        return refs[half], at * HD, (HALF + at) * HD
-    return refs[0], (2 * half * HALF + at) * HD, ((2 * half + 1) * HALF + at) * HD
-
-
-def score_group(query_of, rows, parts, cache_len, limits, out_ref, out_row):
+def score_group(query_of, rows, block, cache_len, limits, out_ref, out_row):
     visible = lax.broadcasted_iota(jnp.int32, (cache_len, GROUPS * rows), 0) <= limits
     for k in range(KVH):
-        block, key_at, value_at = head_of(parts, k)
+        key_at, value_at = k * HD, (KVH + k) * HD
         query = jnp.concatenate([query_of(k, g) for g in range(GROUPS)], axis=0)
         scores = lax.dot_general(
             block[:cache_len, key_at : key_at + HD],
@@ -55,17 +42,8 @@
             out_ref[out_row : out_row + rows, column : column + HD] = mixed[g * rows : (g + 1) * rows]
 
 
-def take(kinds, refs):
-    refs, blocks = list(refs), []
-    for kind in kinds:
-        count = 2 if kind == "halves" else 1
-        blocks.append((kind, refs[:count]))
-        del refs[:count]
-    return blocks
-
-
-def step_kernel(spots, kinds, rows, cache_len, limits_ref, query_ref, *refs):
-    blocks, out_ref = take(kinds, refs[:-1]), refs[-1]
+def step_kernel(spots, rows, cache_len, limits_ref, query_ref, *refs):
+    blocks, out_ref = refs[:-1], refs[-1]
     for i, spot in enumerate(spots):
 
         def query_of(k, g, row=spot * rows):
@@ -82,7 +60,7 @@
         def query_of(k, g, guest_ref=guest_ref):
             return guest_ref[k * rows : (k + 1) * rows, g * HD : (g + 1) * HD]
 
-        score_group(query_of, rows, ("joined", [block]), cache_len, limits, out_ref, 0)
+        score_group(query_of, rows, block, cache_len, limits, out_ref, 0)
 
 
 def place_kernel(ref_spots, rows, again, where_ref, *refs):
@@ -102,20 +80,19 @@
         copy.wait()
 
 
-def join_kernel(spots, rows, limits_ref, query_ref, first_ref, second_ref, out_ref):
-    cache_len, width = first_ref.shape
-    out_ref[:cache_len, :width] = first_ref[...]
-    out_ref[:cache_len, width:] = second_ref[...]
+def join_kernel(spots, rows, limits_ref, query_ref, block_ref, out_ref):
+    cache_len, width = block_ref.shape
+    out_ref[:cache_len, :] = block_ref[...]
     for i, spot in enumerate(spots):
         base = cache_len + i * (KVH + 1) * rows
         for k in range(KVH):
-            heads = query_ref[spot * rows : (spot + 1) * rows, 2 * k * width : 2 * (k + 1) * width]
+            heads = query_ref[spot * rows : (spot + 1) * rows, k * width : (k + 1) * width]
             out_ref[base + k * rows : base + (k + 1) * rows, :] = heads
         places = jnp.broadcast_to(limits_ref[spot : spot + 1, :], (rows, limits_ref.shape[1]))
         row = lax.broadcasted_iota(jnp.int32, places.shape, 0)
         places = jnp.where(row == 0, places >> 4, jnp.where(row == 1, places & 15, 0))
         below = base + KVH * rows
-        out_ref[below : below + rows, :] = jnp.zeros((rows, 2 * width), out_ref.dtype)
+        out_ref[below : below + rows, :] = jnp.zeros((rows, width), out_ref.dtype)
         out_ref[below : below + rows, : places.shape[1]] = places.astype(jnp.float32).astype(out_ref.dtype)
 
 
@@ -130,32 +107,30 @@
 PARAMS = pltpu.CompilerParams(vmem_limit_bytes=10 * 2**20)
 
 
-def join(limits, packed, halves, spots, rows):
-    cache_len, width = halves[0].shape
-    shape = (cache_len + len(spots) * (KVH + 1) * rows, 2 * width)
+def join(limits, packed, block, spots, rows):
+    cache_len, width = block.shape
+    shape = (cache_len + len(spots) * (KVH + 1) * rows, width)
     return pl.pallas_call(
         functools.partial(join_kernel, spots, rows),
         out_shape=jax.ShapeDtypeStruct(shape, packed.dtype),
-        in_specs=[VMEM] * 4,
+        in_specs=[VMEM] * 3,
         out_specs=VMEM,
         compiler_params=PARAMS,
         cost_estimate=pl.CostEstimate(flops=0, bytes_accessed=4 * shape[0] * shape[1], transcendentals=0),
         name="join",
-    )(limits, packed, *halves)
+    )(limits, packed, block)
 
 
 def attend_step(limits, packed, spots, blocks, rows, cache_len):
-    kinds = tuple(kind for kind, _ in blocks)
-    arrays = [a for _, arrays in blocks for a in arrays]
-    return pl.pallas_call(
-        functools.partial(step_kernel, spots, kinds, rows, cache_len),
+    return pl.pallas_call(
+        functools.partial(step_kernel, spots, rows, cache_len),
         out_shape=jax.ShapeDtypeStruct((len(spots) * rows, packed.shape[1]), packed.dtype),
-        in_specs=[VMEM] * (2 + len(arrays)),
+        in_specs=[VMEM] * (2 + len(blocks)),
         out_specs=VMEM,
         compiler_params=PARAMS,
         cost_estimate=cost(spots, rows, cache_len),
         name="attend_%d" % spots[0],
-    )(limits, packed, *arrays)
+    )(limits, packed, *blocks)
 
 
 def attend_guests(guests, block, rows, cache_len):
@@ -238,45 +213,40 @@
     mine, behind_far, ahead_far, opposite = (ring - 1,), (2 * far,), (2 * far + 1,), (2 * far + 2,)
     guest_rows = (KVH + 1) * group_rows
 
-    span, half = KVH * HD, HALF * HD
-
-    def halves_of(block):
-        return tuple(
-            jnp.concatenate([block[:, lo : lo + half], block[:, span + lo : span + lo + half]], axis=1)
-            for lo in (0, half)
-        )
-
     held, held_spots = [], []
 
     def score(spot_list, blocks):
         held.append(attend_step(limits, packed, spot_list, blocks, group_rows, cache_len))
         held_spots.append(spot_list)
 
-    up, down = shifted(kv, 1), shifted(kv, -1)
-    blocks_of = [[("cached", [up]), ("cached", [down])]]
-    up, down = halves_of(up), halves_of(down)
-    for step in (1, 2):
+    def turn(up, down, down_rows=None):
+        down, _ = tie(down, up if up is not kv else place)
+        return shifted(up, 1), shifted(down[:down_rows], -1)
+
+    up, down = kv, kv
+    blocks_of = []
+    for step in range(3):
+        if step == 1:
+            up, ordered = tie(up, ordered)
         if step == 2:
-            first, ordered = tie(up[0], ordered)
-            up = (first, up[1])
-        up = tuple(shifted(x, 1) for x in up)
-        down = tuple(shifted(x, -1) for x in down)
-        blocks_of.append([("halves", list(up)), ("halves", list(down))])
+            up, arrived = tie(up, arrived)
+        up, down = turn(up, down)
+        blocks_of.append((up, down))
     up = join(limits, packed, up, ahead_far, group_rows)
     down = join(limits, packed, down, opposite + behind_far, group_rows)
-    up, down = shifted(up, 1), shifted(down, -1)
-    blocks_of.append([("joined", [up]), ("joined", [down])])
+    up, down = turn(up, down)
+    blocks_of.append((up, down))
     ahead_guest, behind_guest = up[cache_len:], down[cache_len + guest_rows :]
-    score(mine, [("cached", [kv])])
+    score(mine, (kv,))
     score((0, 1), blocks_of[0])
+    up, held = tie(up[:cache_len], held)
+    up, down = turn(up, down, cache_len + guest_rows)
+    blocks_of.append((up, down))
+    opposite_guest = down[cache_len:]
     score((2, 3), blocks_of[1])
-    up, held = tie(up[:cache_len], held)
-    up, down = shifted(up, 1), shifted(down[: cache_len + guest_rows], -1)
-    blocks_of.append([("joined", [up]), ("joined", [down])])
-    opposite_guest = down[cache_len:]
     score((4, 5), blocks_of[2])
     up, held = tie(up, held)
-    up, down = shifted(up, 1), shifted(down[:cache_len], -1)
+    up, down = turn(up, down, cache_len)
     score((6, 7), blocks_of[3])
     score((8, 9), blocks_of[4])
     out = place_rows(where, held, held_spots, group_rows, None, packed.shape)
@@ -286,7 +256,7 @@
     (ahead_out,) = attend_guests([ahead_guest], down, group_rows, cache_len)
     ahead_out = shifted(ahead_out, -1)
     held, held_spots = [], []
-    score((2 * far - 2, 2 * far - 1), [("joined", [up]), ("joined", [down])])
+    score((2 * far - 2, 2 * far - 1), (up, down))
     out = place_rows(
         where,
         [*held, opposite_out, behind_out, ahead_out],

time: 158 us -> 160 us (1.013)
  the two profiles are of different devices: /device:TPU:4 before, /device:TPU:26 now
where the time goes in v8:
time: 160 us
  waiting for transfers between devices  69.9 us (44%)
  starting transfers between devices  65 us (41%)
  Pallas kernels  16.4 us (10%)
  matrix products  5.02 us (3%)
  local copies, waits for them, and re-layouts  1.81 us (1%)
    ppermute x15, waiting for transfers between devices, shifted(): lax.ppermute(x, 'prompt', [(i, (i + by) % ring) for i in range(ring)])  69.9 us
    ppermute x15, starting transfers between devices, shifted(): lax.ppermute(x, 'prompt', [(i, (i + by) % ring) for i in range(ring)])  57.5 us
    pallas_call x7, Pallas kernels, attend_step(): pl.pallas_call(functools.partial(step_kernel, spots, rows, cache_len), ou...  10.3 us
    all_to_all x1, starting transfers between devices, body(): lax.all_to_all(ordered.reshape(dp_count, row_count // dp_count, width), '...  7.53 us
    dot_general x2, matrix products, move_rows(): jnp.dot(pick, rows, preferred_element_type=jnp.float32).astype(rows.dtype)  5.02 us
  transfers between devices with their start and end apart: 16, of which 9 were waited for; matrix products, arithmetic and copies ran while one was open for 4% of the time, Pallas kernels for 9%

profile of v8, /device:TPU:26, one launch (start us, length us, event | category | flops | bytes accessed | tf_op | source)
XLA Modules:
  0.0 159.6 jit_solution(15140034667657192479)
XLA Ops:
  0.0 3.9 %collective-permute-start = (bf16[384,1024]{1,0:T(8,128)(2,1)}, bf16[384,1024]{1,0:T(8,128)(2,1)S(1)}, u32[]{:S(2)}, u32[]{:S(2)}) collective-permute-start(bf16[384,1024]{1,0:T(8,128)(2,1)} %bitcast.15), channel_id=1, source_target_pairs={{0,1},{1,2},{2,3},{3,4},{4,5},{5,6},{6,7},{7,8},{8,9},{9,10},{10,1... | collective-permute-start | bytes 2359304 | tf_op jit(solution)/shard_map/ppermute | solution.py:184
  4.0 9.5 %collective-permute-start.4 = (bf16[384,1024]{1,0:T(8,128)(2,1)}, bf16[384,1024]{1,0:T(8,128)(2,1)}, u32[]{:S(2)}, u32[]{:S(2)}) collective-permute-start(bf16[384,1024]{1,0:T(8,128)(2,1)} %bitcast.16), channel_id=1, source_target_pairs={{0,15},{1,0},{2,1},{3,2},{4,3},{5,4},{6,5},{7,6},{8,7},{9,8},{10,9... | collective-permute-start | bytes 2359304 | tf_op jit(solution)/shard_map/ppermute | solution.py:184
  13.5 2.7 %convolution_convert_fusion.1 = bf16[256,4096]{1,0:T(8,128)(2,1)} fusion(bf16[1,1,256,4096]{3,2,1,0:T(8,128)(2,1)S(1)} %copy-done, s32[256]{0:T(256)} %bitcast.19), kind=kOutput, calls=%fused_computation.1 | convolution fusion | flops 537985024 | bytes 4195328 | tf_op jit(solution)/shard_map/dot_general | solution.py:167
  16.2 7.5 %all-to-all-start = ((bf16[32,8,4096]{2,1,0:T(8,128)(2,1)}), bf16[32,8,4096]{2,1,0:T(8,128)(2,1)}, u32[]{:S(2)}, u32[]{:S(2)}) async-start(bf16[32,8,4096]{2,1,0:T(8,128)(2,1)} %bitcast.18), calls=%async_computation | async-start | bytes 4194304 | tf_op jit(solution)/shard_map/all_to_all | solution.py:189
  23.7 5.5 %collective-permute-done.refs_0_ = bf16[384,1024]{1,0:T(8,128)(2,1)S(1)} collective-permute-done((bf16[384,1024]{1,0:T(8,128)(2,1)}, bf16[384,1024]{1,0:T(8,128)(2,1)S(1)}, u32[]{:S(2)}, u32[]{:S(2)}) %collective-permute-start) | collective-permute-done | bytes 786464 | tf_op jit(solution)/shard_map/ppermute | solution.py:184
  29.3 1.9 %collective-permute-start.1 = (bf16[384,1024]{1,0:T(8,128)(2,1)S(1)}, bf16[384,1024]{1,0:T(8,128)(2,1)}, u32[]{:S(2)}, u32[]{:S(2)}) collective-permute-start(bf16[384,1024]{1,0:T(8,128)(2,1)S(1)} %collective-permute-done.refs_0_), channel_id=1, source_target_pairs={{0,1},{1,2},{2,3},{3,4},{4,5},{5,6},{6,7},{7,8},{8,9},{9,10},{10,1... | collective-permute-start | bytes 2359304 | tf_op jit(solution)/shard_map/ppermute | solution.py:184
  31.2 0.9 copy-done.2
  32.1 5.1 %collective-permute-start.6 = (bf16[384,1024]{1,0:T(8,128)(2,1)}, bf16[384,1024]{1,0:T(8,128)(2,1)}, u32[]{:S(2)}, u32[]{:S(2)}) collective-permute-start(bf16[384,1024]{1,0:T(8,128)(2,1)} %collective-permute-done.4.refs_1_), channel_id=1, source_target_pairs={{0,15},{1,0},{2,1},{3,2},{4,3},{5,4},{6,5},{7,6},{8,7},{9,8},{10,9... | collective-permute-start | bytes 2359304 | tf_op jit(solution)/shard_map/ppermute | solution.py:184
  37.2 0.5 broadcast.191
  37.8 0.6 reduce.3
  38.4 0.1 broadcast_in_dim.64
  38.5 0.1 select_reduce_fusion
  38.7 0.1 tile.10.limits_ref
  38.7 12.6 %collective-permute-done.1.refs_0_ = bf16[384,1024]{1,0:T(8,128)(2,1)} collective-permute-done((bf16[384,1024]{1,0:T(8,128)(2,1)S(1)}, bf16[384,1024]{1,0:T(8,128)(2,1)}, u32[]{:S(2)}, u32[]{:S(2)}) %collective-permute-start.1) | collective-permute-done | bytes 786464 | tf_op jit(solution)/shard_map/ppermute | solution.py:184
  51.3 1.9 %collective-permute-start.2 = (bf16[384,1024]{1,0:T(8,128)(2,1)}, bf16[384,1024]{1,0:T(8,128)(2,1)S(1)}, u32[]{:S(2)}, u32[]{:S(2)}) collective-permute-start(bf16[384,1024]{1,0:T(8,128)(2,1)} %collective-permute-done.1.refs_0_), channel_id=1, source_target_pairs={{0,1},{1,2},{2,3},{3,4},{4,5},{5,6},{6,7},{7,8},{8,9},{9,10},{10,1... | collective-permute-start | bytes 2359304 | tf_op jit(solution)/shard_map/ppermute | solution.py:184
  53.2 0.4 collective-permute-done.6.refs_1_
  53.6 5.6 %collective-permute-start.7 = (bf16[384,1024]{1,0:T(8,128)(2,1)}, bf16[384,1024]{1,0:T(8,128)(2,1)}, u32[]{:S(2)}, u32[]{:S(2)}) collective-permute-start(bf16[384,1024]{1,0:T(8,128)(2,1)} %collective-permute-done.6.refs_1_), channel_id=1, source_target_pairs={{0,15},{1,0},{2,1},{3,2},{4,3},{5,4},{6,5},{7,6},{8,7},{9,8},{10,9... | collective-permute-start | bytes 2359304 | tf_op jit(solution)/shard_map/ppermute | solution.py:184
  59.2 0.1 select_reduce_fusion.1
  59.3 2.3 %convolution_convert_fusion.query_ref = bf16[256,4096]{1,0:T(8,128)(2,1)S(1)} fusion(s32[256]{0:T(256)S(1)} %fusion.3, bf16[32,8,4096]{2,1,0:T(8,128)(2,1)} %all-to-all-done), kind=kOutput, calls=%fused_computation | convolution fusion | flops 537985024 | bytes 4195328 | tf_op jit(solution)/shard_map/dot_general | solution.py:167
  61.6 10.9 %collective-permute-done.2.block_ref.refs_0_ = bf16[384,1024]{1,0:T(8,128)(2,1)S(1)} collective-permute-done((bf16[384,1024]{1,0:T(8,128)(2,1)}, bf16[384,1024]{1,0:T(8,128)(2,1)S(1)}, u32[]{:S(2)}, u32[]{:S(2)}) %collective-permute-start.2) | collective-permute-done | bytes 786464 | tf_op jit(solution)/shard_map/ppermute | solution.py:184
  72.5 0.1 join.2
  72.6 2.0 %collective-permute-done.7.refs_1_.block_ref = bf16[384,1024]{1,0:T(8,128)(2,1)} collective-permute-done((bf16[384,1024]{1,0:T(8,128)(2,1)}, bf16[384,1024]{1,0:T(8,128)(2,1)}, u32[]{:S(2)}, u32[]{:S(2)}) %collective-permute-start.7) | collective-permute-done | bytes 786464 | tf_op jit(solution)/shard_map/ppermute | solution.py:184
  74.6 1.2 join.3
  75.8 5.7 %collective-permute-start.9 = (bf16[544,1024]{1,0:T(8,128)(2,1)S(1)}, bf16[544,1024]{1,0:T(8,128)(2,1)S(1)}, u32[]{:S(2)}, u32[]{:S(2)}) collective-permute-start(bf16[544,1024]{1,0:T(8,128)(2,1)S(1)} %join.3), channel_id=1, source_target_pairs={{0,15},{1,0},{2,1},{3,2},{4,3},{5,4},{6,5},{7,6},{8,7},{9,8},{10,9... | collective-permute-start | bytes 3342344 | tf_op jit(solution)/shard_map/ppermute | solution.py:184
  81.6 1.9 %collective-permute-start.3 = (bf16[464,1024]{1,0:T(8,128)(2,1)S(1)}, bf16[464,1024]{1,0:T(8,128)(2,1)S(1)}, u32[]{:S(2)}, u32[]{:S(2)}) collective-permute-start(bf16[464,1024]{1,0:T(8,128)(2,1)S(1)} %join.2), channel_id=1, source_target_pairs={{0,1},{1,2},{2,3},{3,4},{4,5},{5,6},{6,7},{7,8},{8,9},{9,10},{10,1... | collective-permute-start | bytes 2850824 | tf_op jit(solution)/shard_map/ppermute | solution.py:184
  83.5 0.6 attend_15.1.refs_0_
  84.2 2.2 %attend_0.1.refs_1_ = bf16[32,4096]{1,0:T(8,128)(2,1)S(1)} custom-call(s32[16,128]{1,0:T(8,128)S(1)} %tile.10.limits_ref, bf16[256,4096]{1,0:T(8,128)(2,1)S(1)} %convolution_convert_fusion.query_ref, bf16[384,1024]{1,0:T(8,128)(2,1)S(1)} %copy-done.3, bf16[384,1024]{1,0:T(8,128)(2,1)} %collective-permute-done.4.refs_1_), custom_call_target="tpu_custom_call" | custom-call | flops 201326592 | bytes 1048576 | tf_op jit(solution)/shard_map/attend_0/pallas_call | solution.py:125
  86.3 18.3 %collective-permute-done.3.refs_0_ = bf16[464,1024]{1,0:T(8,128)(2,1)S(1)} collective-permute-done((bf16[464,1024]{1,0:T(8,128)(2,1)S(1)}, bf16[464,1024]{1,0:T(8,128)(2,1)S(1)}, u32[]{:S(2)}, u32[]{:S(2)}) %collective-permute-start.3) | collective-permute-done | bytes 950304 | tf_op jit(solution)/shard_map/ppermute | solution.py:184
  104.8 3.7 %collective-permute-start.10 = (bf16[464,1024]{1,0:T(8,128)(2,1)S(1)}, bf16[464,1024]{1,0:T(8,128)(2,1)S(1)}, u32[]{:S(2)}, u32[]{:S(2)}) collective-permute-start(bf16[464,1024]{1,0:T(8,128)(2,1)S(1)} %slice.19), channel_id=1, source_target_pairs={{0,15},{1,0},{2,1},{3,2},{4,3},{5,4},{6,5},{7,6},{8,7},{9,8},{10,9... | collective-permute-start | bytes 2850824 | tf_op jit(solution)/shard_map/ppermute | solution.py:184
  108.5 2.1 %collective-permute-start.5 = (bf16[384,1024]{1,0:T(8,128)(2,1)S(1)}, bf16[384,1024]{1,0:T(8,128)(2,1)S(1)}, u32[]{:S(2)}, u32[]{:S(2)}) collective-permute-start(bf16[384,1024]{1,0:T(8,128)(2,1)S(1)} %slice.24), channel_id=1, source_target_pairs={{0,1},{1,2},{2,3},{3,4},{4,5},{5,6},{6,7},{7,8},{8,9},{9,10},{10,1... | collective-permute-start | bytes 2359304 | tf_op jit(solution)/shard_map/ppermute | solution.py:184
  110.6 2.4 %attend_2.1.refs_2_ = bf16[32,4096]{1,0:T(8,128)(2,1)S(1)} custom-call(s32[16,128]{1,0:T(8,128)S(1)} %tile.10.limits_ref, bf16[256,4096]{1,0:T(8,128)(2,1)S(1)} %convolution_convert_fusion.query_ref, bf16[384,1024]{1,0:T(8,128)(2,1)} %collective-permute-done.1.refs_0_, bf16[384,1024]{1,0:T(8,128)(2,1)} %collective-permute-done.6.refs_1_), custom_call_target="tpu_custom_call" | custom-call | flops 201326592 | bytes 1048576 | tf_op jit(solution)/shard_map/attend_2/pallas_call | solution.py:125
  113.0 2.2 %attend_4.1.refs_3_ = bf16[32,4096]{1,0:T(8,128)(2,1)S(1)} custom-call(s32[16,128]{1,0:T(8,128)S(1)} %tile.10.limits_ref, bf16[256,4096]{1,0:T(8,128)(2,1)S(1)} %convolution_convert_fusion.query_ref, bf16[384,1024]{1,0:T(8,128)(2,1)S(1)} %collective-permute-done.2.block_ref.refs_0_, bf16[384,1024]{1,0:T(8,128)(2,1)} %collective-permute-done.7.refs_1_.block_ref), custom_call_target="tpu_custom_call" | custom-call | flops 201326592 | bytes 1048576 | tf_op jit(solution)/shard_map/attend_4/pallas_call | solution.py:125
  115.1 11.9 %collective-permute-done.5.refs_0_ = bf16[384,1024]{1,0:T(8,128)(2,1)S(1)} collective-permute-done((bf16[384,1024]{1,0:T(8,128)(2,1)S(1)}, bf16[384,1024]{1,0:T(8,128)(2,1)S(1)}, u32[]{:S(2)}, u32[]{:S(2)}) %collective-permute-start.5) | collective-permute-done | bytes 786464 | tf_op jit(solution)/shard_map/ppermute | solution.py:184
  127.1 1.9 %collective-permute-start.8 = (bf16[384,1024]{1,0:T(8,128)(2,1)S(1)}, bf16[384,1024]{1,0:T(8,128)(2,1)S(1)}, u32[]{:S(2)}, u32[]{:S(2)}) collective-permute-start(bf16[384,1024]{1,0:T(8,128)(2,1)S(1)} %collective-permute-done.5.refs_0_), channel_id=1, source_target_pairs={{0,1},{1,2},{2,3},{3,4},{4,5},{5,6},{6,7},{7,8},{8,9},{9,10},{10,1... | collective-permute-start | bytes 2359304 | tf_op jit(solution)/shard_map/ppermute | solution.py:184
  129.1 5.1 %collective-permute-start.11 = (bf16[384,1024]{1,0:T(8,128)(2,1)S(1)}, bf16[384,1024]{1,0:T(8,128)(2,1)S(1)}, u32[]{:S(2)}, u32[]{:S(2)}) collective-permute-start(bf16[384,1024]{1,0:T(8,128)(2,1)S(1)} %slice.20), channel_id=1, source_target_pairs={{0,15},{1,0},{2,1},{3,2},{4,3},{5,4},{6,5},{7,6},{8,7},{9,8},{10,9... | collective-permute-start | bytes 2359304 | tf_op jit(solution)/shard_map/ppermute | solution.py:184
  134.2 0.1 select_reduce_fusion.2.where_ref
  134.4 1.0 attend_6.1.refs_4_
  135.4 1.0 attend_8.1.refs_5_
  136.4 1.7 %place_held.1.refs_0_ = bf16[256,4096]{1,0:T(8,128)(2,1)} custom-call(s32[16]{0:T(128)S(1)} %select_reduce_fusion.2.where_ref, bf16[16,4096]{1,0:T(8,128)(2,1)S(1)} %attend_15.1.refs_0_, bf16[32,4096]{1,0:T(8,128)(2,1)S(1)} %attend_0.1.refs_1_, bf16[32,4096]{1,0:T(8,128)(2,1)S(1)} %attend_2.1.refs_2_, bf16[32,4096]{1,0:T(8,128)(2,1)S(1)} %attend_4.1.refs_3_, ...), custom_call_target="tpu_custom_call" | custom-call | bytes 131072 | tf_op jit(solution)/shard_map/place_held/pallas_call | solution.py:151
  138.1 6.8 %collective-permute-done.8.refs_0_.block = bf16[384,1024]{1,0:T(8,128)(2,1)S(1)} collective-permute-done((bf16[384,1024]{1,0:T(8,128)(2,1)S(1)}, bf16[384,1024]{1,0:T(8,128)(2,1)S(1)}, u32[]{:S(2)}, u32[]{:S(2)}) %collective-permute-start.8) | collective-permute-done | bytes 786464 | tf_op jit(solution)/shard_map/ppermute | solution.py:184
  145.0 1.0 attend_guests.2
  146.0 1.9 %collective-permute-start.12 = (bf16[16,4096]{1,0:T(8,128)(2,1)S(1)}, bf16[16,4096]{1,0:T(8,128)(2,1)S(1)}, u32[]{:S(2)}, u32[]{:S(2)}) collective-permute-start(bf16[16,4096]{1,0:T(8,128)(2,1)S(1)} %get-tuple-element.41), channel_id=1, source_target_pairs={{0,2},{1,3},{2,4},{3,5},{4,6},{5,7},{6,8},{7,9},{8,10},{9,11},{10,... | collective-permute-start | bytes 393224 | tf_op jit(solution)/shard_map/ppermute | solution.py:184
  147.9 1.9 %collective-permute-start.13 = (bf16[16,4096]{1,0:T(8,128)(2,1)S(1)}, bf16[16,4096]{1,0:T(8,128)(2,1)S(1)}, u32[]{:S(2)}, u32[]{:S(2)}) collective-permute-start(bf16[16,4096]{1,0:T(8,128)(2,1)S(1)} %get-tuple-element.42), channel_id=1, source_target_pairs={{0,1},{1,2},{2,3},{3,4},{4,5},{5,6},{6,7},{7,8},{8,9},{9,10},{10,1... | collective-permute-start | bytes 393224 | tf_op jit(solution)/shard_map/ppermute | solution.py:184
  149.9 0.6 attend_guests.3
  150.5 5.1 %collective-permute-start.14 = (bf16[16,4096]{1,0:T(8,128)(2,1)S(1)}, bf16[16,4096]{1,0:T(8,128)(2,1)S(1)}, u32[]{:S(2)}, u32[]{:S(2)}) collective-permute-start(bf16[16,4096]{1,0:T(8,128)(2,1)S(1)} %attend_guests.3), channel_id=1, source_target_pairs={{0,15},{1,0},{2,1},{3,2},{4,3},{5,4},{6,5},{7,6},{8,7},{9,8},{10,9... | collective-permute-start | bytes 393224 | tf_op jit(solution)/shard_map/ppermute | solution.py:184
  155.6 1.0 attend_10.1.refs_1_
  156.7 1.5 collective-permute-done.14.refs_4_
  158.1 1.4 place_last.1
  (31 shorter events, 0.3 us)
Async XLA Ops:
  0.0 13.5 %copy-start = (bf16[1,1,256,4096]{3,2,1,0:T(8,128)(2,1)S(1)}, bf16[1,1,256,4096]{3,2,1,0:T(8,128)(2,1)}, u32[]{:S(2)}) copy-start(bf16[1,1,256,4096]{3,2,1,0:T(8,128)(2,1)} %param.6) | copy-start | bytes 6291460
  0.0 29.3 %collective-permute-start = (bf16[384,1024]{1,0:T(8,128)(2,1)}, bf16[384,1024]{1,0:T(8,128)(2,1)S(1)}, u32[]{:S(2)}, u32[]{:S(2)}) collective-permute-start(bf16[384,1024]{1,0:T(8,128)(2,1)} %bitcast.15), channel_id=1, source_target_pairs={{0,1},{1,2},{2,3},{3,4},{4,5},{5,6},{6,7},{7,8},{8,9},{9,10},{10,1... | collective-permute-start | bytes 2359304 | tf_op jit(solution)/shard_map/ppermute | solution.py:184
  4.0 28.1 %collective-permute-start.4 = (bf16[384,1024]{1,0:T(8,128)(2,1)}, bf16[384,1024]{1,0:T(8,128)(2,1)}, u32[]{:S(2)}, u32[]{:S(2)}) collective-permute-start(bf16[384,1024]{1,0:T(8,128)(2,1)} %bitcast.16), channel_id=1, source_target_pairs={{0,15},{1,0},{2,1},{3,2},{4,3},{5,4},{6,5},{7,6},{8,7},{9,8},{10,9... | collective-permute-start | bytes 2359304 | tf_op jit(solution)/shard_map/ppermute | solution.py:184
  16.2 21.6 %copy-start.5 = (s32[1,1,256]{2,1,0:T(1,128)S(1)}, s32[1,1,256]{2,1,0:T(1,128)}, u32[]{:S(2)}) copy-start(s32[1,1,256]{2,1,0:T(1,128)} %param.9) | copy-start | bytes 3076
  16.2 22.3 %copy-start.6 = (s32[1,1,16]{2,1,0:T(1,128)S(1)}, s32[1,1,16]{2,1,0:T(1,128)}, u32[]{:S(2)}) copy-start(s32[1,1,16]{2,1,0:T(1,128)} %param.10) | copy-start | bytes 196
  16.2 43.0 %copy-start.4 = (s32[1,1,256]{2,1,0:T(1,128)S(1)}, s32[1,1,256]{2,1,0:T(1,128)}, u32[]{:S(2)}) copy-start(s32[1,1,256]{2,1,0:T(1,128)} %param.8) | copy-start | bytes 3076
  16.2 43.1 %all-to-all-start = ((bf16[32,8,4096]{2,1,0:T(8,128)(2,1)}), bf16[32,8,4096]{2,1,0:T(8,128)(2,1)}, u32[]{:S(2)}, u32[]{:S(2)}) async-start(bf16[32,8,4096]{2,1,0:T(8,128)(2,1)} %bitcast.18), calls=%async_computation | async-start | bytes 4194304 | tf_op jit(solution)/shard_map/all_to_all | solution.py:189
  29.3 22.0 %collective-permute-start.1 = (bf16[384,1024]{1,0:T(8,128)(2,1)S(1)}, bf16[384,1024]{1,0:T(8,128)(2,1)}, u32[]{:S(2)}, u32[]{:S(2)}) collective-permute-start(bf16[384,1024]{1,0:T(8,128)(2,1)S(1)} %collective-permute-done.refs_0_), channel_id=1, source_target_pairs={{0,1},{1,2},{2,3},{3,4},{4,5},{5,6},{6,7},{7,8},{8,9},{9,10},{10,1... | collective-permute-start | bytes 2359304 | tf_op jit(solution)/shard_map/ppermute | solution.py:184
  31.2 0.9 copy-start.2
  32.1 21.5 %collective-permute-start.6 = (bf16[384,1024]{1,0:T(8,128)(2,1)}, bf16[384,1024]{1,0:T(8,128)(2,1)}, u32[]{:S(2)}, u32[]{:S(2)}) collective-permute-start(bf16[384,1024]{1,0:T(8,128)(2,1)} %collective-permute-done.4.refs_1_), channel_id=1, source_target_pairs={{0,15},{1,0},{2,1},{3,2},{4,3},{5,4},{6,5},{7,6},{8,7},{9,8},{10,9... | collective-permute-start | bytes 2359304 | tf_op jit(solution)/shard_map/ppermute | solution.py:184
  51.3 21.2 %collective-permute-start.2 = (bf16[384,1024]{1,0:T(8,128)(2,1)}, bf16[384,1024]{1,0:T(8,128)(2,1)S(1)}, u32[]{:S(2)}, u32[]{:S(2)}) collective-permute-start(bf16[384,1024]{1,0:T(8,128)(2,1)} %collective-permute-done.1.refs_0_), channel_id=1, source_target_pairs={{0,1},{1,2},{2,3},{3,4},{4,5},{5,6},{6,7},{7,8},{8,9},{9,10},{10,1... | collective-permute-start | bytes 2359304 | tf_op jit(solution)/shard_map/ppermute | solution.py:184
  53.6 21.0 %collective-permute-start.7 = (bf16[384,1024]{1,0:T(8,128)(2,1)}, bf16[384,1024]{1,0:T(8,128)(2,1)}, u32[]{:S(2)}, u32[]{:S(2)}) collective-permute-start(bf16[384,1024]{1,0:T(8,128)(2,1)} %collective-permute-done.6.refs_1_), channel_id=1, source_target_pairs={{0,15},{1,0},{2,1},{3,2},{4,3},{5,4},{6,5},{7,6},{8,7},{9,8},{10,9... | collective-permute-start | bytes 2359304 | tf_op jit(solution)/shard_map/ppermute | solution.py:184
  72.6 10.9 %copy-start.1 = (bf16[1,1,384,1024]{3,2,1,0:T(8,128)(2,1)S(1)}, bf16[1,1,384,1024]{3,2,1,0:T(8,128)(2,1)}, u32[]{:S(2)}) copy-start(bf16[1,1,384,1024]{3,2,1,0:T(8,128)(2,1)} %param.11) | copy-start | bytes 2359300
  75.8 8.3 %copy-start.3 = (bf16[384,1024]{1,0:T(8,128)(2,1)S(1)}, bf16[384,1024]{1,0:T(8,128)(2,1)}, u32[]{:S(2)}) copy-start(bf16[384,1024]{1,0:T(8,128)(2,1)} %copy-done.2) | copy-start | bytes 2359300
  75.8 28.8 %collective-permute-start.9 = (bf16[544,1024]{1,0:T(8,128)(2,1)S(1)}, bf16[544,1024]{1,0:T(8,128)(2,1)S(1)}, u32[]{:S(2)}, u32[]{:S(2)}) collective-permute-start(bf16[544,1024]{1,0:T(8,128)(2,1)S(1)} %join.3), channel_id=1, source_target_pairs={{0,15},{1,0},{2,1},{3,2},{4,3},{5,4},{6,5},{7,6},{8,7},{9,8},{10,9... | collective-permute-start | bytes 3342344 | tf_op jit(solution)/shard_map/ppermute | solution.py:184
  81.6 23.0 %collective-permute-start.3 = (bf16[464,1024]{1,0:T(8,128)(2,1)S(1)}, bf16[464,1024]{1,0:T(8,128)(2,1)S(1)}, u32[]{:S(2)}, u32[]{:S(2)}) collective-permute-start(bf16[464,1024]{1,0:T(8,128)(2,1)S(1)} %join.2), channel_id=1, source_target_pairs={{0,1},{1,2},{2,3},{3,4},{4,5},{5,6},{6,7},{7,8},{8,9},{9,10},{10,1... | collective-permute-start | bytes 2850824 | tf_op jit(solution)/shard_map/ppermute | solution.py:184
  104.8 24.3 %collective-permute-start.10 = (bf16[464,1024]{1,0:T(8,128)(2,1)S(1)}, bf16[464,1024]{1,0:T(8,128)(2,1)S(1)}, u32[]{:S(2)}, u32[]{:S(2)}) collective-permute-start(bf16[464,1024]{1,0:T(8,128)(2,1)S(1)} %slice.19), channel_id=1, source_target_pairs={{0,15},{1,0},{2,1},{3,2},{4,3},{5,4},{6,5},{7,6},{8,7},{9,8},{10,9... | collective-permute-start | bytes 2850824 | tf_op jit(solution)/shard_map/ppermute | solution.py:184
  108.5 18.6 %collective-permute-start.5 = (bf16[384,1024]{1,0:T(8,128)(2,1)S(1)}, bf16[384,1024]{1,0:T(8,128)(2,1)S(1)}, u32[]{:S(2)}, u32[]{:S(2)}) collective-permute-start(bf16[384,1024]{1,0:T(8,128)(2,1)S(1)} %slice.24), channel_id=1, source_target_pairs={{0,1},{1,2},{2,3},{3,4},{4,5},{5,6},{6,7},{7,8},{8,9},{9,10},{10,1... | collective-permute-start | bytes 2359304 | tf_op jit(solution)/shard_map/ppermute | solution.py:184
  127.1 17.9 %collective-permute-start.8 = (bf16[384,1024]{1,0:T(8,128)(2,1)S(1)}, bf16[384,1024]{1,0:T(8,128)(2,1)S(1)}, u32[]{:S(2)}, u32[]{:S(2)}) collective-permute-start(bf16[384,1024]{1,0:T(8,128)(2,1)S(1)} %collective-permute-done.5.refs_0_), channel_id=1, source_target_pairs={{0,1},{1,2},{2,3},{3,4},{4,5},{5,6},{6,7},{7,8},{8,9},{9,10},{10,1... | collective-permute-start | bytes 2359304 | tf_op jit(solution)/shard_map/ppermute | solution.py:184
  129.1 20.8 %collective-permute-start.11 = (bf16[384,1024]{1,0:T(8,128)(2,1)S(1)}, bf16[384,1024]{1,0:T(8,128)(2,1)S(1)}, u32[]{:S(2)}, u32[]{:S(2)}) collective-permute-start(bf16[384,1024]{1,0:T(8,128)(2,1)S(1)} %slice.20), channel_id=1, source_target_pairs={{0,15},{1,0},{2,1},{3,2},{4,3},{5,4},{6,5},{7,6},{8,7},{9,8},{10,9... | collective-permute-start | bytes 2359304 | tf_op jit(solution)/shard_map/ppermute | solution.py:184
  146.0 10.7 %collective-permute-start.12 = (bf16[16,4096]{1,0:T(8,128)(2,1)S(1)}, bf16[16,4096]{1,0:T(8,128)(2,1)S(1)}, u32[]{:S(2)}, u32[]{:S(2)}) collective-permute-start(bf16[16,4096]{1,0:T(8,128)(2,1)S(1)} %get-tuple-element.41), channel_id=1, source_target_pairs={{0,2},{1,3},{2,4},{3,5},{4,6},{5,7},{6,8},{7,9},{8,10},{9,11},{10,... | collective-permute-start | bytes 393224 | tf_op jit(solution)/shard_map/ppermute | solution.py:184
  147.9 8.8 %collective-permute-start.13 = (bf16[16,4096]{1,0:T(8,128)(2,1)S(1)}, bf16[16,4096]{1,0:T(8,128)(2,1)S(1)}, u32[]{:S(2)}, u32[]{:S(2)}) collective-permute-start(bf16[16,4096]{1,0:T(8,128)(2,1)S(1)} %get-tuple-element.42), channel_id=1, source_target_pairs={{0,1},{1,2},{2,3},{3,4},{4,5},{5,6},{6,7},{7,8},{8,9},{9,10},{10,1... | collective-permute-start | bytes 393224 | tf_op jit(solution)/shard_map/ppermute | solution.py:184
  150.5 7.6 %collective-permute-start.14 = (bf16[16,4096]{1,0:T(8,128)(2,1)S(1)}, bf16[16,4096]{1,0:T(8,128)(2,1)S(1)}, u32[]{:S(2)}, u32[]{:S(2)}) collective-permute-start(bf16[16,4096]{1,0:T(8,128)(2,1)S(1)} %attend_guests.3), channel_id=1, source_target_pairs={{0,15},{1,0},{2,1},{3,2},{4,3},{5,4},{6,5},{7,6},{8,7},{9,8},{10,9... | collective-permute-start | bytes 393224 | tf_op jit(solution)/shard_map/ppermute | solution.py:184

commit v9 on v4

--- a/solution.py
+++ b/solution.py
@@ -195,8 +195,9 @@
             up, ordered = tie(up, ordered)
         if step == 3:
             guests = [payload(s[0]) for s in (opposite, behind_far, ahead_far)]
+            guests[1], guests[2] = shifted(guests[1], -1), shifted(guests[2], 1)
             up, guests = tie(up, guests)
-            guests = [shifted(g, by) for g, by in zip(guests, (-2, -1, 1))]
+            guests[0] = shifted(guests[0], -2)
         if step == 4:
             score(mine, (kv,))
             score((0, 1), blocks_of[0])
@@ -212,8 +213,9 @@
     score((8, 9), blocks_of[4])
     out = place_rows(where, held, held_spots, group_rows, None, packed.shape)
     up, out = tie(up, out)
-    back = attend_guests(guests, (0, 0, 1), (up, down), group_rows)
-    back = [shifted(g, by) for g, by in zip(back, (2, 1, -1))]
+    back = attend_guests(guests[:2], (0, 0), (up,), group_rows)
+    back = [shifted(g, by) for g, by in zip(back, (2, 1))]
+    back += [shifted(g, -1) for g in attend_guests(guests[2:], (0,), (down,), group_rows)]
     held, held_spots = [], []
     score((2 * far - 2, 2 * far - 1), (up, down))
     out = place_rows(

time: 157 us -> 161 us (1.025)
  the two profiles are of different devices: /device:TPU:126 before, /device:TPU:60 now
where the time goes in v9:
time: 161 us; the launch traced here: 160 us
  starting transfers between devices  83.3 us (52%)
  waiting for transfers between devices  48.8 us (30%)
  Pallas kernels  17.1 us (11%)
  matrix products  5.02 us (3%)
  local copies, waits for them, and re-layouts  3.94 us (2%)
    ppermute x18, starting transfers between devices, shifted(): lax.ppermute(x, 'prompt', [(i, (i + by) % ring) for i in range(ring)])  75 us
    ppermute x18, waiting for transfers between devices, shifted(): lax.ppermute(x, 'prompt', [(i, (i + by) % ring) for i in range(ring)])  48.8 us
    pallas_call x7, Pallas kernels, attend_step(): pl.pallas_call(functools.partial(step_kernel, spots, rows), out_shape=jax...  12.3 us
    all_to_all x1, starting transfers between devices, body(): lax.all_to_all(ordered.reshape(dp_count, row_count // dp_count, width), '...  8.3 us
    dot_general x2, matrix products, move_rows(): jnp.dot(pick, rows, preferred_element_type=jnp.float32).astype(rows.dtype)  5.02 us
    unnamed x17, local copies, waits for them, and re-layouts  3.49 us
  transfers between devices with their start and end apart: 19, of which 7 were waited for; matrix products, arithmetic and copies ran while one was open for 4% of the time, Pallas kernels for 10%

profile of v9, /device:TPU:60, one launch (start us, length us, event | category | flops | bytes accessed | tf_op | source)
XLA Modules:
  0.0 159.7 jit_solution(7821405360098453519)
XLA Ops:
  0.0 3.9 %collective-permute-start = (bf16[384,1024]{1,0:T(8,128)(2,1)}, bf16[384,1024]{1,0:T(8,128)(2,1)}, u32[]{:S(2)}, u32[]{:S(2)}) collective-permute-start(bf16[384,1024]{1,0:T(8,128)(2,1)} %bitcast.21), channel_id=1, source_target_pairs={{0,1},{1,2},{2,3},{3,4},{4,5},{5,6},{6,7},{7,8},{8,9},{9,10},{10,1... | collective-permute-start | bytes 2359304 | tf_op jit(solution)/shard_map/ppermute | solution.py:149
  4.0 2.0 %collective-permute-start.7 = (bf16[384,1024]{1,0:T(8,128)(2,1)}, bf16[384,1024]{1,0:T(8,128)(2,1)}, u32[]{:S(2)}, u32[]{:S(2)}) collective-permute-start(bf16[384,1024]{1,0:T(8,128)(2,1)} %bitcast.22), channel_id=1, source_target_pairs={{0,15},{1,0},{2,1},{3,2},{4,3},{5,4},{6,5},{7,6},{8,7},{9,8},{10,9... | collective-permute-start | bytes 2359304 | tf_op jit(solution)/shard_map/ppermute | solution.py:149
  6.0 2.7 %convolution_convert_fusion.1 = bf16[256,4096]{1,0:T(8,128)(2,1)} fusion(bf16[1,1,256,4096]{3,2,1,0:T(8,128)(2,1)S(1)} %copy-done, s32[256]{0:T(256)} %bitcast.25), kind=kOutput, calls=%fused_computation.1 | convolution fusion | flops 537985024 | bytes 4195328 | tf_op jit(solution)/shard_map/dot_general | solution.py:132
  8.7 8.3 %all-to-all-start = ((bf16[32,8,4096]{2,1,0:T(8,128)(2,1)}), bf16[32,8,4096]{2,1,0:T(8,128)(2,1)}, u32[]{:S(2)}, u32[]{:S(2)}) async-start(bf16[32,8,4096]{2,1,0:T(8,128)(2,1)} %bitcast.24), calls=%async_computation | async-start | bytes 4194304 | tf_op jit(solution)/shard_map/all_to_all | solution.py:154
  17.0 0.6 broadcast.561
  17.6 0.6 reduce.3
  18.3 0.1 select_reduce_fusion
  18.6 0.1 tile.24
  18.7 0.1 tile.26
  18.8 2.8 %collective-permute-done.refs_0_ = bf16[384,1024]{1,0:T(8,128)(2,1)} collective-permute-done((bf16[384,1024]{1,0:T(8,128)(2,1)}, bf16[384,1024]{1,0:T(8,128)(2,1)}, u32[]{:S(2)}, u32[]{:S(2)}) %collective-permute-start) | collective-permute-done | bytes 786464 | tf_op jit(solution)/shard_map/ppermute | solution.py:149
  21.6 3.8 %collective-permute-start.1 = (bf16[384,1024]{1,0:T(8,128)(2,1)}, bf16[384,1024]{1,0:T(8,128)(2,1)}, u32[]{:S(2)}, u32[]{:S(2)}) collective-permute-start(bf16[384,1024]{1,0:T(8,128)(2,1)} %collective-permute-done.refs_0_), channel_id=1, source_target_pairs={{0,1},{1,2},{2,3},{3,4},{4,5},{5,6},{6,7},{7,8},{8,9},{9,10},{10,1... | collective-permute-start | bytes 2359304 | tf_op jit(solution)/shard_map/ppermute | solution.py:149
  25.5 7.9 %collective-permute-start.9 = (bf16[384,1024]{1,0:T(8,128)(2,1)}, bf16[384,1024]{1,0:T(8,128)(2,1)}, u32[]{:S(2)}, u32[]{:S(2)}) collective-permute-start(bf16[384,1024]{1,0:T(8,128)(2,1)} %collective-permute-done.7.refs_1_), channel_id=1, source_target_pairs={{0,15},{1,0},{2,1},{3,2},{4,3},{5,4},{6,5},{7,6},{8,7},{9,8},{10,9... | collective-permute-start | bytes 2359304 | tf_op jit(solution)/shard_map/ppermute | solution.py:149
  33.4 0.1 select_reduce_fusion.1
  33.5 15.2 %collective-permute-done.1.refs_0_ = bf16[384,1024]{1,0:T(8,128)(2,1)} collective-permute-done((bf16[384,1024]{1,0:T(8,128)(2,1)}, bf16[384,1024]{1,0:T(8,128)(2,1)}, u32[]{:S(2)}, u32[]{:S(2)}) %collective-permute-start.1) | collective-permute-done | bytes 786464 | tf_op jit(solution)/shard_map/ppermute | solution.py:149
  48.7 1.9 %collective-permute-start.2 = (bf16[384,1024]{1,0:T(8,128)(2,1)}, bf16[384,1024]{1,0:T(8,128)(2,1)}, u32[]{:S(2)}, u32[]{:S(2)}) collective-permute-start(bf16[384,1024]{1,0:T(8,128)(2,1)} %collective-permute-done.1.refs_0_), channel_id=1, source_target_pairs={{0,1},{1,2},{2,3},{3,4},{4,5},{5,6},{6,7},{7,8},{8,9},{9,10},{10,1... | collective-permute-start | bytes 2359304 | tf_op jit(solution)/shard_map/ppermute | solution.py:149
  50.6 4.9 %collective-permute-start.10 = (bf16[384,1024]{1,0:T(8,128)(2,1)}, bf16[384,1024]{1,0:T(8,128)(2,1)}, u32[]{:S(2)}, u32[]{:S(2)}) collective-permute-start(bf16[384,1024]{1,0:T(8,128)(2,1)} %collective-permute-done.9.refs_1_), channel_id=1, source_target_pairs={{0,15},{1,0},{2,1},{3,2},{4,3},{5,4},{6,5},{7,6},{8,7},{9,8},{10,9... | collective-permute-start | bytes 2359304 | tf_op jit(solution)/shard_map/ppermute | solution.py:149
  55.5 2.3 %convolution_convert_fusion.query_ref = bf16[256,4096]{1,0:T(8,128)(2,1)S(1)} fusion(bf16[32,8,4096]{2,1,0:T(8,128)(2,1)} %all-to-all-done, s32[256]{0:T(256)S(1)} %fusion.13), kind=kOutput, calls=%fused_computation | convolution fusion | flops 537985024 | bytes 4195328 | tf_op jit(solution)/shard_map/dot_general | solution.py:132
  57.8 1.3 copy-done.1
  59.2 5.1 %collective-permute-start.3 = (bf16[16,4224]{1,0:T(8,128)(2,1)S(1)}, bf16[16,4224]{1,0:T(8,128)(2,1)S(1)}, u32[]{:S(2)}, u32[]{:S(2)}) collective-permute-start(bf16[16,4224]{1,0:T(8,128)(2,1)S(1)} %pad_maximum_fusion.1), channel_id=1, source_target_pairs={{0,15},{1,0},{2,1},{3,2},{4,3},{5,4},{6,5},{7,6},{8,7},{9,8},{10,9... | collective-permute-start | bytes 405512 | tf_op jit(solution)/shard_map/ppermute | solution.py:149
  64.3 1.9 %collective-permute-start.4 = (bf16[16,4224]{1,0:T(8,128)(2,1)S(1)}, bf16[16,4224]{1,0:T(8,128)(2,1)S(1)}, u32[]{:S(2)}, u32[]{:S(2)}) collective-permute-start(bf16[16,4224]{1,0:T(8,128)(2,1)S(1)} %pad_maximum_fusion.2), channel_id=1, source_target_pairs={{0,1},{1,2},{2,3},{3,4},{4,5},{5,6},{6,7},{7,8},{8,9},{9,10},{10,1... | collective-permute-start | bytes 405512 | tf_op jit(solution)/shard_map/ppermute | solution.py:149
  66.3 7.6 %collective-permute-done.3.refs_2_ = bf16[16,4224]{1,0:T(8,128)(2,1)S(1)} collective-permute-done((bf16[16,4224]{1,0:T(8,128)(2,1)S(1)}, bf16[16,4224]{1,0:T(8,128)(2,1)S(1)}, u32[]{:S(2)}, u32[]{:S(2)}) %collective-permute-start.3) | collective-permute-done | bytes 135200 | tf_op jit(solution)/shard_map/ppermute | solution.py:149
  73.9 2.0 %collective-permute-start.5 = (bf16[384,1024]{1,0:T(8,128)(2,1)}, bf16[384,1024]{1,0:T(8,128)(2,1)}, u32[]{:S(2)}, u32[]{:S(2)}) collective-permute-start(bf16[384,1024]{1,0:T(8,128)(2,1)} %collective-permute-done.2.refs_0_), channel_id=1, source_target_pairs={{0,1},{1,2},{2,3},{3,4},{4,5},{5,6},{6,7},{7,8},{8,9},{9,10},{10,1... | collective-permute-start | bytes 2359304 | tf_op jit(solution)/shard_map/ppermute | solution.py:149
  75.9 4.7 %collective-permute-start.12 = (bf16[384,1024]{1,0:T(8,128)(2,1)}, bf16[384,1024]{1,0:T(8,128)(2,1)}, u32[]{:S(2)}, u32[]{:S(2)}) collective-permute-start(bf16[384,1024]{1,0:T(8,128)(2,1)} %collective-permute-done.10.refs_1_), channel_id=1, source_target_pairs={{0,15},{1,0},{2,1},{3,2},{4,3},{5,4},{6,5},{7,6},{8,7},{9,8},{10,9... | collective-permute-start | bytes 2359304 | tf_op jit(solution)/shard_map/ppermute | solution.py:149
  80.7 7.1 %collective-permute-start.6 = (bf16[16,4224]{1,0:T(8,128)(2,1)S(1)}, bf16[16,4224]{1,0:T(8,128)(2,1)S(1)}, u32[]{:S(2)}, u32[]{:S(2)}) collective-permute-start(bf16[16,4224]{1,0:T(8,128)(2,1)S(1)} %pad_maximum_fusion), channel_id=1, source_target_pairs={{0,14},{1,15},{2,0},{3,1},{4,2},{5,3},{6,4},{7,5},{8,6},{9,7},{10,... | collective-permute-start | bytes 405512 | tf_op jit(solution)/shard_map/ppermute | solution.py:149
  87.8 1.6 copy-done.2
  89.4 0.6 attend_15.1.refs_0_
  90.1 2.4 %attend_0.1.refs_1_ = bf16[32,4096]{1,0:T(8,128)(2,1)S(1)} custom-call(s32[16,128]{1,0:T(8,128)S(1)} %tile.28.limits_ref, bf16[256,4096]{1,0:T(8,128)(2,1)S(1)} %copy-done.2, bf16[384,1024]{1,0:T(8,128)(2,1)} %collective-permute-done.refs_0_, bf16[384,1024]{1,0:T(8,128)(2,1)} %collective-permute-done.7.refs_1_), custom_call_target="tpu_custom_call" | custom-call | flops 201326592 | bytes 1048576 | tf_op jit(solution)/shard_map/attend_0/pallas_call | solution.py:90
  92.4 8.5 %collective-permute-done.6.refs_1_ = bf16[16,4224]{1,0:T(8,128)(2,1)S(1)} collective-permute-done((bf16[16,4224]{1,0:T(8,128)(2,1)S(1)}, bf16[16,4224]{1,0:T(8,128)(2,1)S(1)}, u32[]{:S(2)}, u32[]{:S(2)}) %collective-permute-start.6) | collective-permute-done | bytes 135200 | tf_op jit(solution)/shard_map/ppermute | solution.py:149
  101.0 4.2 %collective-permute-start.8 = (bf16[384,1024]{1,0:T(8,128)(2,1)}, bf16[384,1024]{1,0:T(8,128)(2,1)S(1)}, u32[]{:S(2)}, u32[]{:S(2)}) collective-permute-start(bf16[384,1024]{1,0:T(8,128)(2,1)} %collective-permute-done.5.refs_0_), channel_id=1, source_target_pairs={{0,1},{1,2},{2,3},{3,4},{4,5},{5,6},{6,7},{7,8},{8,9},{9,10},{10,1... | collective-permute-start | bytes 2359304 | tf_op jit(solution)/shard_map/ppermute | solution.py:149
  105.2 3.3 %collective-permute-start.13 = (bf16[384,1024]{1,0:T(8,128)(2,1)}, bf16[384,1024]{1,0:T(8,128)(2,1)S(1)}, u32[]{:S(2)}, u32[]{:S(2)}) collective-permute-start(bf16[384,1024]{1,0:T(8,128)(2,1)} %collective-permute-done.12.refs_1_), channel_id=1, source_target_pairs={{0,15},{1,0},{2,1},{3,2},{4,3},{5,4},{6,5},{7,6},{8,7},{9,8},{10,9... | collective-permute-start | bytes 2359304 | tf_op jit(solution)/shard_map/ppermute | solution.py:149
  108.4 2.4 %attend_2.1.refs_2_ = bf16[32,4096]{1,0:T(8,128)(2,1)S(1)} custom-call(s32[16,128]{1,0:T(8,128)S(1)} %tile.28.limits_ref, bf16[256,4096]{1,0:T(8,128)(2,1)S(1)} %copy-done.2, bf16[384,1024]{1,0:T(8,128)(2,1)} %collective-permute-done.1.refs_0_, bf16[384,1024]{1,0:T(8,128)(2,1)} %collective-permute-done.9.refs_1_), custom_call_target="tpu_custom_call" | custom-call | flops 201326592 | bytes 1048576 | tf_op jit(solution)/shard_map/attend_2/pallas_call | solution.py:90
  110.8 2.5 %attend_4.1.refs_3_ = bf16[32,4096]{1,0:T(8,128)(2,1)S(1)} custom-call(s32[16,128]{1,0:T(8,128)S(1)} %tile.28.limits_ref, bf16[256,4096]{1,0:T(8,128)(2,1)S(1)} %copy-done.2, bf16[384,1024]{1,0:T(8,128)(2,1)} %collective-permute-done.2.refs_0_, bf16[384,1024]{1,0:T(8,128)(2,1)} %collective-permute-done.10.refs_1_), custom_call_target="tpu_custom_call" | custom-call | flops 201326592 | bytes 1048576 | tf_op jit(solution)/shard_map/attend_4/pallas_call | solution.py:90
  113.3 6.3 %collective-permute-done.8.refs_0_ = bf16[384,1024]{1,0:T(8,128)(2,1)S(1)} collective-permute-done((bf16[384,1024]{1,0:T(8,128)(2,1)}, bf16[384,1024]{1,0:T(8,128)(2,1)S(1)}, u32[]{:S(2)}, u32[]{:S(2)}) %collective-permute-start.8) | collective-permute-done | bytes 786464 | tf_op jit(solution)/shard_map/ppermute | solution.py:149
  119.6 3.5 %collective-permute-start.11 = (bf16[384,1024]{1,0:T(8,128)(2,1)S(1)}, bf16[384,1024]{1,0:T(8,128)(2,1)S(1)}, u32[]{:S(2)}, u32[]{:S(2)}) collective-permute-start(bf16[384,1024]{1,0:T(8,128)(2,1)S(1)} %collective-permute-done.8.refs_0_), channel_id=1, source_target_pairs={{0,1},{1,2},{2,3},{3,4},{4,5},{5,6},{6,7},{7,8},{8,9},{9,10},{10,1... | collective-permute-start | bytes 2359304 | tf_op jit(solution)/shard_map/ppermute | solution.py:149
  123.1 3.3 %collective-permute-start.14 = (bf16[384,1024]{1,0:T(8,128)(2,1)S(1)}, bf16[384,1024]{1,0:T(8,128)(2,1)S(1)}, u32[]{:S(2)}, u32[]{:S(2)}) collective-permute-start(bf16[384,1024]{1,0:T(8,128)(2,1)S(1)} %collective-permute-done.13.refs_1_), channel_id=1, source_target_pairs={{0,15},{1,0},{2,1},{3,2},{4,3},{5,4},{6,5},{7,6},{8,7},{9,8},{10,9... | collective-permute-start | bytes 2359304 | tf_op jit(solution)/shard_map/ppermute | solution.py:149
  126.3 0.1 select_reduce_fusion.2.where_ref
  126.5 2.4 %attend_6.1.refs_4_ = bf16[32,4096]{1,0:T(8,128)(2,1)S(1)} custom-call(s32[16,128]{1,0:T(8,128)S(1)} %tile.28.limits_ref, bf16[256,4096]{1,0:T(8,128)(2,1)S(1)} %copy-done.3, bf16[384,1024]{1,0:T(8,128)(2,1)} %collective-permute-done.5.refs_0_, bf16[384,1024]{1,0:T(8,128)(2,1)} %collective-permute-done.12.refs_1_), custom_call_target="tpu_custom_call" | custom-call | flops 201326592 | bytes 1048576 | tf_op jit(solution)/shard_map/attend_6/pallas_call | solution.py:90
  128.8 1.0 attend_8.1.refs_5_
  129.9 1.7 %place_held.1.refs_0_ = bf16[256,4096]{1,0:T(8,128)(2,1)} custom-call(s32[16]{0:T(128)S(1)} %select_reduce_fusion.2.where_ref, bf16[16,4096]{1,0:T(8,128)(2,1)S(1)} %attend_15.1.refs_0_, bf16[32,4096]{1,0:T(8,128)(2,1)S(1)} %attend_0.1.refs_1_, bf16[32,4096]{1,0:T(8,128)(2,1)S(1)} %attend_2.1.refs_2_, bf16[32,4096]{1,0:T(8,128)(2,1)S(1)} %attend_4.1.refs_3_, ...), custom_call_target="tpu_custom_call" | custom-call | bytes 131072 | tf_op jit(solution)/shard_map/place_held/pallas_call | solution.py:116
  131.6 4.5 %collective-permute-done.11.refs_0_ = bf16[384,1024]{1,0:T(8,128)(2,1)S(1)} collective-permute-done((bf16[384,1024]{1,0:T(8,128)(2,1)S(1)}, bf16[384,1024]{1,0:T(8,128)(2,1)S(1)}, u32[]{:S(2)}, u32[]{:S(2)}) %collective-permute-start.11) | collective-permute-done | bytes 786464 | tf_op jit(solution)/shard_map/ppermute | solution.py:149
  136.1 1.0 attend_guests.2
  137.2 7.8 %collective-permute-start.15 = (bf16[16,4096]{1,0:T(8,128)(2,1)S(1)}, bf16[16,4096]{1,0:T(8,128)(2,1)S(1)}, u32[]{:S(2)}, u32[]{:S(2)}) collective-permute-start(bf16[16,4096]{1,0:T(8,128)(2,1)S(1)} %get-tuple-element.42), channel_id=1, source_target_pairs={{0,2},{1,3},{2,4},{3,5},{4,6},{5,7},{6,8},{7,9},{8,10},{9,11},{10,... | collective-permute-start | bytes 393224 | tf_op jit(solution)/shard_map/ppermute | solution.py:149
  145.0 5.7 %collective-permute-start.16 = (bf16[16,4096]{1,0:T(8,128)(2,1)S(1)}, bf16[16,4096]{1,0:T(8,128)(2,1)S(1)}, u32[]{:S(2)}, u32[]{:S(2)}) collective-permute-start(bf16[16,4096]{1,0:T(8,128)(2,1)S(1)} %get-tuple-element.43), channel_id=1, source_target_pairs={{0,1},{1,2},{2,3},{3,4},{4,5},{5,6},{6,7},{7,8},{8,9},{9,10},{10,1... | collective-permute-start | bytes 393224 | tf_op jit(solution)/shard_map/ppermute | solution.py:149
  150.8 0.6 attend_guests.3
  151.4 1.9 %collective-permute-start.17 = (bf16[16,4096]{1,0:T(8,128)(2,1)S(1)}, bf16[16,4096]{1,0:T(8,128)(2,1)S(1)}, u32[]{:S(2)}, u32[]{:S(2)}) collective-permute-start(bf16[16,4096]{1,0:T(8,128)(2,1)S(1)} %attend_guests.3), channel_id=1, source_target_pairs={{0,15},{1,0},{2,1},{3,2},{4,3},{5,4},{6,5},{7,6},{8,7},{9,8},{10,9... | collective-permute-start | bytes 393224 | tf_op jit(solution)/shard_map/ppermute | solution.py:149
  153.4 1.0 attend_10.1.refs_1_
  154.4 3.9 %collective-permute-done.17.refs_4_ = bf16[16,4096]{1,0:T(8,128)(2,1)S(1)} collective-permute-done((bf16[16,4096]{1,0:T(8,128)(2,1)S(1)}, bf16[16,4096]{1,0:T(8,128)(2,1)S(1)}, u32[]{:S(2)}, u32[]{:S(2)}) %collective-permute-start.17) | collective-permute-done | bytes 131104 | tf_op jit(solution)/shard_map/ppermute | solution.py:149
  158.3 1.4 place_last.1
  (48 shorter events, 0.5 us)
Async XLA Ops:
  0.0 6.0 %copy-start = (bf16[1,1,256,4096]{3,2,1,0:T(8,128)(2,1)S(1)}, bf16[1,1,256,4096]{3,2,1,0:T(8,128)(2,1)}, u32[]{:S(2)}) copy-start(bf16[1,1,256,4096]{3,2,1,0:T(8,128)(2,1)} %param.6) | copy-start | bytes 6291460
  0.0 21.6 %collective-permute-start = (bf16[384,1024]{1,0:T(8,128)(2,1)}, bf16[384,1024]{1,0:T(8,128)(2,1)}, u32[]{:S(2)}, u32[]{:S(2)}) collective-permute-start(bf16[384,1024]{1,0:T(8,128)(2,1)} %bitcast.21), channel_id=1, source_target_pairs={{0,1},{1,2},{2,3},{3,4},{4,5},{5,6},{6,7},{7,8},{8,9},{9,10},{10,1... | collective-permute-start | bytes 2359304 | tf_op jit(solution)/shard_map/ppermute | solution.py:149
  4.0 21.5 %collective-permute-start.7 = (bf16[384,1024]{1,0:T(8,128)(2,1)}, bf16[384,1024]{1,0:T(8,128)(2,1)}, u32[]{:S(2)}, u32[]{:S(2)}) collective-permute-start(bf16[384,1024]{1,0:T(8,128)(2,1)} %bitcast.22), channel_id=1, source_target_pairs={{0,15},{1,0},{2,1},{3,2},{4,3},{5,4},{6,5},{7,6},{8,7},{9,8},{10,9... | collective-permute-start | bytes 2359304 | tf_op jit(solution)/shard_map/ppermute | solution.py:149
  8.7 8.9 %copy-start.6 = (s32[1,1,256]{2,1,0:T(1,128)S(1)}, s32[1,1,256]{2,1,0:T(1,128)}, u32[]{:S(2)}) copy-start(s32[1,1,256]{2,1,0:T(1,128)} %param.9) | copy-start | bytes 3076
  8.7 9.6 %copy-start.7 = (s32[1,1,16]{2,1,0:T(1,128)S(1)}, s32[1,1,16]{2,1,0:T(1,128)}, u32[]{:S(2)}) copy-start(s32[1,1,16]{2,1,0:T(1,128)} %param.10) | copy-start | bytes 196
  8.7 24.7 %copy-start.5 = (s32[1,1,256]{2,1,0:T(1,128)S(1)}, s32[1,1,256]{2,1,0:T(1,128)}, u32[]{:S(2)}) copy-start(s32[1,1,256]{2,1,0:T(1,128)} %param.8) | copy-start | bytes 3076
  8.7 46.8 %all-to-all-start = ((bf16[32,8,4096]{2,1,0:T(8,128)(2,1)}), bf16[32,8,4096]{2,1,0:T(8,128)(2,1)}, u32[]{:S(2)}, u32[]{:S(2)}) async-start(bf16[32,8,4096]{2,1,0:T(8,128)(2,1)} %bitcast.24), calls=%async_computation | async-start | bytes 4194304 | tf_op jit(solution)/shard_map/all_to_all | solution.py:154
  21.6 27.1 %collective-permute-start.1 = (bf16[384,1024]{1,0:T(8,128)(2,1)}, bf16[384,1024]{1,0:T(8,128)(2,1)}, u32[]{:S(2)}, u32[]{:S(2)}) collective-permute-start(bf16[384,1024]{1,0:T(8,128)(2,1)} %collective-permute-done.refs_0_), channel_id=1, source_target_pairs={{0,1},{1,2},{2,3},{3,4},{4,5},{5,6},{6,7},{7,8},{8,9},{9,10},{10,1... | collective-permute-start | bytes 2359304 | tf_op jit(solution)/shard_map/ppermute | solution.py:149
  25.5 25.1 %collective-permute-start.9 = (bf16[384,1024]{1,0:T(8,128)(2,1)}, bf16[384,1024]{1,0:T(8,128)(2,1)}, u32[]{:S(2)}, u32[]{:S(2)}) collective-permute-start(bf16[384,1024]{1,0:T(8,128)(2,1)} %collective-permute-done.7.refs_1_), channel_id=1, source_target_pairs={{0,15},{1,0},{2,1},{3,2},{4,3},{5,4},{6,5},{7,6},{8,7},{9,8},{10,9... | collective-permute-start | bytes 2359304 | tf_op jit(solution)/shard_map/ppermute | solution.py:149
  33.5 54.3 %copy-start.4 = (bf16[1,1,384,1024]{3,2,1,0:T(8,128)(2,1)S(1)}, bf16[1,1,384,1024]{3,2,1,0:T(8,128)(2,1)}, u32[]{:S(2)}) copy-start(bf16[1,1,384,1024]{3,2,1,0:T(8,128)(2,1)} %param.11) | copy-start | bytes 2359300
  48.7 25.2 %collective-permute-start.2 = (bf16[384,1024]{1,0:T(8,128)(2,1)}, bf16[384,1024]{1,0:T(8,128)(2,1)}, u32[]{:S(2)}, u32[]{:S(2)}) collective-permute-start(bf16[384,1024]{1,0:T(8,128)(2,1)} %collective-permute-done.1.refs_0_), channel_id=1, source_target_pairs={{0,1},{1,2},{2,3},{3,4},{4,5},{5,6},{6,7},{7,8},{8,9},{9,10},{10,1... | collective-permute-start | bytes 2359304 | tf_op jit(solution)/shard_map/ppermute | solution.py:149
  50.6 25.3 %collective-permute-start.10 = (bf16[384,1024]{1,0:T(8,128)(2,1)}, bf16[384,1024]{1,0:T(8,128)(2,1)}, u32[]{:S(2)}, u32[]{:S(2)}) collective-permute-start(bf16[384,1024]{1,0:T(8,128)(2,1)} %collective-permute-done.9.refs_1_), channel_id=1, source_target_pairs={{0,15},{1,0},{2,1},{3,2},{4,3},{5,4},{6,5},{7,6},{8,7},{9,8},{10,9... | collective-permute-start | bytes 2359304 | tf_op jit(solution)/shard_map/ppermute | solution.py:149
  57.8 1.3 copy-start.1
  59.2 14.7 %collective-permute-start.3 = (bf16[16,4224]{1,0:T(8,128)(2,1)S(1)}, bf16[16,4224]{1,0:T(8,128)(2,1)S(1)}, u32[]{:S(2)}, u32[]{:S(2)}) collective-permute-start(bf16[16,4224]{1,0:T(8,128)(2,1)S(1)} %pad_maximum_fusion.1), channel_id=1, source_target_pairs={{0,15},{1,0},{2,1},{3,2},{4,3},{5,4},{6,5},{7,6},{8,7},{9,8},{10,9... | collective-permute-start | bytes 405512 | tf_op jit(solution)/shard_map/ppermute | solution.py:149
  64.3 9.6 %collective-permute-start.4 = (bf16[16,4224]{1,0:T(8,128)(2,1)S(1)}, bf16[16,4224]{1,0:T(8,128)(2,1)S(1)}, u32[]{:S(2)}, u32[]{:S(2)}) collective-permute-start(bf16[16,4224]{1,0:T(8,128)(2,1)S(1)} %pad_maximum_fusion.2), channel_id=1, source_target_pairs={{0,1},{1,2},{2,3},{3,4},{4,5},{5,6},{6,7},{7,8},{8,9},{9,10},{10,1... | collective-permute-start | bytes 405512 | tf_op jit(solution)/shard_map/ppermute | solution.py:149
  73.9 27.1 %collective-permute-start.5 = (bf16[384,1024]{1,0:T(8,128)(2,1)}, bf16[384,1024]{1,0:T(8,128)(2,1)}, u32[]{:S(2)}, u32[]{:S(2)}) collective-permute-start(bf16[384,1024]{1,0:T(8,128)(2,1)} %collective-permute-done.2.refs_0_), channel_id=1, source_target_pairs={{0,1},{1,2},{2,3},{3,4},{4,5},{5,6},{6,7},{7,8},{8,9},{9,10},{10,1... | collective-permute-start | bytes 2359304 | tf_op jit(solution)/shard_map/ppermute | solution.py:149
  75.9 29.2 %collective-permute-start.12 = (bf16[384,1024]{1,0:T(8,128)(2,1)}, bf16[384,1024]{1,0:T(8,128)(2,1)}, u32[]{:S(2)}, u32[]{:S(2)}) collective-permute-start(bf16[384,1024]{1,0:T(8,128)(2,1)} %collective-permute-done.10.refs_1_), channel_id=1, source_target_pairs={{0,15},{1,0},{2,1},{3,2},{4,3},{5,4},{6,5},{7,6},{8,7},{9,8},{10,9... | collective-permute-start | bytes 2359304 | tf_op jit(solution)/shard_map/ppermute | solution.py:149
  80.7 20.3 %collective-permute-start.6 = (bf16[16,4224]{1,0:T(8,128)(2,1)S(1)}, bf16[16,4224]{1,0:T(8,128)(2,1)S(1)}, u32[]{:S(2)}, u32[]{:S(2)}) collective-permute-start(bf16[16,4224]{1,0:T(8,128)(2,1)S(1)} %pad_maximum_fusion), channel_id=1, source_target_pairs={{0,14},{1,15},{2,0},{3,1},{4,2},{5,3},{6,4},{7,5},{8,6},{9,7},{10,... | collective-permute-start | bytes 405512 | tf_op jit(solution)/shard_map/ppermute | solution.py:149
  87.8 1.6 copy-start.2
  101.0 18.6 %collective-permute-start.8 = (bf16[384,1024]{1,0:T(8,128)(2,1)}, bf16[384,1024]{1,0:T(8,128)(2,1)S(1)}, u32[]{:S(2)}, u32[]{:S(2)}) collective-permute-start(bf16[384,1024]{1,0:T(8,128)(2,1)} %collective-permute-done.5.refs_0_), channel_id=1, source_target_pairs={{0,1},{1,2},{2,3},{3,4},{4,5},{5,6},{6,7},{7,8},{8,9},{9,10},{10,1... | collective-permute-start | bytes 2359304 | tf_op jit(solution)/shard_map/ppermute | solution.py:149
  105.2 17.9 %collective-permute-start.13 = (bf16[384,1024]{1,0:T(8,128)(2,1)}, bf16[384,1024]{1,0:T(8,128)(2,1)S(1)}, u32[]{:S(2)}, u32[]{:S(2)}) collective-permute-start(bf16[384,1024]{1,0:T(8,128)(2,1)} %collective-permute-done.12.refs_1_), channel_id=1, source_target_pairs={{0,15},{1,0},{2,1},{3,2},{4,3},{5,4},{6,5},{7,6},{8,7},{9,8},{10,9... | collective-permute-start | bytes 2359304 | tf_op jit(solution)/shard_map/ppermute | solution.py:149
  110.8 15.7 %copy-start.3 = (bf16[256,4096]{1,0:T(8,128)(2,1)S(1)}, bf16[256,4096]{1,0:T(8,128)(2,1)}, u32[]{:S(2)}) copy-start(bf16[256,4096]{1,0:T(8,128)(2,1)} %copy-done.1) | copy-start | bytes 6291460
  119.6 16.6 %collective-permute-start.11 = (bf16[384,1024]{1,0:T(8,128)(2,1)S(1)}, bf16[384,1024]{1,0:T(8,128)(2,1)S(1)}, u32[]{:S(2)}, u32[]{:S(2)}) collective-permute-start(bf16[384,1024]{1,0:T(8,128)(2,1)S(1)} %collective-permute-done.8.refs_0_), channel_id=1, source_target_pairs={{0,1},{1,2},{2,3},{3,4},{4,5},{5,6},{6,7},{7,8},{8,9},{9,10},{10,1... | collective-permute-start | bytes 2359304 | tf_op jit(solution)/shard_map/ppermute | solution.py:149
  123.1 27.7 %collective-permute-start.14 = (bf16[384,1024]{1,0:T(8,128)(2,1)S(1)}, bf16[384,1024]{1,0:T(8,128)(2,1)S(1)}, u32[]{:S(2)}, u32[]{:S(2)}) collective-permute-start(bf16[384,1024]{1,0:T(8,128)(2,1)S(1)} %collective-permute-done.13.refs_1_), channel_id=1, source_target_pairs={{0,15},{1,0},{2,1},{3,2},{4,3},{5,4},{6,5},{7,6},{8,7},{9,8},{10,9... | collective-permute-start | bytes 2359304 | tf_op jit(solution)/shard_map/ppermute | solution.py:149
  137.2 17.2 %collective-permute-start.15 = (bf16[16,4096]{1,0:T(8,128)(2,1)S(1)}, bf16[16,4096]{1,0:T(8,128)(2,1)S(1)}, u32[]{:S(2)}, u32[]{:S(2)}) collective-permute-start(bf16[16,4096]{1,0:T(8,128)(2,1)S(1)} %get-tuple-element.42), channel_id=1, source_target_pairs={{0,2},{1,3},{2,4},{3,5},{4,6},{5,7},{6,8},{7,9},{8,10},{9,11},{10,... | collective-permute-start | bytes 393224 | tf_op jit(solution)/shard_map/ppermute | solution.py:149
  145.0 9.4 %collective-permute-start.16 = (bf16[16,4096]{1,0:T(8,128)(2,1)S(1)}, bf16[16,4096]{1,0:T(8,128)(2,1)S(1)}, u32[]{:S(2)}, u32[]{:S(2)}) collective-permute-start(bf16[16,4096]{1,0:T(8,128)(2,1)S(1)} %get-tuple-element.43), channel_id=1, source_target_pairs={{0,1},{1,2},{2,3},{3,4},{4,5},{5,6},{6,7},{7,8},{8,9},{9,10},{10,1... | collective-permute-start | bytes 393224 | tf_op jit(solution)/shard_map/ppermute | solution.py:149
  151.4 6.9 %collective-permute-start.17 = (bf16[16,4096]{1,0:T(8,128)(2,1)S(1)}, bf16[16,4096]{1,0:T(8,128)(2,1)S(1)}, u32[]{:S(2)}, u32[]{:S(2)}) collective-permute-start(bf16[16,4096]{1,0:T(8,128)(2,1)S(1)} %attend_guests.3), channel_id=1, source_target_pairs={{0,15},{1,0},{2,1},{3,2},{4,3},{5,4},{6,5},{7,6},{8,7},{9,8},{10,9... | collective-permute-start | bytes 393224 | tf_op jit(solution)/shard_map/ppermute | solution.py:149

commit v10 on v4

--- a/solution.py
+++ b/solution.py
@@ -212,12 +212,12 @@
     score((8, 9), blocks_of[4])
     out = place_rows(where, held, held_spots, group_rows, None, packed.shape)
     up, out = tie(up, out)
-    back = attend_guests(guests, (0, 0, 1), (up, down), group_rows)
-    back = [shifted(g, by) for g, by in zip(back, (2, 1, -1))]
+    back = attend_guests([guests[2], *guests[:2]], (1, 0, 0), (up, down), group_rows)
+    back = [shifted(g, by) for g, by in zip(back, (-1, 2, 1))]
     held, held_spots = [], []
     score((2 * far - 2, 2 * far - 1), (up, down))
     out = place_rows(
-        where, [*held, *back], [*held_spots, opposite, behind_far, ahead_far], group_rows, out, packed.shape
+        where, [*held, *back], [*held_spots, ahead_far, opposite, behind_far], group_rows, out, packed.shape
     )
     return out[None, None]
 

time: 157 us -> 160 us (1.019)
  the two profiles are of different devices: /device:TPU:126 before, /device:TPU:2 now
where the time goes in v10:
time: 160 us
  starting transfers between devices  74 us (46%)
  waiting for transfers between devices  57.5 us (36%)
  Pallas kernels  16.9 us (11%)
  matrix products  5.01 us (3%)
  local copies, waits for them, and re-layouts  3.95 us (2%)
  other arithmetic  1.83 us (1%)
    ppermute x18, starting transfers between devices, shifted(): lax.ppermute(x, 'prompt', [(i, (i + by) % ring) for i in range(ring)])  66.2 us
    ppermute x18, waiting for transfers between devices, shifted(): lax.ppermute(x, 'prompt', [(i, (i + by) % ring) for i in range(ring)])  57.5 us
    pallas_call x7, Pallas kernels, attend_step(): pl.pallas_call(functools.partial(step_kernel, spots, rows), out_shape=jax...  12.2 us
    all_to_all x1, starting transfers between devices, body(): lax.all_to_all(ordered.reshape(dp_count, row_count // dp_count, width), '...  7.81 us
    dot_general x2, matrix products, move_rows(): jnp.dot(pick, rows, preferred_element_type=jnp.float32).astype(rows.dtype)  5.01 us
    unnamed x17, local copies, waits for them, and re-layouts  3.5 us
  transfers between devices with their start and end apart: 19, of which 10 were waited for; matrix products, arithmetic and copies ran while one was open for 5% of the time, Pallas kernels for 9%

profile of v10, /device:TPU:2, one launch (start us, length us, event | category | flops | bytes accessed | tf_op | source)
XLA Modules:
  0.0 159.6 jit_solution(7593766860286797791)
XLA Ops:
  0.0 3.9 %collective-permute-start = (bf16[384,1024]{1,0:T(8,128)(2,1)}, bf16[384,1024]{1,0:T(8,128)(2,1)}, u32[]{:S(2)}, u32[]{:S(2)}) collective-permute-start(bf16[384,1024]{1,0:T(8,128)(2,1)} %bitcast.21), channel_id=1, source_target_pairs={{0,1},{1,2},{2,3},{3,4},{4,5},{5,6},{6,7},{7,8},{8,9},{9,10},{10,1... | collective-permute-start | bytes 2359304 | tf_op jit(solution)/shard_map/ppermute | solution.py:149
  4.0 9.5 %collective-permute-start.7 = (bf16[384,1024]{1,0:T(8,128)(2,1)}, bf16[384,1024]{1,0:T(8,128)(2,1)}, u32[]{:S(2)}, u32[]{:S(2)}) collective-permute-start(bf16[384,1024]{1,0:T(8,128)(2,1)} %bitcast.22), channel_id=1, source_target_pairs={{0,15},{1,0},{2,1},{3,2},{4,3},{5,4},{6,5},{7,6},{8,7},{9,8},{10,9... | collective-permute-start | bytes 2359304 | tf_op jit(solution)/shard_map/ppermute | solution.py:149
  13.5 2.7 %convolution_convert_fusion.1 = bf16[256,4096]{1,0:T(8,128)(2,1)} fusion(bf16[1,1,256,4096]{3,2,1,0:T(8,128)(2,1)S(1)} %copy-done, s32[256]{0:T(256)} %bitcast.25), kind=kOutput, calls=%fused_computation.1 | convolution fusion | flops 537985024 | bytes 4195328 | tf_op jit(solution)/shard_map/dot_general | solution.py:132
  16.2 7.8 %all-to-all-start = ((bf16[32,8,4096]{2,1,0:T(8,128)(2,1)}), bf16[32,8,4096]{2,1,0:T(8,128)(2,1)}, u32[]{:S(2)}, u32[]{:S(2)}) async-start(bf16[32,8,4096]{2,1,0:T(8,128)(2,1)} %bitcast.24), calls=%async_computation | async-start | bytes 4194304 | tf_op jit(solution)/shard_map/all_to_all | solution.py:154
  24.0 0.6 broadcast.561
  24.6 0.6 reduce.3
  25.4 0.1 select_reduce_fusion
  25.8 3.5 %collective-permute-done.refs_0_ = bf16[384,1024]{1,0:T(8,128)(2,1)} collective-permute-done((bf16[384,1024]{1,0:T(8,128)(2,1)}, bf16[384,1024]{1,0:T(8,128)(2,1)}, u32[]{:S(2)}, u32[]{:S(2)}) %collective-permute-start) | collective-permute-done | bytes 786464 | tf_op jit(solution)/shard_map/ppermute | solution.py:149
  29.4 1.9 %collective-permute-start.1 = (bf16[384,1024]{1,0:T(8,128)(2,1)}, bf16[384,1024]{1,0:T(8,128)(2,1)}, u32[]{:S(2)}, u32[]{:S(2)}) collective-permute-start(bf16[384,1024]{1,0:T(8,128)(2,1)} %collective-permute-done.refs_0_), channel_id=1, source_target_pairs={{0,1},{1,2},{2,3},{3,4},{4,5},{5,6},{6,7},{7,8},{8,9},{9,10},{10,1... | collective-permute-start | bytes 2359304 | tf_op jit(solution)/shard_map/ppermute | solution.py:149
  31.3 5.1 %collective-permute-start.9 = (bf16[384,1024]{1,0:T(8,128)(2,1)}, bf16[384,1024]{1,0:T(8,128)(2,1)}, u32[]{:S(2)}, u32[]{:S(2)}) collective-permute-start(bf16[384,1024]{1,0:T(8,128)(2,1)} %collective-permute-done.7.refs_1_), channel_id=1, source_target_pairs={{0,15},{1,0},{2,1},{3,2},{4,3},{5,4},{6,5},{7,6},{8,7},{9,8},{10,9... | collective-permute-start | bytes 2359304 | tf_op jit(solution)/shard_map/ppermute | solution.py:149
  36.6 14.9 %collective-permute-done.1.refs_0_ = bf16[384,1024]{1,0:T(8,128)(2,1)} collective-permute-done((bf16[384,1024]{1,0:T(8,128)(2,1)}, bf16[384,1024]{1,0:T(8,128)(2,1)}, u32[]{:S(2)}, u32[]{:S(2)}) %collective-permute-start.1) | collective-permute-done | bytes 786464 | tf_op jit(solution)/shard_map/ppermute | solution.py:149
  51.5 1.9 %collective-permute-start.2 = (bf16[384,1024]{1,0:T(8,128)(2,1)}, bf16[384,1024]{1,0:T(8,128)(2,1)}, u32[]{:S(2)}, u32[]{:S(2)}) collective-permute-start(bf16[384,1024]{1,0:T(8,128)(2,1)} %collective-permute-done.1.refs_0_), channel_id=1, source_target_pairs={{0,1},{1,2},{2,3},{3,4},{4,5},{5,6},{6,7},{7,8},{8,9},{9,10},{10,1... | collective-permute-start | bytes 2359304 | tf_op jit(solution)/shard_map/ppermute | solution.py:149
  53.4 5.1 %collective-permute-start.10 = (bf16[384,1024]{1,0:T(8,128)(2,1)}, bf16[384,1024]{1,0:T(8,128)(2,1)}, u32[]{:S(2)}, u32[]{:S(2)}) collective-permute-start(bf16[384,1024]{1,0:T(8,128)(2,1)} %collective-permute-done.9.refs_1_), channel_id=1, source_target_pairs={{0,15},{1,0},{2,1},{3,2},{4,3},{5,4},{6,5},{7,6},{8,7},{9,8},{10,9... | collective-permute-start | bytes 2359304 | tf_op jit(solution)/shard_map/ppermute | solution.py:149
  58.6 2.3 %convolution_convert_fusion.query_ref = bf16[256,4096]{1,0:T(8,128)(2,1)S(1)} fusion(bf16[32,8,4096]{2,1,0:T(8,128)(2,1)} %all-to-all-done, s32[256]{0:T(256)S(1)} %fusion.13), kind=kOutput, calls=%fused_computation | convolution fusion | flops 537985024 | bytes 4195328 | tf_op jit(solution)/shard_map/dot_general | solution.py:132
  61.0 1.3 copy-done.1
  62.3 0.7 pad_maximum_fusion
  63.0 9.7 %collective-permute-done.2.refs_0_ = bf16[384,1024]{1,0:T(8,128)(2,1)} collective-permute-done((bf16[384,1024]{1,0:T(8,128)(2,1)}, bf16[384,1024]{1,0:T(8,128)(2,1)}, u32[]{:S(2)}, u32[]{:S(2)}) %collective-permute-start.2) | collective-permute-done | bytes 786464 | tf_op jit(solution)/shard_map/ppermute | solution.py:149
  72.7 1.9 %collective-permute-start.3 = (bf16[384,1024]{1,0:T(8,128)(2,1)}, bf16[384,1024]{1,0:T(8,128)(2,1)}, u32[]{:S(2)}, u32[]{:S(2)}) collective-permute-start(bf16[384,1024]{1,0:T(8,128)(2,1)} %collective-permute-done.2.refs_0_), channel_id=1, source_target_pairs={{0,1},{1,2},{2,3},{3,4},{4,5},{5,6},{6,7},{7,8},{8,9},{9,10},{10,1... | collective-permute-start | bytes 2359304 | tf_op jit(solution)/shard_map/ppermute | solution.py:149
  74.7 5.1 %collective-permute-start.12 = (bf16[384,1024]{1,0:T(8,128)(2,1)}, bf16[384,1024]{1,0:T(8,128)(2,1)}, u32[]{:S(2)}, u32[]{:S(2)}) collective-permute-start(bf16[384,1024]{1,0:T(8,128)(2,1)} %collective-permute-done.10.refs_1_), channel_id=1, source_target_pairs={{0,15},{1,0},{2,1},{3,2},{4,3},{5,4},{6,5},{7,6},{8,7},{9,8},{10,9... | collective-permute-start | bytes 2359304 | tf_op jit(solution)/shard_map/ppermute | solution.py:149
  79.8 1.9 %collective-permute-start.4 = (bf16[16,4224]{1,0:T(8,128)(2,1)}, bf16[16,4224]{1,0:T(8,128)(2,1)S(1)}, u32[]{:S(2)}, u32[]{:S(2)}) collective-permute-start(bf16[16,4224]{1,0:T(8,128)(2,1)} %get-tuple-element.28), channel_id=1, source_target_pairs={{0,14},{1,15},{2,0},{3,1},{4,2},{5,3},{6,4},{7,5},{8,6},{9,7},{10,... | collective-permute-start | bytes 405512 | tf_op jit(solution)/shard_map/ppermute | solution.py:149
  81.7 3.4 %collective-permute-start.5 = (bf16[16,4224]{1,0:T(8,128)(2,1)}, bf16[16,4224]{1,0:T(8,128)(2,1)S(1)}, u32[]{:S(2)}, u32[]{:S(2)}) collective-permute-start(bf16[16,4224]{1,0:T(8,128)(2,1)} %get-tuple-element.29), channel_id=1, source_target_pairs={{0,15},{1,0},{2,1},{3,2},{4,3},{5,4},{6,5},{7,6},{8,7},{9,8},{10,9... | collective-permute-start | bytes 405512 | tf_op jit(solution)/shard_map/ppermute | solution.py:149
  85.2 2.4 %collective-permute-start.6 = (bf16[16,4224]{1,0:T(8,128)(2,1)S(1)}, bf16[16,4224]{1,0:T(8,128)(2,1)S(1)}, u32[]{:S(2)}, u32[]{:S(2)}) collective-permute-start(bf16[16,4224]{1,0:T(8,128)(2,1)S(1)} %pad_maximum_fusion.2), channel_id=1, source_target_pairs={{0,1},{1,2},{2,3},{3,4},{4,5},{5,6},{6,7},{7,8},{8,9},{9,10},{10,1... | collective-permute-start | bytes 405512 | tf_op jit(solution)/shard_map/ppermute | solution.py:149
  87.7 1.6 copy-done.2
  89.3 0.6 attend_15.1.refs_0_
  89.9 2.4 %attend_0.1.refs_1_ = bf16[32,4096]{1,0:T(8,128)(2,1)S(1)} custom-call(s32[16,128]{1,0:T(8,128)S(1)} %tile.28.limits_ref, bf16[256,4096]{1,0:T(8,128)(2,1)S(1)} %copy-done.2, bf16[384,1024]{1,0:T(8,128)(2,1)} %collective-permute-done.refs_0_, bf16[384,1024]{1,0:T(8,128)(2,1)} %collective-permute-done.7.refs_1_), custom_call_target="tpu_custom_call" | custom-call | flops 201326592 | bytes 1048576 | tf_op jit(solution)/shard_map/attend_0/pallas_call | solution.py:90
  92.3 9.2 %collective-permute-done.4.refs_3_ = bf16[16,4224]{1,0:T(8,128)(2,1)S(1)} collective-permute-done((bf16[16,4224]{1,0:T(8,128)(2,1)}, bf16[16,4224]{1,0:T(8,128)(2,1)S(1)}, u32[]{:S(2)}, u32[]{:S(2)}) %collective-permute-start.4) | collective-permute-done | bytes 135200 | tf_op jit(solution)/shard_map/ppermute | solution.py:149
  101.5 1.4 collective-permute-done.5.refs_4_
  102.9 1.9 %collective-permute-start.8 = (bf16[384,1024]{1,0:T(8,128)(2,1)}, bf16[384,1024]{1,0:T(8,128)(2,1)S(1)}, u32[]{:S(2)}, u32[]{:S(2)}) collective-permute-start(bf16[384,1024]{1,0:T(8,128)(2,1)} %collective-permute-done.3.refs_0_), channel_id=1, source_target_pairs={{0,1},{1,2},{2,3},{3,4},{4,5},{5,6},{6,7},{7,8},{8,9},{9,10},{10,1... | collective-permute-start | bytes 2359304 | tf_op jit(solution)/shard_map/ppermute | solution.py:149
  104.8 5.5 %collective-permute-start.13 = (bf16[384,1024]{1,0:T(8,128)(2,1)}, bf16[384,1024]{1,0:T(8,128)(2,1)S(1)}, u32[]{:S(2)}, u32[]{:S(2)}) collective-permute-start(bf16[384,1024]{1,0:T(8,128)(2,1)} %collective-permute-done.12.refs_1_), channel_id=1, source_target_pairs={{0,15},{1,0},{2,1},{3,2},{4,3},{5,4},{6,5},{7,6},{8,7},{9,8},{10,9... | collective-permute-start | bytes 2359304 | tf_op jit(solution)/shard_map/ppermute | solution.py:149
  110.3 2.4 %attend_2.1.refs_2_ = bf16[32,4096]{1,0:T(8,128)(2,1)S(1)} custom-call(s32[16,128]{1,0:T(8,128)S(1)} %tile.28.limits_ref, bf16[256,4096]{1,0:T(8,128)(2,1)S(1)} %copy-done.2, bf16[384,1024]{1,0:T(8,128)(2,1)} %collective-permute-done.1.refs_0_, bf16[384,1024]{1,0:T(8,128)(2,1)} %collective-permute-done.9.refs_1_), custom_call_target="tpu_custom_call" | custom-call | flops 201326592 | bytes 1048576 | tf_op jit(solution)/shard_map/attend_2/pallas_call | solution.py:90
  112.7 2.5 %attend_4.1.refs_3_ = bf16[32,4096]{1,0:T(8,128)(2,1)S(1)} custom-call(s32[16,128]{1,0:T(8,128)S(1)} %tile.28.limits_ref, bf16[256,4096]{1,0:T(8,128)(2,1)S(1)} %copy-done.2, bf16[384,1024]{1,0:T(8,128)(2,1)} %collective-permute-done.2.refs_0_, bf16[384,1024]{1,0:T(8,128)(2,1)} %collective-permute-done.10.refs_1_), custom_call_target="tpu_custom_call" | custom-call | flops 201326592 | bytes 1048576 | tf_op jit(solution)/shard_map/attend_4/pallas_call | solution.py:90
  115.2 6.3 %collective-permute-done.8.refs_0_ = bf16[384,1024]{1,0:T(8,128)(2,1)S(1)} collective-permute-done((bf16[384,1024]{1,0:T(8,128)(2,1)}, bf16[384,1024]{1,0:T(8,128)(2,1)S(1)}, u32[]{:S(2)}, u32[]{:S(2)}) %collective-permute-start.8) | collective-permute-done | bytes 786464 | tf_op jit(solution)/shard_map/ppermute | solution.py:149
  121.5 1.9 %collective-permute-start.11 = (bf16[384,1024]{1,0:T(8,128)(2,1)S(1)}, bf16[384,1024]{1,0:T(8,128)(2,1)S(1)}, u32[]{:S(2)}, u32[]{:S(2)}) collective-permute-start(bf16[384,1024]{1,0:T(8,128)(2,1)S(1)} %collective-permute-done.8.refs_0_), channel_id=1, source_target_pairs={{0,1},{1,2},{2,3},{3,4},{4,5},{5,6},{6,7},{7,8},{8,9},{9,10},{10,1... | collective-permute-start | bytes 2359304 | tf_op jit(solution)/shard_map/ppermute | solution.py:149
  123.5 5.1 %collective-permute-start.14 = (bf16[384,1024]{1,0:T(8,128)(2,1)S(1)}, bf16[384,1024]{1,0:T(8,128)(2,1)S(1)}, u32[]{:S(2)}, u32[]{:S(2)}) collective-permute-start(bf16[384,1024]{1,0:T(8,128)(2,1)S(1)} %collective-permute-done.13.refs_1_), channel_id=1, source_target_pairs={{0,15},{1,0},{2,1},{3,2},{4,3},{5,4},{6,5},{7,6},{8,7},{9,8},{10,9... | collective-permute-start | bytes 2359304 | tf_op jit(solution)/shard_map/ppermute | solution.py:149
  128.6 0.1 select_reduce_fusion.2.where_ref
  128.7 2.4 %attend_6.1.refs_4_ = bf16[32,4096]{1,0:T(8,128)(2,1)S(1)} custom-call(s32[16,128]{1,0:T(8,128)S(1)} %tile.28.limits_ref, bf16[256,4096]{1,0:T(8,128)(2,1)S(1)} %copy-done.3, bf16[384,1024]{1,0:T(8,128)(2,1)} %collective-permute-done.3.refs_0_, bf16[384,1024]{1,0:T(8,128)(2,1)} %collective-permute-done.12.refs_1_), custom_call_target="tpu_custom_call" | custom-call | flops 201326592 | bytes 1048576 | tf_op jit(solution)/shard_map/attend_6/pallas_call | solution.py:90
  131.1 1.0 attend_8.1.refs_5_
  132.1 1.7 %place_held.1.refs_0_ = bf16[256,4096]{1,0:T(8,128)(2,1)} custom-call(s32[16]{0:T(128)S(1)} %select_reduce_fusion.2.where_ref, bf16[16,4096]{1,0:T(8,128)(2,1)S(1)} %attend_15.1.refs_0_, bf16[32,4096]{1,0:T(8,128)(2,1)S(1)} %attend_0.1.refs_1_, bf16[32,4096]{1,0:T(8,128)(2,1)S(1)} %attend_2.1.refs_2_, bf16[32,4096]{1,0:T(8,128)(2,1)S(1)} %attend_4.1.refs_3_, ...), custom_call_target="tpu_custom_call" | custom-call | bytes 131072 | tf_op jit(solution)/shard_map/place_held/pallas_call | solution.py:116
  133.9 4.8 %collective-permute-done.11.refs_0_ = bf16[384,1024]{1,0:T(8,128)(2,1)S(1)} collective-permute-done((bf16[384,1024]{1,0:T(8,128)(2,1)S(1)}, bf16[384,1024]{1,0:T(8,128)(2,1)S(1)}, u32[]{:S(2)}, u32[]{:S(2)}) %collective-permute-start.11) | collective-permute-done | bytes 786464 | tf_op jit(solution)/shard_map/ppermute | solution.py:149
  138.7 1.2 collective-permute-done.14.refs_1_
  139.9 1.5 attend_guests.1
  141.3 5.6 %collective-permute-start.15 = (bf16[16,4096]{1,0:T(8,128)(2,1)S(1)}, bf16[16,4096]{1,0:T(8,128)(2,1)S(1)}, u32[]{:S(2)}, u32[]{:S(2)}) collective-permute-start(bf16[16,4096]{1,0:T(8,128)(2,1)S(1)} %get-tuple-element.44), channel_id=1, source_target_pairs={{0,15},{1,0},{2,1},{3,2},{4,3},{5,4},{6,5},{7,6},{8,7},{9,8},{10,9... | collective-permute-start | bytes 393224 | tf_op jit(solution)/shard_map/ppermute | solution.py:149
  147.0 1.9 %collective-permute-start.16 = (bf16[16,4096]{1,0:T(8,128)(2,1)S(1)}, bf16[16,4096]{1,0:T(8,128)(2,1)S(1)}, u32[]{:S(2)}, u32[]{:S(2)}) collective-permute-start(bf16[16,4096]{1,0:T(8,128)(2,1)S(1)} %get-tuple-element.45), channel_id=1, source_target_pairs={{0,2},{1,3},{2,4},{3,5},{4,6},{5,7},{6,8},{7,9},{8,10},{9,11},{10,... | collective-permute-start | bytes 393224 | tf_op jit(solution)/shard_map/ppermute | solution.py:149
  148.9 1.9 %collective-permute-start.17 = (bf16[16,4096]{1,0:T(8,128)(2,1)S(1)}, bf16[16,4096]{1,0:T(8,128)(2,1)S(1)}, u32[]{:S(2)}, u32[]{:S(2)}) collective-permute-start(bf16[16,4096]{1,0:T(8,128)(2,1)S(1)} %get-tuple-element.46), channel_id=1, source_target_pairs={{0,1},{1,2},{2,3},{3,4},{4,5},{5,6},{6,7},{7,8},{8,9},{9,10},{10,1... | collective-permute-start | bytes 393224 | tf_op jit(solution)/shard_map/ppermute | solution.py:149
  150.8 1.0 attend_10.1.refs_1_
  151.8 5.1 %collective-permute-done.16.refs_3_ = bf16[16,4096]{1,0:T(8,128)(2,1)S(1)} collective-permute-done((bf16[16,4096]{1,0:T(8,128)(2,1)S(1)}, bf16[16,4096]{1,0:T(8,128)(2,1)S(1)}, u32[]{:S(2)}, u32[]{:S(2)}) %collective-permute-start.16) | collective-permute-done | bytes 131104 | tf_op jit(solution)/shard_map/ppermute | solution.py:149
  156.9 1.3 collective-permute-done.17.refs_4_
  158.2 1.4 place_last.1
  (46 shorter events, 0.7 us)
Async XLA Ops:
  0.0 13.5 %copy-start = (bf16[1,1,256,4096]{3,2,1,0:T(8,128)(2,1)S(1)}, bf16[1,1,256,4096]{3,2,1,0:T(8,128)(2,1)}, u32[]{:S(2)}) copy-start(bf16[1,1,256,4096]{3,2,1,0:T(8,128)(2,1)} %param.6) | copy-start | bytes 6291460
  0.0 29.4 %collective-permute-start = (bf16[384,1024]{1,0:T(8,128)(2,1)}, bf16[384,1024]{1,0:T(8,128)(2,1)}, u32[]{:S(2)}, u32[]{:S(2)}) collective-permute-start(bf16[384,1024]{1,0:T(8,128)(2,1)} %bitcast.21), channel_id=1, source_target_pairs={{0,1},{1,2},{2,3},{3,4},{4,5},{5,6},{6,7},{7,8},{8,9},{9,10},{10,1... | collective-permute-start | bytes 2359304 | tf_op jit(solution)/shard_map/ppermute | solution.py:149
  4.0 27.3 %collective-permute-start.7 = (bf16[384,1024]{1,0:T(8,128)(2,1)}, bf16[384,1024]{1,0:T(8,128)(2,1)}, u32[]{:S(2)}, u32[]{:S(2)}) collective-permute-start(bf16[384,1024]{1,0:T(8,128)(2,1)} %bitcast.22), channel_id=1, source_target_pairs={{0,15},{1,0},{2,1},{3,2},{4,3},{5,4},{6,5},{7,6},{8,7},{9,8},{10,9... | collective-permute-start | bytes 2359304 | tf_op jit(solution)/shard_map/ppermute | solution.py:149
  16.2 8.4 %copy-start.6 = (s32[1,1,256]{2,1,0:T(1,128)S(1)}, s32[1,1,256]{2,1,0:T(1,128)}, u32[]{:S(2)}) copy-start(s32[1,1,256]{2,1,0:T(1,128)} %param.9) | copy-start | bytes 3076
  16.2 9.1 %copy-start.7 = (s32[1,1,16]{2,1,0:T(1,128)S(1)}, s32[1,1,16]{2,1,0:T(1,128)}, u32[]{:S(2)}) copy-start(s32[1,1,16]{2,1,0:T(1,128)} %param.10) | copy-start | bytes 196
  16.2 20.3 %copy-start.5 = (s32[1,1,256]{2,1,0:T(1,128)S(1)}, s32[1,1,256]{2,1,0:T(1,128)}, u32[]{:S(2)}) copy-start(s32[1,1,256]{2,1,0:T(1,128)} %param.8) | copy-start | bytes 3076
  16.2 42.4 %all-to-all-start = ((bf16[32,8,4096]{2,1,0:T(8,128)(2,1)}), bf16[32,8,4096]{2,1,0:T(8,128)(2,1)}, u32[]{:S(2)}, u32[]{:S(2)}) async-start(bf16[32,8,4096]{2,1,0:T(8,128)(2,1)} %bitcast.24), calls=%async_computation | async-start | bytes 4194304 | tf_op jit(solution)/shard_map/all_to_all | solution.py:154
  29.4 22.1 %collective-permute-start.1 = (bf16[384,1024]{1,0:T(8,128)(2,1)}, bf16[384,1024]{1,0:T(8,128)(2,1)}, u32[]{:S(2)}, u32[]{:S(2)}) collective-permute-start(bf16[384,1024]{1,0:T(8,128)(2,1)} %collective-permute-done.refs_0_), channel_id=1, source_target_pairs={{0,1},{1,2},{2,3},{3,4},{4,5},{5,6},{6,7},{7,8},{8,9},{9,10},{10,1... | collective-permute-start | bytes 2359304 | tf_op jit(solution)/shard_map/ppermute | solution.py:149
  31.3 22.1 %collective-permute-start.9 = (bf16[384,1024]{1,0:T(8,128)(2,1)}, bf16[384,1024]{1,0:T(8,128)(2,1)}, u32[]{:S(2)}, u32[]{:S(2)}) collective-permute-start(bf16[384,1024]{1,0:T(8,128)(2,1)} %collective-permute-done.7.refs_1_), channel_id=1, source_target_pairs={{0,15},{1,0},{2,1},{3,2},{4,3},{5,4},{6,5},{7,6},{8,7},{9,8},{10,9... | collective-permute-start | bytes 2359304 | tf_op jit(solution)/shard_map/ppermute | solution.py:149
  36.6 51.1 %copy-start.4 = (bf16[1,1,384,1024]{3,2,1,0:T(8,128)(2,1)S(1)}, bf16[1,1,384,1024]{3,2,1,0:T(8,128)(2,1)}, u32[]{:S(2)}) copy-start(bf16[1,1,384,1024]{3,2,1,0:T(8,128)(2,1)} %param.11) | copy-start | bytes 2359300
  51.5 21.2 %collective-permute-start.2 = (bf16[384,1024]{1,0:T(8,128)(2,1)}, bf16[384,1024]{1,0:T(8,128)(2,1)}, u32[]{:S(2)}, u32[]{:S(2)}) collective-permute-start(bf16[384,1024]{1,0:T(8,128)(2,1)} %collective-permute-done.1.refs_0_), channel_id=1, source_target_pairs={{0,1},{1,2},{2,3},{3,4},{4,5},{5,6},{6,7},{7,8},{8,9},{9,10},{10,1... | collective-permute-start | bytes 2359304 | tf_op jit(solution)/shard_map/ppermute | solution.py:149
  53.4 21.2 %collective-permute-start.10 = (bf16[384,1024]{1,0:T(8,128)(2,1)}, bf16[384,1024]{1,0:T(8,128)(2,1)}, u32[]{:S(2)}, u32[]{:S(2)}) collective-permute-start(bf16[384,1024]{1,0:T(8,128)(2,1)} %collective-permute-done.9.refs_1_), channel_id=1, source_target_pairs={{0,15},{1,0},{2,1},{3,2},{4,3},{5,4},{6,5},{7,6},{8,7},{9,8},{10,9... | collective-permute-start | bytes 2359304 | tf_op jit(solution)/shard_map/ppermute | solution.py:149
  60.9 1.3 copy-start.1
  72.7 30.2 %collective-permute-start.3 = (bf16[384,1024]{1,0:T(8,128)(2,1)}, bf16[384,1024]{1,0:T(8,128)(2,1)}, u32[]{:S(2)}, u32[]{:S(2)}) collective-permute-start(bf16[384,1024]{1,0:T(8,128)(2,1)} %collective-permute-done.2.refs_0_), channel_id=1, source_target_pairs={{0,1},{1,2},{2,3},{3,4},{4,5},{5,6},{6,7},{7,8},{8,9},{9,10},{10,1... | collective-permute-start | bytes 2359304 | tf_op jit(solution)/shard_map/ppermute | solution.py:149
  74.7 30.2 %collective-permute-start.12 = (bf16[384,1024]{1,0:T(8,128)(2,1)}, bf16[384,1024]{1,0:T(8,128)(2,1)}, u32[]{:S(2)}, u32[]{:S(2)}) collective-permute-start(bf16[384,1024]{1,0:T(8,128)(2,1)} %collective-permute-done.10.refs_1_), channel_id=1, source_target_pairs={{0,15},{1,0},{2,1},{3,2},{4,3},{5,4},{6,5},{7,6},{8,7},{9,8},{10,9... | collective-permute-start | bytes 2359304 | tf_op jit(solution)/shard_map/ppermute | solution.py:149
  79.8 21.7 %collective-permute-start.4 = (bf16[16,4224]{1,0:T(8,128)(2,1)}, bf16[16,4224]{1,0:T(8,128)(2,1)S(1)}, u32[]{:S(2)}, u32[]{:S(2)}) collective-permute-start(bf16[16,4224]{1,0:T(8,128)(2,1)} %get-tuple-element.28), channel_id=1, source_target_pairs={{0,14},{1,15},{2,0},{3,1},{4,2},{5,3},{6,4},{7,5},{8,6},{9,7},{10,... | collective-permute-start | bytes 405512 | tf_op jit(solution)/shard_map/ppermute | solution.py:149
  81.7 21.2 %collective-permute-start.5 = (bf16[16,4224]{1,0:T(8,128)(2,1)}, bf16[16,4224]{1,0:T(8,128)(2,1)S(1)}, u32[]{:S(2)}, u32[]{:S(2)}) collective-permute-start(bf16[16,4224]{1,0:T(8,128)(2,1)} %get-tuple-element.29), channel_id=1, source_target_pairs={{0,15},{1,0},{2,1},{3,2},{4,3},{5,4},{6,5},{7,6},{8,7},{9,8},{10,9... | collective-permute-start | bytes 405512 | tf_op jit(solution)/shard_map/ppermute | solution.py:149
  85.2 17.7 %collective-permute-start.6 = (bf16[16,4224]{1,0:T(8,128)(2,1)S(1)}, bf16[16,4224]{1,0:T(8,128)(2,1)S(1)}, u32[]{:S(2)}, u32[]{:S(2)}) collective-permute-start(bf16[16,4224]{1,0:T(8,128)(2,1)S(1)} %pad_maximum_fusion.2), channel_id=1, source_target_pairs={{0,1},{1,2},{2,3},{3,4},{4,5},{5,6},{6,7},{7,8},{8,9},{9,10},{10,1... | collective-permute-start | bytes 405512 | tf_op jit(solution)/shard_map/ppermute | solution.py:149
  87.7 1.6 copy-start.2
  102.9 18.6 %collective-permute-start.8 = (bf16[384,1024]{1,0:T(8,128)(2,1)}, bf16[384,1024]{1,0:T(8,128)(2,1)S(1)}, u32[]{:S(2)}, u32[]{:S(2)}) collective-permute-start(bf16[384,1024]{1,0:T(8,128)(2,1)} %collective-permute-done.3.refs_0_), channel_id=1, source_target_pairs={{0,1},{1,2},{2,3},{3,4},{4,5},{5,6},{6,7},{7,8},{8,9},{9,10},{10,1... | collective-permute-start | bytes 2359304 | tf_op jit(solution)/shard_map/ppermute | solution.py:149
  104.8 18.6 %collective-permute-start.13 = (bf16[384,1024]{1,0:T(8,128)(2,1)}, bf16[384,1024]{1,0:T(8,128)(2,1)S(1)}, u32[]{:S(2)}, u32[]{:S(2)}) collective-permute-start(bf16[384,1024]{1,0:T(8,128)(2,1)} %collective-permute-done.12.refs_1_), channel_id=1, source_target_pairs={{0,15},{1,0},{2,1},{3,2},{4,3},{5,4},{6,5},{7,6},{8,7},{9,8},{10,9... | collective-permute-start | bytes 2359304 | tf_op jit(solution)/shard_map/ppermute | solution.py:149
  112.7 16.0 %copy-start.3 = (bf16[256,4096]{1,0:T(8,128)(2,1)S(1)}, bf16[256,4096]{1,0:T(8,128)(2,1)}, u32[]{:S(2)}) copy-start(bf16[256,4096]{1,0:T(8,128)(2,1)} %copy-done.1) | copy-start | bytes 6291460
  121.5 17.1 %collective-permute-start.11 = (bf16[384,1024]{1,0:T(8,128)(2,1)S(1)}, bf16[384,1024]{1,0:T(8,128)(2,1)S(1)}, u32[]{:S(2)}, u32[]{:S(2)}) collective-permute-start(bf16[384,1024]{1,0:T(8,128)(2,1)S(1)} %collective-permute-done.8.refs_0_), channel_id=1, source_target_pairs={{0,1},{1,2},{2,3},{3,4},{4,5},{5,6},{6,7},{7,8},{8,9},{9,10},{10,1... | collective-permute-start | bytes 2359304 | tf_op jit(solution)/shard_map/ppermute | solution.py:149
  123.5 16.4 %collective-permute-start.14 = (bf16[384,1024]{1,0:T(8,128)(2,1)S(1)}, bf16[384,1024]{1,0:T(8,128)(2,1)S(1)}, u32[]{:S(2)}, u32[]{:S(2)}) collective-permute-start(bf16[384,1024]{1,0:T(8,128)(2,1)S(1)} %collective-permute-done.13.refs_1_), channel_id=1, source_target_pairs={{0,15},{1,0},{2,1},{3,2},{4,3},{5,4},{6,5},{7,6},{8,7},{9,8},{10,9... | collective-permute-start | bytes 2359304 | tf_op jit(solution)/shard_map/ppermute | solution.py:149
  141.3 10.5 %collective-permute-start.15 = (bf16[16,4096]{1,0:T(8,128)(2,1)S(1)}, bf16[16,4096]{1,0:T(8,128)(2,1)S(1)}, u32[]{:S(2)}, u32[]{:S(2)}) collective-permute-start(bf16[16,4096]{1,0:T(8,128)(2,1)S(1)} %get-tuple-element.44), channel_id=1, source_target_pairs={{0,15},{1,0},{2,1},{3,2},{4,3},{5,4},{6,5},{7,6},{8,7},{9,8},{10,9... | collective-permute-start | bytes 393224 | tf_op jit(solution)/shard_map/ppermute | solution.py:149
  147.0 10.0 %collective-permute-start.16 = (bf16[16,4096]{1,0:T(8,128)(2,1)S(1)}, bf16[16,4096]{1,0:T(8,128)(2,1)S(1)}, u32[]{:S(2)}, u32[]{:S(2)}) collective-permute-start(bf16[16,4096]{1,0:T(8,128)(2,1)S(1)} %get-tuple-element.45), channel_id=1, source_target_pairs={{0,2},{1,3},{2,4},{3,5},{4,6},{5,7},{6,8},{7,9},{8,10},{9,11},{10,... | collective-permute-start | bytes 393224 | tf_op jit(solution)/shard_map/ppermute | solution.py:149
  148.9 9.3 %collective-permute-start.17 = (bf16[16,4096]{1,0:T(8,128)(2,1)S(1)}, bf16[16,4096]{1,0:T(8,128)(2,1)S(1)}, u32[]{:S(2)}, u32[]{:S(2)}) collective-permute-start(bf16[16,4096]{1,0:T(8,128)(2,1)S(1)} %get-tuple-element.46), channel_id=1, source_target_pairs={{0,1},{1,2},{2,3},{3,4},{4,5},{5,6},{6,7},{7,8},{8,9},{9,10},{10,1... | collective-permute-start | bytes 393224 | tf_op jit(solution)/shard_map/ppermute | solution.py:149
